TPU v7x, 32 devices: a whole 2x2x4 slice. The times are simulated.
32 devices in a mesh: groups: 2 (over y), sky: 16 (over z, x, core).
Axes of the slice: x: 2, y: 2, z: 4, core: 2. Of those that a mesh axis runs over, the one named last changes fastest.
Arguments:
- model: float32 [64, 6, 256, 128], P(('groups', 'sky')), parts along dimension 0, may hold values from 0 to 2
- exposures: bfloat16 [4096, 16, 128], P(('groups', 'sky')), parts along dimension 0, may hold values from -6 to 6
- inv_var: float32 [4096], P(('groups', 'sky')), parts along dimension 0, may hold values from 0.5 to 2
- step_size: float32 [6], replicated, may hold values from 0.2 to 0.6
- psf_taps: float32 [64, 56], P(('groups', 'sky')), parts along dimension 0, may hold values from 0.05 to 1
- exp_batch: int32 [4096], P(('groups', 'sky')), parts along dimension 0, may hold values from 0 to 31
- send_plane: int32 [512, 16], P(('groups', 'sky')), parts along dimension 0, may hold values from -1 to 11, as said below
- send_row: int32 [512, 16], P(('groups', 'sky')), parts along dimension 0, may hold values from 0 to 248, as said below
- send_cover: int32 [512, 16], P(('groups', 'sky')), parts along dimension 0, may hold values from 0 to 16, as said below
- use_slot: int32 [4096, 2], P(('groups', 'sky')), parts along dimension 0, may hold values from -1 to 255, as said below
- use_start: int32 [4096, 2], P(('groups', 'sky')), parts along dimension 0, may hold values from 0 to 8, as said below
- use_stop: int32 [4096, 2], P(('groups', 'sky')), parts along dimension 0, may hold values from 0 to 16
- foot_lo: int32 [64], P(('groups', 'sky')), parts along dimension 0, may hold values from 0 to 63
- foot_hi: int32 [64], P(('groups', 'sky')), parts along dimension 0, may hold values from 193 to 256
Outputs:
- updated_model: float32 [64, 6, 256, 128], P(('groups', 'sky')), parts along dimension 0
- residual: float32 [4096, 16, 128], P(('groups', 'sky')), parts along dimension 0
There are 2 independent parts, one for each index of `groups`. A program takes and returns all parts, laid end to end along the dimension named above; an argument that names none is the same for every part. Nothing has to cross between parts.
Inputs may be any that keep to these rules, and one draw needn't show every extreme that they name: In each row of send_plane the covered rows of the live slots (send_cover) sum to at most 128, and on every device some row reaches it. A live slot of exposure owner d is used by exactly one intersection of one exposure on d, and every intersection with use_slot >= 0 names a live slot; all pieces of an exposure come from planes of one band. `send_row`: for a live slot, the tile rows that its piece covers lie inside the tile. send_cover of a live slot equals use_stop - use_start of the intersection that uses it. `use_slot`: each exposure has 1 to 2 live intersections, first in order; -1 after them. `use_start`: the live intersections of an exposure cover rows 0 to 15 in order without gaps; dead ones have start and stop 0.
All inputs are finite; a program needn't handle non-finite values.
Results may differ from a plain program's by a relative error of at most 0.0011.
Values may be sent and summed in bfloat16 or wider, within the bound.
No kernel may reach another device: no remote copies, remote signals or barrier semaphores. Data moves between devices by JAX's collectives and lax.ppermute only.
A program may use at most 128 MiB of HBM per device.

v0:
```python
import functools

import jax
import jax.numpy as jnp
from jax import lax
from jax.experimental import pallas as pl
from jax.experimental.pallas import tpu as pltpu
from jax.sharding import PartitionSpec as P

NPSF = 4
TAPS = 7
ITERS = 2
LANES = 128
HALF = TAPS // 2
FLIP = 64
F32 = jnp.float32
BF16 = jnp.bfloat16
I32 = jnp.int32
VMEM_BYTES = 24 * 1024 * 1024

smem = lambda: pl.BlockSpec(memory_space=pltpu.SMEM)
vmem = lambda: pl.BlockSpec(memory_space=pltpu.VMEM)
hbm = lambda: pl.BlockSpec(memory_space=pl.ANY)


def params():
    return pltpu.CompilerParams(vmem_limit_bytes=VMEM_BYTES)


def aligned(rows):
    return -(-rows // 16) * 16


def pack_slots(plane_ref, row_ref, cover_ref, tile_rows, height, rows_each, x_ref, packed_ref):
    peers, capacity = plane_ref.shape

    def peer(d, _):
        at = d * rows_each
        for c in range(capacity):
            first = jnp.maximum(plane_ref[d, c], 0) * tile_rows + row_ref[d, c]
            packed_ref[pl.ds(at, height), :] = x_ref[pl.ds(first, height), :]
            at = at + cover_ref[d, c]
        return 0

    lax.fori_loop(0, peers, peer, 0)


def bank_rows(taps):
    hp = lax.Precision.HIGHEST
    width = taps.shape[1]

    def grid(columns):
        return (
            lax.broadcasted_iota(I32, (width, columns), 0),
            lax.broadcasted_iota(I32, (width, columns), 1),
        )

    k, l = grid(width)
    total = jnp.dot(taps, (k // TAPS == l // TAPS).astype(F32), precision=hp, preferred_element_type=F32)
    unit = taps / total
    k, l = grid(NPSF * LANES)
    j, l = l // LANES, (l + HALF) % LANES
    wanted = jnp.where(l < TAPS, j * TAPS + TAPS - 1 - l, -1)
    wanted = jnp.where((l >= FLIP) & (l < FLIP + TAPS), j * TAPS + l - FLIP, wanted)
    row_part = jnp.dot(unit, (k == wanted).astype(F32), precision=hp, preferred_element_type=F32)
    k, l = grid(NPSF * TAPS * LANES)
    ji, l = l // LANES, (l + HALF) % LANES
    j, i = ji // TAPS, ji % TAPS
    wanted = NPSF * TAPS + j * TAPS + jnp.where(l < FLIP, i, TAPS - 1 - i)
    col_part = jnp.dot(unit, (k == wanted).astype(F32), precision=hp, preferred_element_type=F32)
    rows = []
    for i in range(TAPS):
        total = 0.0
        for j in range(NPSF):
            at = (j * TAPS + i) * LANES
            total = total + row_part[:, j * LANES : (j + 1) * LANES] * col_part[:, at : at + LANES]
        rows.append(total * (1.0 / NPSF))
    return rows


def first_send_kernel(
    tile_rows, height, rows_each, plane_ref, row_ref, cover_ref, taps_ref, model_ref, out_ref, x_ref, packed_ref, bank_ref, sem
):
    peers = plane_ref.shape[0]
    total = model_ref.shape[0]
    load = pltpu.make_async_copy(model_ref, x_ref.at[pl.ds(0, total), :], sem)
    load.start()
    bank_ref[...] = jnp.zeros(bank_ref.shape, F32)
    for i, row in enumerate(bank_rows(taps_ref[...])):
        for n in range(taps_ref.shape[0]):
            bank_ref[n * TAPS + i : n * TAPS + i + 1, :] = row[n : n + 1, :]
    bank = bank_ref[...].astype(BF16)
    load.wait()
    pack_slots(plane_ref, row_ref, cover_ref, tile_rows, height, rows_each, x_ref, packed_ref)
    for d in range(peers):
        out_ref[d, :rows_each, :] = packed_ref[d * rows_each : (d + 1) * rows_each, :].astype(BF16)
        out_ref[d, rows_each:, :] = bank


def update_kernel(
    bands,
    tile_rows,
    height,
    rows_each,
    last,
    plane_ref,
    row_ref,
    cover_ref,
    step_ref,
    lo_ref,
    hi_ref,
    returned_ref,
    model_ref,
    *rest,
):
    if last:
        new_ref, x_ref, back_ref, scale_ref, sem = rest
    else:
        new_ref, out_ref, x_ref, back_ref, scale_ref, sem, packed_ref = rest
    peers, capacity = plane_ref.shape
    total = model_ref.shape[0]
    planes = total // tile_rows
    load = pltpu.make_async_copy(model_ref, x_ref.at[pl.ds(0, total), :], sem)
    load.start()
    for p in range(planes):
        scale_ref[p] = step_ref[p % bands]
    for d in range(peers):
        back_ref[d * rows_each : (d + 1) * rows_each, :] = returned_ref[d].astype(F32)
    load.wait()
    place = lax.broadcasted_iota(I32, (height, LANES), 0)

    def peer(d, _):
        at = d * rows_each
        for c in range(capacity):
            p = jnp.maximum(plane_ref[d, c], 0)
            first = p * tile_rows + row_ref[d, c]
            cover = cover_ref[d, c]
            piece = jnp.where(place < cover, back_ref[pl.ds(at, height), :], 0.0)
            x_ref[pl.ds(first, height), :] = x_ref[pl.ds(first, height), :] - scale_ref[p] * piece
            at = at + cover
        return 0

    lax.fori_loop(0, peers, peer, 0)

    pos = lax.broadcasted_iota(I32, (tile_rows, LANES), 0)
    for p in range(planes):
        inside = (pos >= lo_ref[p // bands]) & (pos < hi_ref[p // bands])
        here = slice(p * tile_rows, (p + 1) * tile_rows)
        x_ref[here, :] = jnp.where(inside, jnp.maximum(x_ref[here, :], 0.0), 0.0)
    save = pltpu.make_async_copy(x_ref.at[pl.ds(0, total), :], new_ref, sem)
    save.start()
    if not last:
        pack_slots(plane_ref, row_ref, cover_ref, tile_rows, height, rows_each, x_ref, packed_ref)
        for d in range(peers):
            out_ref[d, :, :] = packed_ref[d * rows_each : (d + 1) * rows_each, :].astype(BF16)
    save.wait()


def tables_kernel(capacity, height, rows_each, slot_ref, start_ref, stop_ref, use_ref, move_ref, length_ref):
    exposures, pieces = slot_ref.shape
    slots = move_ref.shape[1]

    def clear(s, _):
        length_ref[s] = 0
        move_ref[0, s] = 0
        return 0

    lax.fori_loop(0, slots, clear, 0, unroll=8)

    def measure(e, _):
        for k in range(pieces):
            s = slot_ref[e, k]

            @pl.when(s >= 0)
            def _():
                length_ref[s] = stop_ref[e, k] - start_ref[e, k]
                move_ref[0, s] = e * height + start_ref[e, k]

        return 0

    lax.fori_loop(0, exposures, measure, 0, unroll=2)

    def lay(o, _):
        at = o * rows_each
        for c in range(capacity):
            s = o * capacity + c
            move_ref[1, s] = at
            at = at + length_ref[s]
        return 0

    lax.fori_loop(0, slots // capacity, lay, 0)

    def point(e, _):
        for k in range(pieces):
            s = slot_ref[e, k]
            live = s >= 0
            begin = move_ref[1, jnp.maximum(s, 0)]
            use_ref[2 * k, e] = jnp.where(live, height + begin - start_ref[e, k], 0)
            use_ref[2 * k + 1, e] = jnp.where(live, start_ref[e, k], height)
        return 0

    lax.fori_loop(0, exposures, point, 0, unroll=2)


def blur_kernel(
    height,
    pieces,
    batches_each,
    last,
    use_ref,
    move_ref,
    weight_ref,
    batch_ref,
    arrived_ref,
    bank_in_ref,
    seen_ref,
    *rest,
):
    if last:
        out_ref, residual_ref, rows_ref, bank_ref, result_ref, packed_ref, fwd_ref, bwd_ref, shift_ref, work_ref = rest
    else:
        out_ref, rows_ref, bank_ref, result_ref, packed_ref, fwd_ref, bwd_ref, shift_ref, work_ref = rest
    peers, rows_each, _ = out_ref.shape
    extra = bank_in_ref.shape[1]
    exposures = batch_ref.shape[0]
    each = LANES // height
    for o in range(peers):
        rows_ref[height + o * rows_each : height + (o + 1) * rows_each, :] = arrived_ref[o].astype(F32)
        bank_ref[o * extra : (o + 1) * extra, :] = bank_in_ref[o].astype(F32)
    place = lax.broadcasted_iota(I32, (height, LANES), 0)
    lane16 = lax.broadcasted_iota(I32, (height, LANES), 1)
    lane = lax.broadcasted_iota(I32, (LANES, LANES), 1)

    def fill_shifts(x):
        for i in range(TAPS):
            v = i - HALF
            if v == 0:
                moved = x
            else:
                moved = pltpu.roll(x, v % LANES, 1)
                moved = jnp.where((lane >= v) & (lane < LANES + v), moved, 0.0)
            shift_ref[i * LANES : (i + 1) * LANES, :] = moved.astype(BF16)

    def group(g, _):
        for n in range(each):
            e = g * each + n
            b = batch_ref[e]
            bank_row = lax.div(b, batches_each) * extra + lax.rem(b, batches_each) * TAPS
            own = (lane16 >= n * height) & (lane16 < (n + 1) * height)
            here = slice(n * height, (n + 1) * height)
            for i in range(TAPS):
                taps = jnp.broadcast_to(bank_ref[pl.ds(bank_row + i, 1), :], (height, LANES))
                there = slice(i * LANES, (i + 1) * LANES)
                f = pltpu.roll(taps, n * height, 1, stride=1, stride_axis=0)
                r = pltpu.roll(taps, (n * height + FLIP) % LANES, 1, stride=1, stride_axis=0)
                fwd_ref[here, there] = jnp.where(own, f, 0.0).astype(BF16)
                bwd_ref[here, there] = jnp.where(own, r, 0.0).astype(BF16)
            stamp = rows_ref[pl.ds(use_ref[0, e], height), :]
            for k in range(1, pieces):
                piece = rows_ref[pl.ds(use_ref[2 * k, e], height), :]
                stamp = jnp.where(place >= use_ref[2 * k + 1, e], piece, stamp)
            work_ref[here, :] = stamp
        fill_shifts(work_ref[...])
        predicted = jnp.dot(fwd_ref[...], shift_ref[...], preferred_element_type=F32)
        for n in range(each):
            e = g * each + n
            here = slice(n * height, (n + 1) * height)
            residual = weight_ref[e] * (predicted[here, :] - seen_ref[e].astype(F32))
            if last:
                residual_ref[e] = residual
            work_ref[here, :] = residual
        fill_shifts(work_ref[...])
        first = pl.multiple_of(g * LANES, LANES)
        result_ref[pl.ds(first, LANES), :] = jnp.dot(bwd_ref[...], shift_ref[...], preferred_element_type=F32)
        return 0

    lax.fori_loop(0, exposures // each, group, 0)

    def move(s, _):
        packed_ref[pl.ds(move_ref[1, s], height), :] = result_ref[pl.ds(move_ref[0, s], height), :]
        return 0

    lax.fori_loop(0, move_ref.shape[1], move, 0, unroll=16)
    for o in range(peers):
        out_ref[o, :, :] = packed_ref[o * rows_each : (o + 1) * rows_each, :].astype(BF16)


def body(
    model,
    exposures,
    inv_var,
    step_size,
    psf_taps,
    exp_batch,
    send_plane,
    send_row,
    send_cover,
    use_slot,
    use_start,
    use_stop,
    foot_lo,
    foot_hi,
):
    tile_count, bands, tile_rows, columns = model.shape
    count, height, _ = exposures.shape
    peers, capacity = send_plane.shape
    pieces = use_slot.shape[1]
    total = tile_count * bands * tile_rows
    rows_each = capacity * height // 2
    extra = aligned(psf_taps.shape[0] * TAPS)
    block = rows_each + extra
    assert columns == LANES and rows_each % extra == 0 and (count * height) % LANES == 0
    x = model.reshape(total, columns)

    def swap(a):
        return lax.all_to_all(a, "sky", split_axis=0, concat_axis=0, tiled=True)

    outbound = pl.pallas_call(
        functools.partial(first_send_kernel, tile_rows, height, rows_each),
        out_shape=jax.ShapeDtypeStruct((peers, block, columns), BF16),
        in_specs=[smem(), smem(), smem(), vmem(), hbm()],
        out_specs=vmem(),
        scratch_shapes=[
            pltpu.VMEM((total + height, columns), F32),
            pltpu.VMEM((peers * rows_each + height, columns), F32),
            pltpu.VMEM((extra, columns), F32),
            pltpu.SemaphoreType.DMA,
        ],
        compiler_params=params(),
        name="first_send",
    )(send_plane, send_row, send_cover, psf_taps, x)
    arrived = swap(outbound)
    use, move = pl.pallas_call(
        functools.partial(tables_kernel, capacity, height, rows_each),
        out_shape=(
            jax.ShapeDtypeStruct((2 * pieces, count), I32),
            jax.ShapeDtypeStruct((2, peers * capacity), I32),
        ),
        in_specs=[smem(), smem(), smem()],
        out_specs=(smem(), smem()),
        scratch_shapes=[pltpu.SMEM((peers * capacity,), I32)],
        cost_estimate=pl.CostEstimate(flops=4_000_000, bytes_accessed=8_000_000, transcendentals=0),
        name="tables",
    )(use_slot, use_start, use_stop)
    with_bank = arrived
    for sweep in range(ITERS):
        last = sweep == ITERS - 1
        rows_shape = jax.ShapeDtypeStruct((peers, rows_each, columns), BF16)
        outs = pl.pallas_call(
            functools.partial(blur_kernel, height, pieces, psf_taps.shape[0], last),
            grid=(1,),
            out_shape=(rows_shape, jax.ShapeDtypeStruct(exposures.shape, F32)) if last else rows_shape,
            in_specs=[
                smem(),
                smem(),
                smem(),
                smem(),
                pl.BlockSpec((peers, rows_each, columns), lambda i: (0, 0, 0)),
                pl.BlockSpec((peers, extra, columns), lambda i: (0, rows_each // extra, 0)),
                vmem(),
            ],
            out_specs=(vmem(), vmem()) if last else vmem(),
            scratch_shapes=[
                pltpu.VMEM((peers * rows_each + 2 * height, columns), F32),
                pltpu.VMEM((peers * extra, columns), F32),
                pltpu.VMEM((count * height + height, columns), F32),
                pltpu.VMEM((peers * rows_each + height, columns), F32),
                pltpu.VMEM((LANES, TAPS * LANES), BF16),
                pltpu.VMEM((LANES, TAPS * LANES), BF16),
                pltpu.VMEM((TAPS * LANES, columns), BF16),
                pltpu.VMEM((LANES, columns), F32),
            ],
            compiler_params=params(),
            name="blur",
        )(use, move, inv_var, exp_batch, arrived, with_bank, exposures)
        outgoing = outs[0] if last else outs
        returned = swap(outgoing)
        new_shape = jax.ShapeDtypeStruct((total, columns), F32)
        scratch = [
            pltpu.VMEM((total + height, columns), F32),
            pltpu.VMEM((peers * rows_each + height, columns), F32),
            pltpu.SMEM((tile_count * bands,), F32),
            pltpu.SemaphoreType.DMA,
        ]
        if not last:
            scratch.append(pltpu.VMEM((peers * rows_each + height, columns), F32))
        res = pl.pallas_call(
            functools.partial(update_kernel, bands, tile_rows, height, rows_each, last),
            out_shape=new_shape if last else (new_shape, rows_shape),
            in_specs=[smem()] * 6 + [vmem(), hbm()],
            out_specs=hbm() if last else (hbm(), vmem()),
            scratch_shapes=scratch,
            compiler_params=params(),
            name="update",
        )(send_plane, send_row, send_cover, step_size, foot_lo, foot_hi, returned, x)
        if last:
            x = res
        else:
            x, outbound = res
            arrived = swap(outbound)
    return (x.reshape(model.shape), outs[1])


def solution(mesh):
    both = ("groups", "sky")
    return jax.shard_map(
        body,
        mesh=mesh,
        in_specs=(
            P(both, None, None, None),
            P(both, None, None),
            P(both),
            P(),
            P(both, None),
            P(both),
            P(both, None),
            P(both, None),
            P(both, None),
            P(both, None),
            P(both, None),
            P(both, None),
            P(both),
            P(both),
        ),
        out_specs=(P(both, None, None, None), P(both, None, None)),
        check_vma=False,
    )
```

profile of v0, /device:TPU:0, one launch (start us, length us, event | category | flops | bytes accessed | tf_op | source)
XLA Modules:
  0.0 121.8 jit_solution(8285037106890962456)
XLA Ops:
  0.6 0.0 copy-start
  0.6 1.4 %copy-done = f32[2,6,256,128]{3,2,1,0:T(8,128)S(1)} copy-done((f32[2,6,256,128]{3,2,1,0:T(8,128)S(1)}, f32[2,6,256,128]{3,2,1,0:T(8,128)}, u32[]{:S(2)}) %copy-start) | copy-done | bytes 1572888
  2.0 0.0 copy-start.3
  2.0 0.7 copy-done.3
  2.7 0.0 copy-start.5
  2.7 0.7 copy-done.5
  3.4 0.0 copy-start.7
  3.4 0.7 copy-done.7
  4.1 0.0 copy-start.16
  4.1 0.7 copy-done.16
  4.8 0.0 copy-start.17
  4.8 0.0 copy-start.18
  4.8 0.0 copy-start.19
  4.8 0.0 copy-start.2
  4.8 0.0 copy-start.14
  4.8 0.0 copy-start.15
  4.8 3.6 %first_send.1 = bf16[16,144,128]{2,1,0:T(8,128)(2,1)} custom-call(s32[16,16]{1,0:T(8,128)S(1)} %copy-done.3, s32[16,16]{1,0:T(8,128)S(1)} %copy-done.5, s32[16,16]{1,0:T(8,128)S(1)} %copy-done.7, f32[2,56]{1,0:T(2,128)S(1)} %copy-done.16, f32[3072,128]{1,0:T(8,128)S(1)} %bitcast.2), custom_call_target="tpu_custom_call" | custom-call | tf_op jit(solution)/shard_map/first_send/pallas_call | solution.py:318
  8.5 7.4 %all-to-all-start = ((bf16[16,144,128]{2,1,0:T(8,128)(2,1)}), bf16[16,144,128]{2,1,0:T(8,128)(2,1)S(1)}, u32[]{:S(2)}, u32[]{:S(2)}) async-start(bf16[16,144,128]{2,1,0:T(8,128)(2,1)} %first_send.1), calls=%async_computation | async-start | bytes 1179648 | tf_op jit(solution)/shard_map/all_to_all | solution.py:316
  15.8 0.0 copy-done.17
  15.8 0.7 copy.16.slot_ref
  16.6 0.0 copy-done.18
  16.6 0.7 copy.17.start_ref
  17.3 0.0 copy-done.19
  17.3 0.7 copy.18.stop_ref
  18.1 9.9 %tables.1 = (s32[4,128]{1,0:T(4,128)}, s32[2,256]{1,0:T(2,128)}) custom-call(s32[128,2]{1,0:T(8,128)} %copy.16.slot_ref, s32[128,2]{1,0:T(8,128)} %copy.17.start_ref, s32[128,2]{1,0:T(8,128)} %copy.18.stop_ref), custom_call_target="tpu_custom_call" | custom-call | flops 4000000 | bytes 8000000 | tf_op jit(solution)/shard_map/tables/pallas_call | solution.py:333
  28.0 3.4 %all-to-all-done.arrived_ref.bank_in_ref = bf16[16,144,128]{2,1,0:T(8,128)(2,1)S(1)} async-done(((bf16[16,144,128]{2,1,0:T(8,128)(2,1)}), bf16[16,144,128]{2,1,0:T(8,128)(2,1)S(1)}, u32[]{:S(2)}, u32[]{:S(2)}) %all-to-all-start) | async-done | bytes 589856 | tf_op jit(solution)/shard_map/all_to_all | solution.py:316
  31.4 0.0 copy-done.2
  31.4 0.0 copy-done.14
  31.4 0.0 copy-done.15
  31.4 0.0 copy-start.9
  31.4 0.7 copy-done.9
  32.1 0.0 copy-start.10
  32.1 0.7 copy-done.10
  32.7 0.0 copy-start.1
  32.7 0.0 copy-start.4
  32.7 0.0 copy-start.6
  32.7 0.0 copy-start.8
  32.7 0.0 copy-start.11
  32.8 0.0 copy-start.12
  32.8 0.0 copy-start.13
  32.8 12.4 %blur.2 = bf16[16,128,128]{2,1,0:T(8,128)(2,1)S(1)} custom-call(s32[4,128]{1,0:T(4,128)S(1)} %copy-done.9, s32[2,256]{1,0:T(2,128)S(1)} %copy-done.10, f32[128]{0:T(128)S(1)} %copy-done.14, s32[128]{0:T(128)S(1)} %copy-done.15, bf16[16,144,128]{2,1,0:T(8,128)(2,1)S(1)} %all-to-all-done.arrived_ref.bank_in_ref, ...), custom_call_target="tpu_custom_call" | custom-call | tf_op jit(solution)/shard_map/blur/pallas_call | solution.py:349
  45.2 18.7 %all_to_all.20.returned_ref = bf16[16,128,128]{2,1,0:T(8,128)(2,1)S(1)} all-to-all(bf16[16,128,128]{2,1,0:T(8,128)(2,1)S(1)} %blur.2), channel_id=1, replica_groups=mesh['groups'=2,'sky'=16] {'sky'}, dimensions={0} | all-to-all | bytes 1048576 | tf_op jit(solution)/shard_map/all_to_all | solution.py:316
  63.9 0.0 copy-done.1
  63.9 0.0 copy-done.4
  63.9 0.0 copy-done.6
  63.9 0.0 copy-done.8
  63.9 0.0 copy-done.11
  63.9 0.0 copy-done.12
  63.9 0.0 copy-done.13
  64.0 3.9 %update.2 = (f32[3072,128]{1,0:T(8,128)S(1)}, bf16[16,128,128]{2,1,0:T(8,128)(2,1)S(1)}) custom-call(s32[16,16]{1,0:T(8,128)S(1)} %copy-done.4, s32[16,16]{1,0:T(8,128)S(1)} %copy-done.6, s32[16,16]{1,0:T(8,128)S(1)} %copy-done.8, f32[6]{0:T(128)S(1)} %copy-done.11, s32[2]{0:T(128)S(1)} %copy-done.12, s32[2]{0:T(128)S(1)} %copy-done.13, ...), custom_call_target="tpu_custom_call" | custom-call | tf_op jit(solution)/shard_map/update/pallas_call | solution.py:387
  67.9 18.4 %all_to_all.21.arrived_ref = bf16[16,128,128]{2,1,0:T(8,128)(2,1)S(1)} all-to-all(bf16[16,128,128]{2,1,0:T(8,128)(2,1)S(1)} %get-tuple-element.10), channel_id=1, replica_groups=mesh['groups'=2,'sky'=16] {'sky'}, dimensions={0} | all-to-all | bytes 1048576 | tf_op jit(solution)/shard_map/all_to_all | solution.py:316
  86.2 13.4 %blur.3 = (bf16[16,128,128]{2,1,0:T(8,128)(2,1)S(1)}, f32[128,16,128]{2,1,0:T(8,128)}) custom-call(s32[4,128]{1,0:T(4,128)S(1)} %copy-done.9, s32[2,256]{1,0:T(2,128)S(1)} %copy-done.10, f32[128]{0:T(128)S(1)} %copy-done.14, s32[128]{0:T(128)S(1)} %copy-done.15, bf16[16,128,128]{2,1,0:T(8,128)(2,1)S(1)} %all_to_all.21.arrived_ref, ...), custom_call_target="tpu_custom_call" | custom-call | tf_op jit(solution)/shard_map/blur/pallas_call | solution.py:349
  99.6 18.4 %all_to_all.22.returned_ref = bf16[16,128,128]{2,1,0:T(8,128)(2,1)S(1)} all-to-all(bf16[16,128,128]{2,1,0:T(8,128)(2,1)S(1)} %get-tuple-element.11), channel_id=1, replica_groups=mesh['groups'=2,'sky'=16] {'sky'}, dimensions={0} | all-to-all | bytes 1048576 | tf_op jit(solution)/shard_map/all_to_all | solution.py:316
  118.0 3.8 %update.3 = f32[3072,128]{1,0:T(8,128)} custom-call(s32[16,16]{1,0:T(8,128)S(1)} %copy-done.4, s32[16,16]{1,0:T(8,128)S(1)} %copy-done.6, s32[16,16]{1,0:T(8,128)S(1)} %copy-done.8, f32[6]{0:T(128)S(1)} %copy-done.11, s32[2]{0:T(128)S(1)} %copy-done.12, s32[2]{0:T(128)S(1)} %copy-done.13, bf16[16,128,128]{2,1,0:T(8,128)(2,1)S(1)} %all_to_all.22.returned_ref, ...), custom_call_target="tpu_custom_call" | custom-call | tf_op jit(solution)/shard_map/update/pallas_call | solution.py:387
Async XLA Ops:
  0.6 1.4 %copy-start = (f32[2,6,256,128]{3,2,1,0:T(8,128)S(1)}, f32[2,6,256,128]{3,2,1,0:T(8,128)}, u32[]{:S(2)}) copy-start(f32[2,6,256,128]{3,2,1,0:T(8,128)} %param.14) | copy-start | bytes 4718596
  2.0 0.7 copy-start.3
  2.7 0.7 copy-start.5
  3.4 0.7 copy-start.7
  4.1 0.7 copy-start.16
  4.8 11.0 %copy-start.17 = (s32[128,2]{0,1:T(2,128)S(1)}, s32[128,2]{0,1:T(2,128)}, u32[]{:S(2)}) copy-start(s32[128,2]{0,1:T(2,128)} %param.23) | copy-start | bytes 3076
  4.8 11.8 %copy-start.18 = (s32[128,2]{0,1:T(2,128)S(1)}, s32[128,2]{0,1:T(2,128)}, u32[]{:S(2)}) copy-start(s32[128,2]{0,1:T(2,128)} %param.24) | copy-start | bytes 3076
  4.8 12.5 %copy-start.19 = (s32[128,2]{0,1:T(2,128)S(1)}, s32[128,2]{0,1:T(2,128)}, u32[]{:S(2)}) copy-start(s32[128,2]{0,1:T(2,128)} %param.25) | copy-start | bytes 3076
  4.8 26.6 %copy-start.2 = (bf16[128,16,128]{2,1,0:T(8,128)(2,1)S(1)}, bf16[128,16,128]{2,1,0:T(8,128)(2,1)}, u32[]{:S(2)}) copy-start(bf16[128,16,128]{2,1,0:T(8,128)(2,1)} %seen_ref.3) | copy-start | bytes 1572868
  4.8 26.6 %copy-start.14 = (f32[128]{0:T(128)S(1)}, f32[128]{0:T(128)}, u32[]{:S(2)}) copy-start(f32[128]{0:T(128)} %weight_ref.3) | copy-start | bytes 1540
  4.8 26.5 %copy-start.15 = (s32[128]{0:T(128)S(1)}, s32[128]{0:T(128)}, u32[]{:S(2)}) copy-start(s32[128]{0:T(128)} %batch_ref.3) | copy-start | bytes 1540
  8.5 22.9 %all-to-all-start = ((bf16[16,144,128]{2,1,0:T(8,128)(2,1)}), bf16[16,144,128]{2,1,0:T(8,128)(2,1)S(1)}, u32[]{:S(2)}, u32[]{:S(2)}) async-start(bf16[16,144,128]{2,1,0:T(8,128)(2,1)} %first_send.1), calls=%async_computation | async-start | bytes 1179648 | tf_op jit(solution)/shard_map/all_to_all | solution.py:316
  31.4 0.7 copy-start.9
  32.1 0.7 copy-start.10
  32.7 31.2 %copy-start.1 = (f32[2,6,256,128]{3,2,1,0:T(8,128)S(1)}, f32[2,6,256,128]{3,2,1,0:T(8,128)}, u32[]{:S(2)}) copy-start(f32[2,6,256,128]{3,2,1,0:T(8,128)} %param.14) | copy-start | bytes 4718596
  32.7 31.2 %copy-start.4 = (s32[16,16]{1,0:T(8,128)S(1)}, s32[16,16]{1,0:T(8,128)}, u32[]{:S(2)}) copy-start(s32[16,16]{1,0:T(8,128)} %plane_ref.5) | copy-start | bytes 3076
  32.7 31.2 %copy-start.6 = (s32[16,16]{1,0:T(8,128)S(1)}, s32[16,16]{1,0:T(8,128)}, u32[]{:S(2)}) copy-start(s32[16,16]{1,0:T(8,128)} %row_ref.5) | copy-start | bytes 3076
  32.7 31.2 %copy-start.8 = (s32[16,16]{1,0:T(8,128)S(1)}, s32[16,16]{1,0:T(8,128)}, u32[]{:S(2)}) copy-start(s32[16,16]{1,0:T(8,128)} %cover_ref.5) | copy-start | bytes 3076
  32.7 31.2 %copy-start.11 = (f32[6]{0:T(128)S(1)}, f32[6]{0:T(128)}, u32[]{:S(2)}) copy-start(f32[6]{0:T(128)} %step_ref.3) | copy-start | bytes 76
  32.8 31.2 %copy-start.12 = (s32[2]{0:T(128)S(1)}, s32[2]{0:T(128)}, u32[]{:S(2)}) copy-start(s32[2]{0:T(128)} %lo_ref.3) | copy-start | bytes 28
  32.8 31.2 %copy-start.13 = (s32[2]{0:T(128)S(1)}, s32[2]{0:T(128)}, u32[]{:S(2)}) copy-start(s32[2]{0:T(128)} %hi_ref.3) | copy-start | bytes 28
where the time goes:
time: 122 us
  blocking collectives  55.4 us (45%)
  Pallas kernels  47 us (39%)
  local copies, waits for them, and re-layouts  7.77 us (6%)
  starting transfers between devices  7.37 us (6%)
  waiting for transfers between devices  3.4 us (3%)
    all_to_all x3, blocking collectives, swap(): return lax.all_to_all(a, 'sky', split_axis=0, concat_axis=0, tiled=True)  55.4 us
    pallas_call x2, Pallas kernels, body(): pl.pallas_call(functools.partial(blur_kernel, height, pieces, psf_taps.sh...  25.8 us
    pallas_call x1, Pallas kernels, body(): pl.pallas_call(functools.partial(tables_kernel, capacity, height, rows_ea...  9.91 us
    unnamed x43, local copies, waits for them, and re-layouts  7.77 us
    pallas_call x2, Pallas kernels, body(): pl.pallas_call(functools.partial(update_kernel, bands, tile_rows, height,...  7.73 us
    all_to_all x1, starting transfers between devices, swap(): return lax.all_to_all(a, 'sky', split_axis=0, concat_axis=0, tiled=True)  7.37 us
    pallas_call x1, Pallas kernels, body(): pl.pallas_call(functools.partial(first_send_kernel, tile_rows, height, ro...  3.6 us
    all_to_all x1, waiting for transfers between devices, swap(): return lax.all_to_all(a, 'sky', split_axis=0, concat_axis=0, tiled=True)  3.4 us
  transfers between devices with their start and end apart: 1, of which 1 were waited for; matrix products, arithmetic and copies ran while one was open for 2% of the time, Pallas kernels for 8%

commit v1 on v0

--- a/solution.py
+++ b/solution.py
@@ -16,7 +16,7 @@
 F32 = jnp.float32
 BF16 = jnp.bfloat16
 I32 = jnp.int32
-VMEM_BYTES = 24 * 1024 * 1024
+VMEM_BYTES = 60 * 1024 * 1024
 
 smem = lambda: pl.BlockSpec(memory_space=pltpu.SMEM)
 vmem = lambda: pl.BlockSpec(memory_space=pltpu.VMEM)
@@ -224,6 +224,7 @@
     extra = bank_in_ref.shape[1]
     exposures = batch_ref.shape[0]
     each = LANES // height
+    abreast = fwd_ref.shape[0]
     for o in range(peers):
         rows_ref[height + o * rows_each : height + (o + 1) * rows_each, :] = arrived_ref[o].astype(F32)
         bank_ref[o * extra : (o + 1) * extra, :] = bank_in_ref[o].astype(F32)
@@ -231,7 +232,7 @@
     lane16 = lax.broadcasted_iota(I32, (height, LANES), 1)
     lane = lax.broadcasted_iota(I32, (LANES, LANES), 1)
 
-    def fill_shifts(x):
+    def fill_shifts(q, x):
         for i in range(TAPS):
             v = i - HALF
             if v == 0:
@@ -239,42 +240,50 @@
             else:
                 moved = pltpu.roll(x, v % LANES, 1)
                 moved = jnp.where((lane >= v) & (lane < LANES + v), moved, 0.0)
-            shift_ref[i * LANES : (i + 1) * LANES, :] = moved.astype(BF16)
-
-    def group(g, _):
-        for n in range(each):
-            e = g * each + n
-            b = batch_ref[e]
-            bank_row = lax.div(b, batches_each) * extra + lax.rem(b, batches_each) * TAPS
-            own = (lane16 >= n * height) & (lane16 < (n + 1) * height)
-            here = slice(n * height, (n + 1) * height)
-            for i in range(TAPS):
-                taps = jnp.broadcast_to(bank_ref[pl.ds(bank_row + i, 1), :], (height, LANES))
-                there = slice(i * LANES, (i + 1) * LANES)
-                f = pltpu.roll(taps, n * height, 1, stride=1, stride_axis=0)
-                r = pltpu.roll(taps, (n * height + FLIP) % LANES, 1, stride=1, stride_axis=0)
-                fwd_ref[here, there] = jnp.where(own, f, 0.0).astype(BF16)
-                bwd_ref[here, there] = jnp.where(own, r, 0.0).astype(BF16)
-            stamp = rows_ref[pl.ds(use_ref[0, e], height), :]
-            for k in range(1, pieces):
-                piece = rows_ref[pl.ds(use_ref[2 * k, e], height), :]
-                stamp = jnp.where(place >= use_ref[2 * k + 1, e], piece, stamp)
-            work_ref[here, :] = stamp
-        fill_shifts(work_ref[...])
-        predicted = jnp.dot(fwd_ref[...], shift_ref[...], preferred_element_type=F32)
-        for n in range(each):
-            e = g * each + n
-            here = slice(n * height, (n + 1) * height)
-            residual = weight_ref[e] * (predicted[here, :] - seen_ref[e].astype(F32))
-            if last:
-                residual_ref[e] = residual
-            work_ref[here, :] = residual
-        fill_shifts(work_ref[...])
-        first = pl.multiple_of(g * LANES, LANES)
-        result_ref[pl.ds(first, LANES), :] = jnp.dot(bwd_ref[...], shift_ref[...], preferred_element_type=F32)
-        return 0
-
-    lax.fori_loop(0, exposures // each, group, 0)
+            shift_ref[q, i * LANES : (i + 1) * LANES, :] = moved.astype(BF16)
+
+    def groups(step, _):
+        for q in range(abreast):
+            g = step * abreast + q
+            for n in range(each):
+                e = g * each + n
+                b = batch_ref[e]
+                bank_row = lax.div(b, batches_each) * extra + lax.rem(b, batches_each) * TAPS
+                own = (lane16 >= n * height) & (lane16 < (n + 1) * height)
+                here = slice(n * height, (n + 1) * height)
+                for i in range(TAPS):
+                    taps = jnp.broadcast_to(bank_ref[pl.ds(bank_row + i, 1), :], (height, LANES))
+                    there = slice(i * LANES, (i + 1) * LANES)
+                    f = pltpu.roll(taps, n * height, 1, stride=1, stride_axis=0)
+                    r = pltpu.roll(taps, (n * height + FLIP) % LANES, 1, stride=1, stride_axis=0)
+                    fwd_ref[q, here, there] = jnp.where(own, f, 0.0).astype(BF16)
+                    bwd_ref[q, here, there] = jnp.where(own, r, 0.0).astype(BF16)
+                stamp = rows_ref[pl.ds(use_ref[0, e], height), :]
+                for k in range(1, pieces):
+                    piece = rows_ref[pl.ds(use_ref[2 * k, e], height), :]
+                    stamp = jnp.where(place >= use_ref[2 * k + 1, e], piece, stamp)
+                work_ref[q, here, :] = stamp
+        for q in range(abreast):
+            fill_shifts(q, work_ref[q])
+        predicted = [
+            jnp.dot(fwd_ref[q], shift_ref[q], preferred_element_type=F32) for q in range(abreast)
+        ]
+        for q in range(abreast):
+            for n in range(each):
+                e = (step * abreast + q) * each + n
+                here = slice(n * height, (n + 1) * height)
+                residual = weight_ref[e] * (predicted[q][here, :] - seen_ref[e].astype(F32))
+                if last:
+                    residual_ref[e] = residual
+                work_ref[q, here, :] = residual
+        for q in range(abreast):
+            fill_shifts(q, work_ref[q])
+        for q in range(abreast):
+            first = pl.multiple_of((step * abreast + q) * LANES, LANES)
+            result_ref[pl.ds(first, LANES), :] = jnp.dot(bwd_ref[q], shift_ref[q], preferred_element_type=F32)
+        return 0
+
+    lax.fori_loop(0, exposures // (each * abreast), groups, 0)
 
     def move(s, _):
         packed_ref[pl.ds(move_ref[1, s], height), :] = result_ref[pl.ds(move_ref[0, s], height), :]
@@ -310,6 +319,8 @@
     extra = aligned(psf_taps.shape[0] * TAPS)
     block = rows_each + extra
     assert columns == LANES and rows_each % extra == 0 and (count * height) % LANES == 0
+    group_count = count * height // LANES
+    abreast = max(n for n in (1, 2, 4) if group_count % n == 0)
     x = model.reshape(total, columns)
 
     def swap(a):
@@ -365,10 +376,10 @@
                 pltpu.VMEM((peers * extra, columns), F32),
                 pltpu.VMEM((count * height + height, columns), F32),
                 pltpu.VMEM((peers * rows_each + height, columns), F32),
-                pltpu.VMEM((LANES, TAPS * LANES), BF16),
-                pltpu.VMEM((LANES, TAPS * LANES), BF16),
-                pltpu.VMEM((TAPS * LANES, columns), BF16),
-                pltpu.VMEM((LANES, columns), F32),
+                pltpu.VMEM((abreast, LANES, TAPS * LANES), BF16),
+                pltpu.VMEM((abreast, LANES, TAPS * LANES), BF16),
+                pltpu.VMEM((abreast, TAPS * LANES, columns), BF16),
+                pltpu.VMEM((abreast, LANES, columns), F32),
             ],
             compiler_params=params(),
             name="blur",

time: 122 us -> 115 us (0.943)
  local copies, waits for them, and re-layouts: 7.77 us -> 3.05 us
  Pallas kernels: 47 us -> 42.8 us
    pallas_call x2, Pallas kernels: 25.8 us -> 17.2 us  [body(): pl.pallas_call(functools.partial(blur_kernel, height, pieces, psf_taps.sh...]
    unnamed x43 -> x11, local copies, waits for them, and re-layouts: 7.77 us -> 3.05 us
    pallas_call x2, Pallas kernels: 7.73 us -> 11.2 us  [body(): pl.pallas_call(functools.partial(update_kernel, bands, tile_rows, height,...]
  transfers between devices with their start and end apart: 1 -> 1, of which waited for: 1 -> 1; matrix products, arithmetic and copies ran while one was open for 2% -> 2% of each run, Pallas kernels for 8% -> 9%
where the time goes in v1:
time: 115 us; the launch traced here: 114 us
  blocking collectives  56.4 us (49%)
  Pallas kernels  42.8 us (37%)
  starting transfers between devices  7.37 us (6%)
  waiting for transfers between devices  3.38 us (3%)
  local copies, waits for them, and re-layouts  3.05 us (3%)
    all_to_all x3, blocking collectives, swap(): return lax.all_to_all(a, 'sky', split_axis=0, concat_axis=0, tiled=True)  56.4 us
    pallas_call x2, Pallas kernels, body(): pl.pallas_call(functools.partial(blur_kernel, height, pieces, psf_taps.sh...  17.2 us
    pallas_call x2, Pallas kernels, body(): pl.pallas_call(functools.partial(update_kernel, bands, tile_rows, height,...  11.2 us
    pallas_call x1, Pallas kernels, body(): pl.pallas_call(functools.partial(tables_kernel, capacity, height, rows_ea...  9.91 us
    all_to_all x1, starting transfers between devices, swap(): return lax.all_to_all(a, 'sky', split_axis=0, concat_axis=0, tiled=True)  7.37 us
    pallas_call x1, Pallas kernels, body(): pl.pallas_call(functools.partial(first_send_kernel, tile_rows, height, ro...  4.41 us
    all_to_all x1, waiting for transfers between devices, swap(): return lax.all_to_all(a, 'sky', split_axis=0, concat_axis=0, tiled=True)  3.38 us
    unnamed x11, local copies, waits for them, and re-layouts  3.05 us
  transfers between devices with their start and end apart: 1, of which 1 were waited for; matrix products, arithmetic and copies ran while one was open for 2% of the time, Pallas kernels for 9%

profile of v1, /device:TPU:0, one launch (start us, length us, event | category | flops | bytes accessed | tf_op | source)
XLA Modules:
  0.0 113.7 jit_solution(1312055071477211077)
XLA Ops:
  0.6 0.0 copy-start.1
  0.6 0.0 copy-start.2
  0.7 0.0 copy-start.3
  0.7 4.4 %first_send.1 = bf16[16,144,128]{2,1,0:T(8,128)(2,1)} custom-call(s32[16,16]{1,0:T(8,128)} %plane_ref.5, s32[16,16]{1,0:T(8,128)} %row_ref.5, s32[16,16]{1,0:T(8,128)} %cover_ref.5, f32[2,56]{1,0:T(2,128)} %taps_ref.1, f32[3072,128]{1,0:T(8,128)} %bitcast.2), custom_call_target="tpu_custom_call" | custom-call | tf_op jit(solution)/shard_map/first_send/pallas_call | solution.py:329
  5.1 7.4 %all-to-all-start = ((bf16[16,144,128]{2,1,0:T(8,128)(2,1)}), bf16[16,144,128]{2,1,0:T(8,128)(2,1)S(1)}, u32[]{:S(2)}, u32[]{:S(2)}) async-start(bf16[16,144,128]{2,1,0:T(8,128)(2,1)} %first_send.1), calls=%async_computation | async-start | bytes 1179648 | tf_op jit(solution)/shard_map/all_to_all | solution.py:327
  12.5 0.0 copy-done.1
  12.5 0.7 copy.16.slot_ref
  13.2 0.0 copy-done.2
  13.2 0.7 copy.17.start_ref
  14.0 0.0 copy-done.3
  14.0 0.7 copy.18.stop_ref
  14.7 9.9 %tables.1 = (s32[4,128]{1,0:T(4,128)}, s32[2,256]{1,0:T(2,128)}) custom-call(s32[128,2]{1,0:T(8,128)} %copy.16.slot_ref, s32[128,2]{1,0:T(8,128)} %copy.17.start_ref, s32[128,2]{1,0:T(8,128)} %copy.18.stop_ref), custom_call_target="tpu_custom_call" | custom-call | flops 4000000 | bytes 8000000 | tf_op jit(solution)/shard_map/tables/pallas_call | solution.py:344
  24.6 3.4 %all-to-all-done.arrived_ref.bank_in_ref = bf16[16,144,128]{2,1,0:T(8,128)(2,1)S(1)} async-done(((bf16[16,144,128]{2,1,0:T(8,128)(2,1)}), bf16[16,144,128]{2,1,0:T(8,128)(2,1)S(1)}, u32[]{:S(2)}, u32[]{:S(2)}) %all-to-all-start) | async-done | bytes 589856 | tf_op jit(solution)/shard_map/all_to_all | solution.py:327
  28.0 0.0 copy-start
  28.0 0.8 copy-done
  28.8 8.4 %blur.2 = bf16[16,128,128]{2,1,0:T(8,128)(2,1)} custom-call(s32[4,128]{1,0:T(4,128)} %get-tuple-element.8.use_ref, s32[2,256]{1,0:T(2,128)} %get-tuple-element.9.move_ref, f32[128]{0:T(128)} %weight_ref.3, s32[128]{0:T(128)} %batch_ref.3, bf16[16,144,128]{2,1,0:T(8,128)(2,1)} %copy-done, bf16[16,144,128]{2,1,0:T(8,128)(2,1)} %copy-done, ...), custom_call_target="tpu_custom_call" | custom-call | tf_op jit(solution)/shard_map/blur/pallas_call | solution.py:360
  37.3 19.0 %all_to_all.20.returned_ref = bf16[16,128,128]{2,1,0:T(8,128)(2,1)} all-to-all(bf16[16,128,128]{2,1,0:T(8,128)(2,1)} %blur.2), channel_id=1, replica_groups=mesh['groups'=2,'sky'=16] {'sky'}, dimensions={0} | all-to-all | bytes 1048576 | tf_op jit(solution)/shard_map/all_to_all | solution.py:327
  56.3 6.0 %update.2 = (f32[3072,128]{1,0:T(8,128)}, bf16[16,128,128]{2,1,0:T(8,128)(2,1)}) custom-call(s32[16,16]{1,0:T(8,128)} %plane_ref.5, s32[16,16]{1,0:T(8,128)} %row_ref.5, s32[16,16]{1,0:T(8,128)} %cover_ref.5, f32[6]{0:T(128)} %step_ref.3, s32[2]{0:T(128)} %lo_ref.3, s32[2]{0:T(128)} %hi_ref.3, bf16[16,128,128]{2,1,0:T(8,128)(2,1)} %all_to_all.20.returned_ref, ...), custom_call_target="tpu_custom_call" | custom-call | tf_op jit(solution)/shard_map/update/pallas_call | solution.py:398
  62.3 18.7 %all_to_all.21.arrived_ref = bf16[16,128,128]{2,1,0:T(8,128)(2,1)} all-to-all(bf16[16,128,128]{2,1,0:T(8,128)(2,1)} %get-tuple-element.10), channel_id=1, replica_groups=mesh['groups'=2,'sky'=16] {'sky'}, dimensions={0} | all-to-all | bytes 1048576 | tf_op jit(solution)/shard_map/all_to_all | solution.py:327
  81.0 8.8 %blur.3 = (bf16[16,128,128]{2,1,0:T(8,128)(2,1)}, f32[128,16,128]{2,1,0:T(8,128)}) custom-call(s32[4,128]{1,0:T(4,128)} %get-tuple-element.8.use_ref, s32[2,256]{1,0:T(2,128)} %get-tuple-element.9.move_ref, f32[128]{0:T(128)} %weight_ref.3, s32[128]{0:T(128)} %batch_ref.3, bf16[16,128,128]{2,1,0:T(8,128)(2,1)} %all_to_all.21.arrived_ref, ...), custom_call_target="tpu_custom_call" | custom-call | tf_op jit(solution)/shard_map/blur/pallas_call | solution.py:360
  89.8 18.7 %all_to_all.22.returned_ref = bf16[16,128,128]{2,1,0:T(8,128)(2,1)} all-to-all(bf16[16,128,128]{2,1,0:T(8,128)(2,1)} %get-tuple-element.11), channel_id=1, replica_groups=mesh['groups'=2,'sky'=16] {'sky'}, dimensions={0} | all-to-all | bytes 1048576 | tf_op jit(solution)/shard_map/all_to_all | solution.py:327
  108.5 5.2 %update.3 = f32[3072,128]{1,0:T(8,128)} custom-call(s32[16,16]{1,0:T(8,128)} %plane_ref.5, s32[16,16]{1,0:T(8,128)} %row_ref.5, s32[16,16]{1,0:T(8,128)} %cover_ref.5, f32[6]{0:T(128)} %step_ref.3, s32[2]{0:T(128)} %lo_ref.3, s32[2]{0:T(128)} %hi_ref.3, bf16[16,128,128]{2,1,0:T(8,128)(2,1)} %all_to_all.22.returned_ref, f32[3072,128]{1,0:T(8,128)} %get-tuple-element.12.model_ref), custom_call_target="tpu_custom_call" | custom-call | tf_op jit(solution)/shard_map/update/pallas_call | solution.py:398
Async XLA Ops:
  0.6 11.8 %copy-start.1 = (s32[128,2]{0,1:T(2,128)S(1)}, s32[128,2]{0,1:T(2,128)}, u32[]{:S(2)}) copy-start(s32[128,2]{0,1:T(2,128)} %param.23) | copy-start | bytes 3076
  0.6 12.6 %copy-start.2 = (s32[128,2]{0,1:T(2,128)S(1)}, s32[128,2]{0,1:T(2,128)}, u32[]{:S(2)}) copy-start(s32[128,2]{0,1:T(2,128)} %param.24) | copy-start | bytes 3076
  0.7 13.3 %copy-start.3 = (s32[128,2]{0,1:T(2,128)S(1)}, s32[128,2]{0,1:T(2,128)}, u32[]{:S(2)}) copy-start(s32[128,2]{0,1:T(2,128)} %param.25) | copy-start | bytes 3076
  5.1 22.9 %all-to-all-start = ((bf16[16,144,128]{2,1,0:T(8,128)(2,1)}), bf16[16,144,128]{2,1,0:T(8,128)(2,1)S(1)}, u32[]{:S(2)}, u32[]{:S(2)}) async-start(bf16[16,144,128]{2,1,0:T(8,128)(2,1)} %first_send.1), calls=%async_computation | async-start | bytes 1179648 | tf_op jit(solution)/shard_map/all_to_all | solution.py:327
  28.0 0.8 copy-start

commit v2 on v1

--- a/solution.py
+++ b/solution.py
@@ -16,15 +16,26 @@
 F32 = jnp.float32
 BF16 = jnp.bfloat16
 I32 = jnp.int32
-VMEM_BYTES = 60 * 1024 * 1024
+VMEM_BYTES = 24 * 1024 * 1024
 
 smem = lambda: pl.BlockSpec(memory_space=pltpu.SMEM)
 vmem = lambda: pl.BlockSpec(memory_space=pltpu.VMEM)
 hbm = lambda: pl.BlockSpec(memory_space=pl.ANY)
 
 
-def params():
-    return pltpu.CompilerParams(vmem_limit_bytes=VMEM_BYTES)
+def params(share=1.0):
+    return pltpu.CompilerParams(vmem_limit_bytes=int(share * VMEM_BYTES))
+
+
+def each_peer(peers, refs):
+    if len(refs) == 1:
+        return [(o, refs[0].at[o]) for o in range(peers)]
+    me = lax.axis_index("sky")
+    return [(me ^ k, ref) for k, ref in enumerate(refs)]
+
+
+def rows_of(o, count, offset=0):
+    return pl.ds(pl.multiple_of(o * count + offset, 16), count)
 
 
 def aligned(rows):
@@ -79,8 +90,9 @@
 
 
 def first_send_kernel(
-    tile_rows, height, rows_each, plane_ref, row_ref, cover_ref, taps_ref, model_ref, out_ref, x_ref, packed_ref, bank_ref, sem
+    tile_rows, height, rows_each, plane_ref, row_ref, cover_ref, taps_ref, model_ref, *rest
 ):
+    *out_refs, x_ref, packed_ref, bank_ref, sem = rest
     peers = plane_ref.shape[0]
     total = model_ref.shape[0]
     load = pltpu.make_async_copy(model_ref, x_ref.at[pl.ds(0, total), :], sem)
@@ -92,9 +104,9 @@
     bank = bank_ref[...].astype(BF16)
     load.wait()
     pack_slots(plane_ref, row_ref, cover_ref, tile_rows, height, rows_each, x_ref, packed_ref)
-    for d in range(peers):
-        out_ref[d, :rows_each, :] = packed_ref[d * rows_each : (d + 1) * rows_each, :].astype(BF16)
-        out_ref[d, rows_each:, :] = bank
+    for d, out_ref in each_peer(peers, out_refs):
+        out_ref[:rows_each, :] = packed_ref[rows_of(d, rows_each), :].astype(BF16)
+        out_ref[rows_each:, :] = bank
 
 
 def update_kernel(
@@ -102,6 +114,7 @@
     tile_rows,
     height,
     rows_each,
+    parts,
     last,
     plane_ref,
     row_ref,
@@ -109,14 +122,14 @@
     step_ref,
     lo_ref,
     hi_ref,
-    returned_ref,
     model_ref,
     *rest,
 ):
+    returned_refs, rest = rest[:parts], rest[parts:]
     if last:
         new_ref, x_ref, back_ref, scale_ref, sem = rest
     else:
-        new_ref, out_ref, x_ref, back_ref, scale_ref, sem, packed_ref = rest
+        new_ref, *out_refs, x_ref, back_ref, scale_ref, sem, packed_ref = rest
     peers, capacity = plane_ref.shape
     total = model_ref.shape[0]
     planes = total // tile_rows
@@ -124,8 +137,8 @@
     load.start()
     for p in range(planes):
         scale_ref[p] = step_ref[p % bands]
-    for d in range(peers):
-        back_ref[d * rows_each : (d + 1) * rows_each, :] = returned_ref[d].astype(F32)
+    for d, returned_ref in each_peer(peers, returned_refs):
+        back_ref[rows_of(d, rows_each), :] = returned_ref[...].astype(F32)
     load.wait()
     place = lax.broadcasted_iota(I32, (height, LANES), 0)
 
@@ -151,8 +164,8 @@
     save.start()
     if not last:
         pack_slots(plane_ref, row_ref, cover_ref, tile_rows, height, rows_each, x_ref, packed_ref)
-        for d in range(peers):
-            out_ref[d, :, :] = packed_ref[d * rows_each : (d + 1) * rows_each, :].astype(BF16)
+        for d, out_ref in each_peer(peers, out_refs):
+            out_ref[...] = packed_ref[rows_of(d, rows_each), :].astype(BF16)
     save.wait()
 
 
@@ -206,28 +219,29 @@
     height,
     pieces,
     batches_each,
+    peers,
+    parts,
     last,
     use_ref,
     move_ref,
     weight_ref,
     batch_ref,
-    arrived_ref,
-    bank_in_ref,
     seen_ref,
     *rest,
 ):
+    arrived_refs, bank_in_refs, out_refs, rest = rest[:parts], rest[parts : 2 * parts], rest[2 * parts : 3 * parts], rest[3 * parts :]
     if last:
-        out_ref, residual_ref, rows_ref, bank_ref, result_ref, packed_ref, fwd_ref, bwd_ref, shift_ref, work_ref = rest
-    else:
-        out_ref, rows_ref, bank_ref, result_ref, packed_ref, fwd_ref, bwd_ref, shift_ref, work_ref = rest
-    peers, rows_each, _ = out_ref.shape
-    extra = bank_in_ref.shape[1]
+        residual_ref, *rest = rest
+    rows_ref, bank_ref, result_ref, packed_ref, fwd_ref, bwd_ref, shift_ref, work_ref = rest
+    rows_each = out_refs[0].shape[-2]
+    extra = bank_in_refs[0].shape[-2]
     exposures = batch_ref.shape[0]
     each = LANES // height
     abreast = fwd_ref.shape[0]
-    for o in range(peers):
-        rows_ref[height + o * rows_each : height + (o + 1) * rows_each, :] = arrived_ref[o].astype(F32)
-        bank_ref[o * extra : (o + 1) * extra, :] = bank_in_ref[o].astype(F32)
+    for o, arrived_ref in each_peer(peers, arrived_refs):
+        rows_ref[rows_of(o, rows_each, height), :] = arrived_ref[...].astype(F32)
+    for o, bank_in_ref in each_peer(peers, bank_in_refs):
+        bank_ref[rows_of(o, extra), :] = bank_in_ref[...].astype(F32)
     place = lax.broadcasted_iota(I32, (height, LANES), 0)
     lane16 = lax.broadcasted_iota(I32, (height, LANES), 1)
     lane = lax.broadcasted_iota(I32, (LANES, LANES), 1)
@@ -290,8 +304,8 @@
         return 0
 
     lax.fori_loop(0, move_ref.shape[1], move, 0, unroll=16)
-    for o in range(peers):
-        out_ref[o, :, :] = packed_ref[o * rows_each : (o + 1) * rows_each, :].astype(BF16)
+    for o, out_ref in each_peer(peers, out_refs):
+        out_ref[...] = packed_ref[rows_of(o, rows_each), :].astype(BF16)
 
 
 def body(
@@ -323,21 +337,39 @@
     abreast = max(n for n in (1, 2, 4) if group_count % n == 0)
     x = model.reshape(total, columns)
 
-    def swap(a):
-        return lax.all_to_all(a, "sky", split_axis=0, concat_axis=0, tiled=True)
+    paired = peers <= 16 and peers & (peers - 1) == 0
+    parts = peers if paired else 1
+
+    def part_shapes(rows):
+        if paired:
+            return [jax.ShapeDtypeStruct((rows, columns), BF16)] * parts
+        return [jax.ShapeDtypeStruct((peers, rows, columns), BF16)]
+
+    def part_specs(rows, at=0):
+        if paired:
+            return [pl.BlockSpec((rows, columns), lambda i: (at, 0))] * parts
+        return [pl.BlockSpec((peers, rows, columns), lambda i: (0, at, 0))]
+
+    def swap(blocks):
+        if not paired:
+            return [lax.all_to_all(blocks[0], "sky", split_axis=0, concat_axis=0, tiled=True)]
+        moved = {0: blocks[0]}
+        for k in range(peers - 1, 0, -1):
+            moved[k] = lax.ppermute(blocks[k], "sky", [(i, i ^ k) for i in range(peers)])
+        return [moved[k] for k in range(peers)]
 
     outbound = pl.pallas_call(
         functools.partial(first_send_kernel, tile_rows, height, rows_each),
-        out_shape=jax.ShapeDtypeStruct((peers, block, columns), BF16),
+        out_shape=part_shapes(block),
         in_specs=[smem(), smem(), smem(), vmem(), hbm()],
-        out_specs=vmem(),
+        out_specs=[vmem()] * parts,
         scratch_shapes=[
             pltpu.VMEM((total + height, columns), F32),
             pltpu.VMEM((peers * rows_each + height, columns), F32),
             pltpu.VMEM((extra, columns), F32),
             pltpu.SemaphoreType.DMA,
         ],
-        compiler_params=params(),
+        compiler_params=params(2.5),
         name="first_send",
     )(send_plane, send_row, send_cover, psf_taps, x)
     arrived = swap(outbound)
@@ -356,21 +388,13 @@
     with_bank = arrived
     for sweep in range(ITERS):
         last = sweep == ITERS - 1
-        rows_shape = jax.ShapeDtypeStruct((peers, rows_each, columns), BF16)
+        residual_shape = [jax.ShapeDtypeStruct(exposures.shape, F32)] if last else []
         outs = pl.pallas_call(
-            functools.partial(blur_kernel, height, pieces, psf_taps.shape[0], last),
+            functools.partial(blur_kernel, height, pieces, psf_taps.shape[0], peers, parts, last),
             grid=(1,),
-            out_shape=(rows_shape, jax.ShapeDtypeStruct(exposures.shape, F32)) if last else rows_shape,
-            in_specs=[
-                smem(),
-                smem(),
-                smem(),
-                smem(),
-                pl.BlockSpec((peers, rows_each, columns), lambda i: (0, 0, 0)),
-                pl.BlockSpec((peers, extra, columns), lambda i: (0, rows_each // extra, 0)),
-                vmem(),
-            ],
-            out_specs=(vmem(), vmem()) if last else vmem(),
+            out_shape=part_shapes(rows_each) + residual_shape,
+            in_specs=[smem()] * 4 + [vmem()] + part_specs(rows_each) + part_specs(extra, rows_each // extra),
+            out_specs=[vmem()] * (parts + len(residual_shape)),
             scratch_shapes=[
                 pltpu.VMEM((peers * rows_each + 2 * height, columns), F32),
                 pltpu.VMEM((peers * extra, columns), F32),
@@ -383,33 +407,29 @@
             ],
             compiler_params=params(),
             name="blur",
-        )(use, move, inv_var, exp_batch, arrived, with_bank, exposures)
-        outgoing = outs[0] if last else outs
-        returned = swap(outgoing)
-        new_shape = jax.ShapeDtypeStruct((total, columns), F32)
+        )(use, move, inv_var, exp_batch, exposures, *arrived, *with_bank)
+        returned = swap(outs[:parts])
         scratch = [
             pltpu.VMEM((total + height, columns), F32),
             pltpu.VMEM((peers * rows_each + height, columns), F32),
             pltpu.SMEM((tile_count * bands,), F32),
             pltpu.SemaphoreType.DMA,
         ]
+        sends = 0 if last else parts
         if not last:
             scratch.append(pltpu.VMEM((peers * rows_each + height, columns), F32))
-        res = pl.pallas_call(
-            functools.partial(update_kernel, bands, tile_rows, height, rows_each, last),
-            out_shape=new_shape if last else (new_shape, rows_shape),
-            in_specs=[smem()] * 6 + [vmem(), hbm()],
-            out_specs=hbm() if last else (hbm(), vmem()),
+        x, *outbound = pl.pallas_call(
+            functools.partial(update_kernel, bands, tile_rows, height, rows_each, parts, last),
+            out_shape=[jax.ShapeDtypeStruct((total, columns), F32)] + part_shapes(rows_each)[:sends],
+            in_specs=[smem()] * 6 + [hbm()] + [vmem()] * parts,
+            out_specs=[hbm()] + [vmem()] * sends,
             scratch_shapes=scratch,
             compiler_params=params(),
             name="update",
-        )(send_plane, send_row, send_cover, step_size, foot_lo, foot_hi, returned, x)
-        if last:
-            x = res
-        else:
-            x, outbound = res
+        )(send_plane, send_row, send_cover, step_size, foot_lo, foot_hi, x, *returned)
+        if not last:
             arrived = swap(outbound)
-    return (x.reshape(model.shape), outs[1])
+    return (x.reshape(model.shape), outs[parts])
 
 
 def solution(mesh):

time: 115 us -> 145 us (1.26)
  starting transfers between devices: 7.37 us -> 83.5 us
  blocking collectives: 56.4 us -> 0 us
  waiting for transfers between devices: 3.38 us -> 14.9 us
  Pallas kernels: 42.8 us -> 37.6 us
  local copies, waits for them, and re-layouts: 3.05 us -> 7.69 us
    ppermute x0 -> x60, starting transfers between devices: none -> 83.5 us  [swap(): lax.ppermute(blocks[k], 'sky', [(i, i ^ k) for i in range(peers)])]
    all_to_all x3 -> x0, blocking collectives: 56.4 us -> none  [swap(): return lax.all_to_all(a, 'sky', split_axis=0, concat_axis=0, tiled=True)]
    ppermute x0 -> x60, waiting for transfers between devices: none -> 14.9 us  [swap(): lax.ppermute(blocks[k], 'sky', [(i, i ^ k) for i in range(peers)])]
    all_to_all x1 -> x0, starting transfers between devices: 7.37 us -> none  [swap(): return lax.all_to_all(a, 'sky', split_axis=0, concat_axis=0, tiled=True)]
    unnamed x11 -> x35, local copies, waits for them, and re-layouts: 3.05 us -> 7.69 us
    all_to_all x1 -> x0, waiting for transfers between devices: 3.38 us -> none  [swap(): return lax.all_to_all(a, 'sky', split_axis=0, concat_axis=0, tiled=True)]
    pallas_call x2, Pallas kernels: 11.2 us -> 8.02 us  [body(): pl.pallas_call(functools.partial(update_kernel, bands, tile_rows, height,...]
    pallas_call x2, Pallas kernels: 17.2 us -> 15.2 us  [body(): pl.pallas_call(functools.partial(blur_kernel, height, pieces, psf_taps.sh...]
  transfers between devices with their start and end apart: 1 -> 60, of which waited for: 1 -> 9; matrix products, arithmetic and copies ran while one was open for 2% -> 3% of each run, Pallas kernels for 9% -> 7%
where the time goes in v2:
time: 145 us
  starting transfers between devices  83.5 us (58%)
  Pallas kernels  37.6 us (26%)
  waiting for transfers between devices  14.9 us (10%)
  local copies, waits for them, and re-layouts  7.69 us (5%)
    ppermute x60, starting transfers between devices, swap(): lax.ppermute(blocks[k], 'sky', [(i, i ^ k) for i in range(peers)])  83.5 us
    pallas_call x2, Pallas kernels, body(): pl.pallas_call(functools.partial(blur_kernel, height, pieces, psf_taps.sh...  15.2 us
    ppermute x60, waiting for transfers between devices, swap(): lax.ppermute(blocks[k], 'sky', [(i, i ^ k) for i in range(peers)])  14.9 us
    pallas_call x1, Pallas kernels, body(): pl.pallas_call(functools.partial(tables_kernel, capacity, height, rows_ea...  9.91 us
    pallas_call x2, Pallas kernels, body(): pl.pallas_call(functools.partial(update_kernel, bands, tile_rows, height,...  8.02 us
    unnamed x35, local copies, waits for them, and re-layouts  7.69 us
    pallas_call x1, Pallas kernels, body(): pl.pallas_call(functools.partial(first_send_kernel, tile_rows, height, ro...  4.42 us
  transfers between devices with their start and end apart: 60, of which 9 were waited for; matrix products, arithmetic and copies ran while one was open for 3% of the time, Pallas kernels for 7%

profile of v2, /device:TPU:0, one launch (start us, length us, event | category | flops | bytes accessed | tf_op | source)
XLA Modules:
  0.0 144.5 jit_solution(12679806245840278121)
XLA Ops:
  0.6 4.4 %first_send.1 = (bf16[144,128]{1,0:T(8,128)(2,1)}, bf16[144,128]{1,0:T(8,128)(2,1)}, bf16[144,128]{1,0:T(8,128)(2,1)}, bf16[144,128]{1,0:T(8,128)(2,1)}, bf16[14...) custom-call(s32[16,16]{1,0:T(8,128)} %plane_ref.5, ...), custom_call_target="tpu_custom_call" | custom-call | tf_op jit(solution)/shard_map/first_send/pallas_call | solution.py:361
  5.1 0.5 collective-permute-start
  5.6 2.6 %collective-permute-start.1 = (bf16[144,128]{1,0:T(8,128)(2,1)}, bf16[144,128]{1,0:T(8,128)(2,1)S(1)}, u32[]{:S(2)}, u32[]{:S(2)}) collective-permute-start(bf16[144,128]{1,0:T(8,128)(2,1)} %get-tuple-element.74), channel_id=1, source_target_pairs={{0,2},{1,3},{2,0},{3,1},{4,6},{5,7},{6,4},{7,5},{8,10},{9,11},{10,... | collective-permute-start | bytes 110600 | tf_op jit(solution)/shard_map/ppermute | solution.py:358
  8.2 1.8 %collective-permute-start.3 = (bf16[144,128]{1,0:T(8,128)(2,1)}, bf16[144,128]{1,0:T(8,128)(2,1)S(1)}, u32[]{:S(2)}, u32[]{:S(2)}) collective-permute-start(bf16[144,128]{1,0:T(8,128)(2,1)} %get-tuple-element.76), channel_id=1, source_target_pairs={{0,4},{1,5},{2,6},{3,7},{4,0},{5,1},{6,2},{7,3},{8,12},{9,13},{10,... | collective-permute-start | bytes 110600 | tf_op jit(solution)/shard_map/ppermute | solution.py:358
  10.1 2.6 %collective-permute-start.5 = (bf16[144,128]{1,0:T(8,128)(2,1)}, bf16[144,128]{1,0:T(8,128)(2,1)S(1)}, u32[]{:S(2)}, u32[]{:S(2)}) collective-permute-start(bf16[144,128]{1,0:T(8,128)(2,1)} %get-tuple-element.78), channel_id=1, source_target_pairs={{0,6},{1,7},{2,4},{3,5},{4,2},{5,3},{6,0},{7,1},{8,14},{9,15},{10,... | collective-permute-start | bytes 110600 | tf_op jit(solution)/shard_map/ppermute | solution.py:358
  12.8 2.7 %collective-permute-start.7 = (bf16[144,128]{1,0:T(8,128)(2,1)}, bf16[144,128]{1,0:T(8,128)(2,1)S(1)}, u32[]{:S(2)}, u32[]{:S(2)}) collective-permute-start(bf16[144,128]{1,0:T(8,128)(2,1)} %get-tuple-element.80), channel_id=1, source_target_pairs={{0,8},{1,9},{2,10},{3,11},{4,12},{5,13},{6,14},{7,15},{8,0},{9,1},... | collective-permute-start | bytes 110600 | tf_op jit(solution)/shard_map/ppermute | solution.py:358
  15.5 0.6 collective-permute-start.8
  16.1 2.9 %collective-permute-start.9 = (bf16[144,128]{1,0:T(8,128)(2,1)}, bf16[144,128]{1,0:T(8,128)(2,1)S(1)}, u32[]{:S(2)}, u32[]{:S(2)}) collective-permute-start(bf16[144,128]{1,0:T(8,128)(2,1)} %get-tuple-element.82), channel_id=1, source_target_pairs={{0,10},{1,11},{2,8},{3,9},{4,14},{5,15},{6,12},{7,13},{8,2},{9,3},... | collective-permute-start | bytes 110600 | tf_op jit(solution)/shard_map/ppermute | solution.py:358
  19.4 3.3 %collective-permute-start.11 = (bf16[144,128]{1,0:T(8,128)(2,1)}, bf16[144,128]{1,0:T(8,128)(2,1)S(1)}, u32[]{:S(2)}, u32[]{:S(2)}) collective-permute-start(bf16[144,128]{1,0:T(8,128)(2,1)} %get-tuple-element.84), channel_id=1, source_target_pairs={{0,12},{1,13},{2,14},{3,15},{4,8},{5,9},{6,10},{7,11},{8,4},{9,5},... | collective-permute-start | bytes 110600 | tf_op jit(solution)/shard_map/ppermute | solution.py:358
  22.7 0.5 collective-permute-start.12
  23.2 3.9 %collective-permute-start.13 = (bf16[144,128]{1,0:T(8,128)(2,1)}, bf16[144,128]{1,0:T(8,128)(2,1)S(1)}, u32[]{:S(2)}, u32[]{:S(2)}) collective-permute-start(bf16[144,128]{1,0:T(8,128)(2,1)} %get-tuple-element.86), channel_id=1, source_target_pairs={{0,14},{1,15},{2,12},{3,13},{4,10},{5,11},{6,8},{7,9},{8,6},{9,7},... | collective-permute-start | bytes 110600 | tf_op jit(solution)/shard_map/ppermute | solution.py:358
  27.5 1.4 copy.16.slot_ref
  28.9 1.4 copy.17.start_ref
  30.3 1.4 copy.18.stop_ref
  31.7 9.9 %tables.1 = (s32[4,128]{1,0:T(4,128)}, s32[2,256]{1,0:T(2,128)}) custom-call(s32[128,2]{1,0:T(8,128)} %copy.16.slot_ref, s32[128,2]{1,0:T(8,128)} %copy.17.start_ref, s32[128,2]{1,0:T(8,128)} %copy.18.stop_ref), custom_call_target="tpu_custom_call" | custom-call | flops 4000000 | bytes 8000000 | tf_op jit(solution)/shard_map/tables/pallas_call | solution.py:376
  41.7 0.8 copy-done.2
  42.5 0.7 copy-done.7
  43.1 0.7 copy-done.9
  43.8 0.7 copy-done.11
  44.4 0.7 copy-done.12
  45.2 7.1 %blur.2 = (bf16[128,128]{1,0:T(8,128)(2,1)S(1)}, bf16[128,128]{1,0:T(8,128)(2,1)S(1)}, bf16[128,128]{1,0:T(8,128)(2,1)S(1)}, bf16[128,128]{1,0:T(8,128)(2,1)S(1)...) custom-call(s32[4,128]{1,0:T(4,128)S(1)} %copy-done.7, ...), custom_call_target="tpu_custom_call" | custom-call | tf_op jit(solution)/shard_map/blur/pallas_call | solution.py:392
  52.3 0.6 collective-permute-start.15
  52.9 1.0 collective-permute-start.16
  54.4 2.1 %collective-permute-start.19 = (bf16[128,128]{1,0:T(8,128)(2,1)S(1)}, bf16[128,128]{1,0:T(8,128)(2,1)S(1)}, u32[]{:S(2)}, u32[]{:S(2)}) collective-permute-start(bf16[128,128]{1,0:T(8,128)(2,1)S(1)} %get-tuple-element.93), channel_id=1, source_target_pairs={{0,5},{1,4},{2,7},{3,6},{4,1},{5,0},{6,3},{7,2},{8,13},{9,12},{10,... | collective-permute-start | bytes 98312 | tf_op jit(solution)/shard_map/ppermute | solution.py:358
  56.4 0.8 collective-permute-start.20
  57.2 1.5 %collective-permute-start.21 = (bf16[128,128]{1,0:T(8,128)(2,1)S(1)}, bf16[128,128]{1,0:T(8,128)(2,1)S(1)}, u32[]{:S(2)}, u32[]{:S(2)}) collective-permute-start(bf16[128,128]{1,0:T(8,128)(2,1)S(1)} %get-tuple-element.95), channel_id=1, source_target_pairs={{0,7},{1,6},{2,5},{3,4},{4,3},{5,2},{6,1},{7,0},{8,15},{9,14},{10,... | collective-permute-start | bytes 98312 | tf_op jit(solution)/shard_map/ppermute | solution.py:358
  58.8 2.2 %collective-permute-start.22 = (bf16[128,128]{1,0:T(8,128)(2,1)S(1)}, bf16[128,128]{1,0:T(8,128)(2,1)S(1)}, u32[]{:S(2)}, u32[]{:S(2)}) collective-permute-start(bf16[128,128]{1,0:T(8,128)(2,1)S(1)} %get-tuple-element.96), channel_id=1, source_target_pairs={{0,8},{1,9},{2,10},{3,11},{4,12},{5,13},{6,14},{7,15},{8,0},{9,1},... | collective-permute-start | bytes 98312 | tf_op jit(solution)/shard_map/ppermute | solution.py:358
  61.0 0.8 collective-permute-start.23
  61.7 2.8 %collective-permute-start.24 = (bf16[128,128]{1,0:T(8,128)(2,1)S(1)}, bf16[128,128]{1,0:T(8,128)(2,1)S(1)}, u32[]{:S(2)}, u32[]{:S(2)}) collective-permute-start(bf16[128,128]{1,0:T(8,128)(2,1)S(1)} %get-tuple-element.98), channel_id=1, source_target_pairs={{0,10},{1,11},{2,8},{3,9},{4,14},{5,15},{6,12},{7,13},{8,2},{9,3},... | collective-permute-start | bytes 98312 | tf_op jit(solution)/shard_map/ppermute | solution.py:358
  64.5 0.4 collective-permute-start.25
  65.0 3.1 %collective-permute-start.26 = (bf16[128,128]{1,0:T(8,128)(2,1)S(1)}, bf16[128,128]{1,0:T(8,128)(2,1)S(1)}, u32[]{:S(2)}, u32[]{:S(2)}) collective-permute-start(bf16[128,128]{1,0:T(8,128)(2,1)S(1)} %get-tuple-element.100), channel_id=1, source_target_pairs={{0,12},{1,13},{2,14},{3,15},{4,8},{5,9},{6,10},{7,11},{8,4},{9,5},... | collective-permute-start | bytes 98312 | tf_op jit(solution)/shard_map/ppermute | solution.py:358
  68.1 0.8 collective-permute-start.27
  68.9 3.9 %collective-permute-start.28 = (bf16[128,128]{1,0:T(8,128)(2,1)S(1)}, bf16[128,128]{1,0:T(8,128)(2,1)S(1)}, u32[]{:S(2)}, u32[]{:S(2)}) collective-permute-start(bf16[128,128]{1,0:T(8,128)(2,1)S(1)} %get-tuple-element.102), channel_id=1, source_target_pairs={{0,14},{1,15},{2,12},{3,13},{4,10},{5,11},{6,8},{7,9},{8,6},{9,7},... | collective-permute-start | bytes 98312 | tf_op jit(solution)/shard_map/ppermute | solution.py:358
  73.3 2.2 %collective-permute-done.28.rest_14_ = bf16[128,128]{1,0:T(8,128)(2,1)S(1)} collective-permute-done((bf16[128,128]{1,0:T(8,128)(2,1)S(1)}, bf16[128,128]{1,0:T(8,128)(2,1)S(1)}, u32[]{:S(2)}, u32[]{:S(2)}) %collective-permute-start.28) | collective-permute-done | bytes 32800 | tf_op jit(solution)/shard_map/ppermute | solution.py:358
  75.5 3.6 %collective-permute-done.29.rest_15_ = bf16[128,128]{1,0:T(8,128)(2,1)S(1)} collective-permute-done((bf16[128,128]{1,0:T(8,128)(2,1)S(1)}, bf16[128,128]{1,0:T(8,128)(2,1)S(1)}, u32[]{:S(2)}, u32[]{:S(2)}) %collective-permute-start.29) | collective-permute-done | bytes 32800 | tf_op jit(solution)/shard_map/ppermute | solution.py:358
  79.1 4.1 %update.2 = (f32[3072,128]{1,0:T(8,128)S(1)}, bf16[128,128]{1,0:T(8,128)(2,1)S(1)}, bf16[128,128]{1,0:T(8,128)(2,1)S(1)}, bf16[128,128]{1,0:T(8,128)(2,1)S(1)}, ...) custom-call(s32[16,16]{1,0:T(8,128)S(1)} %copy-done.4, ...), custom_call_target="tpu_custom_call" | custom-call | tf_op jit(solution)/shard_map/update/pallas_call | solution.py:421
  83.4 0.5 collective-permute-start.31
  84.0 1.2 collective-permute-start.32
  85.2 1.8 %collective-permute-start.34 = (bf16[128,128]{1,0:T(8,128)(2,1)S(1)}, bf16[128,128]{1,0:T(8,128)(2,1)S(1)}, u32[]{:S(2)}, u32[]{:S(2)}) collective-permute-start(bf16[128,128]{1,0:T(8,128)(2,1)S(1)} %get-tuple-element.110), channel_id=1, source_target_pairs={{0,5},{1,4},{2,7},{3,6},{4,1},{5,0},{6,3},{7,2},{8,13},{9,12},{10,... | collective-permute-start | bytes 98312 | tf_op jit(solution)/shard_map/ppermute | solution.py:358
  87.7 1.9 %collective-permute-start.36 = (bf16[128,128]{1,0:T(8,128)(2,1)S(1)}, bf16[128,128]{1,0:T(8,128)(2,1)S(1)}, u32[]{:S(2)}, u32[]{:S(2)}) collective-permute-start(bf16[128,128]{1,0:T(8,128)(2,1)S(1)} %get-tuple-element.112), channel_id=1, source_target_pairs={{0,7},{1,6},{2,5},{3,4},{4,3},{5,2},{6,1},{7,0},{8,15},{9,14},{10,... | collective-permute-start | bytes 98312 | tf_op jit(solution)/shard_map/ppermute | solution.py:358
  89.6 2.7 %collective-permute-start.38 = (bf16[128,128]{1,0:T(8,128)(2,1)S(1)}, bf16[128,128]{1,0:T(8,128)(2,1)S(1)}, u32[]{:S(2)}, u32[]{:S(2)}) collective-permute-start(bf16[128,128]{1,0:T(8,128)(2,1)S(1)} %get-tuple-element.114), channel_id=1, source_target_pairs={{0,9},{1,8},{2,11},{3,10},{4,13},{5,12},{6,15},{7,14},{8,1},{9,0},... | collective-permute-start | bytes 98312 | tf_op jit(solution)/shard_map/ppermute | solution.py:358
  92.6 3.2 %collective-permute-start.40 = (bf16[128,128]{1,0:T(8,128)(2,1)S(1)}, bf16[128,128]{1,0:T(8,128)(2,1)S(1)}, u32[]{:S(2)}, u32[]{:S(2)}) collective-permute-start(bf16[128,128]{1,0:T(8,128)(2,1)S(1)} %get-tuple-element.116), channel_id=1, source_target_pairs={{0,11},{1,10},{2,9},{3,8},{4,15},{5,14},{6,13},{7,12},{8,3},{9,2},... | collective-permute-start | bytes 98312 | tf_op jit(solution)/shard_map/ppermute | solution.py:358
  95.8 0.5 collective-permute-start.41
  96.2 3.1 %collective-permute-start.42 = (bf16[128,128]{1,0:T(8,128)(2,1)S(1)}, bf16[128,128]{1,0:T(8,128)(2,1)S(1)}, u32[]{:S(2)}, u32[]{:S(2)}) collective-permute-start(bf16[128,128]{1,0:T(8,128)(2,1)S(1)} %get-tuple-element.118), channel_id=1, source_target_pairs={{0,13},{1,12},{2,15},{3,14},{4,9},{5,8},{6,11},{7,10},{8,5},{9,4},... | collective-permute-start | bytes 98312 | tf_op jit(solution)/shard_map/ppermute | solution.py:358
  99.4 0.8 collective-permute-start.43
  100.2 3.6 %collective-permute-start.44 = (bf16[128,128]{1,0:T(8,128)(2,1)S(1)}, bf16[128,128]{1,0:T(8,128)(2,1)S(1)}, u32[]{:S(2)}, u32[]{:S(2)}) collective-permute-start(bf16[128,128]{1,0:T(8,128)(2,1)S(1)} %get-tuple-element.120), channel_id=1, source_target_pairs={{0,15},{1,14},{2,13},{3,12},{4,11},{5,10},{6,9},{7,8},{8,7},{9,6},... | collective-permute-start | bytes 98312 | tf_op jit(solution)/shard_map/ppermute | solution.py:358
  103.8 2.3 %collective-permute-done.43.rest_14_ = bf16[128,128]{1,0:T(8,128)(2,1)S(1)} collective-permute-done((bf16[128,128]{1,0:T(8,128)(2,1)S(1)}, bf16[128,128]{1,0:T(8,128)(2,1)S(1)}, u32[]{:S(2)}, u32[]{:S(2)}) %collective-permute-start.43) | collective-permute-done | bytes 32800 | tf_op jit(solution)/shard_map/ppermute | solution.py:358
  106.4 8.1 %blur.3 = (bf16[128,128]{1,0:T(8,128)(2,1)S(1)}, bf16[128,128]{1,0:T(8,128)(2,1)S(1)}, bf16[128,128]{1,0:T(8,128)(2,1)S(1)}, bf16[128,128]{1,0:T(8,128)(2,1)S(1)...) custom-call(s32[4,128]{1,0:T(4,128)S(1)} %copy-done.8, ...), custom_call_target="tpu_custom_call" | custom-call | tf_op jit(solution)/shard_map/blur/pallas_call | solution.py:392
  114.7 0.9 collective-permute-start.46
  115.5 0.9 collective-permute-start.47
  116.4 1.8 %collective-permute-start.49 = (bf16[128,128]{1,0:T(8,128)(2,1)S(1)}, bf16[128,128]{1,0:T(8,128)(2,1)S(1)}, u32[]{:S(2)}, u32[]{:S(2)}) collective-permute-start(bf16[128,128]{1,0:T(8,128)(2,1)S(1)} %get-tuple-element.126), channel_id=1, source_target_pairs={{0,5},{1,4},{2,7},{3,6},{4,1},{5,0},{6,3},{7,2},{8,13},{9,12},{10,... | collective-permute-start | bytes 98312 | tf_op jit(solution)/shard_map/ppermute | solution.py:358
  118.2 0.6 collective-permute-start.50
  118.8 2.0 %collective-permute-start.51 = (bf16[128,128]{1,0:T(8,128)(2,1)S(1)}, bf16[128,128]{1,0:T(8,128)(2,1)S(1)}, u32[]{:S(2)}, u32[]{:S(2)}) collective-permute-start(bf16[128,128]{1,0:T(8,128)(2,1)S(1)} %get-tuple-element.128), channel_id=1, source_target_pairs={{0,7},{1,6},{2,5},{3,4},{4,3},{5,2},{6,1},{7,0},{8,15},{9,14},{10,... | collective-permute-start | bytes 98312 | tf_op jit(solution)/shard_map/ppermute | solution.py:358
  120.8 1.9 %collective-permute-start.52 = (bf16[128,128]{1,0:T(8,128)(2,1)S(1)}, bf16[128,128]{1,0:T(8,128)(2,1)S(1)}, u32[]{:S(2)}, u32[]{:S(2)}) collective-permute-start(bf16[128,128]{1,0:T(8,128)(2,1)S(1)} %get-tuple-element.129), channel_id=1, source_target_pairs={{0,8},{1,9},{2,10},{3,11},{4,12},{5,13},{6,14},{7,15},{8,0},{9,1},... | collective-permute-start | bytes 98312 | tf_op jit(solution)/shard_map/ppermute | solution.py:358
  122.7 0.8 collective-permute-start.53
  123.5 2.7 %collective-permute-start.54 = (bf16[128,128]{1,0:T(8,128)(2,1)S(1)}, bf16[128,128]{1,0:T(8,128)(2,1)S(1)}, u32[]{:S(2)}, u32[]{:S(2)}) collective-permute-start(bf16[128,128]{1,0:T(8,128)(2,1)S(1)} %get-tuple-element.131), channel_id=1, source_target_pairs={{0,10},{1,11},{2,8},{3,9},{4,14},{5,15},{6,12},{7,13},{8,2},{9,3},... | collective-permute-start | bytes 98312 | tf_op jit(solution)/shard_map/ppermute | solution.py:358
  126.2 0.8 collective-permute-start.55
  127.0 2.9 %collective-permute-start.56 = (bf16[128,128]{1,0:T(8,128)(2,1)S(1)}, bf16[128,128]{1,0:T(8,128)(2,1)S(1)}, u32[]{:S(2)}, u32[]{:S(2)}) collective-permute-start(bf16[128,128]{1,0:T(8,128)(2,1)S(1)} %get-tuple-element.133), channel_id=1, source_target_pairs={{0,12},{1,13},{2,14},{3,15},{4,8},{5,9},{6,10},{7,11},{8,4},{9,5},... | collective-permute-start | bytes 98312 | tf_op jit(solution)/shard_map/ppermute | solution.py:358
  129.9 0.7 collective-permute-start.57
  130.6 3.8 %collective-permute-start.58 = (bf16[128,128]{1,0:T(8,128)(2,1)S(1)}, bf16[128,128]{1,0:T(8,128)(2,1)S(1)}, u32[]{:S(2)}, u32[]{:S(2)}) collective-permute-start(bf16[128,128]{1,0:T(8,128)(2,1)S(1)} %get-tuple-element.135), channel_id=1, source_target_pairs={{0,14},{1,15},{2,12},{3,13},{4,10},{5,11},{6,8},{7,9},{8,6},{9,7},... | collective-permute-start | bytes 98312 | tf_op jit(solution)/shard_map/ppermute | solution.py:358
  134.4 0.6 collective-permute-start.59
  135.2 2.0 %collective-permute-done.58.rest_14_ = bf16[128,128]{1,0:T(8,128)(2,1)S(1)} collective-permute-done((bf16[128,128]{1,0:T(8,128)(2,1)S(1)}, bf16[128,128]{1,0:T(8,128)(2,1)S(1)}, u32[]{:S(2)}, u32[]{:S(2)}) %collective-permute-start.58) | collective-permute-done | bytes 32800 | tf_op jit(solution)/shard_map/ppermute | solution.py:358
  137.2 3.3 %collective-permute-done.59.rest_15_ = bf16[128,128]{1,0:T(8,128)(2,1)S(1)} collective-permute-done((bf16[128,128]{1,0:T(8,128)(2,1)S(1)}, bf16[128,128]{1,0:T(8,128)(2,1)S(1)}, u32[]{:S(2)}, u32[]{:S(2)}) %collective-permute-start.59) | collective-permute-done | bytes 32800 | tf_op jit(solution)/shard_map/ppermute | solution.py:358
  140.6 3.9 %update.3 = f32[3072,128]{1,0:T(8,128)} custom-call(s32[16,16]{1,0:T(8,128)S(1)} %copy-done.4, s32[16,16]{1,0:T(8,128)S(1)} %copy-done.5, s32[16,16]{1,0:T(8,128)S(1)} %copy-done.6, f32[6]{0:T(128)S(1)} %copy-done.13, s32[2]{0:T(128)S(1)} %copy-done.14, s32[2]{0:T(128)S(1)} %copy-done.15, f32[3072,128]{1,0:T(8,128)S(1)} %get-tuple-element.104.model_ref, ...), custom_call_target="tpu_custom_call" | custom-call | tf_op jit(solution)/shard_map/update/pallas_call | solution.py:421
  (97 shorter events, 3.9 us)
Async XLA Ops:
  0.6 78.4 %copy-start = (f32[2,6,256,128]{3,2,1,0:T(8,128)S(1)}, f32[2,6,256,128]{3,2,1,0:T(8,128)}, u32[]{:S(2)}) copy-start(f32[2,6,256,128]{3,2,1,0:T(8,128)} %param.14) | copy-start | bytes 4718596
  5.1 5.0 %collective-permute-start = (bf16[144,128]{1,0:T(8,128)(2,1)}, bf16[144,128]{1,0:T(8,128)(2,1)S(1)}, u32[]{:S(2)}, u32[]{:S(2)}) collective-permute-start(bf16[144,128]{1,0:T(8,128)(2,1)} %get-tuple-element.73), channel_id=1, source_target_pairs={{0,1},{1,0},{2,3},{3,2},{4,5},{5,4},{6,7},{7,6},{8,9},{9,8},{10,11... | collective-permute-start | bytes 110600 | tf_op jit(solution)/shard_map/ppermute | solution.py:358
  5.6 7.1 %collective-permute-start.1 = (bf16[144,128]{1,0:T(8,128)(2,1)}, bf16[144,128]{1,0:T(8,128)(2,1)S(1)}, u32[]{:S(2)}, u32[]{:S(2)}) collective-permute-start(bf16[144,128]{1,0:T(8,128)(2,1)} %get-tuple-element.74), channel_id=1, source_target_pairs={{0,2},{1,3},{2,0},{3,1},{4,6},{5,7},{6,4},{7,5},{8,10},{9,11},{10,... | collective-permute-start | bytes 110600 | tf_op jit(solution)/shard_map/ppermute | solution.py:358
  8.2 4.6 %collective-permute-start.2 = (bf16[144,128]{1,0:T(8,128)(2,1)}, bf16[144,128]{1,0:T(8,128)(2,1)S(1)}, u32[]{:S(2)}, u32[]{:S(2)}) collective-permute-start(bf16[144,128]{1,0:T(8,128)(2,1)} %get-tuple-element.75), channel_id=1, source_target_pairs={{0,3},{1,2},{2,1},{3,0},{4,7},{5,6},{6,5},{7,4},{8,11},{9,10},{10,... | collective-permute-start | bytes 110600 | tf_op jit(solution)/shard_map/ppermute | solution.py:358
  8.2 7.2 %collective-permute-start.3 = (bf16[144,128]{1,0:T(8,128)(2,1)}, bf16[144,128]{1,0:T(8,128)(2,1)S(1)}, u32[]{:S(2)}, u32[]{:S(2)}) collective-permute-start(bf16[144,128]{1,0:T(8,128)(2,1)} %get-tuple-element.76), channel_id=1, source_target_pairs={{0,4},{1,5},{2,6},{3,7},{4,0},{5,1},{6,2},{7,3},{8,12},{9,13},{10,... | collective-permute-start | bytes 110600 | tf_op jit(solution)/shard_map/ppermute | solution.py:358
  10.1 6.0 %collective-permute-start.4 = (bf16[144,128]{1,0:T(8,128)(2,1)}, bf16[144,128]{1,0:T(8,128)(2,1)S(1)}, u32[]{:S(2)}, u32[]{:S(2)}) collective-permute-start(bf16[144,128]{1,0:T(8,128)(2,1)} %get-tuple-element.77), channel_id=1, source_target_pairs={{0,5},{1,4},{2,7},{3,6},{4,1},{5,0},{6,3},{7,2},{8,13},{9,12},{10,... | collective-permute-start | bytes 110600 | tf_op jit(solution)/shard_map/ppermute | solution.py:358
  10.1 8.9 %collective-permute-start.5 = (bf16[144,128]{1,0:T(8,128)(2,1)}, bf16[144,128]{1,0:T(8,128)(2,1)S(1)}, u32[]{:S(2)}, u32[]{:S(2)}) collective-permute-start(bf16[144,128]{1,0:T(8,128)(2,1)} %get-tuple-element.78), channel_id=1, source_target_pairs={{0,6},{1,7},{2,4},{3,5},{4,2},{5,3},{6,0},{7,1},{8,14},{9,15},{10,... | collective-permute-start | bytes 110600 | tf_op jit(solution)/shard_map/ppermute | solution.py:358
  12.7 6.7 %collective-permute-start.6 = (bf16[144,128]{1,0:T(8,128)(2,1)}, bf16[144,128]{1,0:T(8,128)(2,1)S(1)}, u32[]{:S(2)}, u32[]{:S(2)}) collective-permute-start(bf16[144,128]{1,0:T(8,128)(2,1)} %get-tuple-element.79), channel_id=1, source_target_pairs={{0,7},{1,6},{2,5},{3,4},{4,3},{5,2},{6,1},{7,0},{8,15},{9,14},{10,... | collective-permute-start | bytes 110600 | tf_op jit(solution)/shard_map/ppermute | solution.py:358
  12.8 9.9 %collective-permute-start.7 = (bf16[144,128]{1,0:T(8,128)(2,1)}, bf16[144,128]{1,0:T(8,128)(2,1)S(1)}, u32[]{:S(2)}, u32[]{:S(2)}) collective-permute-start(bf16[144,128]{1,0:T(8,128)(2,1)} %get-tuple-element.80), channel_id=1, source_target_pairs={{0,8},{1,9},{2,10},{3,11},{4,12},{5,13},{6,14},{7,15},{8,0},{9,1},... | collective-permute-start | bytes 110600 | tf_op jit(solution)/shard_map/ppermute | solution.py:358
  15.5 7.7 %collective-permute-start.8 = (bf16[144,128]{1,0:T(8,128)(2,1)}, bf16[144,128]{1,0:T(8,128)(2,1)S(1)}, u32[]{:S(2)}, u32[]{:S(2)}) collective-permute-start(bf16[144,128]{1,0:T(8,128)(2,1)} %get-tuple-element.81), channel_id=1, source_target_pairs={{0,9},{1,8},{2,11},{3,10},{4,13},{5,12},{6,15},{7,14},{8,1},{9,0},... | collective-permute-start | bytes 110600 | tf_op jit(solution)/shard_map/ppermute | solution.py:358
  16.1 11.0 %collective-permute-start.9 = (bf16[144,128]{1,0:T(8,128)(2,1)}, bf16[144,128]{1,0:T(8,128)(2,1)S(1)}, u32[]{:S(2)}, u32[]{:S(2)}) collective-permute-start(bf16[144,128]{1,0:T(8,128)(2,1)} %get-tuple-element.82), channel_id=1, source_target_pairs={{0,10},{1,11},{2,8},{3,9},{4,14},{5,15},{6,12},{7,13},{8,2},{9,3},... | collective-permute-start | bytes 110600 | tf_op jit(solution)/shard_map/ppermute | solution.py:358
  19.0 22.6 %collective-permute-start.10 = (bf16[144,128]{1,0:T(8,128)(2,1)}, bf16[144,128]{1,0:T(8,128)(2,1)S(1)}, u32[]{:S(2)}, u32[]{:S(2)}) collective-permute-start(bf16[144,128]{1,0:T(8,128)(2,1)} %get-tuple-element.83), channel_id=1, source_target_pairs={{0,11},{1,10},{2,9},{3,8},{4,15},{5,14},{6,13},{7,12},{8,3},{9,2},... | collective-permute-start | bytes 110600 | tf_op jit(solution)/shard_map/ppermute | solution.py:358
  19.4 22.3 %collective-permute-start.11 = (bf16[144,128]{1,0:T(8,128)(2,1)}, bf16[144,128]{1,0:T(8,128)(2,1)S(1)}, u32[]{:S(2)}, u32[]{:S(2)}) collective-permute-start(bf16[144,128]{1,0:T(8,128)(2,1)} %get-tuple-element.84), channel_id=1, source_target_pairs={{0,12},{1,13},{2,14},{3,15},{4,8},{5,9},{6,10},{7,11},{8,4},{9,5},... | collective-permute-start | bytes 110600 | tf_op jit(solution)/shard_map/ppermute | solution.py:358
  22.7 19.0 %collective-permute-start.12 = (bf16[144,128]{1,0:T(8,128)(2,1)}, bf16[144,128]{1,0:T(8,128)(2,1)S(1)}, u32[]{:S(2)}, u32[]{:S(2)}) collective-permute-start(bf16[144,128]{1,0:T(8,128)(2,1)} %get-tuple-element.85), channel_id=1, source_target_pairs={{0,13},{1,12},{2,15},{3,14},{4,9},{5,8},{6,11},{7,10},{8,5},{9,4},... | collective-permute-start | bytes 110600 | tf_op jit(solution)/shard_map/ppermute | solution.py:358
  23.2 18.5 %collective-permute-start.13 = (bf16[144,128]{1,0:T(8,128)(2,1)}, bf16[144,128]{1,0:T(8,128)(2,1)S(1)}, u32[]{:S(2)}, u32[]{:S(2)}) collective-permute-start(bf16[144,128]{1,0:T(8,128)(2,1)} %get-tuple-element.86), channel_id=1, source_target_pairs={{0,14},{1,15},{2,12},{3,13},{4,10},{5,11},{6,8},{7,9},{8,6},{9,7},... | collective-permute-start | bytes 110600 | tf_op jit(solution)/shard_map/ppermute | solution.py:358
  27.1 14.6 %collective-permute-start.14 = (bf16[144,128]{1,0:T(8,128)(2,1)}, bf16[144,128]{1,0:T(8,128)(2,1)S(1)}, u32[]{:S(2)}, u32[]{:S(2)}) collective-permute-start(bf16[144,128]{1,0:T(8,128)(2,1)} %get-tuple-element.87), channel_id=1, source_target_pairs={{0,15},{1,14},{2,13},{3,12},{4,11},{5,10},{6,9},{7,8},{8,7},{9,6},... | collective-permute-start | bytes 110600 | tf_op jit(solution)/shard_map/ppermute | solution.py:358
  45.1 61.3 %copy-start.3 = (bf16[144,128]{1,0:T(8,128)(2,1)S(1)}, bf16[144,128]{1,0:T(8,128)(2,1)}, u32[]{:S(2)}) copy-start(bf16[144,128]{1,0:T(8,128)(2,1)} %get-tuple-element.72.rest_0_.rest_16_) | copy-start | bytes 110596
  45.1 61.3 %copy-start.8 = (s32[4,128]{1,0:T(4,128)S(1)}, s32[4,128]{1,0:T(4,128)}, u32[]{:S(2)}) copy-start(s32[4,128]{1,0:T(4,128)} %get-tuple-element.70.use_ref) | copy-start | bytes 6148
  45.2 61.3 %copy-start.10 = (s32[2,256]{1,0:T(2,128)S(1)}, s32[2,256]{1,0:T(2,128)}, u32[]{:S(2)}) copy-start(s32[2,256]{1,0:T(2,128)} %get-tuple-element.71.move_ref) | copy-start | bytes 6148
  52.3 4.1 %collective-permute-start.15 = (bf16[128,128]{1,0:T(8,128)(2,1)S(1)}, bf16[128,128]{1,0:T(8,128)(2,1)S(1)}, u32[]{:S(2)}, u32[]{:S(2)}) collective-permute-start(bf16[128,128]{1,0:T(8,128)(2,1)S(1)} %get-tuple-element.89), channel_id=1, source_target_pairs={{0,1},{1,0},{2,3},{3,2},{4,5},{5,4},{6,7},{7,6},{8,9},{9,8},{10,11... | collective-permute-start | bytes 98312 | tf_op jit(solution)/shard_map/ppermute | solution.py:358
  52.9 4.3 %collective-permute-start.16 = (bf16[128,128]{1,0:T(8,128)(2,1)S(1)}, bf16[128,128]{1,0:T(8,128)(2,1)S(1)}, u32[]{:S(2)}, u32[]{:S(2)}) collective-permute-start(bf16[128,128]{1,0:T(8,128)(2,1)S(1)} %get-tuple-element.90), channel_id=1, source_target_pairs={{0,2},{1,3},{2,0},{3,1},{4,6},{5,7},{6,4},{7,5},{8,10},{9,11},{10,... | collective-permute-start | bytes 98312 | tf_op jit(solution)/shard_map/ppermute | solution.py:358
  54.0 4.8 %collective-permute-start.17 = (bf16[128,128]{1,0:T(8,128)(2,1)S(1)}, bf16[128,128]{1,0:T(8,128)(2,1)S(1)}, u32[]{:S(2)}, u32[]{:S(2)}) collective-permute-start(bf16[128,128]{1,0:T(8,128)(2,1)S(1)} %get-tuple-element.91), channel_id=1, source_target_pairs={{0,3},{1,2},{2,1},{3,0},{4,7},{5,6},{6,5},{7,4},{8,11},{9,10},{10,... | collective-permute-start | bytes 98312 | tf_op jit(solution)/shard_map/ppermute | solution.py:358
  54.4 6.6 %collective-permute-start.18 = (bf16[128,128]{1,0:T(8,128)(2,1)S(1)}, bf16[128,128]{1,0:T(8,128)(2,1)S(1)}, u32[]{:S(2)}, u32[]{:S(2)}) collective-permute-start(bf16[128,128]{1,0:T(8,128)(2,1)S(1)} %get-tuple-element.92), channel_id=1, source_target_pairs={{0,4},{1,5},{2,6},{3,7},{4,0},{5,1},{6,2},{7,3},{8,12},{9,13},{10,... | collective-permute-start | bytes 98312 | tf_op jit(solution)/shard_map/ppermute | solution.py:358
  54.4 7.4 %collective-permute-start.19 = (bf16[128,128]{1,0:T(8,128)(2,1)S(1)}, bf16[128,128]{1,0:T(8,128)(2,1)S(1)}, u32[]{:S(2)}, u32[]{:S(2)}) collective-permute-start(bf16[128,128]{1,0:T(8,128)(2,1)S(1)} %get-tuple-element.93), channel_id=1, source_target_pairs={{0,5},{1,4},{2,7},{3,6},{4,1},{5,0},{6,3},{7,2},{8,13},{9,12},{10,... | collective-permute-start | bytes 98312 | tf_op jit(solution)/shard_map/ppermute | solution.py:358
  56.4 8.1 %collective-permute-start.20 = (bf16[128,128]{1,0:T(8,128)(2,1)S(1)}, bf16[128,128]{1,0:T(8,128)(2,1)S(1)}, u32[]{:S(2)}, u32[]{:S(2)}) collective-permute-start(bf16[128,128]{1,0:T(8,128)(2,1)S(1)} %get-tuple-element.94), channel_id=1, source_target_pairs={{0,6},{1,7},{2,4},{3,5},{4,2},{5,3},{6,0},{7,1},{8,14},{9,15},{10,... | collective-permute-start | bytes 98312 | tf_op jit(solution)/shard_map/ppermute | solution.py:358
  57.2 7.7 %collective-permute-start.21 = (bf16[128,128]{1,0:T(8,128)(2,1)S(1)}, bf16[128,128]{1,0:T(8,128)(2,1)S(1)}, u32[]{:S(2)}, u32[]{:S(2)}) collective-permute-start(bf16[128,128]{1,0:T(8,128)(2,1)S(1)} %get-tuple-element.95), channel_id=1, source_target_pairs={{0,7},{1,6},{2,5},{3,4},{4,3},{5,2},{6,1},{7,0},{8,15},{9,14},{10,... | collective-permute-start | bytes 98312 | tf_op jit(solution)/shard_map/ppermute | solution.py:358
  58.8 9.3 %collective-permute-start.22 = (bf16[128,128]{1,0:T(8,128)(2,1)S(1)}, bf16[128,128]{1,0:T(8,128)(2,1)S(1)}, u32[]{:S(2)}, u32[]{:S(2)}) collective-permute-start(bf16[128,128]{1,0:T(8,128)(2,1)S(1)} %get-tuple-element.96), channel_id=1, source_target_pairs={{0,8},{1,9},{2,10},{3,11},{4,12},{5,13},{6,14},{7,15},{8,0},{9,1},... | collective-permute-start | bytes 98312 | tf_op jit(solution)/shard_map/ppermute | solution.py:358
  61.0 7.9 %collective-permute-start.23 = (bf16[128,128]{1,0:T(8,128)(2,1)S(1)}, bf16[128,128]{1,0:T(8,128)(2,1)S(1)}, u32[]{:S(2)}, u32[]{:S(2)}) collective-permute-start(bf16[128,128]{1,0:T(8,128)(2,1)S(1)} %get-tuple-element.97), channel_id=1, source_target_pairs={{0,9},{1,8},{2,11},{3,10},{4,13},{5,12},{6,15},{7,14},{8,1},{9,0},... | collective-permute-start | bytes 98312 | tf_op jit(solution)/shard_map/ppermute | solution.py:358
  61.7 11.0 %collective-permute-start.24 = (bf16[128,128]{1,0:T(8,128)(2,1)S(1)}, bf16[128,128]{1,0:T(8,128)(2,1)S(1)}, u32[]{:S(2)}, u32[]{:S(2)}) collective-permute-start(bf16[128,128]{1,0:T(8,128)(2,1)S(1)} %get-tuple-element.98), channel_id=1, source_target_pairs={{0,10},{1,11},{2,8},{3,9},{4,14},{5,15},{6,12},{7,13},{8,2},{9,3},... | collective-permute-start | bytes 98312 | tf_op jit(solution)/shard_map/ppermute | solution.py:358
  64.5 8.5 %collective-permute-start.25 = (bf16[128,128]{1,0:T(8,128)(2,1)S(1)}, bf16[128,128]{1,0:T(8,128)(2,1)S(1)}, u32[]{:S(2)}, u32[]{:S(2)}) collective-permute-start(bf16[128,128]{1,0:T(8,128)(2,1)S(1)} %get-tuple-element.99), channel_id=1, source_target_pairs={{0,11},{1,10},{2,9},{3,8},{4,15},{5,14},{6,13},{7,12},{8,3},{9,2},... | collective-permute-start | bytes 98312 | tf_op jit(solution)/shard_map/ppermute | solution.py:358
  65.0 8.0 %collective-permute-start.26 = (bf16[128,128]{1,0:T(8,128)(2,1)S(1)}, bf16[128,128]{1,0:T(8,128)(2,1)S(1)}, u32[]{:S(2)}, u32[]{:S(2)}) collective-permute-start(bf16[128,128]{1,0:T(8,128)(2,1)S(1)} %get-tuple-element.100), channel_id=1, source_target_pairs={{0,12},{1,13},{2,14},{3,15},{4,8},{5,9},{6,10},{7,11},{8,4},{9,5},... | collective-permute-start | bytes 98312 | tf_op jit(solution)/shard_map/ppermute | solution.py:358
  68.1 5.2 %collective-permute-start.27 = (bf16[128,128]{1,0:T(8,128)(2,1)S(1)}, bf16[128,128]{1,0:T(8,128)(2,1)S(1)}, u32[]{:S(2)}, u32[]{:S(2)}) collective-permute-start(bf16[128,128]{1,0:T(8,128)(2,1)S(1)} %get-tuple-element.101), channel_id=1, source_target_pairs={{0,13},{1,12},{2,15},{3,14},{4,9},{5,8},{6,11},{7,10},{8,5},{9,4},... | collective-permute-start | bytes 98312 | tf_op jit(solution)/shard_map/ppermute | solution.py:358
  68.9 6.6 %collective-permute-start.28 = (bf16[128,128]{1,0:T(8,128)(2,1)S(1)}, bf16[128,128]{1,0:T(8,128)(2,1)S(1)}, u32[]{:S(2)}, u32[]{:S(2)}) collective-permute-start(bf16[128,128]{1,0:T(8,128)(2,1)S(1)} %get-tuple-element.102), channel_id=1, source_target_pairs={{0,14},{1,15},{2,12},{3,13},{4,10},{5,11},{6,8},{7,9},{8,6},{9,7},... | collective-permute-start | bytes 98312 | tf_op jit(solution)/shard_map/ppermute | solution.py:358
  72.8 6.3 %collective-permute-start.29 = (bf16[128,128]{1,0:T(8,128)(2,1)S(1)}, bf16[128,128]{1,0:T(8,128)(2,1)S(1)}, u32[]{:S(2)}, u32[]{:S(2)}) collective-permute-start(bf16[128,128]{1,0:T(8,128)(2,1)S(1)} %get-tuple-element.103), channel_id=1, source_target_pairs={{0,15},{1,14},{2,13},{3,12},{4,11},{5,10},{6,9},{7,8},{8,7},{9,6},... | collective-permute-start | bytes 98312 | tf_op jit(solution)/shard_map/ppermute | solution.py:358
  83.2 3.7 %collective-permute-start.30 = (bf16[128,128]{1,0:T(8,128)(2,1)S(1)}, bf16[128,128]{1,0:T(8,128)(2,1)S(1)}, u32[]{:S(2)}, u32[]{:S(2)}) collective-permute-start(bf16[128,128]{1,0:T(8,128)(2,1)S(1)} %get-tuple-element.106), channel_id=1, source_target_pairs={{0,1},{1,0},{2,3},{3,2},{4,5},{5,4},{6,7},{7,6},{8,9},{9,8},{10,11... | collective-permute-start | bytes 98312 | tf_op jit(solution)/shard_map/ppermute | solution.py:358
  83.4 4.2 %collective-permute-start.31 = (bf16[128,128]{1,0:T(8,128)(2,1)S(1)}, bf16[128,128]{1,0:T(8,128)(2,1)S(1)}, u32[]{:S(2)}, u32[]{:S(2)}) collective-permute-start(bf16[128,128]{1,0:T(8,128)(2,1)S(1)} %get-tuple-element.107), channel_id=1, source_target_pairs={{0,2},{1,3},{2,0},{3,1},{4,6},{5,7},{6,4},{7,5},{8,10},{9,11},{10,... | collective-permute-start | bytes 98312 | tf_op jit(solution)/shard_map/ppermute | solution.py:358
  84.0 5.6 %collective-permute-start.32 = (bf16[128,128]{1,0:T(8,128)(2,1)S(1)}, bf16[128,128]{1,0:T(8,128)(2,1)S(1)}, u32[]{:S(2)}, u32[]{:S(2)}) collective-permute-start(bf16[128,128]{1,0:T(8,128)(2,1)S(1)} %get-tuple-element.108), channel_id=1, source_target_pairs={{0,3},{1,2},{2,1},{3,0},{4,7},{5,6},{6,5},{7,4},{8,11},{9,10},{10,... | collective-permute-start | bytes 98312 | tf_op jit(solution)/shard_map/ppermute | solution.py:358
  85.2 4.4 %collective-permute-start.33 = (bf16[128,128]{1,0:T(8,128)(2,1)S(1)}, bf16[128,128]{1,0:T(8,128)(2,1)S(1)}, u32[]{:S(2)}, u32[]{:S(2)}) collective-permute-start(bf16[128,128]{1,0:T(8,128)(2,1)S(1)} %get-tuple-element.109), channel_id=1, source_target_pairs={{0,4},{1,5},{2,6},{3,7},{4,0},{5,1},{6,2},{7,3},{8,12},{9,13},{10,... | collective-permute-start | bytes 98312 | tf_op jit(solution)/shard_map/ppermute | solution.py:358
  85.2 7.1 %collective-permute-start.34 = (bf16[128,128]{1,0:T(8,128)(2,1)S(1)}, bf16[128,128]{1,0:T(8,128)(2,1)S(1)}, u32[]{:S(2)}, u32[]{:S(2)}) collective-permute-start(bf16[128,128]{1,0:T(8,128)(2,1)S(1)} %get-tuple-element.110), channel_id=1, source_target_pairs={{0,5},{1,4},{2,7},{3,6},{4,1},{5,0},{6,3},{7,2},{8,13},{9,12},{10,... | collective-permute-start | bytes 98312 | tf_op jit(solution)/shard_map/ppermute | solution.py:358
  87.0 5.6 %collective-permute-start.35 = (bf16[128,128]{1,0:T(8,128)(2,1)S(1)}, bf16[128,128]{1,0:T(8,128)(2,1)S(1)}, u32[]{:S(2)}, u32[]{:S(2)}) collective-permute-start(bf16[128,128]{1,0:T(8,128)(2,1)S(1)} %get-tuple-element.111), channel_id=1, source_target_pairs={{0,6},{1,7},{2,4},{3,5},{4,2},{5,3},{6,0},{7,1},{8,14},{9,15},{10,... | collective-permute-start | bytes 98312 | tf_op jit(solution)/shard_map/ppermute | solution.py:358
  87.7 8.1 %collective-permute-start.36 = (bf16[128,128]{1,0:T(8,128)(2,1)S(1)}, bf16[128,128]{1,0:T(8,128)(2,1)S(1)}, u32[]{:S(2)}, u32[]{:S(2)}) collective-permute-start(bf16[128,128]{1,0:T(8,128)(2,1)S(1)} %get-tuple-element.112), channel_id=1, source_target_pairs={{0,7},{1,6},{2,5},{3,4},{4,3},{5,2},{6,1},{7,0},{8,15},{9,14},{10,... | collective-permute-start | bytes 98312 | tf_op jit(solution)/shard_map/ppermute | solution.py:358
  89.6 6.7 %collective-permute-start.37 = (bf16[128,128]{1,0:T(8,128)(2,1)S(1)}, bf16[128,128]{1,0:T(8,128)(2,1)S(1)}, u32[]{:S(2)}, u32[]{:S(2)}) collective-permute-start(bf16[128,128]{1,0:T(8,128)(2,1)S(1)} %get-tuple-element.113), channel_id=1, source_target_pairs={{0,8},{1,9},{2,10},{3,11},{4,12},{5,13},{6,14},{7,15},{8,0},{9,1},... | collective-permute-start | bytes 98312 | tf_op jit(solution)/shard_map/ppermute | solution.py:358
  89.6 9.8 %collective-permute-start.38 = (bf16[128,128]{1,0:T(8,128)(2,1)S(1)}, bf16[128,128]{1,0:T(8,128)(2,1)S(1)}, u32[]{:S(2)}, u32[]{:S(2)}) collective-permute-start(bf16[128,128]{1,0:T(8,128)(2,1)S(1)} %get-tuple-element.114), channel_id=1, source_target_pairs={{0,9},{1,8},{2,11},{3,10},{4,13},{5,12},{6,15},{7,14},{8,1},{9,0},... | collective-permute-start | bytes 98312 | tf_op jit(solution)/shard_map/ppermute | solution.py:358
  92.3 7.9 %collective-permute-start.39 = (bf16[128,128]{1,0:T(8,128)(2,1)S(1)}, bf16[128,128]{1,0:T(8,128)(2,1)S(1)}, u32[]{:S(2)}, u32[]{:S(2)}) collective-permute-start(bf16[128,128]{1,0:T(8,128)(2,1)S(1)} %get-tuple-element.115), channel_id=1, source_target_pairs={{0,10},{1,11},{2,8},{3,9},{4,14},{5,15},{6,12},{7,13},{8,2},{9,3},... | collective-permute-start | bytes 98312 | tf_op jit(solution)/shard_map/ppermute | solution.py:358
  92.6 11.2 %collective-permute-start.40 = (bf16[128,128]{1,0:T(8,128)(2,1)S(1)}, bf16[128,128]{1,0:T(8,128)(2,1)S(1)}, u32[]{:S(2)}, u32[]{:S(2)}) collective-permute-start(bf16[128,128]{1,0:T(8,128)(2,1)S(1)} %get-tuple-element.116), channel_id=1, source_target_pairs={{0,11},{1,10},{2,9},{3,8},{4,15},{5,14},{6,13},{7,12},{8,3},{9,2},... | collective-permute-start | bytes 98312 | tf_op jit(solution)/shard_map/ppermute | solution.py:358
  95.8 8.0 %collective-permute-start.41 = (bf16[128,128]{1,0:T(8,128)(2,1)S(1)}, bf16[128,128]{1,0:T(8,128)(2,1)S(1)}, u32[]{:S(2)}, u32[]{:S(2)}) collective-permute-start(bf16[128,128]{1,0:T(8,128)(2,1)S(1)} %get-tuple-element.117), channel_id=1, source_target_pairs={{0,12},{1,13},{2,14},{3,15},{4,8},{5,9},{6,10},{7,11},{8,4},{9,5},... | collective-permute-start | bytes 98312 | tf_op jit(solution)/shard_map/ppermute | solution.py:358
  96.2 7.5 %collective-permute-start.42 = (bf16[128,128]{1,0:T(8,128)(2,1)S(1)}, bf16[128,128]{1,0:T(8,128)(2,1)S(1)}, u32[]{:S(2)}, u32[]{:S(2)}) collective-permute-start(bf16[128,128]{1,0:T(8,128)(2,1)S(1)} %get-tuple-element.118), channel_id=1, source_target_pairs={{0,13},{1,12},{2,15},{3,14},{4,9},{5,8},{6,11},{7,10},{8,5},{9,4},... | collective-permute-start | bytes 98312 | tf_op jit(solution)/shard_map/ppermute | solution.py:358
  99.4 6.7 %collective-permute-start.43 = (bf16[128,128]{1,0:T(8,128)(2,1)S(1)}, bf16[128,128]{1,0:T(8,128)(2,1)S(1)}, u32[]{:S(2)}, u32[]{:S(2)}) collective-permute-start(bf16[128,128]{1,0:T(8,128)(2,1)S(1)} %get-tuple-element.119), channel_id=1, source_target_pairs={{0,14},{1,15},{2,12},{3,13},{4,10},{5,11},{6,8},{7,9},{8,6},{9,7},... | collective-permute-start | bytes 98312 | tf_op jit(solution)/shard_map/ppermute | solution.py:358
  100.2 6.2 %collective-permute-start.44 = (bf16[128,128]{1,0:T(8,128)(2,1)S(1)}, bf16[128,128]{1,0:T(8,128)(2,1)S(1)}, u32[]{:S(2)}, u32[]{:S(2)}) collective-permute-start(bf16[128,128]{1,0:T(8,128)(2,1)S(1)} %get-tuple-element.120), channel_id=1, source_target_pairs={{0,15},{1,14},{2,13},{3,12},{4,11},{5,10},{6,9},{7,8},{8,7},{9,6},... | collective-permute-start | bytes 98312 | tf_op jit(solution)/shard_map/ppermute | solution.py:358
  114.6 3.7 %collective-permute-start.45 = (bf16[128,128]{1,0:T(8,128)(2,1)S(1)}, bf16[128,128]{1,0:T(8,128)(2,1)S(1)}, u32[]{:S(2)}, u32[]{:S(2)}) collective-permute-start(bf16[128,128]{1,0:T(8,128)(2,1)S(1)} %get-tuple-element.122), channel_id=1, source_target_pairs={{0,1},{1,0},{2,3},{3,2},{4,5},{5,4},{6,7},{7,6},{8,9},{9,8},{10,11... | collective-permute-start | bytes 98312 | tf_op jit(solution)/shard_map/ppermute | solution.py:358
  114.7 4.1 %collective-permute-start.46 = (bf16[128,128]{1,0:T(8,128)(2,1)S(1)}, bf16[128,128]{1,0:T(8,128)(2,1)S(1)}, u32[]{:S(2)}, u32[]{:S(2)}) collective-permute-start(bf16[128,128]{1,0:T(8,128)(2,1)S(1)} %get-tuple-element.123), channel_id=1, source_target_pairs={{0,2},{1,3},{2,0},{3,1},{4,6},{5,7},{6,4},{7,5},{8,10},{9,11},{10,... | collective-permute-start | bytes 98312 | tf_op jit(solution)/shard_map/ppermute | solution.py:358
  115.5 5.3 %collective-permute-start.47 = (bf16[128,128]{1,0:T(8,128)(2,1)S(1)}, bf16[128,128]{1,0:T(8,128)(2,1)S(1)}, u32[]{:S(2)}, u32[]{:S(2)}) collective-permute-start(bf16[128,128]{1,0:T(8,128)(2,1)S(1)} %get-tuple-element.124), channel_id=1, source_target_pairs={{0,3},{1,2},{2,1},{3,0},{4,7},{5,6},{6,5},{7,4},{8,11},{9,10},{10,... | collective-permute-start | bytes 98312 | tf_op jit(solution)/shard_map/ppermute | solution.py:358
  116.4 6.3 %collective-permute-start.48 = (bf16[128,128]{1,0:T(8,128)(2,1)S(1)}, bf16[128,128]{1,0:T(8,128)(2,1)S(1)}, u32[]{:S(2)}, u32[]{:S(2)}) collective-permute-start(bf16[128,128]{1,0:T(8,128)(2,1)S(1)} %get-tuple-element.125), channel_id=1, source_target_pairs={{0,4},{1,5},{2,6},{3,7},{4,0},{5,1},{6,2},{7,3},{8,12},{9,13},{10,... | collective-permute-start | bytes 98312 | tf_op jit(solution)/shard_map/ppermute | solution.py:358
  116.4 7.1 %collective-permute-start.49 = (bf16[128,128]{1,0:T(8,128)(2,1)S(1)}, bf16[128,128]{1,0:T(8,128)(2,1)S(1)}, u32[]{:S(2)}, u32[]{:S(2)}) collective-permute-start(bf16[128,128]{1,0:T(8,128)(2,1)S(1)} %get-tuple-element.126), channel_id=1, source_target_pairs={{0,5},{1,4},{2,7},{3,6},{4,1},{5,0},{6,3},{7,2},{8,13},{9,12},{10,... | collective-permute-start | bytes 98312 | tf_op jit(solution)/shard_map/ppermute | solution.py:358
  118.2 8.0 %collective-permute-start.50 = (bf16[128,128]{1,0:T(8,128)(2,1)S(1)}, bf16[128,128]{1,0:T(8,128)(2,1)S(1)}, u32[]{:S(2)}, u32[]{:S(2)}) collective-permute-start(bf16[128,128]{1,0:T(8,128)(2,1)S(1)} %get-tuple-element.127), channel_id=1, source_target_pairs={{0,6},{1,7},{2,4},{3,5},{4,2},{5,3},{6,0},{7,1},{8,14},{9,15},{10,... | collective-permute-start | bytes 98312 | tf_op jit(solution)/shard_map/ppermute | solution.py:358
  118.8 8.2 %collective-permute-start.51 = (bf16[128,128]{1,0:T(8,128)(2,1)S(1)}, bf16[128,128]{1,0:T(8,128)(2,1)S(1)}, u32[]{:S(2)}, u32[]{:S(2)}) collective-permute-start(bf16[128,128]{1,0:T(8,128)(2,1)S(1)} %get-tuple-element.128), channel_id=1, source_target_pairs={{0,7},{1,6},{2,5},{3,4},{4,3},{5,2},{6,1},{7,0},{8,15},{9,14},{10,... | collective-permute-start | bytes 98312 | tf_op jit(solution)/shard_map/ppermute | solution.py:358
  120.8 9.1 %collective-permute-start.52 = (bf16[128,128]{1,0:T(8,128)(2,1)S(1)}, bf16[128,128]{1,0:T(8,128)(2,1)S(1)}, u32[]{:S(2)}, u32[]{:S(2)}) collective-permute-start(bf16[128,128]{1,0:T(8,128)(2,1)S(1)} %get-tuple-element.129), channel_id=1, source_target_pairs={{0,8},{1,9},{2,10},{3,11},{4,12},{5,13},{6,14},{7,15},{8,0},{9,1},... | collective-permute-start | bytes 98312 | tf_op jit(solution)/shard_map/ppermute | solution.py:358
  122.7 8.0 %collective-permute-start.53 = (bf16[128,128]{1,0:T(8,128)(2,1)S(1)}, bf16[128,128]{1,0:T(8,128)(2,1)S(1)}, u32[]{:S(2)}, u32[]{:S(2)}) collective-permute-start(bf16[128,128]{1,0:T(8,128)(2,1)S(1)} %get-tuple-element.130), channel_id=1, source_target_pairs={{0,9},{1,8},{2,11},{3,10},{4,13},{5,12},{6,15},{7,14},{8,1},{9,0},... | collective-permute-start | bytes 98312 | tf_op jit(solution)/shard_map/ppermute | solution.py:358
  123.5 10.9 %collective-permute-start.54 = (bf16[128,128]{1,0:T(8,128)(2,1)S(1)}, bf16[128,128]{1,0:T(8,128)(2,1)S(1)}, u32[]{:S(2)}, u32[]{:S(2)}) collective-permute-start(bf16[128,128]{1,0:T(8,128)(2,1)S(1)} %get-tuple-element.131), channel_id=1, source_target_pairs={{0,10},{1,11},{2,8},{3,9},{4,14},{5,15},{6,12},{7,13},{8,2},{9,3},... | collective-permute-start | bytes 98312 | tf_op jit(solution)/shard_map/ppermute | solution.py:358
  126.2 8.8 %collective-permute-start.55 = (bf16[128,128]{1,0:T(8,128)(2,1)S(1)}, bf16[128,128]{1,0:T(8,128)(2,1)S(1)}, u32[]{:S(2)}, u32[]{:S(2)}) collective-permute-start(bf16[128,128]{1,0:T(8,128)(2,1)S(1)} %get-tuple-element.132), channel_id=1, source_target_pairs={{0,11},{1,10},{2,9},{3,8},{4,15},{5,14},{6,13},{7,12},{8,3},{9,2},... | collective-permute-start | bytes 98312 | tf_op jit(solution)/shard_map/ppermute | solution.py:358
  127.0 8.0 %collective-permute-start.56 = (bf16[128,128]{1,0:T(8,128)(2,1)S(1)}, bf16[128,128]{1,0:T(8,128)(2,1)S(1)}, u32[]{:S(2)}, u32[]{:S(2)}) collective-permute-start(bf16[128,128]{1,0:T(8,128)(2,1)S(1)} %get-tuple-element.133), channel_id=1, source_target_pairs={{0,12},{1,13},{2,14},{3,15},{4,8},{5,9},{6,10},{7,11},{8,4},{9,5},... | collective-permute-start | bytes 98312 | tf_op jit(solution)/shard_map/ppermute | solution.py:358
  129.9 5.3 %collective-permute-start.57 = (bf16[128,128]{1,0:T(8,128)(2,1)S(1)}, bf16[128,128]{1,0:T(8,128)(2,1)S(1)}, u32[]{:S(2)}, u32[]{:S(2)}) collective-permute-start(bf16[128,128]{1,0:T(8,128)(2,1)S(1)} %get-tuple-element.134), channel_id=1, source_target_pairs={{0,13},{1,12},{2,15},{3,14},{4,9},{5,8},{6,11},{7,10},{8,5},{9,4},... | collective-permute-start | bytes 98312 | tf_op jit(solution)/shard_map/ppermute | solution.py:358
  130.6 6.6 %collective-permute-start.58 = (bf16[128,128]{1,0:T(8,128)(2,1)S(1)}, bf16[128,128]{1,0:T(8,128)(2,1)S(1)}, u32[]{:S(2)}, u32[]{:S(2)}) collective-permute-start(bf16[128,128]{1,0:T(8,128)(2,1)S(1)} %get-tuple-element.135), channel_id=1, source_target_pairs={{0,14},{1,15},{2,12},{3,13},{4,10},{5,11},{6,8},{7,9},{8,6},{9,7},... | collective-permute-start | bytes 98312 | tf_op jit(solution)/shard_map/ppermute | solution.py:358
  134.4 6.1 %collective-permute-start.59 = (bf16[128,128]{1,0:T(8,128)(2,1)S(1)}, bf16[128,128]{1,0:T(8,128)(2,1)S(1)}, u32[]{:S(2)}, u32[]{:S(2)}) collective-permute-start(bf16[128,128]{1,0:T(8,128)(2,1)S(1)} %get-tuple-element.136), channel_id=1, source_target_pairs={{0,15},{1,14},{2,13},{3,12},{4,11},{5,10},{6,9},{7,8},{8,7},{9,6},... | collective-permute-start | bytes 98312 | tf_op jit(solution)/shard_map/ppermute | solution.py:358
  (12 other events, 248.4 us)

commit v3 on v0

--- a/solution.py
+++ b/solution.py
@@ -12,7 +12,6 @@
 ITERS = 2
 LANES = 128
 HALF = TAPS // 2
-FLIP = 64
 F32 = jnp.float32
 BF16 = jnp.bfloat16
 I32 = jnp.int32
@@ -23,8 +22,8 @@
 hbm = lambda: pl.BlockSpec(memory_space=pl.ANY)
 
 
-def params():
-    return pltpu.CompilerParams(vmem_limit_bytes=VMEM_BYTES)
+def params(share=1.0):
+    return pltpu.CompilerParams(vmem_limit_bytes=int(share * VMEM_BYTES))
 
 
 def aligned(rows):
@@ -45,7 +44,7 @@
     lax.fori_loop(0, peers, peer, 0)
 
 
-def bank_rows(taps):
+def bank_rows(taps, height):
     hp = lax.Precision.HIGHEST
     width = taps.shape[1]
 
@@ -58,24 +57,18 @@
     k, l = grid(width)
     total = jnp.dot(taps, (k // TAPS == l // TAPS).astype(F32), precision=hp, preferred_element_type=F32)
     unit = taps / total
-    k, l = grid(NPSF * LANES)
-    j, l = l // LANES, (l + HALF) % LANES
-    wanted = jnp.where(l < TAPS, j * TAPS + TAPS - 1 - l, -1)
-    wanted = jnp.where((l >= FLIP) & (l < FLIP + TAPS), j * TAPS + l - FLIP, wanted)
-    row_part = jnp.dot(unit, (k == wanted).astype(F32), precision=hp, preferred_element_type=F32)
-    k, l = grid(NPSF * TAPS * LANES)
-    ji, l = l // LANES, (l + HALF) % LANES
-    j, i = ji // TAPS, ji % TAPS
-    wanted = NPSF * TAPS + j * TAPS + jnp.where(l < FLIP, i, TAPS - 1 - i)
-    col_part = jnp.dot(unit, (k == wanted).astype(F32), precision=hp, preferred_element_type=F32)
-    rows = []
-    for i in range(TAPS):
-        total = 0.0
-        for j in range(NPSF):
-            at = (j * TAPS + i) * LANES
-            total = total + row_part[:, j * LANES : (j + 1) * LANES] * col_part[:, at : at + LANES]
-        rows.append(total * (1.0 / NPSF))
-    return rows
+    k, l = grid(2 * NPSF * LANES)
+    mirror, j, l = l // (NPSF * LANES), l // LANES % NPSF, (l + HALF) % LANES
+    i, t = l // height, l % height
+    valid = (i < TAPS) & (t < TAPS)
+    row_tap = j * TAPS + jnp.where(mirror == 1, t, TAPS - 1 - t)
+    col_tap = (NPSF + j) * TAPS + jnp.where(mirror == 1, TAPS - 1 - i, i)
+    row_part = jnp.dot(unit, (valid & (k == row_tap)).astype(F32), precision=hp, preferred_element_type=F32)
+    col_part = jnp.dot(unit, (valid & (k == col_tap)).astype(F32), precision=hp, preferred_element_type=F32)
+    product = row_part * col_part * (1.0 / NPSF)
+    return [
+        sum(product[:, (m * NPSF + j) * LANES : (m * NPSF + j + 1) * LANES] for j in range(NPSF)) for m in range(2)
+    ]
 
 
 def first_send_kernel(
@@ -86,9 +79,9 @@
     load = pltpu.make_async_copy(model_ref, x_ref.at[pl.ds(0, total), :], sem)
     load.start()
     bank_ref[...] = jnp.zeros(bank_ref.shape, F32)
-    for i, row in enumerate(bank_rows(taps_ref[...])):
+    for m, row in enumerate(bank_rows(taps_ref[...], height)):
         for n in range(taps_ref.shape[0]):
-            bank_ref[n * TAPS + i : n * TAPS + i + 1, :] = row[n : n + 1, :]
+            bank_ref[2 * n + m : 2 * n + m + 1, :] = row[n : n + 1, :]
     bank = bank_ref[...].astype(BF16)
     load.wait()
     pack_slots(plane_ref, row_ref, cover_ref, tile_rows, height, rows_each, x_ref, packed_ref)
@@ -156,13 +149,14 @@
     save.wait()
 
 
-def tables_kernel(capacity, height, rows_each, slot_ref, start_ref, stop_ref, use_ref, move_ref, length_ref):
+def tables_kernel(capacity, height, rows_each, slot_ref, start_ref, stop_ref, table_ref, length_ref):
     exposures, pieces = slot_ref.shape
-    slots = move_ref.shape[1]
+    slots = length_ref.shape[0]
+    stamp_row, return_row = 2 * pieces, 2 * pieces + 1
 
     def clear(s, _):
         length_ref[s] = 0
-        move_ref[0, s] = 0
+        table_ref[stamp_row, s] = 0
         return 0
 
     lax.fori_loop(0, slots, clear, 0, unroll=8)
@@ -174,7 +168,7 @@
             @pl.when(s >= 0)
             def _():
                 length_ref[s] = stop_ref[e, k] - start_ref[e, k]
-                move_ref[0, s] = e * height + start_ref[e, k]
+                table_ref[stamp_row, s] = e * height + start_ref[e, k]
 
         return 0
 
@@ -184,7 +178,7 @@
         at = o * rows_each
         for c in range(capacity):
             s = o * capacity + c
-            move_ref[1, s] = at
+            table_ref[return_row, s] = at
             at = at + length_ref[s]
         return 0
 
@@ -194,9 +188,9 @@
         for k in range(pieces):
             s = slot_ref[e, k]
             live = s >= 0
-            begin = move_ref[1, jnp.maximum(s, 0)]
-            use_ref[2 * k, e] = jnp.where(live, height + begin - start_ref[e, k], 0)
-            use_ref[2 * k + 1, e] = jnp.where(live, start_ref[e, k], height)
+            begin = table_ref[return_row, jnp.maximum(s, 0)]
+            table_ref[2 * k, e] = jnp.where(live, height + begin - start_ref[e, k], 0)
+            table_ref[2 * k + 1, e] = jnp.where(live, start_ref[e, k], height)
         return 0
 
     lax.fori_loop(0, exposures, point, 0, unroll=2)
@@ -207,8 +201,7 @@
     pieces,
     batches_each,
     last,
-    use_ref,
-    move_ref,
+    table_ref,
     weight_ref,
     batch_ref,
     arrived_ref,
@@ -217,70 +210,68 @@
     *rest,
 ):
     if last:
-        out_ref, residual_ref, rows_ref, bank_ref, result_ref, packed_ref, fwd_ref, bwd_ref, shift_ref, work_ref = rest
+        out_ref, residual_ref, rows_ref, bank_ref, result_ref, packed_ref, blur_ref, back_ref = rest
     else:
-        out_ref, rows_ref, bank_ref, result_ref, packed_ref, fwd_ref, bwd_ref, shift_ref, work_ref = rest
+        out_ref, rows_ref, bank_ref, result_ref, packed_ref, blur_ref, back_ref = rest
     peers, rows_each, _ = out_ref.shape
     extra = bank_in_ref.shape[1]
     exposures = batch_ref.shape[0]
-    each = LANES // height
+    slots = peers * (2 * rows_each // height)
+    abreast = max(n for n in (1, 2, 4, 8, 16) if exposures % n == 0)
+    place = lax.broadcasted_iota(I32, (height, LANES), 0)
+    lane = lax.broadcasted_iota(I32, (height, LANES), 1)
     for o in range(peers):
         rows_ref[height + o * rows_each : height + (o + 1) * rows_each, :] = arrived_ref[o].astype(F32)
         bank_ref[o * extra : (o + 1) * extra, :] = bank_in_ref[o].astype(F32)
-    place = lax.broadcasted_iota(I32, (height, LANES), 0)
-    lane16 = lax.broadcasted_iota(I32, (height, LANES), 1)
-    lane = lax.broadcasted_iota(I32, (LANES, LANES), 1)
-
-    def fill_shifts(x):
-        for i in range(TAPS):
-            v = i - HALF
-            if v == 0:
-                moved = x
-            else:
-                moved = pltpu.roll(x, v % LANES, 1)
-                moved = jnp.where((lane >= v) & (lane < LANES + v), moved, 0.0)
-            shift_ref[i * LANES : (i + 1) * LANES, :] = moved.astype(BF16)
-
-    def group(g, _):
-        for n in range(each):
-            e = g * each + n
+
+    gap = lane % height - place
+    near = (gap <= HALF) & (gap >= -HALF) & (lane < TAPS * height)
+
+    def operators(o, _):
+        for n in range(batches_each):
+            for m, ref in enumerate((blur_ref, back_ref)):
+                taps = jnp.broadcast_to(bank_ref[pl.ds(o * extra + 2 * n + m, 1), :], (height, LANES))
+                ref[o * batches_each + n] = jnp.where(
+                    near, pltpu.roll(taps, 0, 1, stride=1, stride_axis=0), 0.0
+                ).astype(BF16)
+        return 0
+
+    lax.fori_loop(0, peers, operators, 0, unroll=4)
+
+    def shifted(x):
+        parts = []
+        for v in range(-HALF, HALF + 1):
+            moved = x if v == 0 else pltpu.roll(x, v % LANES, 1)
+            parts.append(jnp.where((lane >= v) & (lane < LANES + v), moved, jnp.zeros((), BF16)))
+        parts.append(jnp.zeros((LANES - TAPS * height, LANES), BF16))
+        return jnp.concatenate(parts, axis=0)
+
+    def step(s, _):
+        for q in range(abreast):
+            e = s * abreast + q
             b = batch_ref[e]
-            bank_row = lax.div(b, batches_each) * extra + lax.rem(b, batches_each) * TAPS
-            own = (lane16 >= n * height) & (lane16 < (n + 1) * height)
-            here = slice(n * height, (n + 1) * height)
-            for i in range(TAPS):
-                taps = jnp.broadcast_to(bank_ref[pl.ds(bank_row + i, 1), :], (height, LANES))
-                there = slice(i * LANES, (i + 1) * LANES)
-                f = pltpu.roll(taps, n * height, 1, stride=1, stride_axis=0)
-                r = pltpu.roll(taps, (n * height + FLIP) % LANES, 1, stride=1, stride_axis=0)
-                fwd_ref[here, there] = jnp.where(own, f, 0.0).astype(BF16)
-                bwd_ref[here, there] = jnp.where(own, r, 0.0).astype(BF16)
-            stamp = rows_ref[pl.ds(use_ref[0, e], height), :]
+            stamp = rows_ref[pl.ds(table_ref[0, e], height), :]
             for k in range(1, pieces):
-                piece = rows_ref[pl.ds(use_ref[2 * k, e], height), :]
-                stamp = jnp.where(place >= use_ref[2 * k + 1, e], piece, stamp)
-            work_ref[here, :] = stamp
-        fill_shifts(work_ref[...])
-        predicted = jnp.dot(fwd_ref[...], shift_ref[...], preferred_element_type=F32)
-        for n in range(each):
-            e = g * each + n
-            here = slice(n * height, (n + 1) * height)
-            residual = weight_ref[e] * (predicted[here, :] - seen_ref[e].astype(F32))
+                piece = rows_ref[pl.ds(table_ref[2 * k, e], height), :]
+                stamp = jnp.where(place >= table_ref[2 * k + 1, e], piece, stamp)
+            predicted = jnp.dot(blur_ref[b], shifted(stamp.astype(BF16)), preferred_element_type=F32)
+            residual = weight_ref[e] * (predicted - seen_ref[e].astype(F32))
             if last:
                 residual_ref[e] = residual
-            work_ref[here, :] = residual
-        fill_shifts(work_ref[...])
-        first = pl.multiple_of(g * LANES, LANES)
-        result_ref[pl.ds(first, LANES), :] = jnp.dot(bwd_ref[...], shift_ref[...], preferred_element_type=F32)
-        return 0
-
-    lax.fori_loop(0, exposures // each, group, 0)
+            result_ref[pl.ds(pl.multiple_of(e * height, height), height), :] = jnp.dot(
+                back_ref[b], shifted(residual.astype(BF16)), preferred_element_type=F32
+            )
+        return 0
+
+    lax.fori_loop(0, exposures // abreast, step, 0)
 
     def move(s, _):
-        packed_ref[pl.ds(move_ref[1, s], height), :] = result_ref[pl.ds(move_ref[0, s], height), :]
-        return 0
-
-    lax.fori_loop(0, move_ref.shape[1], move, 0, unroll=16)
+        packed_ref[pl.ds(table_ref[2 * pieces + 1, s], height), :] = result_ref[
+            pl.ds(table_ref[2 * pieces, s], height), :
+        ]
+        return 0
+
+    lax.fori_loop(0, slots, move, 0, unroll=16)
     for o in range(peers):
         out_ref[o, :, :] = packed_ref[o * rows_each : (o + 1) * rows_each, :].astype(BF16)
 
@@ -307,9 +298,10 @@
     pieces = use_slot.shape[1]
     total = tile_count * bands * tile_rows
     rows_each = capacity * height // 2
-    extra = aligned(psf_taps.shape[0] * TAPS)
+    batches_each = psf_taps.shape[0]
+    extra = aligned(batches_each * 2)
     block = rows_each + extra
-    assert columns == LANES and rows_each % extra == 0 and (count * height) % LANES == 0
+    assert columns == LANES and rows_each % extra == 0 and TAPS * height <= LANES - HALF
     x = model.reshape(total, columns)
 
     def swap(a):
@@ -326,18 +318,15 @@
             pltpu.VMEM((extra, columns), F32),
             pltpu.SemaphoreType.DMA,
         ],
-        compiler_params=params(),
+        compiler_params=params(2.5),
         name="first_send",
     )(send_plane, send_row, send_cover, psf_taps, x)
     arrived = swap(outbound)
-    use, move = pl.pallas_call(
+    table = pl.pallas_call(
         functools.partial(tables_kernel, capacity, height, rows_each),
-        out_shape=(
-            jax.ShapeDtypeStruct((2 * pieces, count), I32),
-            jax.ShapeDtypeStruct((2, peers * capacity), I32),
-        ),
+        out_shape=jax.ShapeDtypeStruct((2 * pieces + 2, max(count, peers * capacity)), I32),
         in_specs=[smem(), smem(), smem()],
-        out_specs=(smem(), smem()),
+        out_specs=smem(),
         scratch_shapes=[pltpu.SMEM((peers * capacity,), I32)],
         cost_estimate=pl.CostEstimate(flops=4_000_000, bytes_accessed=8_000_000, transcendentals=0),
         name="tables",
@@ -347,11 +336,10 @@
         last = sweep == ITERS - 1
         rows_shape = jax.ShapeDtypeStruct((peers, rows_each, columns), BF16)
         outs = pl.pallas_call(
-            functools.partial(blur_kernel, height, pieces, psf_taps.shape[0], last),
+            functools.partial(blur_kernel, height, pieces, batches_each, last),
             grid=(1,),
             out_shape=(rows_shape, jax.ShapeDtypeStruct(exposures.shape, F32)) if last else rows_shape,
             in_specs=[
-                smem(),
                 smem(),
                 smem(),
                 smem(),
@@ -365,14 +353,12 @@
                 pltpu.VMEM((peers * extra, columns), F32),
                 pltpu.VMEM((count * height + height, columns), F32),
                 pltpu.VMEM((peers * rows_each + height, columns), F32),
-                pltpu.VMEM((LANES, TAPS * LANES), BF16),
-                pltpu.VMEM((LANES, TAPS * LANES), BF16),
-                pltpu.VMEM((TAPS * LANES, columns), BF16),
-                pltpu.VMEM((LANES, columns), F32),
+                pltpu.VMEM((peers * batches_each, height, LANES), BF16),
+                pltpu.VMEM((peers * batches_each, height, LANES), BF16),
             ],
             compiler_params=params(),
             name="blur",
-        )(use, move, inv_var, exp_batch, arrived, with_bank, exposures)
+        )(table, inv_var, exp_batch, arrived, with_bank, exposures)
         outgoing = outs[0] if last else outs
         returned = swap(outgoing)
         new_shape = jax.ShapeDtypeStruct((total, columns), F32)

time: 122 us -> 108 us (0.89)
  Pallas kernels: 47 us -> 37.5 us
  local copies, waits for them, and re-layouts: 7.77 us -> 2.97 us
    pallas_call x2, Pallas kernels: 25.8 us -> 15.5 us  [body(): pl.pallas_call(functools.partial(blur_kernel, height, pieces, batches_eac...]
    unnamed x43 -> x31, local copies, waits for them, and re-layouts: 7.77 us -> 2.97 us
  transfers between devices with their start and end apart: 1 -> 1, of which waited for: 1 -> 1; matrix products, arithmetic and copies ran while one was open for 2% -> 2% of each run, Pallas kernels for 8% -> 9%
where the time goes in v3:
time: 108 us; the launch traced here: 107 us
  blocking collectives  55.4 us (51%)
  Pallas kernels  37.5 us (35%)
  starting transfers between devices  7.37 us (7%)
  waiting for transfers between devices  3.32 us (3%)
  local copies, waits for them, and re-layouts  2.97 us (3%)
    all_to_all x3, blocking collectives, swap(): return lax.all_to_all(a, 'sky', split_axis=0, concat_axis=0, tiled=True)  55.4 us
    pallas_call x2, Pallas kernels, body(): pl.pallas_call(functools.partial(blur_kernel, height, pieces, batches_eac...  15.5 us
    pallas_call x1, Pallas kernels, body(): pl.pallas_call(functools.partial(tables_kernel, capacity, height, rows_ea...  9.94 us
    pallas_call x2, Pallas kernels, body(): pl.pallas_call(functools.partial(update_kernel, bands, tile_rows, height,...  7.72 us
    all_to_all x1, starting transfers between devices, swap(): return lax.all_to_all(a, 'sky', split_axis=0, concat_axis=0, tiled=True)  7.37 us
    pallas_call x1, Pallas kernels, body(): pl.pallas_call(functools.partial(first_send_kernel, tile_rows, height, ro...  4.41 us
    all_to_all x1, waiting for transfers between devices, swap(): return lax.all_to_all(a, 'sky', split_axis=0, concat_axis=0, tiled=True)  3.32 us
    unnamed x31, local copies, waits for them, and re-layouts  2.97 us
  transfers between devices with their start and end apart: 1, of which 1 were waited for; matrix products, arithmetic and copies ran while one was open for 2% of the time, Pallas kernels for 9%

profile of v3, /device:TPU:0, one launch (start us, length us, event | category | flops | bytes accessed | tf_op | source)
XLA Modules:
  0.0 107.4 jit_solution(1697742017788227977)
XLA Ops:
  0.6 0.0 copy-start.11
  0.6 0.0 copy-start.12
  0.7 0.0 copy-start.13
  0.7 0.0 copy-start.1
  0.7 0.0 copy-start.9
  0.7 0.0 copy-start.10
  0.7 4.4 %first_send.1 = bf16[16,144,128]{2,1,0:T(8,128)(2,1)} custom-call(s32[16,16]{1,0:T(8,128)} %plane_ref.5, s32[16,16]{1,0:T(8,128)} %row_ref.5, s32[16,16]{1,0:T(8,128)} %cover_ref.5, f32[2,56]{1,0:T(2,128)} %taps_ref.1, f32[3072,128]{1,0:T(8,128)} %bitcast.2), custom_call_target="tpu_custom_call" | custom-call | tf_op jit(solution)/shard_map/first_send/pallas_call | solution.py:310
  5.1 7.4 %all-to-all-start = ((bf16[16,144,128]{2,1,0:T(8,128)(2,1)}), bf16[16,144,128]{2,1,0:T(8,128)(2,1)S(1)}, u32[]{:S(2)}, u32[]{:S(2)}) async-start(bf16[16,144,128]{2,1,0:T(8,128)(2,1)} %first_send.1), calls=%async_computation | async-start | bytes 1179648 | tf_op jit(solution)/shard_map/all_to_all | solution.py:308
  12.5 0.0 copy-done.11
  12.5 0.7 copy.16.slot_ref
  13.2 0.0 copy-done.12
  13.2 0.7 copy.17.start_ref
  14.0 0.0 copy-done.13
  14.0 0.7 copy.18.stop_ref
  14.7 9.9 %tables.1.table_ref = s32[6,256]{1,0:T(8,128)} custom-call(s32[128,2]{1,0:T(8,128)} %copy.16.slot_ref, s32[128,2]{1,0:T(8,128)} %copy.17.start_ref, s32[128,2]{1,0:T(8,128)} %copy.18.stop_ref), custom_call_target="tpu_custom_call" | custom-call | flops 4000000 | bytes 8000000 | tf_op jit(solution)/shard_map/tables/pallas_call | solution.py:325
  24.7 0.0 copy-start
  24.7 0.0 copy-start.2
  24.7 0.0 copy-start.3
  24.7 0.0 copy-start.4
  24.7 3.3 %all-to-all-done.arrived_ref.bank_in_ref = bf16[16,144,128]{2,1,0:T(8,128)(2,1)S(1)} async-done(((bf16[16,144,128]{2,1,0:T(8,128)(2,1)}), bf16[16,144,128]{2,1,0:T(8,128)(2,1)S(1)}, u32[]{:S(2)}, u32[]{:S(2)}) %all-to-all-start) | async-done | bytes 589856 | tf_op jit(solution)/shard_map/all_to_all | solution.py:308
  28.0 0.0 copy-done.1
  28.0 0.0 copy-done.9
  28.0 0.0 copy-done.10
  28.0 0.0 copy-start.5
  28.1 0.7 copy-done.5
  28.7 0.0 copy-start.6
  28.7 0.0 copy-start.7
  28.8 0.0 copy-start.8
  28.8 7.3 %blur.2 = bf16[16,128,128]{2,1,0:T(8,128)(2,1)S(1)} custom-call(s32[6,256]{1,0:T(8,128)S(1)} %copy-done.5, f32[128]{0:T(128)S(1)} %copy-done.9, s32[128]{0:T(128)S(1)} %copy-done.10, bf16[16,144,128]{2,1,0:T(8,128)(2,1)S(1)} %all-to-all-done.arrived_ref.bank_in_ref, bf16[16,144,128]{2,1,0:T(8,128)(2,1)S(1)} %all-to-all-done.arrived_ref.bank_in_ref, ...), custom_call_target="tpu_custom_call" | custom-call | tf_op jit(solution)/shard_map/blur/pallas_call | solution.py:338
  36.0 18.7 %all_to_all.20.returned_ref = bf16[16,128,128]{2,1,0:T(8,128)(2,1)S(1)} all-to-all(bf16[16,128,128]{2,1,0:T(8,128)(2,1)S(1)} %blur.2), channel_id=1, replica_groups=mesh['groups'=2,'sky'=16] {'sky'}, dimensions={0} | all-to-all | bytes 1048576 | tf_op jit(solution)/shard_map/all_to_all | solution.py:308
  54.7 0.0 copy-done
  54.7 0.0 copy-done.2
  54.7 0.0 copy-done.3
  54.7 0.0 copy-done.4
  54.7 0.0 copy-done.6
  54.8 0.0 copy-done.7
  54.8 0.0 copy-done.8
  54.8 3.9 %update.2 = (f32[3072,128]{1,0:T(8,128)S(1)}, bf16[16,128,128]{2,1,0:T(8,128)(2,1)S(1)}) custom-call(s32[16,16]{1,0:T(8,128)S(1)} %copy-done.2, s32[16,16]{1,0:T(8,128)S(1)} %copy-done.3, s32[16,16]{1,0:T(8,128)S(1)} %copy-done.4, f32[6]{0:T(128)S(1)} %copy-done.6, s32[2]{0:T(128)S(1)} %copy-done.7, s32[2]{0:T(128)S(1)} %copy-done.8, ...), custom_call_target="tpu_custom_call" | custom-call | tf_op jit(solution)/shard_map/update/pallas_call | solution.py:373
  58.7 18.4 %all_to_all.21.arrived_ref = bf16[16,128,128]{2,1,0:T(8,128)(2,1)S(1)} all-to-all(bf16[16,128,128]{2,1,0:T(8,128)(2,1)S(1)} %get-tuple-element.6), channel_id=1, replica_groups=mesh['groups'=2,'sky'=16] {'sky'}, dimensions={0} | all-to-all | bytes 1048576 | tf_op jit(solution)/shard_map/all_to_all | solution.py:308
  77.1 8.2 %blur.3 = (bf16[16,128,128]{2,1,0:T(8,128)(2,1)S(1)}, f32[128,16,128]{2,1,0:T(8,128)}) custom-call(s32[6,256]{1,0:T(8,128)S(1)} %copy-done.5, f32[128]{0:T(128)S(1)} %copy-done.9, s32[128]{0:T(128)S(1)} %copy-done.10, bf16[16,128,128]{2,1,0:T(8,128)(2,1)S(1)} %all_to_all.21.arrived_ref, bf16[16,144,128]{2,1,0:T(8,128)(2,1)S(1)} %all-to-all-done.arrived_ref.bank_in_ref, ...), custom_call_target="tpu_custom_call" | custom-call | tf_op jit(solution)/shard_map/blur/pallas_call | solution.py:338
  85.2 18.4 %all_to_all.22.returned_ref = bf16[16,128,128]{2,1,0:T(8,128)(2,1)S(1)} all-to-all(bf16[16,128,128]{2,1,0:T(8,128)(2,1)S(1)} %get-tuple-element.7), channel_id=1, replica_groups=mesh['groups'=2,'sky'=16] {'sky'}, dimensions={0} | all-to-all | bytes 1048576 | tf_op jit(solution)/shard_map/all_to_all | solution.py:308
  103.6 3.8 %update.3 = f32[3072,128]{1,0:T(8,128)} custom-call(s32[16,16]{1,0:T(8,128)S(1)} %copy-done.2, s32[16,16]{1,0:T(8,128)S(1)} %copy-done.3, s32[16,16]{1,0:T(8,128)S(1)} %copy-done.4, f32[6]{0:T(128)S(1)} %copy-done.6, s32[2]{0:T(128)S(1)} %copy-done.7, s32[2]{0:T(128)S(1)} %copy-done.8, bf16[16,128,128]{2,1,0:T(8,128)(2,1)S(1)} %all_to_all.22.returned_ref, ...), custom_call_target="tpu_custom_call" | custom-call | tf_op jit(solution)/shard_map/update/pallas_call | solution.py:373
Async XLA Ops:
  0.6 11.9 %copy-start.11 = (s32[128,2]{0,1:T(2,128)S(1)}, s32[128,2]{0,1:T(2,128)}, u32[]{:S(2)}) copy-start(s32[128,2]{0,1:T(2,128)} %param.23) | copy-start | bytes 3076
  0.6 12.6 %copy-start.12 = (s32[128,2]{0,1:T(2,128)S(1)}, s32[128,2]{0,1:T(2,128)}, u32[]{:S(2)}) copy-start(s32[128,2]{0,1:T(2,128)} %param.24) | copy-start | bytes 3076
  0.7 13.3 %copy-start.13 = (s32[128,2]{0,1:T(2,128)S(1)}, s32[128,2]{0,1:T(2,128)}, u32[]{:S(2)}) copy-start(s32[128,2]{0,1:T(2,128)} %param.25) | copy-start | bytes 3076
  0.7 27.4 %copy-start.1 = (bf16[128,16,128]{2,1,0:T(8,128)(2,1)S(1)}, bf16[128,16,128]{2,1,0:T(8,128)(2,1)}, u32[]{:S(2)}) copy-start(bf16[128,16,128]{2,1,0:T(8,128)(2,1)} %seen_ref.3) | copy-start | bytes 1572868
  0.7 27.4 %copy-start.9 = (f32[128]{0:T(128)S(1)}, f32[128]{0:T(128)}, u32[]{:S(2)}) copy-start(f32[128]{0:T(128)} %weight_ref.3) | copy-start | bytes 1540
  0.7 27.4 %copy-start.10 = (s32[128]{0:T(128)S(1)}, s32[128]{0:T(128)}, u32[]{:S(2)}) copy-start(s32[128]{0:T(128)} %batch_ref.3) | copy-start | bytes 1540
  5.1 22.9 %all-to-all-start = ((bf16[16,144,128]{2,1,0:T(8,128)(2,1)}), bf16[16,144,128]{2,1,0:T(8,128)(2,1)S(1)}, u32[]{:S(2)}, u32[]{:S(2)}) async-start(bf16[16,144,128]{2,1,0:T(8,128)(2,1)} %first_send.1), calls=%async_computation | async-start | bytes 1179648 | tf_op jit(solution)/shard_map/all_to_all | solution.py:308
  24.7 30.1 %copy-start = (f32[2,6,256,128]{3,2,1,0:T(8,128)S(1)}, f32[2,6,256,128]{3,2,1,0:T(8,128)}, u32[]{:S(2)}) copy-start(f32[2,6,256,128]{3,2,1,0:T(8,128)} %param.14) | copy-start | bytes 4718596
  24.7 30.0 %copy-start.2 = (s32[16,16]{1,0:T(8,128)S(1)}, s32[16,16]{1,0:T(8,128)}, u32[]{:S(2)}) copy-start(s32[16,16]{1,0:T(8,128)} %plane_ref.5) | copy-start | bytes 3076
  24.7 30.0 %copy-start.3 = (s32[16,16]{1,0:T(8,128)S(1)}, s32[16,16]{1,0:T(8,128)}, u32[]{:S(2)}) copy-start(s32[16,16]{1,0:T(8,128)} %row_ref.5) | copy-start | bytes 3076
  24.7 30.0 %copy-start.4 = (s32[16,16]{1,0:T(8,128)S(1)}, s32[16,16]{1,0:T(8,128)}, u32[]{:S(2)}) copy-start(s32[16,16]{1,0:T(8,128)} %cover_ref.5) | copy-start | bytes 3076
  28.0 0.7 copy-start.5
  28.7 26.0 %copy-start.6 = (f32[6]{0:T(128)S(1)}, f32[6]{0:T(128)}, u32[]{:S(2)}) copy-start(f32[6]{0:T(128)} %step_ref.3) | copy-start | bytes 76
  28.7 26.0 %copy-start.7 = (s32[2]{0:T(128)S(1)}, s32[2]{0:T(128)}, u32[]{:S(2)}) copy-start(s32[2]{0:T(128)} %lo_ref.3) | copy-start | bytes 28
  28.8 26.0 %copy-start.8 = (s32[2]{0:T(128)S(1)}, s32[2]{0:T(128)}, u32[]{:S(2)}) copy-start(s32[2]{0:T(128)} %hi_ref.3) | copy-start | bytes 28

commit v4 on v3

--- a/solution.py
+++ b/solution.py
@@ -28,6 +28,12 @@
 
 def aligned(rows):
     return -(-rows // 16) * 16
+
+
+def exchange_order(peers):
+    if peers % 2:
+        return list(range(peers))
+    return [p // 2 + p % 2 * (peers // 2) for p in range(peers)]
 
 
 def pack_slots(plane_ref, row_ref, cover_ref, tile_rows, height, rows_each, x_ref, packed_ref):
@@ -85,9 +91,9 @@
     bank = bank_ref[...].astype(BF16)
     load.wait()
     pack_slots(plane_ref, row_ref, cover_ref, tile_rows, height, rows_each, x_ref, packed_ref)
-    for d in range(peers):
-        out_ref[d, :rows_each, :] = packed_ref[d * rows_each : (d + 1) * rows_each, :].astype(BF16)
-        out_ref[d, rows_each:, :] = bank
+    for p, d in enumerate(exchange_order(peers)):
+        out_ref[p, :rows_each, :] = packed_ref[d * rows_each : (d + 1) * rows_each, :].astype(BF16)
+        out_ref[p, rows_each:, :] = bank
 
 
 def update_kernel(
@@ -117,8 +123,8 @@
     load.start()
     for p in range(planes):
         scale_ref[p] = step_ref[p % bands]
-    for d in range(peers):
-        back_ref[d * rows_each : (d + 1) * rows_each, :] = returned_ref[d].astype(F32)
+    for p, d in enumerate(exchange_order(peers)):
+        back_ref[d * rows_each : (d + 1) * rows_each, :] = returned_ref[p].astype(F32)
     load.wait()
     place = lax.broadcasted_iota(I32, (height, LANES), 0)
 
@@ -144,8 +150,8 @@
     save.start()
     if not last:
         pack_slots(plane_ref, row_ref, cover_ref, tile_rows, height, rows_each, x_ref, packed_ref)
-        for d in range(peers):
-            out_ref[d, :, :] = packed_ref[d * rows_each : (d + 1) * rows_each, :].astype(BF16)
+        for p, d in enumerate(exchange_order(peers)):
+            out_ref[p, :, :] = packed_ref[d * rows_each : (d + 1) * rows_each, :].astype(BF16)
     save.wait()
 
 
@@ -210,9 +216,9 @@
     *rest,
 ):
     if last:
-        out_ref, residual_ref, rows_ref, bank_ref, result_ref, packed_ref, blur_ref, back_ref = rest
+        out_ref, residual_ref, rows_ref, bank_ref, result_ref, packed_ref, held_ref, blur_ref, back_ref = rest
     else:
-        out_ref, rows_ref, bank_ref, result_ref, packed_ref, blur_ref, back_ref = rest
+        out_ref, rows_ref, bank_ref, result_ref, packed_ref, held_ref, blur_ref, back_ref = rest
     peers, rows_each, _ = out_ref.shape
     extra = bank_in_ref.shape[1]
     exposures = batch_ref.shape[0]
@@ -220,9 +226,9 @@
     abreast = max(n for n in (1, 2, 4, 8, 16) if exposures % n == 0)
     place = lax.broadcasted_iota(I32, (height, LANES), 0)
     lane = lax.broadcasted_iota(I32, (height, LANES), 1)
-    for o in range(peers):
-        rows_ref[height + o * rows_each : height + (o + 1) * rows_each, :] = arrived_ref[o].astype(F32)
-        bank_ref[o * extra : (o + 1) * extra, :] = bank_in_ref[o].astype(F32)
+    for p, o in enumerate(exchange_order(peers)):
+        rows_ref[height + o * rows_each : height + (o + 1) * rows_each, :] = arrived_ref[p].astype(F32)
+        bank_ref[o * extra : (o + 1) * extra, :] = bank_in_ref[p].astype(F32)
 
     gap = lane % height - place
     near = (gap <= HALF) & (gap >= -HALF) & (lane < TAPS * height)
@@ -246,24 +252,38 @@
         parts.append(jnp.zeros((LANES - TAPS * height, LANES), BF16))
         return jnp.concatenate(parts, axis=0)
 
-    def step(s, _):
+    def correlate(s):
         for q in range(abreast):
             e = s * abreast + q
-            b = batch_ref[e]
+            here = pl.ds(pl.multiple_of(e * height, height), height)
+            result_ref[here, :] = jnp.dot(
+                back_ref[batch_ref[e]], shifted(held_ref[here, :]), preferred_element_type=F32
+            )
+
+    def blur(s):
+        for q in range(abreast):
+            e = s * abreast + q
             stamp = rows_ref[pl.ds(table_ref[0, e], height), :]
             for k in range(1, pieces):
                 piece = rows_ref[pl.ds(table_ref[2 * k, e], height), :]
                 stamp = jnp.where(place >= table_ref[2 * k + 1, e], piece, stamp)
-            predicted = jnp.dot(blur_ref[b], shifted(stamp.astype(BF16)), preferred_element_type=F32)
+            predicted = jnp.dot(
+                blur_ref[batch_ref[e]], shifted(stamp.astype(BF16)), preferred_element_type=F32
+            )
             residual = weight_ref[e] * (predicted - seen_ref[e].astype(F32))
             if last:
                 residual_ref[e] = residual
-            result_ref[pl.ds(pl.multiple_of(e * height, height), height), :] = jnp.dot(
-                back_ref[b], shifted(residual.astype(BF16)), preferred_element_type=F32
-            )
-        return 0
-
-    lax.fori_loop(0, exposures // abreast, step, 0)
+            held_ref[pl.ds(pl.multiple_of(e * height, height), height), :] = residual.astype(BF16)
+
+    def step(s, _):
+        correlate(s - 1)
+        blur(s)
+        return 0
+
+    steps = exposures // abreast
+    blur(0)
+    lax.fori_loop(1, steps, step, 0)
+    correlate(steps - 1)
 
     def move(s, _):
         packed_ref[pl.ds(table_ref[2 * pieces + 1, s], height), :] = result_ref[
@@ -272,8 +292,8 @@
         return 0
 
     lax.fori_loop(0, slots, move, 0, unroll=16)
-    for o in range(peers):
-        out_ref[o, :, :] = packed_ref[o * rows_each : (o + 1) * rows_each, :].astype(BF16)
+    for p, o in enumerate(exchange_order(peers)):
+        out_ref[p, :, :] = packed_ref[o * rows_each : (o + 1) * rows_each, :].astype(BF16)
 
 
 def body(
@@ -305,7 +325,9 @@
     x = model.reshape(total, columns)
 
     def swap(a):
-        return lax.all_to_all(a, "sky", split_axis=0, concat_axis=0, tiled=True)
+        return lax.all_to_all(
+            a, "sky", split_axis=0, concat_axis=0, tiled=True, axis_index_groups=[exchange_order(peers)]
+        )
 
     outbound = pl.pallas_call(
         functools.partial(first_send_kernel, tile_rows, height, rows_each),
@@ -353,6 +375,7 @@
                 pltpu.VMEM((peers * extra, columns), F32),
                 pltpu.VMEM((count * height + height, columns), F32),
                 pltpu.VMEM((peers * rows_each + height, columns), F32),
+                pltpu.VMEM((count * height, columns), BF16),
                 pltpu.VMEM((peers * batches_each, height, LANES), BF16),
                 pltpu.VMEM((peers * batches_each, height, LANES), BF16),
             ],

time: 108 us -> 106 us (0.981)
  Pallas kernels: 37.5 us -> 34.3 us
  waiting for transfers between devices: 3.32 us -> 4.48 us
    pallas_call x2, Pallas kernels: 15.5 us -> 12.2 us  [body(): pl.pallas_call(functools.partial(blur_kernel, height, pieces, batches_eac...]
    all_to_all x1, waiting for transfers between devices: 3.32 us -> 4.48 us  [swap(): lax.all_to_all(a, 'sky', split_axis=0, concat_axis=0, tiled=True, axis_in...]
where the time goes in v4:
time: 106 us; the launch traced here: 105 us
  blocking collectives  55.3 us (52%)
  Pallas kernels  34.3 us (32%)
  starting transfers between devices  7.37 us (7%)
  waiting for transfers between devices  4.48 us (4%)
  local copies, waits for them, and re-layouts  2.97 us (3%)
    all_to_all x3, blocking collectives, swap(): lax.all_to_all(a, 'sky', split_axis=0, concat_axis=0, tiled=True, axis_in...  55.3 us
    pallas_call x2, Pallas kernels, body(): pl.pallas_call(functools.partial(blur_kernel, height, pieces, batches_eac...  12.2 us
    pallas_call x1, Pallas kernels, body(): pl.pallas_call(functools.partial(tables_kernel, capacity, height, rows_ea...  9.94 us
    pallas_call x2, Pallas kernels, body(): pl.pallas_call(functools.partial(update_kernel, bands, tile_rows, height,...  7.74 us
    all_to_all x1, starting transfers between devices, swap(): lax.all_to_all(a, 'sky', split_axis=0, concat_axis=0, tiled=True, axis_in...  7.37 us
    all_to_all x1, waiting for transfers between devices, swap(): lax.all_to_all(a, 'sky', split_axis=0, concat_axis=0, tiled=True, axis_in...  4.48 us
    pallas_call x1, Pallas kernels, body(): pl.pallas_call(functools.partial(first_send_kernel, tile_rows, height, ro...  4.41 us
    unnamed x31, local copies, waits for them, and re-layouts  2.97 us
  transfers between devices with their start and end apart: 1, of which 1 were waited for; matrix products, arithmetic and copies ran while one was open for 2% of the time, Pallas kernels for 9%

profile of v4, /device:TPU:0, one launch (start us, length us, event | category | flops | bytes accessed | tf_op | source)
XLA Modules:
  0.0 105.2 jit_solution(1886319562094171800)
XLA Ops:
  0.6 0.0 copy-start.11
  0.6 0.0 copy-start.12
  0.7 0.0 copy-start.13
  0.7 0.0 copy-start.1
  0.7 0.0 copy-start.9
  0.7 0.0 copy-start.10
  0.7 4.4 %first_send.1 = bf16[16,144,128]{2,1,0:T(8,128)(2,1)} custom-call(s32[16,16]{1,0:T(8,128)} %plane_ref.5, s32[16,16]{1,0:T(8,128)} %row_ref.5, s32[16,16]{1,0:T(8,128)} %cover_ref.5, f32[2,56]{1,0:T(2,128)} %taps_ref.1, f32[3072,128]{1,0:T(8,128)} %bitcast.2), custom_call_target="tpu_custom_call" | custom-call | tf_op jit(solution)/shard_map/first_send/pallas_call | solution.py:332
  5.1 7.4 %all-to-all-start = ((bf16[16,144,128]{2,1,0:T(8,128)(2,1)}), bf16[16,144,128]{2,1,0:T(8,128)(2,1)S(1)}, u32[]{:S(2)}, u32[]{:S(2)}) async-start(bf16[16,144,128]{2,1,0:T(8,128)(2,1)} %first_send.1), calls=%async_computation | async-start | bytes 1179648 | tf_op jit(solution)/shard_map/all_to_all | solution.py:328
  12.5 0.0 copy-done.11
  12.5 0.7 copy.16.slot_ref
  13.2 0.0 copy-done.12
  13.2 0.7 copy.17.start_ref
  14.0 0.0 copy-done.13
  14.0 0.7 copy.18.stop_ref
  14.7 9.9 %tables.1.table_ref = s32[6,256]{1,0:T(8,128)} custom-call(s32[128,2]{1,0:T(8,128)} %copy.16.slot_ref, s32[128,2]{1,0:T(8,128)} %copy.17.start_ref, s32[128,2]{1,0:T(8,128)} %copy.18.stop_ref), custom_call_target="tpu_custom_call" | custom-call | flops 4000000 | bytes 8000000 | tf_op jit(solution)/shard_map/tables/pallas_call | solution.py:347
  24.7 0.0 copy-start
  24.7 0.0 copy-start.2
  24.7 0.0 copy-start.3
  24.7 0.0 copy-start.4
  24.7 4.5 %all-to-all-done.arrived_ref.bank_in_ref = bf16[16,144,128]{2,1,0:T(8,128)(2,1)S(1)} async-done(((bf16[16,144,128]{2,1,0:T(8,128)(2,1)}), bf16[16,144,128]{2,1,0:T(8,128)(2,1)S(1)}, u32[]{:S(2)}, u32[]{:S(2)}) %all-to-all-start) | async-done | bytes 589856 | tf_op jit(solution)/shard_map/all_to_all | solution.py:328
  29.2 0.0 copy-done.1
  29.2 0.0 copy-done.9
  29.2 0.0 copy-done.10
  29.2 0.0 copy-start.5
  29.2 0.7 copy-done.5
  29.9 0.0 copy-start.6
  29.9 0.0 copy-start.7
  29.9 0.0 copy-start.8
  29.9 5.6 %blur.2 = bf16[16,128,128]{2,1,0:T(8,128)(2,1)S(1)} custom-call(s32[6,256]{1,0:T(8,128)S(1)} %copy-done.5, f32[128]{0:T(128)S(1)} %copy-done.9, s32[128]{0:T(128)S(1)} %copy-done.10, bf16[16,144,128]{2,1,0:T(8,128)(2,1)S(1)} %all-to-all-done.arrived_ref.bank_in_ref, bf16[16,144,128]{2,1,0:T(8,128)(2,1)S(1)} %all-to-all-done.arrived_ref.bank_in_ref, ...), custom_call_target="tpu_custom_call" | custom-call | tf_op jit(solution)/shard_map/blur/pallas_call | solution.py:360
  35.6 18.4 %all_to_all.20.returned_ref = bf16[16,128,128]{2,1,0:T(8,128)(2,1)S(1)} all-to-all(bf16[16,128,128]{2,1,0:T(8,128)(2,1)S(1)} %blur.2), channel_id=1, replica_groups={{0,8,1,9,2,10,3,11,4,12,5,13,6,14,7,15},{16,24,17,25,18,26,19,27,20,28,..., dimensions={0} | all-to-all | bytes 1048576 | tf_op jit(solution)/shard_map/all_to_all | solution.py:328
  53.9 0.0 copy-done
  53.9 0.0 copy-done.2
  53.9 0.0 copy-done.3
  53.9 0.0 copy-done.4
  54.0 0.0 copy-done.6
  54.0 0.0 copy-done.7
  54.0 0.0 copy-done.8
  54.0 3.9 %update.2 = (f32[3072,128]{1,0:T(8,128)S(1)}, bf16[16,128,128]{2,1,0:T(8,128)(2,1)S(1)}) custom-call(s32[16,16]{1,0:T(8,128)S(1)} %copy-done.2, s32[16,16]{1,0:T(8,128)S(1)} %copy-done.3, s32[16,16]{1,0:T(8,128)S(1)} %copy-done.4, f32[6]{0:T(128)S(1)} %copy-done.6, s32[2]{0:T(128)S(1)} %copy-done.7, s32[2]{0:T(128)S(1)} %copy-done.8, ...), custom_call_target="tpu_custom_call" | custom-call | tf_op jit(solution)/shard_map/update/pallas_call | solution.py:396
  57.9 18.5 %all_to_all.21.arrived_ref = bf16[16,128,128]{2,1,0:T(8,128)(2,1)S(1)} all-to-all(bf16[16,128,128]{2,1,0:T(8,128)(2,1)S(1)} %get-tuple-element.6), channel_id=1, replica_groups={{0,8,1,9,2,10,3,11,4,12,5,13,6,14,7,15},{16,24,17,25,18,26,19,27,20,28,..., dimensions={0} | all-to-all | bytes 1048576 | tf_op jit(solution)/shard_map/all_to_all | solution.py:328
  76.3 6.5 %blur.3 = (bf16[16,128,128]{2,1,0:T(8,128)(2,1)S(1)}, f32[128,16,128]{2,1,0:T(8,128)}) custom-call(s32[6,256]{1,0:T(8,128)S(1)} %copy-done.5, f32[128]{0:T(128)S(1)} %copy-done.9, s32[128]{0:T(128)S(1)} %copy-done.10, bf16[16,128,128]{2,1,0:T(8,128)(2,1)S(1)} %all_to_all.21.arrived_ref, bf16[16,144,128]{2,1,0:T(8,128)(2,1)S(1)} %all-to-all-done.arrived_ref.bank_in_ref, ...), custom_call_target="tpu_custom_call" | custom-call | tf_op jit(solution)/shard_map/blur/pallas_call | solution.py:360
  82.9 18.4 %all_to_all.22.returned_ref = bf16[16,128,128]{2,1,0:T(8,128)(2,1)S(1)} all-to-all(bf16[16,128,128]{2,1,0:T(8,128)(2,1)S(1)} %get-tuple-element.7), channel_id=1, replica_groups={{0,8,1,9,2,10,3,11,4,12,5,13,6,14,7,15},{16,24,17,25,18,26,19,27,20,28,..., dimensions={0} | all-to-all | bytes 1048576 | tf_op jit(solution)/shard_map/all_to_all | solution.py:328
  101.3 3.8 %update.3 = f32[3072,128]{1,0:T(8,128)} custom-call(s32[16,16]{1,0:T(8,128)S(1)} %copy-done.2, s32[16,16]{1,0:T(8,128)S(1)} %copy-done.3, s32[16,16]{1,0:T(8,128)S(1)} %copy-done.4, f32[6]{0:T(128)S(1)} %copy-done.6, s32[2]{0:T(128)S(1)} %copy-done.7, s32[2]{0:T(128)S(1)} %copy-done.8, bf16[16,128,128]{2,1,0:T(8,128)(2,1)S(1)} %all_to_all.22.returned_ref, ...), custom_call_target="tpu_custom_call" | custom-call | tf_op jit(solution)/shard_map/update/pallas_call | solution.py:396
Async XLA Ops:
  0.6 11.9 %copy-start.11 = (s32[128,2]{0,1:T(2,128)S(1)}, s32[128,2]{0,1:T(2,128)}, u32[]{:S(2)}) copy-start(s32[128,2]{0,1:T(2,128)} %param.23) | copy-start | bytes 3076
  0.6 12.6 %copy-start.12 = (s32[128,2]{0,1:T(2,128)S(1)}, s32[128,2]{0,1:T(2,128)}, u32[]{:S(2)}) copy-start(s32[128,2]{0,1:T(2,128)} %param.24) | copy-start | bytes 3076
  0.7 13.3 %copy-start.13 = (s32[128,2]{0,1:T(2,128)S(1)}, s32[128,2]{0,1:T(2,128)}, u32[]{:S(2)}) copy-start(s32[128,2]{0,1:T(2,128)} %param.25) | copy-start | bytes 3076
  0.7 28.5 %copy-start.1 = (bf16[128,16,128]{2,1,0:T(8,128)(2,1)S(1)}, bf16[128,16,128]{2,1,0:T(8,128)(2,1)}, u32[]{:S(2)}) copy-start(bf16[128,16,128]{2,1,0:T(8,128)(2,1)} %seen_ref.3) | copy-start | bytes 1572868
  0.7 28.5 %copy-start.9 = (f32[128]{0:T(128)S(1)}, f32[128]{0:T(128)}, u32[]{:S(2)}) copy-start(f32[128]{0:T(128)} %weight_ref.3) | copy-start | bytes 1540
  0.7 28.5 %copy-start.10 = (s32[128]{0:T(128)S(1)}, s32[128]{0:T(128)}, u32[]{:S(2)}) copy-start(s32[128]{0:T(128)} %batch_ref.3) | copy-start | bytes 1540
  5.1 24.1 %all-to-all-start = ((bf16[16,144,128]{2,1,0:T(8,128)(2,1)}), bf16[16,144,128]{2,1,0:T(8,128)(2,1)S(1)}, u32[]{:S(2)}, u32[]{:S(2)}) async-start(bf16[16,144,128]{2,1,0:T(8,128)(2,1)} %first_send.1), calls=%async_computation | async-start | bytes 1179648 | tf_op jit(solution)/shard_map/all_to_all | solution.py:328
  24.7 29.3 %copy-start = (f32[2,6,256,128]{3,2,1,0:T(8,128)S(1)}, f32[2,6,256,128]{3,2,1,0:T(8,128)}, u32[]{:S(2)}) copy-start(f32[2,6,256,128]{3,2,1,0:T(8,128)} %param.14) | copy-start | bytes 4718596
  24.7 29.3 %copy-start.2 = (s32[16,16]{1,0:T(8,128)S(1)}, s32[16,16]{1,0:T(8,128)}, u32[]{:S(2)}) copy-start(s32[16,16]{1,0:T(8,128)} %plane_ref.5) | copy-start | bytes 3076
  24.7 29.2 %copy-start.3 = (s32[16,16]{1,0:T(8,128)S(1)}, s32[16,16]{1,0:T(8,128)}, u32[]{:S(2)}) copy-start(s32[16,16]{1,0:T(8,128)} %row_ref.5) | copy-start | bytes 3076
  24.7 29.2 %copy-start.4 = (s32[16,16]{1,0:T(8,128)S(1)}, s32[16,16]{1,0:T(8,128)}, u32[]{:S(2)}) copy-start(s32[16,16]{1,0:T(8,128)} %cover_ref.5) | copy-start | bytes 3076
  29.2 0.7 copy-start.5
  29.9 24.0 %copy-start.6 = (f32[6]{0:T(128)S(1)}, f32[6]{0:T(128)}, u32[]{:S(2)}) copy-start(f32[6]{0:T(128)} %step_ref.3) | copy-start | bytes 76
  29.9 24.1 %copy-start.7 = (s32[2]{0:T(128)S(1)}, s32[2]{0:T(128)}, u32[]{:S(2)}) copy-start(s32[2]{0:T(128)} %lo_ref.3) | copy-start | bytes 28
  29.9 24.1 %copy-start.8 = (s32[2]{0:T(128)S(1)}, s32[2]{0:T(128)}, u32[]{:S(2)}) copy-start(s32[2]{0:T(128)} %hi_ref.3) | copy-start | bytes 28

commit v5 on v4

--- a/solution.py
+++ b/solution.py
@@ -30,10 +30,11 @@
     return -(-rows // 16) * 16
 
 
-def exchange_order(peers):
-    if peers % 2:
-        return list(range(peers))
-    return [p // 2 + p % 2 * (peers // 2) for p in range(peers)]
+def fold(top, bottom, side):
+    lane = lax.broadcasted_iota(I32, top.shape, 1)
+    if side == 0:
+        return jnp.where(lane < LANES // 2, top, pltpu.roll(bottom, LANES // 2, 1))
+    return jnp.where(lane < LANES // 2, pltpu.roll(top, LANES // 2, 1), bottom)
 
 
 def pack_slots(plane_ref, row_ref, cover_ref, tile_rows, height, rows_each, x_ref, packed_ref):
@@ -91,9 +92,9 @@
     bank = bank_ref[...].astype(BF16)
     load.wait()
     pack_slots(plane_ref, row_ref, cover_ref, tile_rows, height, rows_each, x_ref, packed_ref)
-    for p, d in enumerate(exchange_order(peers)):
-        out_ref[p, :rows_each, :] = packed_ref[d * rows_each : (d + 1) * rows_each, :].astype(BF16)
-        out_ref[p, rows_each:, :] = bank
+    for d in range(peers):
+        out_ref[d, :rows_each, :] = packed_ref[d * rows_each : (d + 1) * rows_each, :].astype(BF16)
+        out_ref[d, rows_each:, :] = bank
 
 
 def update_kernel(
@@ -101,6 +102,7 @@
     tile_rows,
     height,
     rows_each,
+    side,
     last,
     plane_ref,
     row_ref,
@@ -119,14 +121,28 @@
     peers, capacity = plane_ref.shape
     total = model_ref.shape[0]
     planes = total // tile_rows
+    half = rows_each // 2
     load = pltpu.make_async_copy(model_ref, x_ref.at[pl.ds(0, total), :], sem)
     load.start()
     for p in range(planes):
         scale_ref[p] = step_ref[p % bands]
-    for p, d in enumerate(exchange_order(peers)):
-        back_ref[d * rows_each : (d + 1) * rows_each, :] = returned_ref[p].astype(F32)
+
+    def on_side(lane):
+        return (lane < LANES // 2) == (side == 0)
+
+    for d in range(peers):
+        at = d * rows_each
+        rows = returned_ref[d].astype(F32)
+        if side is None:
+            back_ref[at : at + rows_each, :] = rows
+        else:
+            moved = pltpu.roll(rows, LANES // 2, 1)
+            back_ref[at : at + half, :] = rows if side == 0 else moved
+            back_ref[at + half : at + rows_each, :] = moved if side == 0 else rows
     load.wait()
     place = lax.broadcasted_iota(I32, (height, LANES), 0)
+    if side is not None:
+        place = jnp.where(on_side(lax.broadcasted_iota(I32, (height, LANES), 1)), place, height)
 
     def peer(d, _):
         at = d * rows_each
@@ -145,13 +161,22 @@
     for p in range(planes):
         inside = (pos >= lo_ref[p // bands]) & (pos < hi_ref[p // bands])
         here = slice(p * tile_rows, (p + 1) * tile_rows)
-        x_ref[here, :] = jnp.where(inside, jnp.maximum(x_ref[here, :], 0.0), 0.0)
+        old = x_ref[here, :]
+        new = jnp.where(inside, jnp.maximum(old, 0.0), 0.0)
+        if side is not None:
+            new = jnp.where(on_side(lax.broadcasted_iota(I32, (tile_rows, LANES), 1)), new, old)
+        x_ref[here, :] = new
     save = pltpu.make_async_copy(x_ref.at[pl.ds(0, total), :], new_ref, sem)
     save.start()
     if not last:
         pack_slots(plane_ref, row_ref, cover_ref, tile_rows, height, rows_each, x_ref, packed_ref)
-        for p, d in enumerate(exchange_order(peers)):
-            out_ref[p, :, :] = packed_ref[d * rows_each : (d + 1) * rows_each, :].astype(BF16)
+        for d in range(peers):
+            at = d * rows_each
+            if side is None:
+                out_ref[d] = packed_ref[at : at + rows_each, :].astype(BF16)
+            else:
+                top, bottom = packed_ref[at : at + half, :], packed_ref[at + half : at + rows_each, :]
+                out_ref[d] = fold(top, bottom, side).astype(BF16)
     save.wait()
 
 
@@ -206,29 +231,39 @@
     height,
     pieces,
     batches_each,
+    sides_in,
+    sides_out,
     last,
     table_ref,
     weight_ref,
     batch_ref,
-    arrived_ref,
     bank_in_ref,
     seen_ref,
     *rest,
 ):
+    arrived_refs, out_refs, rest = rest[:sides_in], rest[sides_in : sides_in + sides_out], rest[sides_in + sides_out :]
     if last:
-        out_ref, residual_ref, rows_ref, bank_ref, result_ref, packed_ref, held_ref, blur_ref, back_ref = rest
+        residual_ref, rows_ref, bank_ref, result_ref, packed_ref, held_ref, blur_ref, back_ref = rest
     else:
-        out_ref, rows_ref, bank_ref, result_ref, packed_ref, held_ref, blur_ref, back_ref = rest
-    peers, rows_each, _ = out_ref.shape
+        rows_ref, bank_ref, result_ref, packed_ref, held_ref, blur_ref, back_ref = rest
+    peers = out_refs[0].shape[0]
+    rows_each = out_refs[0].shape[1] * sides_out
+    half = rows_each // 2
     extra = bank_in_ref.shape[1]
     exposures = batch_ref.shape[0]
     slots = peers * (2 * rows_each // height)
     abreast = max(n for n in (1, 2, 4, 8, 16) if exposures % n == 0)
     place = lax.broadcasted_iota(I32, (height, LANES), 0)
     lane = lax.broadcasted_iota(I32, (height, LANES), 1)
-    for p, o in enumerate(exchange_order(peers)):
-        rows_ref[height + o * rows_each : height + (o + 1) * rows_each, :] = arrived_ref[p].astype(F32)
-        bank_ref[o * extra : (o + 1) * extra, :] = bank_in_ref[p].astype(F32)
+    for o in range(peers):
+        at = height + o * rows_each
+        parts = [ref[o].astype(F32) for ref in arrived_refs]
+        if sides_in == 1:
+            rows_ref[at : at + rows_each, :] = parts[0]
+        else:
+            rows_ref[at : at + half, :] = fold(*parts, 0)
+            rows_ref[at + half : at + rows_each, :] = fold(*parts, 1)
+        bank_ref[o * extra : (o + 1) * extra, :] = bank_in_ref[o].astype(F32)
 
     gap = lane % height - place
     near = (gap <= HALF) & (gap >= -HALF) & (lane < TAPS * height)
@@ -292,8 +327,14 @@
         return 0
 
     lax.fori_loop(0, slots, move, 0, unroll=16)
-    for p, o in enumerate(exchange_order(peers)):
-        out_ref[p, :, :] = packed_ref[o * rows_each : (o + 1) * rows_each, :].astype(BF16)
+    for o in range(peers):
+        at = o * rows_each
+        if sides_out == 1:
+            out_refs[0][o] = packed_ref[at : at + rows_each, :].astype(BF16)
+        else:
+            top, bottom = packed_ref[at : at + half, :], packed_ref[at + half : at + rows_each, :]
+            for side, out_ref in enumerate(out_refs):
+                out_ref[o] = fold(top, bottom, side).astype(BF16)
 
 
 def body(
@@ -325,9 +366,7 @@
     x = model.reshape(total, columns)
 
     def swap(a):
-        return lax.all_to_all(
-            a, "sky", split_axis=0, concat_axis=0, tiled=True, axis_index_groups=[exchange_order(peers)]
-        )
+        return lax.all_to_all(a, "sky", split_axis=0, concat_axis=0, tiled=True)
 
     outbound = pl.pallas_call(
         functools.partial(first_send_kernel, tile_rows, height, rows_each),
@@ -353,23 +392,27 @@
         cost_estimate=pl.CostEstimate(flops=4_000_000, bytes_accessed=8_000_000, transcendentals=0),
         name="tables",
     )(use_slot, use_start, use_stop)
-    with_bank = arrived
+    with_bank, arrived = arrived, [arrived]
+    sides = 2 if rows_each % 32 == 0 else 1
     for sweep in range(ITERS):
         last = sweep == ITERS - 1
-        rows_shape = jax.ShapeDtypeStruct((peers, rows_each, columns), BF16)
+        sides_in, sides_out = len(arrived), 1 if last else sides
+        residual_shape = [jax.ShapeDtypeStruct(exposures.shape, F32)] if last else []
+        whole = pl.BlockSpec((peers, rows_each // sides_in, columns), lambda i: (0, 0, 0))
         outs = pl.pallas_call(
-            functools.partial(blur_kernel, height, pieces, batches_each, last),
+            functools.partial(blur_kernel, height, pieces, batches_each, sides_in, sides_out, last),
             grid=(1,),
-            out_shape=(rows_shape, jax.ShapeDtypeStruct(exposures.shape, F32)) if last else rows_shape,
+            out_shape=[jax.ShapeDtypeStruct((peers, rows_each // sides_out, columns), BF16)] * sides_out
+            + residual_shape,
             in_specs=[
                 smem(),
                 smem(),
                 smem(),
-                pl.BlockSpec((peers, rows_each, columns), lambda i: (0, 0, 0)),
                 pl.BlockSpec((peers, extra, columns), lambda i: (0, rows_each // extra, 0)),
                 vmem(),
-            ],
-            out_specs=(vmem(), vmem()) if last else vmem(),
+            ]
+            + [whole] * sides_in,
+            out_specs=[vmem()] * (sides_out + len(residual_shape)),
             scratch_shapes=[
                 pltpu.VMEM((peers * rows_each + 2 * height, columns), F32),
                 pltpu.VMEM((peers * extra, columns), F32),
@@ -381,32 +424,38 @@
             ],
             compiler_params=params(),
             name="blur",
-        )(table, inv_var, exp_batch, arrived, with_bank, exposures)
-        outgoing = outs[0] if last else outs
-        returned = swap(outgoing)
-        new_shape = jax.ShapeDtypeStruct((total, columns), F32)
-        scratch = [
-            pltpu.VMEM((total + height, columns), F32),
-            pltpu.VMEM((peers * rows_each + height, columns), F32),
-            pltpu.SMEM((tile_count * bands,), F32),
-            pltpu.SemaphoreType.DMA,
-        ]
-        if not last:
-            scratch.append(pltpu.VMEM((peers * rows_each + height, columns), F32))
-        res = pl.pallas_call(
-            functools.partial(update_kernel, bands, tile_rows, height, rows_each, last),
-            out_shape=new_shape if last else (new_shape, rows_shape),
-            in_specs=[smem()] * 6 + [vmem(), hbm()],
-            out_specs=hbm() if last else (hbm(), vmem()),
-            scratch_shapes=scratch,
-            compiler_params=params(),
-            name="update",
-        )(send_plane, send_row, send_cover, step_size, foot_lo, foot_hi, returned, x)
-        if last:
-            x = res
-        else:
-            x, outbound = res
-            arrived = swap(outbound)
+        )(table, inv_var, exp_batch, with_bank, exposures, *arrived)
+        returned = [swap(out) for out in outs[:sides_out]]
+        arrived = []
+        for side, back in enumerate(returned):
+            scratch = [
+                pltpu.VMEM((total + height, columns), F32),
+                pltpu.VMEM((peers * rows_each + height, columns), F32),
+                pltpu.SMEM((tile_count * bands,), F32),
+                pltpu.SemaphoreType.DMA,
+            ]
+            if not last:
+                scratch.append(pltpu.VMEM((peers * rows_each + height, columns), F32))
+            sent = [] if last else [jax.ShapeDtypeStruct(back.shape, BF16)]
+            x, *outbound = pl.pallas_call(
+                functools.partial(
+                    update_kernel,
+                    bands,
+                    tile_rows,
+                    height,
+                    rows_each,
+                    side if sides_out == 2 else None,
+                    last,
+                ),
+                out_shape=[jax.ShapeDtypeStruct((total, columns), F32)] + sent,
+                in_specs=[smem()] * 6 + [vmem(), hbm()],
+                out_specs=[hbm()] + [vmem()] * len(sent),
+                scratch_shapes=scratch,
+                compiler_params=params(),
+                cost_estimate=pl.CostEstimate(flops=4_000_000, bytes_accessed=8_000_000, transcendentals=0),
+                name="update",
+            )(send_plane, send_row, send_cover, step_size, foot_lo, foot_hi, back, x)
+            arrived += [swap(out) for out in outbound]
     return (x.reshape(model.shape), outs[1])
 
 

time: 106 us -> 118 us (1.11)
  blocking collectives: 55.3 us -> 44.3 us
  starting transfers between devices: 7.37 us -> 14.6 us
  waiting for transfers between devices: 4.48 us -> 11.7 us
  Pallas kernels: 34.3 us -> 40.3 us
  local copies, waits for them, and re-layouts: 2.97 us -> 5.52 us
    all_to_all x3, blocking collectives: 55.3 us -> 44.3 us  [swap(): return lax.all_to_all(a, 'sky', split_axis=0, concat_axis=0, tiled=True)]
    all_to_all x1 -> x3, starting transfers between devices: 7.37 us -> 14.6 us  [swap(): return lax.all_to_all(a, 'sky', split_axis=0, concat_axis=0, tiled=True)]
    all_to_all x1 -> x3, waiting for transfers between devices: 4.48 us -> 11.7 us  [swap(): return lax.all_to_all(a, 'sky', split_axis=0, concat_axis=0, tiled=True)]
    pallas_call x2 -> x3, Pallas kernels: 7.74 us -> 12.8 us  [body(): pl.pallas_call(functools.partial(update_kernel, bands, tile_rows, height,...]
    unnamed x31 -> x37, local copies, waits for them, and re-layouts: 2.97 us -> 5.52 us
  transfers between devices with their start and end apart: 1 -> 3, of which waited for: 1 -> 3; matrix products, arithmetic and copies ran while one was open for 2% -> 2% of each run, Pallas kernels for 9% -> 16%
where the time goes in v5:
time: 118 us; the launch traced here: 117 us
  blocking collectives  44.3 us (38%)
  Pallas kernels  40.3 us (34%)
  starting transfers between devices  14.6 us (12%)
  waiting for transfers between devices  11.7 us (10%)
  local copies, waits for them, and re-layouts  5.52 us (5%)
    all_to_all x3, blocking collectives, swap(): return lax.all_to_all(a, 'sky', split_axis=0, concat_axis=0, tiled=True)  44.3 us
    all_to_all x3, starting transfers between devices, swap(): return lax.all_to_all(a, 'sky', split_axis=0, concat_axis=0, tiled=True)  14.6 us
    pallas_call x2, Pallas kernels, body(): pl.pallas_call(functools.partial(blur_kernel, height, pieces, batches_eac...  13.2 us
    pallas_call x3, Pallas kernels, body(): pl.pallas_call(functools.partial(update_kernel, bands, tile_rows, height,...  12.8 us
    all_to_all x3, waiting for transfers between devices, swap(): return lax.all_to_all(a, 'sky', split_axis=0, concat_axis=0, tiled=True)  11.7 us
    pallas_call x1, Pallas kernels, body(): pl.pallas_call(functools.partial(tables_kernel, capacity, height, rows_ea...  9.94 us
    unnamed x37, local copies, waits for them, and re-layouts  5.52 us
    pallas_call x1, Pallas kernels, body(): pl.pallas_call(functools.partial(first_send_kernel, tile_rows, height, ro...  4.41 us
  transfers between devices with their start and end apart: 3, of which 3 were waited for; matrix products, arithmetic and copies ran while one was open for 2% of the time, Pallas kernels for 16%

profile of v5, /device:TPU:0, one launch (start us, length us, event | category | flops | bytes accessed | tf_op | source)
XLA Modules:
  0.0 117.3 jit_solution(2670491421670713968)
XLA Ops:
  0.6 0.0 copy-start.14
  0.6 0.0 copy-start.15
  0.7 0.0 copy-start.16
  0.7 0.0 copy-start.1
  0.7 0.0 copy-start.12
  0.7 0.0 copy-start.13
  0.7 4.4 %first_send.1 = bf16[16,144,128]{2,1,0:T(8,128)(2,1)} custom-call(s32[16,16]{1,0:T(8,128)} %plane_ref.7, s32[16,16]{1,0:T(8,128)} %row_ref.7, s32[16,16]{1,0:T(8,128)} %cover_ref.7, f32[2,56]{1,0:T(2,128)} %taps_ref.1, f32[3072,128]{1,0:T(8,128)} %bitcast.2), custom_call_target="tpu_custom_call" | custom-call | tf_op jit(solution)/shard_map/first_send/pallas_call | solution.py:371
  5.1 0.0 copy-start.9
  5.1 0.0 copy-start.10
  5.1 0.0 copy-start.11
  5.1 7.5 %all-to-all-start = ((bf16[16,144,128]{2,1,0:T(8,128)(2,1)}), bf16[16,144,128]{2,1,0:T(8,128)(2,1)S(1)}, u32[]{:S(2)}, u32[]{:S(2)}) async-start(bf16[16,144,128]{2,1,0:T(8,128)(2,1)} %first_send.1), calls=%async_computation | async-start | bytes 1179648 | tf_op jit(solution)/shard_map/all_to_all | solution.py:369
  12.7 0.0 copy-done.14
  12.7 0.0 copy-start
  12.7 0.0 copy-start.4
  12.7 0.0 copy-start.5
  12.7 0.0 copy-start.6
  12.7 0.7 copy.16.slot_ref
  13.5 0.0 copy-done.15
  13.5 0.7 copy.17.start_ref
  14.2 0.0 copy-done.16
  14.2 0.7 copy.18.stop_ref
  14.9 9.9 %tables.1.table_ref = s32[6,256]{1,0:T(8,128)} custom-call(s32[128,2]{1,0:T(8,128)} %copy.16.slot_ref, s32[128,2]{1,0:T(8,128)} %copy.17.start_ref, s32[128,2]{1,0:T(8,128)} %copy.18.stop_ref), custom_call_target="tpu_custom_call" | custom-call | flops 4000000 | bytes 8000000 | tf_op jit(solution)/shard_map/tables/pallas_call | solution.py:386
  24.9 3.3 %all-to-all-done.bank_in_ref.rest_0_ = bf16[16,144,128]{2,1,0:T(8,128)(2,1)S(1)} async-done(((bf16[16,144,128]{2,1,0:T(8,128)(2,1)}), bf16[16,144,128]{2,1,0:T(8,128)(2,1)S(1)}, u32[]{:S(2)}, u32[]{:S(2)}) %all-to-all-start) | async-done | bytes 589856 | tf_op jit(solution)/shard_map/all_to_all | solution.py:369
  28.2 0.0 copy-done.1
  28.2 0.0 copy-done.12
  28.2 0.0 copy-done.13
  28.2 0.0 copy-start.7
  28.2 0.7 copy-done.7
  28.9 6.5 %blur.2 = (bf16[16,64,128]{2,1,0:T(8,128)(2,1)S(1)}, bf16[16,64,128]{2,1,0:T(8,128)(2,1)}) custom-call(s32[6,256]{1,0:T(8,128)S(1)} %copy-done.7, f32[128]{0:T(128)S(1)} %copy-done.12, s32[128]{0:T(128)S(1)} %copy-done.13, bf16[16,144,128]{2,1,0:T(8,128)(2,1)S(1)} %all-to-all-done.bank_in_ref.rest_0_, bf16[128,16,128]{2,1,0:T(8,128)(2,1)S(1)} %copy-done.1, ...), custom_call_target="tpu_custom_call" | custom-call | tf_op jit(solution)/shard_map/blur/pallas_call | solution.py:402
  35.4 14.3 %all_to_all.30.returned_ref = bf16[16,64,128]{2,1,0:T(8,128)(2,1)S(1)} all-to-all(bf16[16,64,128]{2,1,0:T(8,128)(2,1)S(1)} %get-tuple-element.10), channel_id=1, replica_groups=mesh['groups'=2,'sky'=16] {'sky'}, dimensions={0} | all-to-all | bytes 524288 | tf_op jit(solution)/shard_map/all_to_all | solution.py:369
  49.6 3.5 %all-to-all-start.3 = ((bf16[16,64,128]{2,1,0:T(8,128)(2,1)}), bf16[16,64,128]{2,1,0:T(8,128)(2,1)S(1)}, u32[]{:S(2)}, u32[]{:S(2)}) async-start(bf16[16,64,128]{2,1,0:T(8,128)(2,1)} %get-tuple-element.12), calls=%async_computation.3 | async-start | bytes 524288 | tf_op jit(solution)/shard_map/all_to_all | solution.py:369
  53.2 0.0 copy-done.9
  53.2 0.0 copy-done.10
  53.2 0.0 copy-done.11
  53.2 0.0 copy-done
  53.2 0.0 copy-done.4
  53.2 0.0 copy-done.5
  53.2 0.0 copy-done.6
  53.3 4.9 %update.3 = (f32[3072,128]{1,0:T(8,128)S(1)}, bf16[16,64,128]{2,1,0:T(8,128)(2,1)}) custom-call(s32[16,16]{1,0:T(8,128)S(1)} %copy-done.4, s32[16,16]{1,0:T(8,128)S(1)} %copy-done.5, s32[16,16]{1,0:T(8,128)S(1)} %copy-done.6, f32[6]{0:T(128)S(1)} %copy-done.9, s32[2]{0:T(128)S(1)} %copy-done.10, s32[2]{0:T(128)S(1)} %copy-done.11, ...), custom_call_target="tpu_custom_call" | custom-call | flops 4000000 | bytes 8000000 | tf_op jit(solution)/shard_map/update/pallas_call | solution.py:440
  58.1 0.0 copy-start.2
  58.1 1.1 copy-done.2
  59.3 0.0 copy-start.8
  59.3 3.9 %all-to-all-done.3.returned_ref = bf16[16,64,128]{2,1,0:T(8,128)(2,1)S(1)} async-done(((bf16[16,64,128]{2,1,0:T(8,128)(2,1)}), bf16[16,64,128]{2,1,0:T(8,128)(2,1)S(1)}, u32[]{:S(2)}, u32[]{:S(2)}) %all-to-all-start.3) | async-done | bytes 262176 | tf_op jit(solution)/shard_map/all_to_all | solution.py:369
  63.2 3.5 %all-to-all-start.2 = ((bf16[16,64,128]{2,1,0:T(8,128)(2,1)}), bf16[16,64,128]{2,1,0:T(8,128)(2,1)S(1)}, u32[]{:S(2)}, u32[]{:S(2)}) async-start(bf16[16,64,128]{2,1,0:T(8,128)(2,1)} %get-tuple-element.11), calls=%async_computation.2 | async-start | bytes 524288 | tf_op jit(solution)/shard_map/all_to_all | solution.py:369
  66.7 0.0 copy-start.3
  66.7 1.4 %copy-done.3 = f32[3072,128]{1,0:T(8,128)S(1)} copy-done((f32[3072,128]{1,0:T(8,128)S(1)}, f32[3072,128]{1,0:T(8,128)}, u32[]{:S(2)}) %copy-start.3) | copy-done | bytes 1572888
  68.1 4.1 %update.4 = (f32[3072,128]{1,0:T(8,128)S(1)}, bf16[16,64,128]{2,1,0:T(8,128)(2,1)S(1)}) custom-call(s32[16,16]{1,0:T(8,128)S(1)} %copy-done.4, s32[16,16]{1,0:T(8,128)S(1)} %copy-done.5, s32[16,16]{1,0:T(8,128)S(1)} %copy-done.6, f32[6]{0:T(128)S(1)} %copy-done.9, s32[2]{0:T(128)S(1)} %copy-done.10, s32[2]{0:T(128)S(1)} %copy-done.11, ...), custom_call_target="tpu_custom_call" | custom-call | flops 4000000 | bytes 8000000 | tf_op jit(solution)/shard_map/update/pallas_call | solution.py:440
  72.3 4.4 %all-to-all-done.2.rest_0_ = bf16[16,64,128]{2,1,0:T(8,128)(2,1)S(1)} async-done(((bf16[16,64,128]{2,1,0:T(8,128)(2,1)}), bf16[16,64,128]{2,1,0:T(8,128)(2,1)S(1)}, u32[]{:S(2)}, u32[]{:S(2)}) %all-to-all-start.2) | async-done | bytes 262176 | tf_op jit(solution)/shard_map/all_to_all | solution.py:369
  76.7 12.8 %all_to_all.31.rest_1_ = bf16[16,64,128]{2,1,0:T(8,128)(2,1)S(1)} all-to-all(bf16[16,64,128]{2,1,0:T(8,128)(2,1)S(1)} %get-tuple-element.14), channel_id=1, replica_groups=mesh['groups'=2,'sky'=16] {'sky'}, dimensions={0} | all-to-all | bytes 524288 | tf_op jit(solution)/shard_map/all_to_all | solution.py:369
  89.6 0.0 copy-done.8
  89.6 6.7 %blur.3 = (bf16[16,128,128]{2,1,0:T(8,128)(2,1)S(1)}, f32[128,16,128]{2,1,0:T(8,128)}) custom-call(s32[6,256]{1,0:T(8,128)S(1)} %copy-done.8, f32[128]{0:T(128)S(1)} %copy-done.12, s32[128]{0:T(128)S(1)} %copy-done.13, bf16[16,144,128]{2,1,0:T(8,128)(2,1)S(1)} %all-to-all-done.bank_in_ref.rest_0_, bf16[128,16,128]{2,1,0:T(8,128)(2,1)S(1)} %copy-done.1, ...), custom_call_target="tpu_custom_call" | custom-call | tf_op jit(solution)/shard_map/blur/pallas_call | solution.py:402
  96.2 17.2 %all_to_all.32.returned_ref = bf16[16,128,128]{2,1,0:T(8,128)(2,1)S(1)} all-to-all(bf16[16,128,128]{2,1,0:T(8,128)(2,1)S(1)} %get-tuple-element.15), channel_id=1, replica_groups=mesh['groups'=2,'sky'=16] {'sky'}, dimensions={0} | all-to-all | bytes 1048576 | tf_op jit(solution)/shard_map/all_to_all | solution.py:369
  113.5 3.8 %update.5 = f32[3072,128]{1,0:T(8,128)} custom-call(s32[16,16]{1,0:T(8,128)S(1)} %copy-done.4, s32[16,16]{1,0:T(8,128)S(1)} %copy-done.5, s32[16,16]{1,0:T(8,128)S(1)} %copy-done.6, f32[6]{0:T(128)S(1)} %copy-done.9, s32[2]{0:T(128)S(1)} %copy-done.10, s32[2]{0:T(128)S(1)} %copy-done.11, bf16[16,128,128]{2,1,0:T(8,128)(2,1)S(1)} %all_to_all.32.returned_ref, ...), custom_call_target="tpu_custom_call" | custom-call | flops 4000000 | bytes 8000000 | tf_op jit(solution)/shard_map/update/pallas_call | solution.py:440
Async XLA Ops:
  0.6 12.0 %copy-start.14 = (s32[128,2]{0,1:T(2,128)S(1)}, s32[128,2]{0,1:T(2,128)}, u32[]{:S(2)}) copy-start(s32[128,2]{0,1:T(2,128)} %param.23) | copy-start | bytes 3076
  0.6 12.8 %copy-start.15 = (s32[128,2]{0,1:T(2,128)S(1)}, s32[128,2]{0,1:T(2,128)}, u32[]{:S(2)}) copy-start(s32[128,2]{0,1:T(2,128)} %param.24) | copy-start | bytes 3076
  0.7 13.6 %copy-start.16 = (s32[128,2]{0,1:T(2,128)S(1)}, s32[128,2]{0,1:T(2,128)}, u32[]{:S(2)}) copy-start(s32[128,2]{0,1:T(2,128)} %param.25) | copy-start | bytes 3076
  0.7 27.5 %copy-start.1 = (bf16[128,16,128]{2,1,0:T(8,128)(2,1)S(1)}, bf16[128,16,128]{2,1,0:T(8,128)(2,1)}, u32[]{:S(2)}) copy-start(bf16[128,16,128]{2,1,0:T(8,128)(2,1)} %seen_ref.3) | copy-start | bytes 1572868
  0.7 27.5 %copy-start.12 = (f32[128]{0:T(128)S(1)}, f32[128]{0:T(128)}, u32[]{:S(2)}) copy-start(f32[128]{0:T(128)} %weight_ref.3) | copy-start | bytes 1540
  0.7 27.5 %copy-start.13 = (s32[128]{0:T(128)S(1)}, s32[128]{0:T(128)}, u32[]{:S(2)}) copy-start(s32[128]{0:T(128)} %batch_ref.3) | copy-start | bytes 1540
  5.1 48.1 %copy-start.9 = (f32[6]{0:T(128)S(1)}, f32[6]{0:T(128)}, u32[]{:S(2)}) copy-start(f32[6]{0:T(128)} %step_ref.5) | copy-start | bytes 76
  5.1 48.1 %copy-start.10 = (s32[2]{0:T(128)S(1)}, s32[2]{0:T(128)}, u32[]{:S(2)}) copy-start(s32[2]{0:T(128)} %lo_ref.5) | copy-start | bytes 28
  5.1 48.1 %copy-start.11 = (s32[2]{0:T(128)S(1)}, s32[2]{0:T(128)}, u32[]{:S(2)}) copy-start(s32[2]{0:T(128)} %hi_ref.5) | copy-start | bytes 28
  5.1 23.1 %all-to-all-start = ((bf16[16,144,128]{2,1,0:T(8,128)(2,1)}), bf16[16,144,128]{2,1,0:T(8,128)(2,1)S(1)}, u32[]{:S(2)}, u32[]{:S(2)}) async-start(bf16[16,144,128]{2,1,0:T(8,128)(2,1)} %first_send.1), calls=%async_computation | async-start | bytes 1179648 | tf_op jit(solution)/shard_map/all_to_all | solution.py:369
  12.7 40.6 %copy-start = (f32[2,6,256,128]{3,2,1,0:T(8,128)S(1)}, f32[2,6,256,128]{3,2,1,0:T(8,128)}, u32[]{:S(2)}) copy-start(f32[2,6,256,128]{3,2,1,0:T(8,128)} %param.14) | copy-start | bytes 4718596
  12.7 40.5 %copy-start.4 = (s32[16,16]{1,0:T(8,128)S(1)}, s32[16,16]{1,0:T(8,128)}, u32[]{:S(2)}) copy-start(s32[16,16]{1,0:T(8,128)} %plane_ref.7) | copy-start | bytes 3076
  12.7 40.5 %copy-start.5 = (s32[16,16]{1,0:T(8,128)S(1)}, s32[16,16]{1,0:T(8,128)}, u32[]{:S(2)}) copy-start(s32[16,16]{1,0:T(8,128)} %row_ref.7) | copy-start | bytes 3076
  12.7 40.5 %copy-start.6 = (s32[16,16]{1,0:T(8,128)S(1)}, s32[16,16]{1,0:T(8,128)}, u32[]{:S(2)}) copy-start(s32[16,16]{1,0:T(8,128)} %cover_ref.7) | copy-start | bytes 3076
  28.2 0.7 copy-start.7
  49.6 13.5 %all-to-all-start.3 = ((bf16[16,64,128]{2,1,0:T(8,128)(2,1)}), bf16[16,64,128]{2,1,0:T(8,128)(2,1)S(1)}, u32[]{:S(2)}, u32[]{:S(2)}) async-start(bf16[16,64,128]{2,1,0:T(8,128)(2,1)} %get-tuple-element.12), calls=%async_computation.3 | async-start | bytes 524288 | tf_op jit(solution)/shard_map/all_to_all | solution.py:369
  58.1 1.1 copy-start.2
  59.3 30.3 %copy-start.8 = (s32[6,256]{1,0:T(8,128)S(1)}, s32[6,256]{1,0:T(8,128)}, u32[]{:S(2)}) copy-start(s32[6,256]{1,0:T(8,128)} %tables.1.table_ref) | copy-start | bytes 18436
  63.2 13.5 %all-to-all-start.2 = ((bf16[16,64,128]{2,1,0:T(8,128)(2,1)}), bf16[16,64,128]{2,1,0:T(8,128)(2,1)S(1)}, u32[]{:S(2)}, u32[]{:S(2)}) async-start(bf16[16,64,128]{2,1,0:T(8,128)(2,1)} %get-tuple-element.11), calls=%async_computation.2 | async-start | bytes 524288 | tf_op jit(solution)/shard_map/all_to_all | solution.py:369
  66.7 1.4 %copy-start.3 = (f32[3072,128]{1,0:T(8,128)S(1)}, f32[3072,128]{1,0:T(8,128)}, u32[]{:S(2)}) copy-start(f32[3072,128]{1,0:T(8,128)} %copy-done.2) | copy-start | bytes 4718596

commit v6 on v3

--- a/solution.py
+++ b/solution.py
@@ -41,12 +41,11 @@
             at = at + cover_ref[d, c]
         return 0
 
-    lax.fori_loop(0, peers, peer, 0)
+    lax.fori_loop(0, peers, peer, 0, unroll=2)
 
 
 def bank_rows(taps, height):
-    hp = lax.Precision.HIGHEST
-    width = taps.shape[1]
+    count, width = taps.shape
 
     def grid(columns):
         return (
@@ -54,17 +53,26 @@
             lax.broadcasted_iota(I32, (width, columns), 1),
         )
 
+    def select(x, mask):
+        parts = []
+        for _ in range(3):
+            parts.append(x.astype(BF16).astype(F32))
+            x = x - parts[-1]
+        picked = jnp.dot(
+            jnp.concatenate(parts, axis=0).astype(BF16), mask.astype(F32).astype(BF16), preferred_element_type=F32
+        )
+        return picked[:count] + picked[count : 2 * count] + picked[2 * count :]
+
     k, l = grid(width)
-    total = jnp.dot(taps, (k // TAPS == l // TAPS).astype(F32), precision=hp, preferred_element_type=F32)
-    unit = taps / total
+    unit = taps / select(taps, k // TAPS == l // TAPS)
     k, l = grid(2 * NPSF * LANES)
     mirror, j, l = l // (NPSF * LANES), l // LANES % NPSF, (l + HALF) % LANES
     i, t = l // height, l % height
     valid = (i < TAPS) & (t < TAPS)
     row_tap = j * TAPS + jnp.where(mirror == 1, t, TAPS - 1 - t)
     col_tap = (NPSF + j) * TAPS + jnp.where(mirror == 1, TAPS - 1 - i, i)
-    row_part = jnp.dot(unit, (valid & (k == row_tap)).astype(F32), precision=hp, preferred_element_type=F32)
-    col_part = jnp.dot(unit, (valid & (k == col_tap)).astype(F32), precision=hp, preferred_element_type=F32)
+    row_part = select(unit, valid & (k == row_tap))
+    col_part = select(unit, valid & (k == col_tap))
     product = row_part * col_part * (1.0 / NPSF)
     return [
         sum(product[:, (m * NPSF + j) * LANES : (m * NPSF + j + 1) * LANES] for j in range(NPSF)) for m in range(2)
@@ -107,9 +115,9 @@
     *rest,
 ):
     if last:
-        new_ref, x_ref, back_ref, scale_ref, sem = rest
+        new_ref, x_ref, back_ref, scale_ref, sem, saved, *more_refs = rest
     else:
-        new_ref, out_ref, x_ref, back_ref, scale_ref, sem, packed_ref = rest
+        new_ref, out_ref, x_ref, back_ref, scale_ref, sem, saved, *more_refs, packed_ref = rest
     peers, capacity = plane_ref.shape
     total = model_ref.shape[0]
     planes = total // tile_rows
@@ -117,36 +125,46 @@
     load.start()
     for p in range(planes):
         scale_ref[p] = step_ref[p % bands]
+    for ref in more_refs:
+        ref[...] = jnp.zeros(ref.shape, F32)
     for d in range(peers):
         back_ref[d * rows_each : (d + 1) * rows_each, :] = returned_ref[d].astype(F32)
     load.wait()
     place = lax.broadcasted_iota(I32, (height, LANES), 0)
 
-    def peer(d, _):
-        at = d * rows_each
+    sums = [x_ref, *more_refs]
+
+    def some_peers(step, _):
+        at = [(step * len(sums) + n) * rows_each for n in range(len(sums))]
         for c in range(capacity):
-            p = jnp.maximum(plane_ref[d, c], 0)
-            first = p * tile_rows + row_ref[d, c]
-            cover = cover_ref[d, c]
-            piece = jnp.where(place < cover, back_ref[pl.ds(at, height), :], 0.0)
-            x_ref[pl.ds(first, height), :] = x_ref[pl.ds(first, height), :] - scale_ref[p] * piece
-            at = at + cover
-        return 0
-
-    lax.fori_loop(0, peers, peer, 0)
+            for n, ref in enumerate(sums):
+                d = step * len(sums) + n
+                p = jnp.maximum(plane_ref[d, c], 0)
+                here = pl.ds(p * tile_rows + row_ref[d, c], height)
+                cover = cover_ref[d, c]
+                piece = jnp.where(place < cover, back_ref[pl.ds(at[n], height), :], 0.0)
+                ref[here, :] = ref[here, :] - scale_ref[p] * piece
+                at[n] = at[n] + cover
+        return 0
+
+    lax.fori_loop(0, peers // len(sums), some_peers, 0)
 
     pos = lax.broadcasted_iota(I32, (tile_rows, LANES), 0)
+    saves = []
     for p in range(planes):
         inside = (pos >= lo_ref[p // bands]) & (pos < hi_ref[p // bands])
         here = slice(p * tile_rows, (p + 1) * tile_rows)
-        x_ref[here, :] = jnp.where(inside, jnp.maximum(x_ref[here, :], 0.0), 0.0)
-    save = pltpu.make_async_copy(x_ref.at[pl.ds(0, total), :], new_ref, sem)
-    save.start()
+        new = sum((ref[here, :] for ref in more_refs), x_ref[here, :])
+        x_ref[here, :] = jnp.where(inside, jnp.maximum(new, 0.0), 0.0)
+        rows = pl.ds(p * tile_rows, tile_rows)
+        saves.append(pltpu.make_async_copy(x_ref.at[rows, :], new_ref.at[rows, :], saved.at[p]))
+        saves[-1].start()
     if not last:
         pack_slots(plane_ref, row_ref, cover_ref, tile_rows, height, rows_each, x_ref, packed_ref)
         for d in range(peers):
             out_ref[d, :, :] = packed_ref[d * rows_each : (d + 1) * rows_each, :].astype(BF16)
-    save.wait()
+    for save in saves:
+        save.wait()
 
 
 def tables_kernel(capacity, height, rows_each, slot_ref, start_ref, stop_ref, table_ref, length_ref):
@@ -201,7 +219,7 @@
     pieces,
     batches_each,
     last,
-    table_ref,
+    table_in_ref,
     weight_ref,
     batch_ref,
     arrived_ref,
@@ -210,14 +228,18 @@
     *rest,
 ):
     if last:
-        out_ref, residual_ref, rows_ref, bank_ref, result_ref, packed_ref, blur_ref, back_ref = rest
+        out_ref, residual_out_ref, *rest = rest
+        *rest, residual_ref, sent = rest
     else:
-        out_ref, rows_ref, bank_ref, result_ref, packed_ref, blur_ref, back_ref = rest
+        out_ref, *rest = rest
+    table_ref, sem, rows_ref, bank_ref, result_ref, packed_ref, held_ref, blur_ref, back_ref = rest
+    load = pltpu.make_async_copy(table_in_ref, table_ref, sem)
+    load.start()
     peers, rows_each, _ = out_ref.shape
     extra = bank_in_ref.shape[1]
     exposures = batch_ref.shape[0]
     slots = peers * (2 * rows_each // height)
-    abreast = max(n for n in (1, 2, 4, 8, 16) if exposures % n == 0)
+    abreast = max(n for n in (1, 2, 4, 8, 16, 32) if exposures % n == 0)
     place = lax.broadcasted_iota(I32, (height, LANES), 0)
     lane = lax.broadcasted_iota(I32, (height, LANES), 1)
     for o in range(peers):
@@ -246,24 +268,43 @@
         parts.append(jnp.zeros((LANES - TAPS * height, LANES), BF16))
         return jnp.concatenate(parts, axis=0)
 
-    def step(s, _):
+    def correlate(s):
         for q in range(abreast):
             e = s * abreast + q
-            b = batch_ref[e]
+            here = pl.ds(e * height, height)
+            result_ref[here, :] = jnp.dot(
+                back_ref[batch_ref[e]], shifted(held_ref[here, :]), preferred_element_type=F32
+            )
+
+    def blur(s):
+        for q in range(abreast):
+            e = s * abreast + q
             stamp = rows_ref[pl.ds(table_ref[0, e], height), :]
             for k in range(1, pieces):
                 piece = rows_ref[pl.ds(table_ref[2 * k, e], height), :]
                 stamp = jnp.where(place >= table_ref[2 * k + 1, e], piece, stamp)
-            predicted = jnp.dot(blur_ref[b], shifted(stamp.astype(BF16)), preferred_element_type=F32)
+            predicted = jnp.dot(
+                blur_ref[batch_ref[e]], shifted(stamp.astype(BF16)), preferred_element_type=F32
+            )
             residual = weight_ref[e] * (predicted - seen_ref[e].astype(F32))
             if last:
                 residual_ref[e] = residual
-            result_ref[pl.ds(pl.multiple_of(e * height, height), height), :] = jnp.dot(
-                back_ref[b], shifted(residual.astype(BF16)), preferred_element_type=F32
-            )
-        return 0
-
-    lax.fori_loop(0, exposures // abreast, step, 0)
+            held_ref[pl.ds(e * height, height), :] = residual.astype(BF16)
+
+    steps = exposures // abreast
+
+    def send(s):
+        some = pl.ds(s * abreast, abreast)
+        return pltpu.make_async_copy(residual_ref.at[some], residual_out_ref.at[some], sent.at[s])
+
+    load.wait()
+    for s in range(steps + 1):
+        if s > 0:
+            correlate(s - 1)
+        if s < steps:
+            blur(s)
+            if last:
+                send(s).start()
 
     def move(s, _):
         packed_ref[pl.ds(table_ref[2 * pieces + 1, s], height), :] = result_ref[
@@ -274,6 +315,9 @@
     lax.fori_loop(0, slots, move, 0, unroll=16)
     for o in range(peers):
         out_ref[o, :, :] = packed_ref[o * rows_each : (o + 1) * rows_each, :].astype(BF16)
+    if last:
+        for s in range(steps):
+            send(s).wait()
 
 
 def body(
@@ -340,22 +384,26 @@
             grid=(1,),
             out_shape=(rows_shape, jax.ShapeDtypeStruct(exposures.shape, F32)) if last else rows_shape,
             in_specs=[
-                smem(),
+                hbm(),
                 smem(),
                 smem(),
                 pl.BlockSpec((peers, rows_each, columns), lambda i: (0, 0, 0)),
                 pl.BlockSpec((peers, extra, columns), lambda i: (0, rows_each // extra, 0)),
                 vmem(),
             ],
-            out_specs=(vmem(), vmem()) if last else vmem(),
+            out_specs=(vmem(), hbm()) if last else vmem(),
             scratch_shapes=[
+                pltpu.SMEM(table.shape, I32),
+                pltpu.SemaphoreType.DMA,
                 pltpu.VMEM((peers * rows_each + 2 * height, columns), F32),
                 pltpu.VMEM((peers * extra, columns), F32),
                 pltpu.VMEM((count * height + height, columns), F32),
                 pltpu.VMEM((peers * rows_each + height, columns), F32),
+                pltpu.VMEM((count * height, columns), BF16),
                 pltpu.VMEM((peers * batches_each, height, LANES), BF16),
                 pltpu.VMEM((peers * batches_each, height, LANES), BF16),
-            ],
+            ]
+            + [pltpu.VMEM(exposures.shape, F32), pltpu.SemaphoreType.DMA((count,))] * last,
             compiler_params=params(),
             name="blur",
         )(table, inv_var, exp_batch, arrived, with_bank, exposures)
@@ -367,7 +415,10 @@
             pltpu.VMEM((peers * rows_each + height, columns), F32),
             pltpu.SMEM((tile_count * bands,), F32),
             pltpu.SemaphoreType.DMA,
+            pltpu.SemaphoreType.DMA((tile_count * bands,)),
         ]
+        sums = max(n for n in (1, 2, 4) if peers % n == 0)
+        scratch += [pltpu.VMEM((total + height, columns), F32)] * (sums - 1)
         if not last:
             scratch.append(pltpu.VMEM((peers * rows_each + height, columns), F32))
         res = pl.pallas_call(

time: 108 us -> 104 us (0.963)
  Pallas kernels: 37.5 us -> 33.3 us
    pallas_call x2, Pallas kernels: 15.5 us -> 9.75 us  [body(): pl.pallas_call(functools.partial(blur_kernel, height, pieces, batches_eac...]
    pallas_call x2, Pallas kernels: 7.72 us -> 9.35 us  [body(): pl.pallas_call(functools.partial(update_kernel, bands, tile_rows, height,...]
  transfers between devices with their start and end apart: 1 -> 1, of which waited for: 1 -> 1; matrix products, arithmetic and copies ran while one was open for 2% -> 2% of each run, Pallas kernels for 9% -> 10%
where the time goes in v6:
time: 104 us; the launch traced here: 103 us
  blocking collectives  55.4 us (53%)
  Pallas kernels  33.3 us (32%)
  starting transfers between devices  7.37 us (7%)
  waiting for transfers between devices  3.32 us (3%)
  local copies, waits for them, and re-layouts  2.97 us (3%)
    all_to_all x3, blocking collectives, swap(): return lax.all_to_all(a, 'sky', split_axis=0, concat_axis=0, tiled=True)  55.4 us
    pallas_call x1, Pallas kernels, body(): pl.pallas_call(functools.partial(tables_kernel, capacity, height, rows_ea...  9.94 us
    pallas_call x2, Pallas kernels, body(): pl.pallas_call(functools.partial(blur_kernel, height, pieces, batches_eac...  9.75 us
    pallas_call x2, Pallas kernels, body(): pl.pallas_call(functools.partial(update_kernel, bands, tile_rows, height,...  9.35 us
    all_to_all x1, starting transfers between devices, swap(): return lax.all_to_all(a, 'sky', split_axis=0, concat_axis=0, tiled=True)  7.37 us
    pallas_call x1, Pallas kernels, body(): pl.pallas_call(functools.partial(first_send_kernel, tile_rows, height, ro...  4.27 us
    all_to_all x1, waiting for transfers between devices, swap(): return lax.all_to_all(a, 'sky', split_axis=0, concat_axis=0, tiled=True)  3.32 us
    unnamed x31, local copies, waits for them, and re-layouts  2.97 us
  transfers between devices with their start and end apart: 1, of which 1 were waited for; matrix products, arithmetic and copies ran while one was open for 2% of the time, Pallas kernels for 10%

profile of v6, /device:TPU:0, one launch (start us, length us, event | category | flops | bytes accessed | tf_op | source)
XLA Modules:
  0.0 103.2 jit_solution(685743701555881710)
XLA Ops:
  0.6 0.0 copy-start.11
  0.6 0.0 copy-start.12
  0.7 0.0 copy-start.13
  0.7 0.0 copy-start.1
  0.7 0.0 copy-start.9
  0.7 0.0 copy-start.10
  0.7 4.3 %first_send.1 = bf16[16,144,128]{2,1,0:T(8,128)(2,1)} custom-call(s32[16,16]{1,0:T(8,128)} %plane_ref.5, s32[16,16]{1,0:T(8,128)} %row_ref.5, s32[16,16]{1,0:T(8,128)} %cover_ref.5, f32[2,56]{1,0:T(2,128)} %taps_ref.1, f32[3072,128]{1,0:T(8,128)} %bitcast.2), custom_call_target="tpu_custom_call" | custom-call | tf_op jit(solution)/shard_map/first_send/pallas_call | solution.py:354
  5.0 7.4 %all-to-all-start = ((bf16[16,144,128]{2,1,0:T(8,128)(2,1)}), bf16[16,144,128]{2,1,0:T(8,128)(2,1)S(1)}, u32[]{:S(2)}, u32[]{:S(2)}) async-start(bf16[16,144,128]{2,1,0:T(8,128)(2,1)} %first_send.1), calls=%async_computation | async-start | bytes 1179648 | tf_op jit(solution)/shard_map/all_to_all | solution.py:352
  12.3 0.0 copy-done.11
  12.4 0.7 copy.16.slot_ref
  13.1 0.0 copy-done.12
  13.1 0.7 copy.17.start_ref
  13.8 0.0 copy-done.13
  13.8 0.7 copy.18.stop_ref
  14.6 9.9 %tables.1.table_in_ref = s32[6,256]{1,0:T(8,128)} custom-call(s32[128,2]{1,0:T(8,128)} %copy.16.slot_ref, s32[128,2]{1,0:T(8,128)} %copy.17.start_ref, s32[128,2]{1,0:T(8,128)} %copy.18.stop_ref), custom_call_target="tpu_custom_call" | custom-call | flops 4000000 | bytes 8000000 | tf_op jit(solution)/shard_map/tables/pallas_call | solution.py:369
  24.5 0.0 copy-start
  24.5 0.0 copy-start.2
  24.6 0.0 copy-start.3
  24.6 0.0 copy-start.4
  24.6 3.3 %all-to-all-done.arrived_ref.bank_in_ref = bf16[16,144,128]{2,1,0:T(8,128)(2,1)S(1)} async-done(((bf16[16,144,128]{2,1,0:T(8,128)(2,1)}), bf16[16,144,128]{2,1,0:T(8,128)(2,1)S(1)}, u32[]{:S(2)}, u32[]{:S(2)}) %all-to-all-start) | async-done | bytes 589856 | tf_op jit(solution)/shard_map/all_to_all | solution.py:352
  27.9 0.0 copy-done.1
  27.9 0.0 copy-done.9
  27.9 0.0 copy-done.10
  27.9 0.0 copy-start.5
  27.9 0.7 copy-done.5
  28.6 0.0 copy-start.6
  28.6 0.0 copy-start.7
  28.6 0.0 copy-start.8
  28.6 4.3 %blur.2 = bf16[16,128,128]{2,1,0:T(8,128)(2,1)S(1)} custom-call(s32[6,256]{1,0:T(8,128)S(1)} %copy-done.5, f32[128]{0:T(128)S(1)} %copy-done.9, s32[128]{0:T(128)S(1)} %copy-done.10, bf16[16,144,128]{2,1,0:T(8,128)(2,1)S(1)} %all-to-all-done.arrived_ref.bank_in_ref, bf16[16,144,128]{2,1,0:T(8,128)(2,1)S(1)} %all-to-all-done.arrived_ref.bank_in_ref, ...), custom_call_target="tpu_custom_call" | custom-call | tf_op jit(solution)/shard_map/blur/pallas_call | solution.py:382
  32.9 18.7 %all_to_all.20.returned_ref = bf16[16,128,128]{2,1,0:T(8,128)(2,1)S(1)} all-to-all(bf16[16,128,128]{2,1,0:T(8,128)(2,1)S(1)} %blur.2), channel_id=1, replica_groups=mesh['groups'=2,'sky'=16] {'sky'}, dimensions={0} | all-to-all | bytes 1048576 | tf_op jit(solution)/shard_map/all_to_all | solution.py:352
  51.6 0.0 copy-done
  51.6 0.0 copy-done.2
  51.6 0.0 copy-done.3
  51.6 0.0 copy-done.4
  51.6 0.0 copy-done.6
  51.6 0.0 copy-done.7
  51.6 0.0 copy-done.8
  51.7 5.8 %update.2 = (f32[3072,128]{1,0:T(8,128)S(1)}, bf16[16,128,128]{2,1,0:T(8,128)(2,1)S(1)}) custom-call(s32[16,16]{1,0:T(8,128)S(1)} %copy-done.2, s32[16,16]{1,0:T(8,128)S(1)} %copy-done.3, s32[16,16]{1,0:T(8,128)S(1)} %copy-done.4, f32[6]{0:T(128)S(1)} %copy-done.6, s32[2]{0:T(128)S(1)} %copy-done.7, s32[2]{0:T(128)S(1)} %copy-done.8, ...), custom_call_target="tpu_custom_call" | custom-call | tf_op jit(solution)/shard_map/update/pallas_call | solution.py:424
  57.4 18.4 %all_to_all.21.arrived_ref = bf16[16,128,128]{2,1,0:T(8,128)(2,1)S(1)} all-to-all(bf16[16,128,128]{2,1,0:T(8,128)(2,1)S(1)} %get-tuple-element.6), channel_id=1, replica_groups=mesh['groups'=2,'sky'=16] {'sky'}, dimensions={0} | all-to-all | bytes 1048576 | tf_op jit(solution)/shard_map/all_to_all | solution.py:352
  75.8 5.5 %blur.3 = (bf16[16,128,128]{2,1,0:T(8,128)(2,1)S(1)}, f32[128,16,128]{2,1,0:T(8,128)}) custom-call(s32[6,256]{1,0:T(8,128)S(1)} %copy-done.5, f32[128]{0:T(128)S(1)} %copy-done.9, s32[128]{0:T(128)S(1)} %copy-done.10, bf16[16,128,128]{2,1,0:T(8,128)(2,1)S(1)} %all_to_all.21.arrived_ref, bf16[16,144,128]{2,1,0:T(8,128)(2,1)S(1)} %all-to-all-done.arrived_ref.bank_in_ref, ...), custom_call_target="tpu_custom_call" | custom-call | tf_op jit(solution)/shard_map/blur/pallas_call | solution.py:382
  81.3 18.4 %all_to_all.22.returned_ref = bf16[16,128,128]{2,1,0:T(8,128)(2,1)S(1)} all-to-all(bf16[16,128,128]{2,1,0:T(8,128)(2,1)S(1)} %get-tuple-element.7), channel_id=1, replica_groups=mesh['groups'=2,'sky'=16] {'sky'}, dimensions={0} | all-to-all | bytes 1048576 | tf_op jit(solution)/shard_map/all_to_all | solution.py:352
  99.6 3.6 %update.3 = f32[3072,128]{1,0:T(8,128)} custom-call(s32[16,16]{1,0:T(8,128)S(1)} %copy-done.2, s32[16,16]{1,0:T(8,128)S(1)} %copy-done.3, s32[16,16]{1,0:T(8,128)S(1)} %copy-done.4, f32[6]{0:T(128)S(1)} %copy-done.6, s32[2]{0:T(128)S(1)} %copy-done.7, s32[2]{0:T(128)S(1)} %copy-done.8, bf16[16,128,128]{2,1,0:T(8,128)(2,1)S(1)} %all_to_all.22.returned_ref, ...), custom_call_target="tpu_custom_call" | custom-call | tf_op jit(solution)/shard_map/update/pallas_call | solution.py:424
Async XLA Ops:
  0.6 11.7 %copy-start.11 = (s32[128,2]{0,1:T(2,128)S(1)}, s32[128,2]{0,1:T(2,128)}, u32[]{:S(2)}) copy-start(s32[128,2]{0,1:T(2,128)} %param.23) | copy-start | bytes 3076
  0.6 12.5 %copy-start.12 = (s32[128,2]{0,1:T(2,128)S(1)}, s32[128,2]{0,1:T(2,128)}, u32[]{:S(2)}) copy-start(s32[128,2]{0,1:T(2,128)} %param.24) | copy-start | bytes 3076
  0.7 13.2 %copy-start.13 = (s32[128,2]{0,1:T(2,128)S(1)}, s32[128,2]{0,1:T(2,128)}, u32[]{:S(2)}) copy-start(s32[128,2]{0,1:T(2,128)} %param.25) | copy-start | bytes 3076
  0.7 27.2 %copy-start.1 = (bf16[128,16,128]{2,1,0:T(8,128)(2,1)S(1)}, bf16[128,16,128]{2,1,0:T(8,128)(2,1)}, u32[]{:S(2)}) copy-start(bf16[128,16,128]{2,1,0:T(8,128)(2,1)} %seen_ref.3) | copy-start | bytes 1572868
  0.7 27.2 %copy-start.9 = (f32[128]{0:T(128)S(1)}, f32[128]{0:T(128)}, u32[]{:S(2)}) copy-start(f32[128]{0:T(128)} %weight_ref.3) | copy-start | bytes 1540
  0.7 27.2 %copy-start.10 = (s32[128]{0:T(128)S(1)}, s32[128]{0:T(128)}, u32[]{:S(2)}) copy-start(s32[128]{0:T(128)} %batch_ref.3) | copy-start | bytes 1540
  5.0 22.9 %all-to-all-start = ((bf16[16,144,128]{2,1,0:T(8,128)(2,1)}), bf16[16,144,128]{2,1,0:T(8,128)(2,1)S(1)}, u32[]{:S(2)}, u32[]{:S(2)}) async-start(bf16[16,144,128]{2,1,0:T(8,128)(2,1)} %first_send.1), calls=%async_computation | async-start | bytes 1179648 | tf_op jit(solution)/shard_map/all_to_all | solution.py:352
  24.5 27.1 %copy-start = (f32[2,6,256,128]{3,2,1,0:T(8,128)S(1)}, f32[2,6,256,128]{3,2,1,0:T(8,128)}, u32[]{:S(2)}) copy-start(f32[2,6,256,128]{3,2,1,0:T(8,128)} %param.14) | copy-start | bytes 4718596
  24.5 27.1 %copy-start.2 = (s32[16,16]{1,0:T(8,128)S(1)}, s32[16,16]{1,0:T(8,128)}, u32[]{:S(2)}) copy-start(s32[16,16]{1,0:T(8,128)} %plane_ref.5) | copy-start | bytes 3076
  24.6 27.1 %copy-start.3 = (s32[16,16]{1,0:T(8,128)S(1)}, s32[16,16]{1,0:T(8,128)}, u32[]{:S(2)}) copy-start(s32[16,16]{1,0:T(8,128)} %row_ref.5) | copy-start | bytes 3076
  24.6 27.1 %copy-start.4 = (s32[16,16]{1,0:T(8,128)S(1)}, s32[16,16]{1,0:T(8,128)}, u32[]{:S(2)}) copy-start(s32[16,16]{1,0:T(8,128)} %cover_ref.5) | copy-start | bytes 3076
  27.9 0.7 copy-start.5
  28.6 23.0 %copy-start.6 = (f32[6]{0:T(128)S(1)}, f32[6]{0:T(128)}, u32[]{:S(2)}) copy-start(f32[6]{0:T(128)} %step_ref.3) | copy-start | bytes 76
  28.6 23.0 %copy-start.7 = (s32[2]{0:T(128)S(1)}, s32[2]{0:T(128)}, u32[]{:S(2)}) copy-start(s32[2]{0:T(128)} %lo_ref.3) | copy-start | bytes 28
  28.6 23.0 %copy-start.8 = (s32[2]{0:T(128)S(1)}, s32[2]{0:T(128)}, u32[]{:S(2)}) copy-start(s32[2]{0:T(128)} %hi_ref.3) | copy-start | bytes 28

commit v7 on v6

--- a/solution.py
+++ b/solution.py
@@ -19,11 +19,11 @@
 
 smem = lambda: pl.BlockSpec(memory_space=pltpu.SMEM)
 vmem = lambda: pl.BlockSpec(memory_space=pltpu.VMEM)
-hbm = lambda: pl.BlockSpec(memory_space=pl.ANY)
-
-
-def params(share=1.0):
-    return pltpu.CompilerParams(vmem_limit_bytes=int(share * VMEM_BYTES))
+hbm = lambda: pl.BlockSpec(memory_space=pltpu.HBM)
+
+
+def params():
+    return pltpu.CompilerParams(vmem_limit_bytes=VMEM_BYTES)
 
 
 def aligned(rows):
@@ -80,18 +80,43 @@
 
 
 def first_send_kernel(
-    tile_rows, height, rows_each, plane_ref, row_ref, cover_ref, taps_ref, model_ref, out_ref, x_ref, packed_ref, bank_ref, sem
+    tile_rows,
+    height,
+    rows_each,
+    plane_in_ref,
+    row_in_ref,
+    cover_in_ref,
+    taps_in_ref,
+    model_ref,
+    out_ref,
+    plane_ref,
+    row_ref,
+    cover_ref,
+    taps_ref,
+    x_ref,
+    packed_ref,
+    bank_ref,
+    sems,
 ):
     peers = plane_ref.shape[0]
-    total = model_ref.shape[0]
-    load = pltpu.make_async_copy(model_ref, x_ref.at[pl.ds(0, total), :], sem)
-    load.start()
+    pairs = (
+        (taps_in_ref, taps_ref),
+        (model_ref, x_ref.at[pl.ds(0, model_ref.shape[0]), :]),
+        (plane_in_ref, plane_ref),
+        (row_in_ref, row_ref),
+        (cover_in_ref, cover_ref),
+    )
+    loads = [pltpu.make_async_copy(*pair, sems.at[n]) for n, pair in enumerate(pairs)]
+    for load in loads:
+        load.start()
     bank_ref[...] = jnp.zeros(bank_ref.shape, F32)
+    loads[0].wait()
     for m, row in enumerate(bank_rows(taps_ref[...], height)):
         for n in range(taps_ref.shape[0]):
             bank_ref[2 * n + m : 2 * n + m + 1, :] = row[n : n + 1, :]
     bank = bank_ref[...].astype(BF16)
-    load.wait()
+    for load in loads[1:]:
+        load.wait()
     pack_slots(plane_ref, row_ref, cover_ref, tile_rows, height, rows_each, x_ref, packed_ref)
     for d in range(peers):
         out_ref[d, :rows_each, :] = packed_ref[d * rows_each : (d + 1) * rows_each, :].astype(BF16)
@@ -115,21 +140,19 @@
     *rest,
 ):
     if last:
-        new_ref, x_ref, back_ref, scale_ref, sem, saved, *more_refs = rest
+        new_ref, back_ref, scale_ref, x_ref, saved, *more_refs = rest
     else:
-        new_ref, out_ref, x_ref, back_ref, scale_ref, sem, saved, *more_refs, packed_ref = rest
+        x_ref, out_ref, back_ref, scale_ref, packed_ref, *more_refs = rest
     peers, capacity = plane_ref.shape
-    total = model_ref.shape[0]
+    total = x_ref.shape[0] - height
     planes = total // tile_rows
-    load = pltpu.make_async_copy(model_ref, x_ref.at[pl.ds(0, total), :], sem)
-    load.start()
     for p in range(planes):
         scale_ref[p] = step_ref[p % bands]
+    x_ref[:total, :] = model_ref[:total, :]
     for ref in more_refs:
         ref[...] = jnp.zeros(ref.shape, F32)
     for d in range(peers):
         back_ref[d * rows_each : (d + 1) * rows_each, :] = returned_ref[d].astype(F32)
-    load.wait()
     place = lax.broadcasted_iota(I32, (height, LANES), 0)
 
     sums = [x_ref, *more_refs]
@@ -156,9 +179,10 @@
         here = slice(p * tile_rows, (p + 1) * tile_rows)
         new = sum((ref[here, :] for ref in more_refs), x_ref[here, :])
         x_ref[here, :] = jnp.where(inside, jnp.maximum(new, 0.0), 0.0)
-        rows = pl.ds(p * tile_rows, tile_rows)
-        saves.append(pltpu.make_async_copy(x_ref.at[rows, :], new_ref.at[rows, :], saved.at[p]))
-        saves[-1].start()
+        if last:
+            rows = pl.ds(p * tile_rows, tile_rows)
+            saves.append(pltpu.make_async_copy(x_ref.at[rows, :], new_ref.at[rows, :], saved.at[p]))
+            saves[-1].start()
     if not last:
         pack_slots(plane_ref, row_ref, cover_ref, tile_rows, height, rows_each, x_ref, packed_ref)
         for d in range(peers):
@@ -230,21 +254,22 @@
     if last:
         out_ref, residual_out_ref, *rest = rest
         *rest, residual_ref, sent = rest
+        send = pltpu.make_async_copy(residual_ref, residual_out_ref, sent)
     else:
         out_ref, *rest = rest
     table_ref, sem, rows_ref, bank_ref, result_ref, packed_ref, held_ref, blur_ref, back_ref = rest
     load = pltpu.make_async_copy(table_in_ref, table_ref, sem)
     load.start()
     peers, rows_each, _ = out_ref.shape
-    extra = bank_in_ref.shape[1]
+    extra = bank_in_ref.shape[1] - rows_each
     exposures = batch_ref.shape[0]
     slots = peers * (2 * rows_each // height)
     abreast = max(n for n in (1, 2, 4, 8, 16, 32) if exposures % n == 0)
     place = lax.broadcasted_iota(I32, (height, LANES), 0)
     lane = lax.broadcasted_iota(I32, (height, LANES), 1)
     for o in range(peers):
-        rows_ref[height + o * rows_each : height + (o + 1) * rows_each, :] = arrived_ref[o].astype(F32)
-        bank_ref[o * extra : (o + 1) * extra, :] = bank_in_ref[o].astype(F32)
+        rows_ref[height + o * rows_each : height + (o + 1) * rows_each, :] = arrived_ref[o, :rows_each, :].astype(F32)
+        bank_ref[o * extra : (o + 1) * extra, :] = bank_in_ref[o, rows_each:, :].astype(F32)
 
     gap = lane % height - place
     near = (gap <= HALF) & (gap >= -HALF) & (lane < TAPS * height)
@@ -293,18 +318,14 @@
 
     steps = exposures // abreast
 
-    def send(s):
-        some = pl.ds(s * abreast, abreast)
-        return pltpu.make_async_copy(residual_ref.at[some], residual_out_ref.at[some], sent.at[s])
-
     load.wait()
     for s in range(steps + 1):
         if s > 0:
             correlate(s - 1)
         if s < steps:
             blur(s)
-            if last:
-                send(s).start()
+    if last:
+        send.start()
 
     def move(s, _):
         packed_ref[pl.ds(table_ref[2 * pieces + 1, s], height), :] = result_ref[
@@ -316,8 +337,7 @@
     for o in range(peers):
         out_ref[o, :, :] = packed_ref[o * rows_each : (o + 1) * rows_each, :].astype(BF16)
     if last:
-        for s in range(steps):
-            send(s).wait()
+        send.wait()
 
 
 def body(
@@ -354,15 +374,19 @@
     outbound = pl.pallas_call(
         functools.partial(first_send_kernel, tile_rows, height, rows_each),
         out_shape=jax.ShapeDtypeStruct((peers, block, columns), BF16),
-        in_specs=[smem(), smem(), smem(), vmem(), hbm()],
+        in_specs=[hbm()] * 5,
         out_specs=vmem(),
         scratch_shapes=[
+            pltpu.SMEM(send_plane.shape, I32),
+            pltpu.SMEM(send_row.shape, I32),
+            pltpu.SMEM(send_cover.shape, I32),
+            pltpu.VMEM(psf_taps.shape, F32),
             pltpu.VMEM((total + height, columns), F32),
             pltpu.VMEM((peers * rows_each + height, columns), F32),
             pltpu.VMEM((extra, columns), F32),
-            pltpu.SemaphoreType.DMA,
+            pltpu.SemaphoreType.DMA((5,)),
         ],
-        compiler_params=params(2.5),
+        compiler_params=params(),
         name="first_send",
     )(send_plane, send_row, send_cover, psf_taps, x)
     arrived = swap(outbound)
@@ -381,14 +405,13 @@
         rows_shape = jax.ShapeDtypeStruct((peers, rows_each, columns), BF16)
         outs = pl.pallas_call(
             functools.partial(blur_kernel, height, pieces, batches_each, last),
-            grid=(1,),
             out_shape=(rows_shape, jax.ShapeDtypeStruct(exposures.shape, F32)) if last else rows_shape,
             in_specs=[
                 hbm(),
                 smem(),
                 smem(),
-                pl.BlockSpec((peers, rows_each, columns), lambda i: (0, 0, 0)),
-                pl.BlockSpec((peers, extra, columns), lambda i: (0, rows_each // extra, 0)),
+                vmem(),
+                vmem(),
                 vmem(),
             ],
             out_specs=(vmem(), hbm()) if last else vmem(),
@@ -403,30 +426,28 @@
                 pltpu.VMEM((peers * batches_each, height, LANES), BF16),
                 pltpu.VMEM((peers * batches_each, height, LANES), BF16),
             ]
-            + [pltpu.VMEM(exposures.shape, F32), pltpu.SemaphoreType.DMA((count,))] * last,
+            + [pltpu.VMEM(exposures.shape, F32), pltpu.SemaphoreType.DMA] * last,
             compiler_params=params(),
             name="blur",
         )(table, inv_var, exp_batch, arrived, with_bank, exposures)
         outgoing = outs[0] if last else outs
         returned = swap(outgoing)
         new_shape = jax.ShapeDtypeStruct((total, columns), F32)
-        scratch = [
-            pltpu.VMEM((total + height, columns), F32),
-            pltpu.VMEM((peers * rows_each + height, columns), F32),
-            pltpu.SMEM((tile_count * bands,), F32),
-            pltpu.SemaphoreType.DMA,
-            pltpu.SemaphoreType.DMA((tile_count * bands,)),
-        ]
+        padded = (total + height, columns)
+        scratch = [pltpu.VMEM((peers * rows_each + height, columns), F32), pltpu.SMEM((tile_count * bands,), F32)]
+        if last:
+            scratch += [pltpu.VMEM(padded, F32), pltpu.SemaphoreType.DMA((tile_count * bands,))]
+        else:
+            scratch.append(pltpu.VMEM((peers * rows_each + height, columns), F32))
         sums = max(n for n in (1, 2, 4) if peers % n == 0)
-        scratch += [pltpu.VMEM((total + height, columns), F32)] * (sums - 1)
-        if not last:
-            scratch.append(pltpu.VMEM((peers * rows_each + height, columns), F32))
         res = pl.pallas_call(
             functools.partial(update_kernel, bands, tile_rows, height, rows_each, last),
-            out_shape=new_shape if last else (new_shape, rows_shape),
-            in_specs=[smem()] * 6 + [vmem(), hbm()],
-            out_specs=hbm() if last else (hbm(), vmem()),
-            scratch_shapes=scratch,
+            out_shape=jax.ShapeDtypeStruct((total, columns), F32)
+            if last
+            else (jax.ShapeDtypeStruct(padded, F32), rows_shape),
+            in_specs=[smem()] * 6 + [vmem(), vmem()],
+            out_specs=hbm() if last else (vmem(), vmem()),
+            scratch_shapes=scratch + [pltpu.VMEM(padded, F32)] * (sums - 1),
             compiler_params=params(),
             name="update",
         )(send_plane, send_row, send_cover, step_size, foot_lo, foot_hi, returned, x)

time: 104 us -> 103 us (level)
  Pallas kernels: 33.3 us -> 28.7 us
  local copies, waits for them, and re-layouts: 2.97 us -> 7.14 us
    unnamed x31 -> x41, local copies, waits for them, and re-layouts: 2.97 us -> 7.14 us
    pallas_call x2, Pallas kernels: 9.35 us -> 7.3 us  [body(): pl.pallas_call(functools.partial(update_kernel, bands, tile_rows, height,...]
    pallas_call x1, Pallas kernels: 4.27 us -> 2.81 us  [body(): pl.pallas_call(functools.partial(first_send_kernel, tile_rows, height, ro...]
    pallas_call x2, Pallas kernels: 9.75 us -> 8.61 us  [body(): pl.pallas_call(functools.partial(blur_kernel, height, pieces, batches_eac...]
where the time goes in v7:
time: 103 us
  blocking collectives  55.4 us (54%)
  Pallas kernels  28.7 us (28%)
  starting transfers between devices  7.37 us (7%)
  local copies, waits for them, and re-layouts  7.14 us (7%)
  waiting for transfers between devices  3.32 us (3%)
    all_to_all x3, blocking collectives, swap(): return lax.all_to_all(a, 'sky', split_axis=0, concat_axis=0, tiled=True)  55.4 us
    pallas_call x1, Pallas kernels, body(): pl.pallas_call(functools.partial(tables_kernel, capacity, height, rows_ea...  9.94 us
    pallas_call x2, Pallas kernels, body(): pl.pallas_call(functools.partial(blur_kernel, height, pieces, batches_eac...  8.61 us
    all_to_all x1, starting transfers between devices, swap(): return lax.all_to_all(a, 'sky', split_axis=0, concat_axis=0, tiled=True)  7.37 us
    pallas_call x2, Pallas kernels, body(): pl.pallas_call(functools.partial(update_kernel, bands, tile_rows, height,...  7.3 us
    unnamed x41, local copies, waits for them, and re-layouts  7.14 us
    all_to_all x1, waiting for transfers between devices, swap(): return lax.all_to_all(a, 'sky', split_axis=0, concat_axis=0, tiled=True)  3.32 us
    pallas_call x1, Pallas kernels, body(): pl.pallas_call(functools.partial(first_send_kernel, tile_rows, height, ro...  2.81 us
  transfers between devices with their start and end apart: 1, of which 1 were waited for; matrix products, arithmetic and copies ran while one was open for 2% of the time, Pallas kernels for 10%

profile of v7, /device:TPU:0, one launch (start us, length us, event | category | flops | bytes accessed | tf_op | source)
XLA Modules:
  0.0 102.7 jit_solution(8353616590215758049)
XLA Ops:
  0.6 0.0 copy-start
  0.6 1.4 %copy-done = f32[2,6,256,128]{3,2,1,0:T(8,128)S(1)} copy-done((f32[2,6,256,128]{3,2,1,0:T(8,128)S(1)}, f32[2,6,256,128]{3,2,1,0:T(8,128)}, u32[]{:S(2)}) %copy-start) | copy-done | bytes 1572888
  2.0 0.0 copy-start.3
  2.0 0.7 copy-done.3
  2.7 0.0 copy-start.5
  2.7 0.7 copy-done.5
  3.4 0.0 copy-start.7
  3.4 0.7 copy-done.7
  4.1 0.0 copy-start.15
  4.1 0.7 copy-done.15
  4.8 0.0 copy-start.16
  4.8 0.0 copy-start.17
  4.8 0.0 copy-start.18
  4.8 0.0 copy-start.2
  4.8 0.0 copy-start.13
  4.8 0.0 copy-start.14
  4.8 2.8 %first_send.1 = bf16[16,144,128]{2,1,0:T(8,128)(2,1)} custom-call(s32[16,16]{1,0:T(8,128)S(1)} %copy-done.3, s32[16,16]{1,0:T(8,128)S(1)} %copy-done.5, s32[16,16]{1,0:T(8,128)S(1)} %copy-done.7, f32[2,56]{1,0:T(2,128)S(1)} %copy-done.15, f32[3072,128]{1,0:T(8,128)S(1)} %bitcast.2), custom_call_target="tpu_custom_call" | custom-call | tf_op jit(solution)/shard_map/first_send/pallas_call | solution.py:374
  7.7 7.4 %all-to-all-start = ((bf16[16,144,128]{2,1,0:T(8,128)(2,1)}), bf16[16,144,128]{2,1,0:T(8,128)(2,1)S(1)}, u32[]{:S(2)}, u32[]{:S(2)}) async-start(bf16[16,144,128]{2,1,0:T(8,128)(2,1)} %first_send.1), calls=%async_computation | async-start | bytes 1179648 | tf_op jit(solution)/shard_map/all_to_all | solution.py:372
  15.0 0.0 copy-done.16
  15.1 0.7 copy.16.slot_ref
  15.8 0.0 copy-done.17
  15.8 0.7 copy.17.start_ref
  16.5 0.0 copy-done.18
  16.5 0.7 copy.18.stop_ref
  17.3 9.9 %tables.1.table_in_ref = s32[6,256]{1,0:T(8,128)} custom-call(s32[128,2]{1,0:T(8,128)} %copy.16.slot_ref, s32[128,2]{1,0:T(8,128)} %copy.17.start_ref, s32[128,2]{1,0:T(8,128)} %copy.18.stop_ref), custom_call_target="tpu_custom_call" | custom-call | flops 4000000 | bytes 8000000 | tf_op jit(solution)/shard_map/tables/pallas_call | solution.py:393
  27.2 0.0 copy-start.1
  27.2 0.0 copy-start.4
  27.2 0.0 copy-start.6
  27.3 0.0 copy-start.8
  27.3 3.3 %all-to-all-done.arrived_ref.bank_in_ref = bf16[16,144,128]{2,1,0:T(8,128)(2,1)S(1)} async-done(((bf16[16,144,128]{2,1,0:T(8,128)(2,1)}), bf16[16,144,128]{2,1,0:T(8,128)(2,1)S(1)}, u32[]{:S(2)}, u32[]{:S(2)}) %all-to-all-start) | async-done | bytes 589856 | tf_op jit(solution)/shard_map/all_to_all | solution.py:372
  30.6 0.0 copy-done.2
  30.6 0.0 copy-done.13
  30.6 0.0 copy-done.14
  30.6 0.0 copy-start.9
  30.6 0.7 copy-done.9
  31.3 0.0 copy-start.10
  31.3 0.0 copy-start.11
  31.3 0.0 copy-start.12
  31.3 4.3 %blur.2 = bf16[16,128,128]{2,1,0:T(8,128)(2,1)S(1)} custom-call(s32[6,256]{1,0:T(8,128)S(1)} %copy-done.9, f32[128]{0:T(128)S(1)} %copy-done.13, s32[128]{0:T(128)S(1)} %copy-done.14, bf16[16,144,128]{2,1,0:T(8,128)(2,1)S(1)} %all-to-all-done.arrived_ref.bank_in_ref, bf16[16,144,128]{2,1,0:T(8,128)(2,1)S(1)} %all-to-all-done.arrived_ref.bank_in_ref, ...), custom_call_target="tpu_custom_call" | custom-call | tf_op jit(solution)/shard_map/blur/pallas_call | solution.py:406
  35.6 18.7 %all_to_all.20.returned_ref = bf16[16,128,128]{2,1,0:T(8,128)(2,1)S(1)} all-to-all(bf16[16,128,128]{2,1,0:T(8,128)(2,1)S(1)} %blur.2), channel_id=1, replica_groups=mesh['groups'=2,'sky'=16] {'sky'}, dimensions={0} | all-to-all | bytes 1048576 | tf_op jit(solution)/shard_map/all_to_all | solution.py:372
  54.3 0.0 copy-done.1
  54.3 0.0 copy-done.4
  54.3 0.0 copy-done.6
  54.3 0.0 copy-done.8
  54.3 0.0 copy-done.10
  54.3 0.0 copy-done.11
  54.3 0.0 copy-done.12
  54.3 3.8 %update.2 = (f32[3088,128]{1,0:T(8,128)S(1)}, bf16[16,128,128]{2,1,0:T(8,128)(2,1)S(1)}) custom-call(s32[16,16]{1,0:T(8,128)S(1)} %copy-done.4, s32[16,16]{1,0:T(8,128)S(1)} %copy-done.6, s32[16,16]{1,0:T(8,128)S(1)} %copy-done.8, f32[6]{0:T(128)S(1)} %copy-done.10, s32[2]{0:T(128)S(1)} %copy-done.11, s32[2]{0:T(128)S(1)} %copy-done.12, ...), custom_call_target="tpu_custom_call" | custom-call | tf_op jit(solution)/shard_map/update/pallas_call | solution.py:443
  58.1 18.4 %all_to_all.21.arrived_ref = bf16[16,128,128]{2,1,0:T(8,128)(2,1)S(1)} all-to-all(bf16[16,128,128]{2,1,0:T(8,128)(2,1)S(1)} %get-tuple-element.6), channel_id=1, replica_groups=mesh['groups'=2,'sky'=16] {'sky'}, dimensions={0} | all-to-all | bytes 1048576 | tf_op jit(solution)/shard_map/all_to_all | solution.py:372
  76.5 4.3 %blur.3 = (bf16[16,128,128]{2,1,0:T(8,128)(2,1)S(1)}, f32[128,16,128]{2,1,0:T(8,128)}) custom-call(s32[6,256]{1,0:T(8,128)S(1)} %copy-done.9, f32[128]{0:T(128)S(1)} %copy-done.13, s32[128]{0:T(128)S(1)} %copy-done.14, bf16[16,128,128]{2,1,0:T(8,128)(2,1)S(1)} %all_to_all.21.arrived_ref, bf16[16,144,128]{2,1,0:T(8,128)(2,1)S(1)} %all-to-all-done.arrived_ref.bank_in_ref, ...), custom_call_target="tpu_custom_call" | custom-call | tf_op jit(solution)/shard_map/blur/pallas_call | solution.py:406
  80.8 18.4 %all_to_all.22.returned_ref = bf16[16,128,128]{2,1,0:T(8,128)(2,1)S(1)} all-to-all(bf16[16,128,128]{2,1,0:T(8,128)(2,1)S(1)} %get-tuple-element.7), channel_id=1, replica_groups=mesh['groups'=2,'sky'=16] {'sky'}, dimensions={0} | all-to-all | bytes 1048576 | tf_op jit(solution)/shard_map/all_to_all | solution.py:372
  99.2 3.6 %update.3 = f32[3072,128]{1,0:T(8,128)} custom-call(s32[16,16]{1,0:T(8,128)S(1)} %copy-done.4, s32[16,16]{1,0:T(8,128)S(1)} %copy-done.6, s32[16,16]{1,0:T(8,128)S(1)} %copy-done.8, f32[6]{0:T(128)S(1)} %copy-done.10, s32[2]{0:T(128)S(1)} %copy-done.11, s32[2]{0:T(128)S(1)} %copy-done.12, bf16[16,128,128]{2,1,0:T(8,128)(2,1)S(1)} %all_to_all.22.returned_ref, ...), custom_call_target="tpu_custom_call" | custom-call | tf_op jit(solution)/shard_map/update/pallas_call | solution.py:443
Async XLA Ops:
  0.6 1.4 %copy-start = (f32[2,6,256,128]{3,2,1,0:T(8,128)S(1)}, f32[2,6,256,128]{3,2,1,0:T(8,128)}, u32[]{:S(2)}) copy-start(f32[2,6,256,128]{3,2,1,0:T(8,128)} %param.14) | copy-start | bytes 4718596
  2.0 0.7 copy-start.3
  2.7 0.7 copy-start.5
  3.4 0.7 copy-start.7
  4.1 0.7 copy-start.15
  4.8 10.2 %copy-start.16 = (s32[128,2]{0,1:T(2,128)S(1)}, s32[128,2]{0,1:T(2,128)}, u32[]{:S(2)}) copy-start(s32[128,2]{0,1:T(2,128)} %param.23) | copy-start | bytes 3076
  4.8 11.0 %copy-start.17 = (s32[128,2]{0,1:T(2,128)S(1)}, s32[128,2]{0,1:T(2,128)}, u32[]{:S(2)}) copy-start(s32[128,2]{0,1:T(2,128)} %param.24) | copy-start | bytes 3076
  4.8 11.7 %copy-start.18 = (s32[128,2]{0,1:T(2,128)S(1)}, s32[128,2]{0,1:T(2,128)}, u32[]{:S(2)}) copy-start(s32[128,2]{0,1:T(2,128)} %param.25) | copy-start | bytes 3076
  4.8 25.8 %copy-start.2 = (bf16[128,16,128]{2,1,0:T(8,128)(2,1)S(1)}, bf16[128,16,128]{2,1,0:T(8,128)(2,1)}, u32[]{:S(2)}) copy-start(bf16[128,16,128]{2,1,0:T(8,128)(2,1)} %seen_ref.3) | copy-start | bytes 1572868
  4.8 25.8 %copy-start.13 = (f32[128]{0:T(128)S(1)}, f32[128]{0:T(128)}, u32[]{:S(2)}) copy-start(f32[128]{0:T(128)} %weight_ref.3) | copy-start | bytes 1540
  4.8 25.8 %copy-start.14 = (s32[128]{0:T(128)S(1)}, s32[128]{0:T(128)}, u32[]{:S(2)}) copy-start(s32[128]{0:T(128)} %batch_ref.3) | copy-start | bytes 1540
  7.7 22.9 %all-to-all-start = ((bf16[16,144,128]{2,1,0:T(8,128)(2,1)}), bf16[16,144,128]{2,1,0:T(8,128)(2,1)S(1)}, u32[]{:S(2)}, u32[]{:S(2)}) async-start(bf16[16,144,128]{2,1,0:T(8,128)(2,1)} %first_send.1), calls=%async_computation | async-start | bytes 1179648 | tf_op jit(solution)/shard_map/all_to_all | solution.py:372
  27.2 27.1 %copy-start.1 = (f32[2,6,256,128]{3,2,1,0:T(8,128)S(1)}, f32[2,6,256,128]{3,2,1,0:T(8,128)}, u32[]{:S(2)}) copy-start(f32[2,6,256,128]{3,2,1,0:T(8,128)} %param.14) | copy-start | bytes 4718596
  27.2 27.1 %copy-start.4 = (s32[16,16]{1,0:T(8,128)S(1)}, s32[16,16]{1,0:T(8,128)}, u32[]{:S(2)}) copy-start(s32[16,16]{1,0:T(8,128)} %plane_ref.3) | copy-start | bytes 3076
  27.2 27.1 %copy-start.6 = (s32[16,16]{1,0:T(8,128)S(1)}, s32[16,16]{1,0:T(8,128)}, u32[]{:S(2)}) copy-start(s32[16,16]{1,0:T(8,128)} %row_ref.3) | copy-start | bytes 3076
  27.3 27.1 %copy-start.8 = (s32[16,16]{1,0:T(8,128)S(1)}, s32[16,16]{1,0:T(8,128)}, u32[]{:S(2)}) copy-start(s32[16,16]{1,0:T(8,128)} %cover_ref.3) | copy-start | bytes 3076
  30.6 0.7 copy-start.9
  31.3 23.0 %copy-start.10 = (f32[6]{0:T(128)S(1)}, f32[6]{0:T(128)}, u32[]{:S(2)}) copy-start(f32[6]{0:T(128)} %step_ref.3) | copy-start | bytes 76
  31.3 23.0 %copy-start.11 = (s32[2]{0:T(128)S(1)}, s32[2]{0:T(128)}, u32[]{:S(2)}) copy-start(s32[2]{0:T(128)} %lo_ref.3) | copy-start | bytes 28
  31.3 23.0 %copy-start.12 = (s32[2]{0:T(128)S(1)}, s32[2]{0:T(128)}, u32[]{:S(2)}) copy-start(s32[2]{0:T(128)} %hi_ref.3) | copy-start | bytes 28

commit v8 on v7

--- a/solution.py
+++ b/solution.py
@@ -22,8 +22,12 @@
 hbm = lambda: pl.BlockSpec(memory_space=pltpu.HBM)
 
 
-def params():
-    return pltpu.CompilerParams(vmem_limit_bytes=VMEM_BYTES)
+def params(share=1.0):
+    return pltpu.CompilerParams(vmem_limit_bytes=int(share * VMEM_BYTES))
+
+
+def table_rows(pieces):
+    return range(2 * pieces, 2 * pieces + 7)
 
 
 def aligned(rows):
@@ -123,31 +127,17 @@
         out_ref[d, rows_each:, :] = bank
 
 
-def update_kernel(
-    bands,
-    tile_rows,
-    height,
-    rows_each,
-    last,
-    plane_ref,
-    row_ref,
-    cover_ref,
-    step_ref,
-    lo_ref,
-    hi_ref,
-    returned_ref,
-    model_ref,
-    *rest,
-):
+def update_kernel(pieces, bands, tile_rows, height, last, table_ref, factor_ref, returned_ref, model_ref, *rest):
     if last:
-        new_ref, back_ref, scale_ref, x_ref, saved, *more_refs = rest
+        new_ref, back_ref, x_ref, saved, *more_refs = rest
     else:
-        x_ref, out_ref, back_ref, scale_ref, packed_ref, *more_refs = rest
-    peers, capacity = plane_ref.shape
+        x_ref, out_ref, back_ref, packed_ref, *more_refs = rest
+    _, _, _, first_row, cover_row, sent_row, foot_row = table_rows(pieces)
+    peers, rows_each, _ = returned_ref.shape
+    capacity = 2 * rows_each // height
     total = x_ref.shape[0] - height
     planes = total // tile_rows
-    for p in range(planes):
-        scale_ref[p] = step_ref[p % bands]
+    tiles = planes // bands
     x_ref[:total, :] = model_ref[:total, :]
     for ref in more_refs:
         ref[...] = jnp.zeros(ref.shape, F32)
@@ -158,16 +148,13 @@
     sums = [x_ref, *more_refs]
 
     def some_peers(step, _):
-        at = [(step * len(sums) + n) * rows_each for n in range(len(sums))]
         for c in range(capacity):
             for n, ref in enumerate(sums):
-                d = step * len(sums) + n
-                p = jnp.maximum(plane_ref[d, c], 0)
-                here = pl.ds(p * tile_rows + row_ref[d, c], height)
-                cover = cover_ref[d, c]
-                piece = jnp.where(place < cover, back_ref[pl.ds(at[n], height), :], 0.0)
-                ref[here, :] = ref[here, :] - scale_ref[p] * piece
-                at[n] = at[n] + cover
+                slot = (step * len(sums) + n) * capacity + c
+                here = pl.ds(table_ref[first_row, slot], height)
+                piece = back_ref[pl.ds(table_ref[sent_row, slot], height), :]
+                piece = jnp.where(place < table_ref[cover_row, slot], piece, 0.0)
+                ref[here, :] = ref[here, :] - factor_ref[1, slot] * piece
         return 0
 
     lax.fori_loop(0, peers // len(sums), some_peers, 0)
@@ -175,7 +162,7 @@
     pos = lax.broadcasted_iota(I32, (tile_rows, LANES), 0)
     saves = []
     for p in range(planes):
-        inside = (pos >= lo_ref[p // bands]) & (pos < hi_ref[p // bands])
+        inside = (pos >= table_ref[foot_row, p // bands]) & (pos < table_ref[foot_row, tiles + p // bands])
         here = slice(p * tile_rows, (p + 1) * tile_rows)
         new = sum((ref[here, :] for ref in more_refs), x_ref[here, :])
         x_ref[here, :] = jnp.where(inside, jnp.maximum(new, 0.0), 0.0)
@@ -184,58 +171,98 @@
             saves.append(pltpu.make_async_copy(x_ref.at[rows, :], new_ref.at[rows, :], saved.at[p]))
             saves[-1].start()
     if not last:
-        pack_slots(plane_ref, row_ref, cover_ref, tile_rows, height, rows_each, x_ref, packed_ref)
+
+        def pack(slot, _):
+            piece = x_ref[pl.ds(table_ref[first_row, slot], height), :]
+            packed_ref[pl.ds(table_ref[sent_row, slot], height), :] = piece
+            return 0
+
+        lax.fori_loop(0, peers * capacity, pack, 0, unroll=16)
         for d in range(peers):
             out_ref[d, :, :] = packed_ref[d * rows_each : (d + 1) * rows_each, :].astype(BF16)
     for save in saves:
         save.wait()
 
 
-def tables_kernel(capacity, height, rows_each, slot_ref, start_ref, stop_ref, table_ref, length_ref):
-    exposures, pieces = slot_ref.shape
-    slots = length_ref.shape[0]
-    stamp_row, return_row = 2 * pieces, 2 * pieces + 1
+def tables_kernel(
+    tile_rows,
+    bands,
+    height,
+    rows_each,
+    slot_ref,
+    start_ref,
+    stop_ref,
+    batch_ref,
+    weight_ref,
+    plane_ref,
+    row_ref,
+    cover_ref,
+    step_ref,
+    lo_ref,
+    hi_ref,
+    table_ref,
+    factor_ref,
+    length_ref,
+    scale_ref,
+):
+    pieces, exposures = slot_ref.shape
+    peers, capacity = plane_ref.shape
+    slots = peers * capacity
+    batch_row, stamp_row, return_row, first_row, cover_row, sent_row, foot_row = table_rows(pieces)
 
     def clear(s, _):
         length_ref[s] = 0
         table_ref[stamp_row, s] = 0
         return 0
 
-    lax.fori_loop(0, slots, clear, 0, unroll=8)
+    lax.fori_loop(0, slots, clear, 0, unroll=16)
+    for p in range(scale_ref.shape[0]):
+        scale_ref[p] = step_ref[p % bands]
+    tiles = lo_ref.shape[0]
+    for t in range(tiles):
+        table_ref[foot_row, t] = lo_ref[t]
+        table_ref[foot_row, tiles + t] = hi_ref[t]
 
     def measure(e, _):
         for k in range(pieces):
-            s = slot_ref[e, k]
-
-            @pl.when(s >= 0)
-            def _():
-                length_ref[s] = stop_ref[e, k] - start_ref[e, k]
-                table_ref[stamp_row, s] = e * height + start_ref[e, k]
-
-        return 0
-
-    lax.fori_loop(0, exposures, measure, 0, unroll=2)
+            s = slot_ref[k, e]
+            s = jnp.where(s >= 0, s, slots)
+            length_ref[s] = stop_ref[k, e] - start_ref[k, e]
+            table_ref[stamp_row, s] = e * height + start_ref[k, e]
+        table_ref[batch_row, e] = batch_ref[e]
+        factor_ref[0, e] = weight_ref[e]
+        return 0
+
+    lax.fori_loop(0, exposures, measure, 0, unroll=8)
 
     def lay(o, _):
-        at = o * rows_each
+        at = sent = o * rows_each
         for c in range(capacity):
             s = o * capacity + c
             table_ref[return_row, s] = at
             at = at + length_ref[s]
-        return 0
-
-    lax.fori_loop(0, slots // capacity, lay, 0)
+            p = jnp.maximum(plane_ref[o, c], 0)
+            table_ref[first_row, s] = p * tile_rows + row_ref[o, c]
+            factor_ref[1, s] = scale_ref[p]
+            cover = cover_ref[o, c]
+            table_ref[cover_row, s] = cover
+            table_ref[sent_row, s] = sent
+            sent = sent + cover
+        return 0
+
+    lax.fori_loop(0, peers, lay, 0)
 
     def point(e, _):
         for k in range(pieces):
-            s = slot_ref[e, k]
+            s = slot_ref[k, e]
             live = s >= 0
             begin = table_ref[return_row, jnp.maximum(s, 0)]
-            table_ref[2 * k, e] = jnp.where(live, height + begin - start_ref[e, k], 0)
-            table_ref[2 * k + 1, e] = jnp.where(live, start_ref[e, k], height)
-        return 0
-
-    lax.fori_loop(0, exposures, point, 0, unroll=2)
+            start = start_ref[k, e]
+            table_ref[2 * k, e] = jnp.where(live, height + begin - start, 0)
+            table_ref[2 * k + 1, e] = jnp.where(live, start, height)
+        return 0
+
+    lax.fori_loop(0, exposures, point, 0, unroll=8)
 
 
 def blur_kernel(
@@ -243,9 +270,8 @@
     pieces,
     batches_each,
     last,
-    table_in_ref,
-    weight_ref,
-    batch_ref,
+    table_ref,
+    factor_ref,
     arrived_ref,
     bank_in_ref,
     seen_ref,
@@ -257,12 +283,11 @@
         send = pltpu.make_async_copy(residual_ref, residual_out_ref, sent)
     else:
         out_ref, *rest = rest
-    table_ref, sem, rows_ref, bank_ref, result_ref, packed_ref, held_ref, blur_ref, back_ref = rest
-    load = pltpu.make_async_copy(table_in_ref, table_ref, sem)
-    load.start()
+    rows_ref, bank_ref, result_ref, packed_ref, held_ref, blur_ref, back_ref = rest
+    batch_row, stamp_row, return_row = table_rows(pieces)[:3]
     peers, rows_each, _ = out_ref.shape
     extra = bank_in_ref.shape[1] - rows_each
-    exposures = batch_ref.shape[0]
+    exposures = seen_ref.shape[0]
     slots = peers * (2 * rows_each // height)
     abreast = max(n for n in (1, 2, 4, 8, 16, 32) if exposures % n == 0)
     place = lax.broadcasted_iota(I32, (height, LANES), 0)
@@ -298,7 +323,7 @@
             e = s * abreast + q
             here = pl.ds(e * height, height)
             result_ref[here, :] = jnp.dot(
-                back_ref[batch_ref[e]], shifted(held_ref[here, :]), preferred_element_type=F32
+                back_ref[table_ref[batch_row, e]], shifted(held_ref[here, :]), preferred_element_type=F32
             )
 
     def blur(s):
@@ -309,16 +334,15 @@
                 piece = rows_ref[pl.ds(table_ref[2 * k, e], height), :]
                 stamp = jnp.where(place >= table_ref[2 * k + 1, e], piece, stamp)
             predicted = jnp.dot(
-                blur_ref[batch_ref[e]], shifted(stamp.astype(BF16)), preferred_element_type=F32
+                blur_ref[table_ref[batch_row, e]], shifted(stamp.astype(BF16)), preferred_element_type=F32
             )
-            residual = weight_ref[e] * (predicted - seen_ref[e].astype(F32))
+            residual = factor_ref[0, e] * (predicted - seen_ref[e].astype(F32))
             if last:
                 residual_ref[e] = residual
             held_ref[pl.ds(e * height, height), :] = residual.astype(BF16)
 
     steps = exposures // abreast
 
-    load.wait()
     for s in range(steps + 1):
         if s > 0:
             correlate(s - 1)
@@ -328,9 +352,7 @@
         send.start()
 
     def move(s, _):
-        packed_ref[pl.ds(table_ref[2 * pieces + 1, s], height), :] = result_ref[
-            pl.ds(table_ref[2 * pieces, s], height), :
-        ]
+        packed_ref[pl.ds(table_ref[return_row, s], height), :] = result_ref[pl.ds(table_ref[stamp_row, s], height), :]
         return 0
 
     lax.fori_loop(0, slots, move, 0, unroll=16)
@@ -386,19 +408,37 @@
             pltpu.VMEM((extra, columns), F32),
             pltpu.SemaphoreType.DMA((5,)),
         ],
-        compiler_params=params(),
+        compiler_params=params(2.5),
         name="first_send",
     )(send_plane, send_row, send_cover, psf_taps, x)
     arrived = swap(outbound)
-    table = pl.pallas_call(
-        functools.partial(tables_kernel, capacity, height, rows_each),
-        out_shape=jax.ShapeDtypeStruct((2 * pieces + 2, max(count, peers * capacity)), I32),
-        in_specs=[smem(), smem(), smem()],
-        out_specs=smem(),
-        scratch_shapes=[pltpu.SMEM((peers * capacity,), I32)],
+    slots = peers * capacity
+    wide = max(count, slots + 1)
+    table, factors = pl.pallas_call(
+        functools.partial(tables_kernel, tile_rows, bands, height, rows_each),
+        out_shape=(
+            jax.ShapeDtypeStruct((table_rows(pieces).stop, wide), I32),
+            jax.ShapeDtypeStruct((2, wide), F32),
+        ),
+        in_specs=[smem()] * 11,
+        out_specs=(smem(), smem()),
+        scratch_shapes=[pltpu.SMEM((slots + 1,), I32), pltpu.SMEM((tile_count * bands,), F32)],
+        compiler_params=params(),
         cost_estimate=pl.CostEstimate(flops=4_000_000, bytes_accessed=8_000_000, transcendentals=0),
         name="tables",
-    )(use_slot, use_start, use_stop)
+    )(
+        use_slot.T,
+        use_start.T,
+        use_stop.T,
+        exp_batch,
+        inv_var,
+        send_plane,
+        send_row,
+        send_cover,
+        step_size,
+        foot_lo,
+        foot_hi,
+    )
     with_bank = arrived
     for sweep in range(ITERS):
         last = sweep == ITERS - 1
@@ -406,18 +446,9 @@
         outs = pl.pallas_call(
             functools.partial(blur_kernel, height, pieces, batches_each, last),
             out_shape=(rows_shape, jax.ShapeDtypeStruct(exposures.shape, F32)) if last else rows_shape,
-            in_specs=[
-                hbm(),
-                smem(),
-                smem(),
-                vmem(),
-                vmem(),
-                vmem(),
-            ],
+            in_specs=[smem()] * 2 + [vmem()] * 3,
             out_specs=(vmem(), hbm()) if last else vmem(),
             scratch_shapes=[
-                pltpu.SMEM(table.shape, I32),
-                pltpu.SemaphoreType.DMA,
                 pltpu.VMEM((peers * rows_each + 2 * height, columns), F32),
                 pltpu.VMEM((peers * extra, columns), F32),
                 pltpu.VMEM((count * height + height, columns), F32),
@@ -429,28 +460,28 @@
             + [pltpu.VMEM(exposures.shape, F32), pltpu.SemaphoreType.DMA] * last,
             compiler_params=params(),
             name="blur",
-        )(table, inv_var, exp_batch, arrived, with_bank, exposures)
+        )(table, factors, arrived, with_bank, exposures)
         outgoing = outs[0] if last else outs
         returned = swap(outgoing)
         new_shape = jax.ShapeDtypeStruct((total, columns), F32)
         padded = (total + height, columns)
-        scratch = [pltpu.VMEM((peers * rows_each + height, columns), F32), pltpu.SMEM((tile_count * bands,), F32)]
+        scratch = [pltpu.VMEM((peers * rows_each + height, columns), F32)]
         if last:
             scratch += [pltpu.VMEM(padded, F32), pltpu.SemaphoreType.DMA((tile_count * bands,))]
         else:
             scratch.append(pltpu.VMEM((peers * rows_each + height, columns), F32))
         sums = max(n for n in (1, 2, 4) if peers % n == 0)
         res = pl.pallas_call(
-            functools.partial(update_kernel, bands, tile_rows, height, rows_each, last),
+            functools.partial(update_kernel, pieces, bands, tile_rows, height, last),
             out_shape=jax.ShapeDtypeStruct((total, columns), F32)
             if last
             else (jax.ShapeDtypeStruct(padded, F32), rows_shape),
-            in_specs=[smem()] * 6 + [vmem(), vmem()],
+            in_specs=[smem()] * 2 + [vmem(), vmem()],
             out_specs=hbm() if last else (vmem(), vmem()),
             scratch_shapes=scratch + [pltpu.VMEM(padded, F32)] * (sums - 1),
             compiler_params=params(),
             name="update",
-        )(send_plane, send_row, send_cover, step_size, foot_lo, foot_hi, returned, x)
+        )(table, factors, returned, x)
         if last:
             x = res
         else:

time: 103 us -> 100 us (0.971)
  local copies, waits for them, and re-layouts: 7.14 us -> 0.05 us
  waiting for transfers between devices: 3.32 us -> 6.85 us
    unnamed x41 -> x26, local copies, waits for them, and re-layouts: 7.14 us -> 0.05 us
    all_to_all x1, waiting for transfers between devices: 3.32 us -> 6.85 us  [swap(): return lax.all_to_all(a, 'sky', split_axis=0, concat_axis=0, tiled=True)]
  transfers between devices with their start and end apart: 1 -> 1, of which waited for: 1 -> 1; matrix products, arithmetic and copies ran while one was open for 2% -> 0% of each run, Pallas kernels for 10% -> 9%
where the time goes in v8:
time: 100 us; the launch traced here: 99.7 us
  blocking collectives  55.4 us (55%)
  Pallas kernels  29.1 us (29%)
  starting transfers between devices  7.37 us (7%)
  waiting for transfers between devices  6.85 us (7%)
    all_to_all x3, blocking collectives, swap(): return lax.all_to_all(a, 'sky', split_axis=0, concat_axis=0, tiled=True)  55.4 us
    pallas_call x2, Pallas kernels, body(): pl.pallas_call(functools.partial(blur_kernel, height, pieces, batches_eac...  9.02 us
    pallas_call x1, Pallas kernels, body(): pl.pallas_call(functools.partial(tables_kernel, tile_rows, bands, height,...  8.58 us
    pallas_call x2, Pallas kernels, body(): pl.pallas_call(functools.partial(update_kernel, pieces, bands, tile_rows,...  8.2 us
    all_to_all x1, starting transfers between devices, swap(): return lax.all_to_all(a, 'sky', split_axis=0, concat_axis=0, tiled=True)  7.37 us
    all_to_all x1, waiting for transfers between devices, swap(): return lax.all_to_all(a, 'sky', split_axis=0, concat_axis=0, tiled=True)  6.85 us
    pallas_call x1, Pallas kernels, body(): pl.pallas_call(functools.partial(first_send_kernel, tile_rows, height, ro...  3.29 us
  transfers between devices with their start and end apart: 1, of which 1 were waited for; matrix products, arithmetic and copies ran while one was open for 0% of the time, Pallas kernels for 9%

profile of v8, /device:TPU:0, one launch (start us, length us, event | category | flops | bytes accessed | tf_op | source)
XLA Modules:
  0.0 99.7 jit_solution(1185182519718386039)
XLA Ops:
  0.6 0.0 copy-start.2
  0.6 0.0 copy-start.3
  0.7 0.0 copy-start.4
  0.7 0.0 copy-start.5
  0.7 0.0 copy-start.6
  0.7 0.0 copy-start.7
  0.7 0.0 copy-start.8
  0.7 0.0 copy-start.9
  0.7 0.0 copy-start.10
  0.7 0.0 copy-start.11
  0.7 0.0 copy-start.12
  0.7 0.0 copy-start.1
  0.8 3.3 %first_send.1 = bf16[16,144,128]{2,1,0:T(8,128)(2,1)} custom-call(s32[16,16]{1,0:T(8,128)} %plane_in_ref.1, s32[16,16]{1,0:T(8,128)} %row_in_ref.1, s32[16,16]{1,0:T(8,128)} %cover_in_ref.1, f32[2,56]{1,0:T(2,128)} %taps_in_ref.1, f32[3072,128]{1,0:T(8,128)} %bitcast.5), custom_call_target="tpu_custom_call" | custom-call | tf_op jit(solution)/shard_map/first_send/pallas_call | solution.py:396
  4.1 7.4 %all-to-all-start = ((bf16[16,144,128]{2,1,0:T(8,128)(2,1)}), bf16[16,144,128]{2,1,0:T(8,128)(2,1)S(1)}, u32[]{:S(2)}, u32[]{:S(2)}) async-start(bf16[16,144,128]{2,1,0:T(8,128)(2,1)} %first_send.1), calls=%async_computation | async-start | bytes 1179648 | tf_op jit(solution)/shard_map/all_to_all | solution.py:394
  11.4 0.0 copy-done.2
  11.4 0.0 copy-done.3
  11.5 0.0 copy-done.4
  11.5 0.0 copy-done.5
  11.5 0.0 copy-done.6
  11.5 0.0 copy-done.7
  11.5 0.0 copy-done.8
  11.5 0.0 copy-done.9
  11.5 0.0 copy-done.10
  11.5 0.0 copy-done.11
  11.5 0.0 copy-done.12
  11.5 8.6 %tables.1 = (s32[11,257]{1,0:T(8,128)S(1)}, f32[2,257]{1,0:T(2,128)S(1)}) custom-call(s32[2,128]{1,0:T(2,128)S(1)} %bitcast.7, s32[2,128]{1,0:T(2,128)S(1)} %bitcast.8, s32[2,128]{1,0:T(2,128)S(1)} %bitcast.9, s32[128]{0:T(128)S(1)} %copy-done.8, f32[128]{0:T(128)S(1)} %copy-done.9, s32[16,16]{1,0:T(8,128)S(1)} %copy-done.2, s32[16,16]{1,0:T(8,128)S(1)} %copy-done.3, ...), custom_call_target="tpu_custom_call" | custom-call | flops 4000000 | bytes 8000000 | tf_op jit(solution)/shard_map/tables/pallas_call | solution.py:417
  20.1 6.8 %all-to-all-done.arrived_ref.bank_in_ref = bf16[16,144,128]{2,1,0:T(8,128)(2,1)S(1)} async-done(((bf16[16,144,128]{2,1,0:T(8,128)(2,1)}), bf16[16,144,128]{2,1,0:T(8,128)(2,1)S(1)}, u32[]{:S(2)}, u32[]{:S(2)}) %all-to-all-start) | async-done | bytes 589856 | tf_op jit(solution)/shard_map/all_to_all | solution.py:394
  27.0 0.0 copy-done.1
  27.0 0.0 copy-start
  27.0 4.5 %blur.2 = bf16[16,128,128]{2,1,0:T(8,128)(2,1)S(1)} custom-call(s32[11,257]{1,0:T(8,128)S(1)} %get-tuple-element.8.table_ref, f32[2,257]{1,0:T(2,128)S(1)} %get-tuple-element.9.factor_ref, bf16[16,144,128]{2,1,0:T(8,128)(2,1)S(1)} %all-to-all-done.arrived_ref.bank_in_ref, bf16[16,144,128]{2,1,0:T(8,128)(2,1)S(1)} %all-to-all-done.arrived_ref.bank_in_ref, ...), custom_call_target="tpu_custom_call" | custom-call | tf_op jit(solution)/shard_map/blur/pallas_call | solution.py:446
  31.5 18.7 %all_to_all.20.returned_ref = bf16[16,128,128]{2,1,0:T(8,128)(2,1)S(1)} all-to-all(bf16[16,128,128]{2,1,0:T(8,128)(2,1)S(1)} %blur.2), channel_id=1, replica_groups=mesh['groups'=2,'sky'=16] {'sky'}, dimensions={0} | all-to-all | bytes 1048576 | tf_op jit(solution)/shard_map/all_to_all | solution.py:394
  50.2 0.0 copy-done
  50.2 4.2 %update.2 = (f32[3088,128]{1,0:T(8,128)S(1)}, bf16[16,128,128]{2,1,0:T(8,128)(2,1)S(1)}) custom-call(s32[11,257]{1,0:T(8,128)S(1)} %get-tuple-element.8.table_ref, f32[2,257]{1,0:T(2,128)S(1)} %get-tuple-element.9.factor_ref, bf16[16,128,128]{2,1,0:T(8,128)(2,1)S(1)} %all_to_all.20.returned_ref, f32[3072,128]{1,0:T(8,128)S(1)} %bitcast.6), custom_call_target="tpu_custom_call" | custom-call | tf_op jit(solution)/shard_map/update/pallas_call | solution.py:474
  54.4 18.4 %all_to_all.21.arrived_ref = bf16[16,128,128]{2,1,0:T(8,128)(2,1)S(1)} all-to-all(bf16[16,128,128]{2,1,0:T(8,128)(2,1)S(1)} %get-tuple-element.10), channel_id=1, replica_groups=mesh['groups'=2,'sky'=16] {'sky'}, dimensions={0} | all-to-all | bytes 1048576 | tf_op jit(solution)/shard_map/all_to_all | solution.py:394
  72.8 4.5 %blur.3 = (bf16[16,128,128]{2,1,0:T(8,128)(2,1)S(1)}, f32[128,16,128]{2,1,0:T(8,128)}) custom-call(s32[11,257]{1,0:T(8,128)S(1)} %get-tuple-element.8.table_ref, f32[2,257]{1,0:T(2,128)S(1)} %get-tuple-element.9.factor_ref, bf16[16,128,128]{2,1,0:T(8,128)(2,1)S(1)} %all_to_all.21.arrived_ref, bf16[16,144,128]{2,1,0:T(8,128)(2,1)S(1)} %all-to-all-done.arrived_ref.bank_in_ref, ...), custom_call_target="tpu_custom_call" | custom-call | tf_op jit(solution)/shard_map/blur/pallas_call | solution.py:446
  77.3 18.4 %all_to_all.22.returned_ref = bf16[16,128,128]{2,1,0:T(8,128)(2,1)S(1)} all-to-all(bf16[16,128,128]{2,1,0:T(8,128)(2,1)S(1)} %get-tuple-element.11), channel_id=1, replica_groups=mesh['groups'=2,'sky'=16] {'sky'}, dimensions={0} | all-to-all | bytes 1048576 | tf_op jit(solution)/shard_map/all_to_all | solution.py:394
  95.7 4.0 %update.3 = f32[3072,128]{1,0:T(8,128)} custom-call(s32[11,257]{1,0:T(8,128)S(1)} %get-tuple-element.8.table_ref, f32[2,257]{1,0:T(2,128)S(1)} %get-tuple-element.9.factor_ref, bf16[16,128,128]{2,1,0:T(8,128)(2,1)S(1)} %all_to_all.22.returned_ref, f32[3088,128]{1,0:T(8,128)S(1)} %get-tuple-element.12.model_ref), custom_call_target="tpu_custom_call" | custom-call | tf_op jit(solution)/shard_map/update/pallas_call | solution.py:474
Async XLA Ops:
  0.6 10.8 %copy-start.2 = (s32[16,16]{1,0:T(8,128)S(1)}, s32[16,16]{1,0:T(8,128)}, u32[]{:S(2)}) copy-start(s32[16,16]{1,0:T(8,128)} %plane_in_ref.1) | copy-start | bytes 3076
  0.6 10.8 %copy-start.3 = (s32[16,16]{1,0:T(8,128)S(1)}, s32[16,16]{1,0:T(8,128)}, u32[]{:S(2)}) copy-start(s32[16,16]{1,0:T(8,128)} %row_in_ref.1) | copy-start | bytes 3076
  0.7 10.8 %copy-start.4 = (s32[16,16]{1,0:T(8,128)S(1)}, s32[16,16]{1,0:T(8,128)}, u32[]{:S(2)}) copy-start(s32[16,16]{1,0:T(8,128)} %cover_in_ref.1) | copy-start | bytes 3076
  0.7 10.8 %copy-start.5 = (s32[128,2]{0,1:T(2,128)S(1)}, s32[128,2]{0,1:T(2,128)}, u32[]{:S(2)}) copy-start(s32[128,2]{0,1:T(2,128)} %param.23) | copy-start | bytes 3076
  0.7 10.8 %copy-start.6 = (s32[128,2]{0,1:T(2,128)S(1)}, s32[128,2]{0,1:T(2,128)}, u32[]{:S(2)}) copy-start(s32[128,2]{0,1:T(2,128)} %param.24) | copy-start | bytes 3076
  0.7 10.8 %copy-start.7 = (s32[128,2]{0,1:T(2,128)S(1)}, s32[128,2]{0,1:T(2,128)}, u32[]{:S(2)}) copy-start(s32[128,2]{0,1:T(2,128)} %param.25) | copy-start | bytes 3076
  0.7 10.8 %copy-start.8 = (s32[128]{0:T(128)S(1)}, s32[128]{0:T(128)}, u32[]{:S(2)}) copy-start(s32[128]{0:T(128)} %batch_ref.1) | copy-start | bytes 1540
  0.7 10.8 %copy-start.9 = (f32[128]{0:T(128)S(1)}, f32[128]{0:T(128)}, u32[]{:S(2)}) copy-start(f32[128]{0:T(128)} %weight_ref.1) | copy-start | bytes 1540
  0.7 10.8 %copy-start.10 = (f32[6]{0:T(128)S(1)}, f32[6]{0:T(128)}, u32[]{:S(2)}) copy-start(f32[6]{0:T(128)} %step_ref.1) | copy-start | bytes 76
  0.7 10.8 %copy-start.11 = (s32[2]{0:T(128)S(1)}, s32[2]{0:T(128)}, u32[]{:S(2)}) copy-start(s32[2]{0:T(128)} %lo_ref.1) | copy-start | bytes 28
  0.7 10.8 %copy-start.12 = (s32[2]{0:T(128)S(1)}, s32[2]{0:T(128)}, u32[]{:S(2)}) copy-start(s32[2]{0:T(128)} %hi_ref.1) | copy-start | bytes 28
  0.7 26.2 %copy-start.1 = (bf16[128,16,128]{2,1,0:T(8,128)(2,1)S(1)}, bf16[128,16,128]{2,1,0:T(8,128)(2,1)}, u32[]{:S(2)}) copy-start(bf16[128,16,128]{2,1,0:T(8,128)(2,1)} %seen_ref.3) | copy-start | bytes 1572868
  4.1 22.9 %all-to-all-start = ((bf16[16,144,128]{2,1,0:T(8,128)(2,1)}), bf16[16,144,128]{2,1,0:T(8,128)(2,1)S(1)}, u32[]{:S(2)}, u32[]{:S(2)}) async-start(bf16[16,144,128]{2,1,0:T(8,128)(2,1)} %first_send.1), calls=%async_computation | async-start | bytes 1179648 | tf_op jit(solution)/shard_map/all_to_all | solution.py:394
  27.0 23.2 %copy-start = (f32[2,6,256,128]{3,2,1,0:T(8,128)S(1)}, f32[2,6,256,128]{3,2,1,0:T(8,128)}, u32[]{:S(2)}) copy-start(f32[2,6,256,128]{3,2,1,0:T(8,128)} %param.14) | copy-start | bytes 4718596

commit v9 on v8

--- a/solution.py
+++ b/solution.py
@@ -26,12 +26,25 @@
     return pltpu.CompilerParams(vmem_limit_bytes=int(share * VMEM_BYTES))
 
 
-def table_rows(pieces):
-    return range(2 * pieces, 2 * pieces + 7)
+SHIFT = 16
+PLACE = 13
+
+
+def low(word):
+    return word & ((1 << SHIFT) - 1)
+
+
+def high(word):
+    return lax.shift_right_logical(word, SHIFT)
 
 
 def aligned(rows):
     return -(-rows // 16) * 16
+
+
+def first_and_sent(word):
+    mask = (1 << PLACE) - 1
+    return word & mask, lax.shift_right_logical(word, PLACE) & mask
 
 
 def pack_slots(plane_ref, row_ref, cover_ref, tile_rows, height, rows_each, x_ref, packed_ref):
@@ -127,14 +140,14 @@
         out_ref[d, rows_each:, :] = bank
 
 
-def update_kernel(pieces, bands, tile_rows, height, last, table_ref, factor_ref, returned_ref, model_ref, *rest):
+def update_kernel(bands, tile_rows, height, last, table_ref, factor_ref, returned_ref, model_ref, *rest):
     if last:
         new_ref, back_ref, x_ref, saved, *more_refs = rest
     else:
         x_ref, out_ref, back_ref, packed_ref, *more_refs = rest
-    _, _, _, first_row, cover_row, sent_row, foot_row = table_rows(pieces)
     peers, rows_each, _ = returned_ref.shape
     capacity = 2 * rows_each // height
+    slots = peers * capacity
     total = x_ref.shape[0] - height
     planes = total // tile_rows
     tiles = planes // bands
@@ -151,10 +164,12 @@
         for c in range(capacity):
             for n, ref in enumerate(sums):
                 slot = (step * len(sums) + n) * capacity + c
-                here = pl.ds(table_ref[first_row, slot], height)
-                piece = back_ref[pl.ds(table_ref[sent_row, slot], height), :]
-                piece = jnp.where(place < table_ref[cover_row, slot], piece, 0.0)
-                ref[here, :] = ref[here, :] - factor_ref[1, slot] * piece
+                word = table_ref[slot]
+                first, sent = first_and_sent(word)
+                here = pl.ds(first, height)
+                cover = lax.shift_right_logical(word, 2 * PLACE)
+                piece = jnp.where(place < cover, back_ref[pl.ds(sent, height), :], 0.0)
+                ref[here, :] = ref[here, :] - factor_ref[slot] * piece
         return 0
 
     lax.fori_loop(0, peers // len(sums), some_peers, 0)
@@ -162,7 +177,7 @@
     pos = lax.broadcasted_iota(I32, (tile_rows, LANES), 0)
     saves = []
     for p in range(planes):
-        inside = (pos >= table_ref[foot_row, p // bands]) & (pos < table_ref[foot_row, tiles + p // bands])
+        inside = (pos >= table_ref[slots + p // bands]) & (pos < table_ref[slots + tiles + p // bands])
         here = slice(p * tile_rows, (p + 1) * tile_rows)
         new = sum((ref[here, :] for ref in more_refs), x_ref[here, :])
         x_ref[here, :] = jnp.where(inside, jnp.maximum(new, 0.0), 0.0)
@@ -173,11 +188,11 @@
     if not last:
 
         def pack(slot, _):
-            piece = x_ref[pl.ds(table_ref[first_row, slot], height), :]
-            packed_ref[pl.ds(table_ref[sent_row, slot], height), :] = piece
+            first, sent = first_and_sent(table_ref[slot])
+            packed_ref[pl.ds(sent, height), :] = x_ref[pl.ds(first, height), :]
             return 0
 
-        lax.fori_loop(0, peers * capacity, pack, 0, unroll=16)
+        lax.fori_loop(0, slots, pack, 0, unroll=16)
         for d in range(peers):
             out_ref[d, :, :] = packed_ref[d * rows_each : (d + 1) * rows_each, :].astype(BF16)
     for save in saves:
@@ -193,26 +208,27 @@
     start_ref,
     stop_ref,
     batch_ref,
-    weight_ref,
     plane_ref,
     row_ref,
     cover_ref,
     step_ref,
     lo_ref,
     hi_ref,
-    table_ref,
+    blur_ref,
+    update_ref,
     factor_ref,
     length_ref,
+    stamp_ref,
+    begin_ref,
     scale_ref,
 ):
     pieces, exposures = slot_ref.shape
     peers, capacity = plane_ref.shape
     slots = peers * capacity
-    batch_row, stamp_row, return_row, first_row, cover_row, sent_row, foot_row = table_rows(pieces)
 
     def clear(s, _):
         length_ref[s] = 0
-        table_ref[stamp_row, s] = 0
+        stamp_ref[s] = 0
         return 0
 
     lax.fori_loop(0, slots, clear, 0, unroll=16)
@@ -220,17 +236,15 @@
         scale_ref[p] = step_ref[p % bands]
     tiles = lo_ref.shape[0]
     for t in range(tiles):
-        table_ref[foot_row, t] = lo_ref[t]
-        table_ref[foot_row, tiles + t] = hi_ref[t]
+        update_ref[slots + t] = lo_ref[t]
+        update_ref[slots + tiles + t] = hi_ref[t]
 
     def measure(e, _):
         for k in range(pieces):
             s = slot_ref[k, e]
             s = jnp.where(s >= 0, s, slots)
             length_ref[s] = stop_ref[k, e] - start_ref[k, e]
-            table_ref[stamp_row, s] = e * height + start_ref[k, e]
-        table_ref[batch_row, e] = batch_ref[e]
-        factor_ref[0, e] = weight_ref[e]
+            stamp_ref[s] = e * height + start_ref[k, e]
         return 0
 
     lax.fori_loop(0, exposures, measure, 0, unroll=8)
@@ -239,14 +253,13 @@
         at = sent = o * rows_each
         for c in range(capacity):
             s = o * capacity + c
-            table_ref[return_row, s] = at
+            begin_ref[s] = at
+            blur_ref[pieces * exposures + s] = stamp_ref[s] | (at << SHIFT)
             at = at + length_ref[s]
             p = jnp.maximum(plane_ref[o, c], 0)
-            table_ref[first_row, s] = p * tile_rows + row_ref[o, c]
-            factor_ref[1, s] = scale_ref[p]
             cover = cover_ref[o, c]
-            table_ref[cover_row, s] = cover
-            table_ref[sent_row, s] = sent
+            update_ref[s] = (p * tile_rows + row_ref[o, c]) | (sent << PLACE) | (cover << 2 * PLACE)
+            factor_ref[s] = scale_ref[p]
             sent = sent + cover
         return 0
 
@@ -256,10 +269,10 @@
         for k in range(pieces):
             s = slot_ref[k, e]
             live = s >= 0
-            begin = table_ref[return_row, jnp.maximum(s, 0)]
             start = start_ref[k, e]
-            table_ref[2 * k, e] = jnp.where(live, height + begin - start, 0)
-            table_ref[2 * k + 1, e] = jnp.where(live, start, height)
+            begin = jnp.where(live, height + begin_ref[jnp.maximum(s, 0)] - start, 0)
+            above = batch_ref[e] if k == 0 else jnp.where(live, start, height)
+            blur_ref[k * exposures + e] = begin | (above << SHIFT)
         return 0
 
     lax.fori_loop(0, exposures, point, 0, unroll=8)
@@ -271,7 +284,7 @@
     batches_each,
     last,
     table_ref,
-    factor_ref,
+    weight_ref,
     arrived_ref,
     bank_in_ref,
     seen_ref,
@@ -284,7 +297,6 @@
     else:
         out_ref, *rest = rest
     rows_ref, bank_ref, result_ref, packed_ref, held_ref, blur_ref, back_ref = rest
-    batch_row, stamp_row, return_row = table_rows(pieces)[:3]
     peers, rows_each, _ = out_ref.shape
     extra = bank_in_ref.shape[1] - rows_each
     exposures = seen_ref.shape[0]
@@ -323,20 +335,20 @@
             e = s * abreast + q
             here = pl.ds(e * height, height)
             result_ref[here, :] = jnp.dot(
-                back_ref[table_ref[batch_row, e]], shifted(held_ref[here, :]), preferred_element_type=F32
+                back_ref[high(table_ref[e])], shifted(held_ref[here, :]), preferred_element_type=F32
             )
 
     def blur(s):
         for q in range(abreast):
             e = s * abreast + q
-            stamp = rows_ref[pl.ds(table_ref[0, e], height), :]
+            stamp = rows_ref[pl.ds(low(table_ref[e]), height), :]
             for k in range(1, pieces):
-                piece = rows_ref[pl.ds(table_ref[2 * k, e], height), :]
-                stamp = jnp.where(place >= table_ref[2 * k + 1, e], piece, stamp)
+                word = table_ref[k * exposures + e]
+                stamp = jnp.where(place >= high(word), rows_ref[pl.ds(low(word), height), :], stamp)
             predicted = jnp.dot(
-                blur_ref[table_ref[batch_row, e]], shifted(stamp.astype(BF16)), preferred_element_type=F32
+                blur_ref[high(table_ref[e])], shifted(stamp.astype(BF16)), preferred_element_type=F32
             )
-            residual = factor_ref[0, e] * (predicted - seen_ref[e].astype(F32))
+            residual = weight_ref[e] * (predicted - seen_ref[e].astype(F32))
             if last:
                 residual_ref[e] = residual
             held_ref[pl.ds(e * height, height), :] = residual.astype(BF16)
@@ -352,7 +364,8 @@
         send.start()
 
     def move(s, _):
-        packed_ref[pl.ds(table_ref[return_row, s], height), :] = result_ref[pl.ds(table_ref[stamp_row, s], height), :]
+        word = table_ref[pieces * exposures + s]
+        packed_ref[pl.ds(high(word), height), :] = result_ref[pl.ds(low(word), height), :]
         return 0
 
     lax.fori_loop(0, slots, move, 0, unroll=16)
@@ -413,16 +426,23 @@
     )(send_plane, send_row, send_cover, psf_taps, x)
     arrived = swap(outbound)
     slots = peers * capacity
-    wide = max(count, slots + 1)
-    table, factors = pl.pallas_call(
+    assert max(total, peers * rows_each) < 1 << PLACE and height < 1 << (31 - 2 * PLACE)
+    assert max(count, peers * capacity + 2) * height < 1 << (SHIFT - 1)
+    blur_table, update_table, factors = pl.pallas_call(
         functools.partial(tables_kernel, tile_rows, bands, height, rows_each),
         out_shape=(
-            jax.ShapeDtypeStruct((table_rows(pieces).stop, wide), I32),
-            jax.ShapeDtypeStruct((2, wide), F32),
+            jax.ShapeDtypeStruct((pieces * count + slots,), I32),
+            jax.ShapeDtypeStruct((slots + 2 * tile_count,), I32),
+            jax.ShapeDtypeStruct((slots,), F32),
         ),
-        in_specs=[smem()] * 11,
-        out_specs=(smem(), smem()),
-        scratch_shapes=[pltpu.SMEM((slots + 1,), I32), pltpu.SMEM((tile_count * bands,), F32)],
+        in_specs=[smem()] * 10,
+        out_specs=(smem(), smem(), smem()),
+        scratch_shapes=[
+            pltpu.SMEM((slots + 1,), I32),
+            pltpu.SMEM((slots + 1,), I32),
+            pltpu.SMEM((slots,), I32),
+            pltpu.SMEM((tile_count * bands,), F32),
+        ],
         compiler_params=params(),
         cost_estimate=pl.CostEstimate(flops=4_000_000, bytes_accessed=8_000_000, transcendentals=0),
         name="tables",
@@ -431,7 +451,6 @@
         use_start.T,
         use_stop.T,
         exp_batch,
-        inv_var,
         send_plane,
         send_row,
         send_cover,
@@ -460,7 +479,7 @@
             + [pltpu.VMEM(exposures.shape, F32), pltpu.SemaphoreType.DMA] * last,
             compiler_params=params(),
             name="blur",
-        )(table, factors, arrived, with_bank, exposures)
+        )(blur_table, inv_var, arrived, with_bank, exposures)
         outgoing = outs[0] if last else outs
         returned = swap(outgoing)
         new_shape = jax.ShapeDtypeStruct((total, columns), F32)
@@ -470,9 +489,9 @@
             scratch += [pltpu.VMEM(padded, F32), pltpu.SemaphoreType.DMA((tile_count * bands,))]
         else:
             scratch.append(pltpu.VMEM((peers * rows_each + height, columns), F32))
-        sums = max(n for n in (1, 2, 4) if peers % n == 0)
+        sums = max(n for n in (1, 2, 4 if last else 2) if peers % n == 0)
         res = pl.pallas_call(
-            functools.partial(update_kernel, pieces, bands, tile_rows, height, last),
+            functools.partial(update_kernel, bands, tile_rows, height, last),
             out_shape=jax.ShapeDtypeStruct((total, columns), F32)
             if last
             else (jax.ShapeDtypeStruct(padded, F32), rows_shape),
@@ -481,7 +500,7 @@
             scratch_shapes=scratch + [pltpu.VMEM(padded, F32)] * (sums - 1),
             compiler_params=params(),
             name="update",
-        )(table, factors, returned, x)
+        )(update_table, factors, returned, x)
         if last:
             x = res
         else:

time: 100 us -> 96.1 us (0.961)
  Pallas kernels: 29.1 us -> 23 us
  waiting for transfers between devices: 6.85 us -> 8.98 us
    pallas_call x2, Pallas kernels: 8.2 us -> 5.53 us  [body(): pl.pallas_call(functools.partial(update_kernel, bands, tile_rows, height,...]
    all_to_all x1, waiting for transfers between devices: 6.85 us -> 8.98 us  [swap(): return lax.all_to_all(a, 'sky', split_axis=0, concat_axis=0, tiled=True)]
    pallas_call x1, Pallas kernels: 8.58 us -> 6.46 us  [body(): pl.pallas_call(functools.partial(tables_kernel, tile_rows, bands, height,...]
    pallas_call x2, Pallas kernels: 9.02 us -> 7.73 us  [body(): pl.pallas_call(functools.partial(blur_kernel, height, pieces, batches_eac...]
  transfers between devices with their start and end apart: 1 -> 1, of which waited for: 1 -> 1; matrix products, arithmetic and copies ran while one was open for 0% -> 0% of each run, Pallas kernels for 9% -> 7%
where the time goes in v9:
time: 96.1 us; the launch traced here: 95.7 us
  blocking collectives  55.4 us (58%)
  Pallas kernels  23 us (24%)
  waiting for transfers between devices  8.98 us (9%)
  starting transfers between devices  7.37 us (8%)
    all_to_all x3, blocking collectives, swap(): return lax.all_to_all(a, 'sky', split_axis=0, concat_axis=0, tiled=True)  55.4 us
    all_to_all x1, waiting for transfers between devices, swap(): return lax.all_to_all(a, 'sky', split_axis=0, concat_axis=0, tiled=True)  8.98 us
    pallas_call x2, Pallas kernels, body(): pl.pallas_call(functools.partial(blur_kernel, height, pieces, batches_eac...  7.73 us
    all_to_all x1, starting transfers between devices, swap(): return lax.all_to_all(a, 'sky', split_axis=0, concat_axis=0, tiled=True)  7.37 us
    pallas_call x1, Pallas kernels, body(): pl.pallas_call(functools.partial(tables_kernel, tile_rows, bands, height,...  6.46 us
    pallas_call x2, Pallas kernels, body(): pl.pallas_call(functools.partial(update_kernel, bands, tile_rows, height,...  5.53 us
    pallas_call x1, Pallas kernels, body(): pl.pallas_call(functools.partial(first_send_kernel, tile_rows, height, ro...  3.29 us
  transfers between devices with their start and end apart: 1, of which 1 were waited for; matrix products, arithmetic and copies ran while one was open for 0% of the time, Pallas kernels for 7%

profile of v9, /device:TPU:0, one launch (start us, length us, event | category | flops | bytes accessed | tf_op | source)
XLA Modules:
  0.0 95.7 jit_solution(6246345593318187192)
XLA Ops:
  0.6 0.0 copy-start.2
  0.6 0.0 copy-start.3
  0.7 0.0 copy-start.4
  0.7 0.0 copy-start.6
  0.7 0.0 copy-start.7
  0.7 0.0 copy-start.8
  0.7 0.0 copy-start.9
  0.7 0.0 copy-start.10
  0.7 0.0 copy-start.11
  0.7 0.0 copy-start.12
  0.7 0.0 copy-start.1
  0.7 0.0 copy-start.5
  0.8 3.3 %first_send.1 = bf16[16,144,128]{2,1,0:T(8,128)(2,1)} custom-call(s32[16,16]{1,0:T(8,128)} %plane_in_ref.1, s32[16,16]{1,0:T(8,128)} %row_in_ref.1, s32[16,16]{1,0:T(8,128)} %cover_in_ref.1, f32[2,56]{1,0:T(2,128)} %taps_in_ref.1, f32[3072,128]{1,0:T(8,128)} %bitcast.5), custom_call_target="tpu_custom_call" | custom-call | tf_op jit(solution)/shard_map/first_send/pallas_call | solution.py:409
  4.1 7.4 %all-to-all-start = ((bf16[16,144,128]{2,1,0:T(8,128)(2,1)}), bf16[16,144,128]{2,1,0:T(8,128)(2,1)S(1)}, u32[]{:S(2)}, u32[]{:S(2)}) async-start(bf16[16,144,128]{2,1,0:T(8,128)(2,1)} %first_send.1), calls=%async_computation | async-start | bytes 1179648 | tf_op jit(solution)/shard_map/all_to_all | solution.py:407
  11.4 0.0 copy-done.2
  11.4 0.0 copy-done.3
  11.5 0.0 copy-done.4
  11.5 0.0 copy-done.6
  11.5 0.0 copy-done.7
  11.5 0.0 copy-done.8
  11.5 0.0 copy-done.9
  11.5 0.0 copy-done.10
  11.5 0.0 copy-done.11
  11.5 0.0 copy-done.12
  11.5 6.5 %tables.1 = (s32[512]{0:T(512)S(1)}, s32[260]{0:T(512)S(1)}, f32[256]{0:T(256)S(1)}) custom-call(s32[2,128]{1,0:T(2,128)S(1)} %bitcast.7, s32[2,128]{1,0:T(2,128)S(1)} %bitcast.8, s32[2,128]{1,0:T(2,128)S(1)} %bitcast.9, s32[128]{0:T(128)S(1)} %copy-done.9, s32[16,16]{1,0:T(8,128)S(1)} %copy-done.2, s32[16,16]{1,0:T(8,128)S(1)} %copy-done.3, ...), custom_call_target="tpu_custom_call" | custom-call | flops 4000000 | bytes 8000000 | tf_op jit(solution)/shard_map/tables/pallas_call | solution.py:431
  18.0 9.0 %all-to-all-done.arrived_ref.bank_in_ref = bf16[16,144,128]{2,1,0:T(8,128)(2,1)S(1)} async-done(((bf16[16,144,128]{2,1,0:T(8,128)(2,1)}), bf16[16,144,128]{2,1,0:T(8,128)(2,1)S(1)}, u32[]{:S(2)}, u32[]{:S(2)}) %all-to-all-start) | async-done | bytes 589856 | tf_op jit(solution)/shard_map/all_to_all | solution.py:407
  27.0 0.0 copy-done.1
  27.0 0.0 copy-done.5
  27.0 0.0 copy-start
  27.0 3.8 %blur.2 = bf16[16,128,128]{2,1,0:T(8,128)(2,1)S(1)} custom-call(s32[512]{0:T(512)S(1)} %get-tuple-element.11.table_ref, f32[128]{0:T(128)S(1)} %copy-done.5, bf16[16,144,128]{2,1,0:T(8,128)(2,1)S(1)} %all-to-all-done.arrived_ref.bank_in_ref, bf16[16,144,128]{2,1,0:T(8,128)(2,1)S(1)} %all-to-all-done.arrived_ref.bank_in_ref, bf16[128,16,128]{2,1,0:T(8,128)(2,1)S(1)} %copy-done.1), custom_call_target="tpu_custom_call" | custom-call | tf_op jit(solution)/shard_map/blur/pallas_call | solution.py:465
  30.8 18.7 %all_to_all.20.returned_ref = bf16[16,128,128]{2,1,0:T(8,128)(2,1)S(1)} all-to-all(bf16[16,128,128]{2,1,0:T(8,128)(2,1)S(1)} %blur.2), channel_id=1, replica_groups=mesh['groups'=2,'sky'=16] {'sky'}, dimensions={0} | all-to-all | bytes 1048576 | tf_op jit(solution)/shard_map/all_to_all | solution.py:407
  49.5 0.0 copy-done
  49.5 2.6 %update.2 = (f32[3088,128]{1,0:T(8,128)S(1)}, bf16[16,128,128]{2,1,0:T(8,128)(2,1)S(1)}) custom-call(s32[260]{0:T(512)S(1)} %get-tuple-element.9.table_ref, f32[256]{0:T(256)S(1)} %get-tuple-element.10.factor_ref, bf16[16,128,128]{2,1,0:T(8,128)(2,1)S(1)} %all_to_all.20.returned_ref, f32[3072,128]{1,0:T(8,128)S(1)} %bitcast.6), custom_call_target="tpu_custom_call" | custom-call | tf_op jit(solution)/shard_map/update/pallas_call | solution.py:493
  52.0 18.4 %all_to_all.21.arrived_ref = bf16[16,128,128]{2,1,0:T(8,128)(2,1)S(1)} all-to-all(bf16[16,128,128]{2,1,0:T(8,128)(2,1)S(1)} %get-tuple-element.12), channel_id=1, replica_groups=mesh['groups'=2,'sky'=16] {'sky'}, dimensions={0} | all-to-all | bytes 1048576 | tf_op jit(solution)/shard_map/all_to_all | solution.py:407
  70.4 4.0 %blur.3 = (bf16[16,128,128]{2,1,0:T(8,128)(2,1)S(1)}, f32[128,16,128]{2,1,0:T(8,128)}) custom-call(s32[512]{0:T(512)S(1)} %get-tuple-element.11.table_ref, f32[128]{0:T(128)S(1)} %copy-done.5, bf16[16,128,128]{2,1,0:T(8,128)(2,1)S(1)} %all_to_all.21.arrived_ref, bf16[16,144,128]{2,1,0:T(8,128)(2,1)S(1)} %all-to-all-done.arrived_ref.bank_in_ref, ...), custom_call_target="tpu_custom_call" | custom-call | tf_op jit(solution)/shard_map/blur/pallas_call | solution.py:465
  74.4 18.4 %all_to_all.22.returned_ref = bf16[16,128,128]{2,1,0:T(8,128)(2,1)S(1)} all-to-all(bf16[16,128,128]{2,1,0:T(8,128)(2,1)S(1)} %get-tuple-element.13), channel_id=1, replica_groups=mesh['groups'=2,'sky'=16] {'sky'}, dimensions={0} | all-to-all | bytes 1048576 | tf_op jit(solution)/shard_map/all_to_all | solution.py:407
  92.7 3.0 %update.3 = f32[3072,128]{1,0:T(8,128)} custom-call(s32[260]{0:T(512)S(1)} %get-tuple-element.9.table_ref, f32[256]{0:T(256)S(1)} %get-tuple-element.10.factor_ref, bf16[16,128,128]{2,1,0:T(8,128)(2,1)S(1)} %all_to_all.22.returned_ref, f32[3088,128]{1,0:T(8,128)S(1)} %get-tuple-element.14.model_ref), custom_call_target="tpu_custom_call" | custom-call | tf_op jit(solution)/shard_map/update/pallas_call | solution.py:493
Async XLA Ops:
  0.6 10.8 %copy-start.2 = (s32[16,16]{1,0:T(8,128)S(1)}, s32[16,16]{1,0:T(8,128)}, u32[]{:S(2)}) copy-start(s32[16,16]{1,0:T(8,128)} %plane_in_ref.1) | copy-start | bytes 3076
  0.6 10.8 %copy-start.3 = (s32[16,16]{1,0:T(8,128)S(1)}, s32[16,16]{1,0:T(8,128)}, u32[]{:S(2)}) copy-start(s32[16,16]{1,0:T(8,128)} %row_in_ref.1) | copy-start | bytes 3076
  0.7 10.8 %copy-start.4 = (s32[16,16]{1,0:T(8,128)S(1)}, s32[16,16]{1,0:T(8,128)}, u32[]{:S(2)}) copy-start(s32[16,16]{1,0:T(8,128)} %cover_in_ref.1) | copy-start | bytes 3076
  0.7 10.8 %copy-start.6 = (s32[128,2]{0,1:T(2,128)S(1)}, s32[128,2]{0,1:T(2,128)}, u32[]{:S(2)}) copy-start(s32[128,2]{0,1:T(2,128)} %param.23) | copy-start | bytes 3076
  0.7 10.8 %copy-start.7 = (s32[128,2]{0,1:T(2,128)S(1)}, s32[128,2]{0,1:T(2,128)}, u32[]{:S(2)}) copy-start(s32[128,2]{0,1:T(2,128)} %param.24) | copy-start | bytes 3076
  0.7 10.8 %copy-start.8 = (s32[128,2]{0,1:T(2,128)S(1)}, s32[128,2]{0,1:T(2,128)}, u32[]{:S(2)}) copy-start(s32[128,2]{0,1:T(2,128)} %param.25) | copy-start | bytes 3076
  0.7 10.8 %copy-start.9 = (s32[128]{0:T(128)S(1)}, s32[128]{0:T(128)}, u32[]{:S(2)}) copy-start(s32[128]{0:T(128)} %batch_ref.1) | copy-start | bytes 1540
  0.7 10.8 %copy-start.10 = (f32[6]{0:T(128)S(1)}, f32[6]{0:T(128)}, u32[]{:S(2)}) copy-start(f32[6]{0:T(128)} %step_ref.1) | copy-start | bytes 76
  0.7 10.8 %copy-start.11 = (s32[2]{0:T(128)S(1)}, s32[2]{0:T(128)}, u32[]{:S(2)}) copy-start(s32[2]{0:T(128)} %lo_ref.1) | copy-start | bytes 28
  0.7 10.8 %copy-start.12 = (s32[2]{0:T(128)S(1)}, s32[2]{0:T(128)}, u32[]{:S(2)}) copy-start(s32[2]{0:T(128)} %hi_ref.1) | copy-start | bytes 28
  0.7 26.2 %copy-start.1 = (bf16[128,16,128]{2,1,0:T(8,128)(2,1)S(1)}, bf16[128,16,128]{2,1,0:T(8,128)(2,1)}, u32[]{:S(2)}) copy-start(bf16[128,16,128]{2,1,0:T(8,128)(2,1)} %seen_ref.3) | copy-start | bytes 1572868
  0.7 26.2 %copy-start.5 = (f32[128]{0:T(128)S(1)}, f32[128]{0:T(128)}, u32[]{:S(2)}) copy-start(f32[128]{0:T(128)} %weight_ref.3) | copy-start | bytes 1540
  4.1 22.9 %all-to-all-start = ((bf16[16,144,128]{2,1,0:T(8,128)(2,1)}), bf16[16,144,128]{2,1,0:T(8,128)(2,1)S(1)}, u32[]{:S(2)}, u32[]{:S(2)}) async-start(bf16[16,144,128]{2,1,0:T(8,128)(2,1)} %first_send.1), calls=%async_computation | async-start | bytes 1179648 | tf_op jit(solution)/shard_map/all_to_all | solution.py:407
  27.0 22.5 %copy-start = (f32[2,6,256,128]{3,2,1,0:T(8,128)S(1)}, f32[2,6,256,128]{3,2,1,0:T(8,128)}, u32[]{:S(2)}) copy-start(f32[2,6,256,128]{3,2,1,0:T(8,128)} %param.14) | copy-start | bytes 4718596

commit v10 on v9

--- a/solution.py
+++ b/solution.py
@@ -47,8 +47,8 @@
     return word & mask, lax.shift_right_logical(word, PLACE) & mask
 
 
-def pack_slots(plane_ref, row_ref, cover_ref, tile_rows, height, rows_each, x_ref, packed_ref):
-    peers, capacity = plane_ref.shape
+def pack_slots(begin, count, plane_ref, row_ref, cover_ref, tile_rows, height, rows_each, x_ref, packed_ref):
+    capacity = plane_ref.shape[1]
 
     def peer(d, _):
         at = d * rows_each
@@ -58,7 +58,7 @@
             at = at + cover_ref[d, c]
         return 0
 
-    lax.fori_loop(0, peers, peer, 0, unroll=2)
+    lax.fori_loop(begin, begin + count, peer, 0, unroll=2)
 
 
 def bank_rows(taps, height):
@@ -113,6 +113,7 @@
     x_ref,
     packed_ref,
     bank_ref,
+    block_ref,
     sems,
 ):
     peers = plane_ref.shape[0]
@@ -134,10 +135,19 @@
     bank = bank_ref[...].astype(BF16)
     for load in loads[1:]:
         load.wait()
-    pack_slots(plane_ref, row_ref, cover_ref, tile_rows, height, rows_each, x_ref, packed_ref)
-    for d in range(peers):
-        out_ref[d, :rows_each, :] = packed_ref[d * rows_each : (d + 1) * rows_each, :].astype(BF16)
-        out_ref[d, rows_each:, :] = bank
+    parts = max(n for n in (1, 2, 4) if peers % n == 0)
+    some = peers // parts
+    sends = []
+    for part in range(parts):
+        here = pl.ds(part * some, some)
+        pack_slots(part * some, some, plane_ref, row_ref, cover_ref, tile_rows, height, rows_each, x_ref, packed_ref)
+        for d in range(part * some, (part + 1) * some):
+            block_ref[d, :rows_each, :] = packed_ref[d * rows_each : (d + 1) * rows_each, :].astype(BF16)
+            block_ref[d, rows_each:, :] = bank
+        sends.append(pltpu.make_async_copy(block_ref.at[here], out_ref.at[here], sems.at[len(loads) + part]))
+        sends[-1].start()
+    for send in sends:
+        send.wait()
 
 
 def update_kernel(bands, tile_rows, height, last, table_ref, factor_ref, returned_ref, model_ref, *rest):
@@ -218,7 +228,6 @@
     update_ref,
     factor_ref,
     length_ref,
-    stamp_ref,
     begin_ref,
     scale_ref,
 ):
@@ -228,7 +237,6 @@
 
     def clear(s, _):
         length_ref[s] = 0
-        stamp_ref[s] = 0
         return 0
 
     lax.fori_loop(0, slots, clear, 0, unroll=16)
@@ -244,7 +252,6 @@
             s = slot_ref[k, e]
             s = jnp.where(s >= 0, s, slots)
             length_ref[s] = stop_ref[k, e] - start_ref[k, e]
-            stamp_ref[s] = e * height + start_ref[k, e]
         return 0
 
     lax.fori_loop(0, exposures, measure, 0, unroll=8)
@@ -254,7 +261,6 @@
         for c in range(capacity):
             s = o * capacity + c
             begin_ref[s] = at
-            blur_ref[pieces * exposures + s] = stamp_ref[s] | (at << SHIFT)
             at = at + length_ref[s]
             p = jnp.maximum(plane_ref[o, c], 0)
             cover = cover_ref[o, c]
@@ -296,11 +302,10 @@
         send = pltpu.make_async_copy(residual_ref, residual_out_ref, sent)
     else:
         out_ref, *rest = rest
-    rows_ref, bank_ref, result_ref, packed_ref, held_ref, blur_ref, back_ref = rest
+    rows_ref, bank_ref, packed_ref, held_ref, blur_ref, back_ref = rest
     peers, rows_each, _ = out_ref.shape
     extra = bank_in_ref.shape[1] - rows_each
     exposures = seen_ref.shape[0]
-    slots = peers * (2 * rows_each // height)
     abreast = max(n for n in (1, 2, 4, 8, 16, 32) if exposures % n == 0)
     place = lax.broadcasted_iota(I32, (height, LANES), 0)
     lane = lax.broadcasted_iota(I32, (height, LANES), 1)
@@ -333,10 +338,18 @@
     def correlate(s):
         for q in range(abreast):
             e = s * abreast + q
-            here = pl.ds(e * height, height)
-            result_ref[here, :] = jnp.dot(
-                back_ref[high(table_ref[e])], shifted(held_ref[here, :]), preferred_element_type=F32
+            result = jnp.dot(
+                back_ref[high(table_ref[e])],
+                shifted(held_ref[e * height : (e + 1) * height, :]),
+                preferred_element_type=F32,
             )
+            words = [table_ref[k * exposures + e] for k in range(pieces)]
+            for k, word in enumerate(words):
+                mask = place >= high(word) if k else None
+                if k + 1 < pieces:
+                    before = place < high(words[k + 1])
+                    mask = before if mask is None else mask & before
+                pltpu.store(packed_ref.at[pl.ds(low(word), height), :], result, mask=mask)
 
     def blur(s):
         for q in range(abreast):
@@ -363,14 +376,9 @@
     if last:
         send.start()
 
-    def move(s, _):
-        word = table_ref[pieces * exposures + s]
-        packed_ref[pl.ds(high(word), height), :] = result_ref[pl.ds(low(word), height), :]
-        return 0
-
-    lax.fori_loop(0, slots, move, 0, unroll=16)
     for o in range(peers):
-        out_ref[o, :, :] = packed_ref[o * rows_each : (o + 1) * rows_each, :].astype(BF16)
+        at = height + o * rows_each
+        out_ref[o, :, :] = packed_ref[at : at + rows_each, :].astype(BF16)
     if last:
         send.wait()
 
@@ -410,7 +418,7 @@
         functools.partial(first_send_kernel, tile_rows, height, rows_each),
         out_shape=jax.ShapeDtypeStruct((peers, block, columns), BF16),
         in_specs=[hbm()] * 5,
-        out_specs=vmem(),
+        out_specs=hbm(),
         scratch_shapes=[
             pltpu.SMEM(send_plane.shape, I32),
             pltpu.SMEM(send_row.shape, I32),
@@ -419,7 +427,8 @@
             pltpu.VMEM((total + height, columns), F32),
             pltpu.VMEM((peers * rows_each + height, columns), F32),
             pltpu.VMEM((extra, columns), F32),
-            pltpu.SemaphoreType.DMA((5,)),
+            pltpu.VMEM((peers, block, columns), BF16),
+            pltpu.SemaphoreType.DMA((9,)),
         ],
         compiler_params=params(2.5),
         name="first_send",
@@ -427,18 +436,17 @@
     arrived = swap(outbound)
     slots = peers * capacity
     assert max(total, peers * rows_each) < 1 << PLACE and height < 1 << (31 - 2 * PLACE)
-    assert max(count, peers * capacity + 2) * height < 1 << (SHIFT - 1)
+    assert max(peers * rows_each + 2 * height, psf_taps.shape[0] * peers) < 1 << (SHIFT - 1)
     blur_table, update_table, factors = pl.pallas_call(
         functools.partial(tables_kernel, tile_rows, bands, height, rows_each),
         out_shape=(
-            jax.ShapeDtypeStruct((pieces * count + slots,), I32),
+            jax.ShapeDtypeStruct((pieces * count,), I32),
             jax.ShapeDtypeStruct((slots + 2 * tile_count,), I32),
             jax.ShapeDtypeStruct((slots,), F32),
         ),
         in_specs=[smem()] * 10,
         out_specs=(smem(), smem(), smem()),
         scratch_shapes=[
-            pltpu.SMEM((slots + 1,), I32),
             pltpu.SMEM((slots + 1,), I32),
             pltpu.SMEM((slots,), I32),
             pltpu.SMEM((tile_count * bands,), F32),
@@ -470,8 +478,7 @@
             scratch_shapes=[
                 pltpu.VMEM((peers * rows_each + 2 * height, columns), F32),
                 pltpu.VMEM((peers * extra, columns), F32),
-                pltpu.VMEM((count * height + height, columns), F32),
-                pltpu.VMEM((peers * rows_each + height, columns), F32),
+                pltpu.VMEM((peers * rows_each + 2 * height, columns), F32),
                 pltpu.VMEM((count * height, columns), BF16),
                 pltpu.VMEM((peers * batches_each, height, LANES), BF16),
                 pltpu.VMEM((peers * batches_each, height, LANES), BF16),
@@ -489,7 +496,7 @@
             scratch += [pltpu.VMEM(padded, F32), pltpu.SemaphoreType.DMA((tile_count * bands,))]
         else:
             scratch.append(pltpu.VMEM((peers * rows_each + height, columns), F32))
-        sums = max(n for n in (1, 2, 4 if last else 2) if peers % n == 0)
+        sums = max(n for n in (1, 2) if peers % n == 0)
         res = pl.pallas_call(
             functools.partial(update_kernel, bands, tile_rows, height, last),
             out_shape=jax.ShapeDtypeStruct((total, columns), F32)

time: 96.1 us -> 95.4 us (level)
  Pallas kernels: 23 us -> 21.6 us
  transfers between devices with their start and end apart: 1 -> 1, of which waited for: 1 -> 1; matrix products, arithmetic and copies ran while one was open for 0% -> 0% of each run, Pallas kernels for 7% -> 6%
where the time goes in v10:
time: 95.4 us; the launch traced here: 95 us
  blocking collectives  55.4 us (58%)
  Pallas kernels  21.6 us (23%)
  waiting for transfers between devices  9.76 us (10%)
  starting transfers between devices  7.37 us (8%)
    all_to_all x3, blocking collectives, swap(): return lax.all_to_all(a, 'sky', split_axis=0, concat_axis=0, tiled=True)  55.4 us
    all_to_all x1, waiting for transfers between devices, swap(): return lax.all_to_all(a, 'sky', split_axis=0, concat_axis=0, tiled=True)  9.76 us
    all_to_all x1, starting transfers between devices, swap(): return lax.all_to_all(a, 'sky', split_axis=0, concat_axis=0, tiled=True)  7.37 us
    pallas_call x2, Pallas kernels, body(): pl.pallas_call(functools.partial(blur_kernel, height, pieces, batches_eac...  7.31 us
    pallas_call x1, Pallas kernels, body(): pl.pallas_call(functools.partial(tables_kernel, tile_rows, bands, height,...  5.68 us
    pallas_call x2, Pallas kernels, body(): pl.pallas_call(functools.partial(update_kernel, bands, tile_rows, height,...  5.39 us
    pallas_call x1, Pallas kernels, body(): pl.pallas_call(functools.partial(first_send_kernel, tile_rows, height, ro...  3.18 us
  transfers between devices with their start and end apart: 1, of which 1 were waited for; matrix products, arithmetic and copies ran while one was open for 0% of the time, Pallas kernels for 6%

profile of v10, /device:TPU:0, one launch (start us, length us, event | category | flops | bytes accessed | tf_op | source)
XLA Modules:
  0.0 95.0 jit_solution(13180323285623197045)
XLA Ops:
  0.6 0.0 copy-start.2
  0.6 0.0 copy-start.3
  0.7 0.0 copy-start.4
  0.7 0.0 copy-start.6
  0.7 0.0 copy-start.7
  0.7 0.0 copy-start.8
  0.7 0.0 copy-start.9
  0.7 0.0 copy-start.10
  0.7 0.0 copy-start.11
  0.7 0.0 copy-start.12
  0.7 0.0 copy-start.1
  0.7 0.0 copy-start.5
  0.8 3.2 %first_send.1 = bf16[16,144,128]{2,1,0:T(8,128)(2,1)} custom-call(s32[16,16]{1,0:T(8,128)} %plane_in_ref.1, s32[16,16]{1,0:T(8,128)} %row_in_ref.1, s32[16,16]{1,0:T(8,128)} %cover_in_ref.1, f32[2,56]{1,0:T(2,128)} %taps_in_ref.1, f32[3072,128]{1,0:T(8,128)} %bitcast.5), custom_call_target="tpu_custom_call" | custom-call | tf_op jit(solution)/shard_map/first_send/pallas_call | solution.py:417
  3.9 7.4 %all-to-all-start = ((bf16[16,144,128]{2,1,0:T(8,128)(2,1)}), bf16[16,144,128]{2,1,0:T(8,128)(2,1)S(1)}, u32[]{:S(2)}, u32[]{:S(2)}) async-start(bf16[16,144,128]{2,1,0:T(8,128)(2,1)} %first_send.1), calls=%async_computation | async-start | bytes 1179648 | tf_op jit(solution)/shard_map/all_to_all | solution.py:415
  11.3 0.0 copy-done.2
  11.3 0.0 copy-done.3
  11.3 0.0 copy-done.4
  11.4 0.0 copy-done.6
  11.4 0.0 copy-done.7
  11.4 0.0 copy-done.8
  11.4 0.0 copy-done.9
  11.4 0.0 copy-done.10
  11.4 0.0 copy-done.11
  11.4 0.0 copy-done.12
  11.4 5.7 %tables.1 = (s32[256]{0:T(256)S(1)}, s32[260]{0:T(512)S(1)}, f32[256]{0:T(256)S(1)}) custom-call(s32[2,128]{1,0:T(2,128)S(1)} %bitcast.7, s32[2,128]{1,0:T(2,128)S(1)} %bitcast.8, s32[2,128]{1,0:T(2,128)S(1)} %bitcast.9, s32[128]{0:T(128)S(1)} %copy-done.9, s32[16,16]{1,0:T(8,128)S(1)} %copy-done.2, s32[16,16]{1,0:T(8,128)S(1)} %copy-done.3, ...), custom_call_target="tpu_custom_call" | custom-call | flops 4000000 | bytes 8000000 | tf_op jit(solution)/shard_map/tables/pallas_call | solution.py:440
  17.1 9.8 %all-to-all-done.arrived_ref.bank_in_ref = bf16[16,144,128]{2,1,0:T(8,128)(2,1)S(1)} async-done(((bf16[16,144,128]{2,1,0:T(8,128)(2,1)}), bf16[16,144,128]{2,1,0:T(8,128)(2,1)S(1)}, u32[]{:S(2)}, u32[]{:S(2)}) %all-to-all-start) | async-done | bytes 589856 | tf_op jit(solution)/shard_map/all_to_all | solution.py:415
  26.9 0.0 copy-done.1
  26.9 0.0 copy-done.5
  26.9 0.0 copy-start
  26.9 3.2 %blur.2 = bf16[16,128,128]{2,1,0:T(8,128)(2,1)S(1)} custom-call(s32[256]{0:T(256)S(1)} %get-tuple-element.11.table_ref, f32[128]{0:T(128)S(1)} %copy-done.5, bf16[16,144,128]{2,1,0:T(8,128)(2,1)S(1)} %all-to-all-done.arrived_ref.bank_in_ref, bf16[16,144,128]{2,1,0:T(8,128)(2,1)S(1)} %all-to-all-done.arrived_ref.bank_in_ref, bf16[128,16,128]{2,1,0:T(8,128)(2,1)S(1)} %copy-done.1), custom_call_target="tpu_custom_call" | custom-call | tf_op jit(solution)/shard_map/blur/pallas_call | solution.py:473
  30.1 18.7 %all_to_all.20.returned_ref = bf16[16,128,128]{2,1,0:T(8,128)(2,1)S(1)} all-to-all(bf16[16,128,128]{2,1,0:T(8,128)(2,1)S(1)} %blur.2), channel_id=1, replica_groups=mesh['groups'=2,'sky'=16] {'sky'}, dimensions={0} | all-to-all | bytes 1048576 | tf_op jit(solution)/shard_map/all_to_all | solution.py:415
  48.8 0.0 copy-done
  48.8 2.6 %update.2 = (f32[3088,128]{1,0:T(8,128)S(1)}, bf16[16,128,128]{2,1,0:T(8,128)(2,1)S(1)}) custom-call(s32[260]{0:T(512)S(1)} %get-tuple-element.9.table_ref, f32[256]{0:T(256)S(1)} %get-tuple-element.10.factor_ref, bf16[16,128,128]{2,1,0:T(8,128)(2,1)S(1)} %all_to_all.20.returned_ref, f32[3072,128]{1,0:T(8,128)S(1)} %bitcast.6), custom_call_target="tpu_custom_call" | custom-call | tf_op jit(solution)/shard_map/update/pallas_call | solution.py:500
  51.4 18.4 %all_to_all.21.arrived_ref = bf16[16,128,128]{2,1,0:T(8,128)(2,1)S(1)} all-to-all(bf16[16,128,128]{2,1,0:T(8,128)(2,1)S(1)} %get-tuple-element.12), channel_id=1, replica_groups=mesh['groups'=2,'sky'=16] {'sky'}, dimensions={0} | all-to-all | bytes 1048576 | tf_op jit(solution)/shard_map/all_to_all | solution.py:415
  69.7 4.1 %blur.3 = (bf16[16,128,128]{2,1,0:T(8,128)(2,1)S(1)}, f32[128,16,128]{2,1,0:T(8,128)}) custom-call(s32[256]{0:T(256)S(1)} %get-tuple-element.11.table_ref, f32[128]{0:T(128)S(1)} %copy-done.5, bf16[16,128,128]{2,1,0:T(8,128)(2,1)S(1)} %all_to_all.21.arrived_ref, bf16[16,144,128]{2,1,0:T(8,128)(2,1)S(1)} %all-to-all-done.arrived_ref.bank_in_ref, ...), custom_call_target="tpu_custom_call" | custom-call | tf_op jit(solution)/shard_map/blur/pallas_call | solution.py:473
  73.8 18.4 %all_to_all.22.returned_ref = bf16[16,128,128]{2,1,0:T(8,128)(2,1)S(1)} all-to-all(bf16[16,128,128]{2,1,0:T(8,128)(2,1)S(1)} %get-tuple-element.13), channel_id=1, replica_groups=mesh['groups'=2,'sky'=16] {'sky'}, dimensions={0} | all-to-all | bytes 1048576 | tf_op jit(solution)/shard_map/all_to_all | solution.py:415
  92.2 2.8 %update.3 = f32[3072,128]{1,0:T(8,128)} custom-call(s32[260]{0:T(512)S(1)} %get-tuple-element.9.table_ref, f32[256]{0:T(256)S(1)} %get-tuple-element.10.factor_ref, bf16[16,128,128]{2,1,0:T(8,128)(2,1)S(1)} %all_to_all.22.returned_ref, f32[3088,128]{1,0:T(8,128)S(1)} %get-tuple-element.14.model_ref), custom_call_target="tpu_custom_call" | custom-call | tf_op jit(solution)/shard_map/update/pallas_call | solution.py:500
Async XLA Ops:
  0.6 10.7 %copy-start.2 = (s32[16,16]{1,0:T(8,128)S(1)}, s32[16,16]{1,0:T(8,128)}, u32[]{:S(2)}) copy-start(s32[16,16]{1,0:T(8,128)} %plane_in_ref.1) | copy-start | bytes 3076
  0.6 10.7 %copy-start.3 = (s32[16,16]{1,0:T(8,128)S(1)}, s32[16,16]{1,0:T(8,128)}, u32[]{:S(2)}) copy-start(s32[16,16]{1,0:T(8,128)} %row_in_ref.1) | copy-start | bytes 3076
  0.7 10.7 %copy-start.4 = (s32[16,16]{1,0:T(8,128)S(1)}, s32[16,16]{1,0:T(8,128)}, u32[]{:S(2)}) copy-start(s32[16,16]{1,0:T(8,128)} %cover_in_ref.1) | copy-start | bytes 3076
  0.7 10.7 %copy-start.6 = (s32[128,2]{0,1:T(2,128)S(1)}, s32[128,2]{0,1:T(2,128)}, u32[]{:S(2)}) copy-start(s32[128,2]{0,1:T(2,128)} %param.23) | copy-start | bytes 3076
  0.7 10.7 %copy-start.7 = (s32[128,2]{0,1:T(2,128)S(1)}, s32[128,2]{0,1:T(2,128)}, u32[]{:S(2)}) copy-start(s32[128,2]{0,1:T(2,128)} %param.24) | copy-start | bytes 3076
  0.7 10.7 %copy-start.8 = (s32[128,2]{0,1:T(2,128)S(1)}, s32[128,2]{0,1:T(2,128)}, u32[]{:S(2)}) copy-start(s32[128,2]{0,1:T(2,128)} %param.25) | copy-start | bytes 3076
  0.7 10.7 %copy-start.9 = (s32[128]{0:T(128)S(1)}, s32[128]{0:T(128)}, u32[]{:S(2)}) copy-start(s32[128]{0:T(128)} %batch_ref.1) | copy-start | bytes 1540
  0.7 10.7 %copy-start.10 = (f32[6]{0:T(128)S(1)}, f32[6]{0:T(128)}, u32[]{:S(2)}) copy-start(f32[6]{0:T(128)} %step_ref.1) | copy-start | bytes 76
  0.7 10.7 %copy-start.11 = (s32[2]{0:T(128)S(1)}, s32[2]{0:T(128)}, u32[]{:S(2)}) copy-start(s32[2]{0:T(128)} %lo_ref.1) | copy-start | bytes 28
  0.7 10.7 %copy-start.12 = (s32[2]{0:T(128)S(1)}, s32[2]{0:T(128)}, u32[]{:S(2)}) copy-start(s32[2]{0:T(128)} %hi_ref.1) | copy-start | bytes 28
  0.7 26.1 %copy-start.1 = (bf16[128,16,128]{2,1,0:T(8,128)(2,1)S(1)}, bf16[128,16,128]{2,1,0:T(8,128)(2,1)}, u32[]{:S(2)}) copy-start(bf16[128,16,128]{2,1,0:T(8,128)(2,1)} %seen_ref.3) | copy-start | bytes 1572868
  0.7 26.1 %copy-start.5 = (f32[128]{0:T(128)S(1)}, f32[128]{0:T(128)}, u32[]{:S(2)}) copy-start(f32[128]{0:T(128)} %weight_ref.3) | copy-start | bytes 1540
  3.9 22.9 %all-to-all-start = ((bf16[16,144,128]{2,1,0:T(8,128)(2,1)}), bf16[16,144,128]{2,1,0:T(8,128)(2,1)S(1)}, u32[]{:S(2)}, u32[]{:S(2)}) async-start(bf16[16,144,128]{2,1,0:T(8,128)(2,1)} %first_send.1), calls=%async_computation | async-start | bytes 1179648 | tf_op jit(solution)/shard_map/all_to_all | solution.py:415
  26.9 21.9 %copy-start = (f32[2,6,256,128]{3,2,1,0:T(8,128)S(1)}, f32[2,6,256,128]{3,2,1,0:T(8,128)}, u32[]{:S(2)}) copy-start(f32[2,6,256,128]{3,2,1,0:T(8,128)} %param.14) | copy-start | bytes 4718596

commit v11 on v10

--- a/solution.py
+++ b/solution.py
@@ -117,23 +117,23 @@
     sems,
 ):
     peers = plane_ref.shape[0]
-    pairs = (
-        (taps_in_ref, taps_ref),
-        (model_ref, x_ref.at[pl.ds(0, model_ref.shape[0]), :]),
-        (plane_in_ref, plane_ref),
-        (row_in_ref, row_ref),
-        (cover_in_ref, cover_ref),
-    )
+    total = model_ref.shape[0]
+    cuts = max(n for n in (1, 2, 4) if total % (16 * n) == 0)
+    pairs = [(plane_in_ref, plane_ref), (row_in_ref, row_ref), (cover_in_ref, cover_ref), (taps_in_ref, taps_ref)]
+    for n in range(cuts):
+        here = pl.ds(n * (total // cuts), total // cuts)
+        pairs.append((model_ref.at[here, :], x_ref.at[here, :]))
     loads = [pltpu.make_async_copy(*pair, sems.at[n]) for n, pair in enumerate(pairs)]
     for load in loads:
         load.start()
     bank_ref[...] = jnp.zeros(bank_ref.shape, F32)
-    loads[0].wait()
+    taps_load = loads.pop(3)
+    taps_load.wait()
     for m, row in enumerate(bank_rows(taps_ref[...], height)):
         for n in range(taps_ref.shape[0]):
             bank_ref[2 * n + m : 2 * n + m + 1, :] = row[n : n + 1, :]
     bank = bank_ref[...].astype(BF16)
-    for load in loads[1:]:
+    for load in loads:
         load.wait()
     parts = max(n for n in (1, 2, 4) if peers % n == 0)
     some = peers // parts
@@ -144,7 +144,7 @@
         for d in range(part * some, (part + 1) * some):
             block_ref[d, :rows_each, :] = packed_ref[d * rows_each : (d + 1) * rows_each, :].astype(BF16)
             block_ref[d, rows_each:, :] = bank
-        sends.append(pltpu.make_async_copy(block_ref.at[here], out_ref.at[here], sems.at[len(loads) + part]))
+        sends.append(pltpu.make_async_copy(block_ref.at[here], out_ref.at[here], sems.at[len(pairs) + part]))
         sends[-1].start()
     for send in sends:
         send.wait()
@@ -292,40 +292,37 @@
     table_ref,
     weight_ref,
     arrived_ref,
-    bank_in_ref,
     seen_ref,
     *rest,
 ):
     if last:
-        out_ref, residual_out_ref, *rest = rest
-        *rest, residual_ref, sent = rest
-        send = pltpu.make_async_copy(residual_ref, residual_out_ref, sent)
+        blur_ref, back_ref, out_ref, residual_out_ref, rows_ref, packed_ref, held_ref, residual_ref, sent = rest
     else:
-        out_ref, *rest = rest
-    rows_ref, bank_ref, packed_ref, held_ref, blur_ref, back_ref = rest
+        out_ref, blur_ref, back_ref, rows_ref, packed_ref, held_ref, bank_ref = rest
     peers, rows_each, _ = out_ref.shape
-    extra = bank_in_ref.shape[1] - rows_each
     exposures = seen_ref.shape[0]
-    abreast = max(n for n in (1, 2, 4, 8, 16, 32) if exposures % n == 0)
     place = lax.broadcasted_iota(I32, (height, LANES), 0)
     lane = lax.broadcasted_iota(I32, (height, LANES), 1)
     for o in range(peers):
-        rows_ref[height + o * rows_each : height + (o + 1) * rows_each, :] = arrived_ref[o, :rows_each, :].astype(F32)
-        bank_ref[o * extra : (o + 1) * extra, :] = bank_in_ref[o, rows_each:, :].astype(F32)
-
-    gap = lane % height - place
-    near = (gap <= HALF) & (gap >= -HALF) & (lane < TAPS * height)
-
-    def operators(o, _):
-        for n in range(batches_each):
-            for m, ref in enumerate((blur_ref, back_ref)):
-                taps = jnp.broadcast_to(bank_ref[pl.ds(o * extra + 2 * n + m, 1), :], (height, LANES))
-                ref[o * batches_each + n] = jnp.where(
-                    near, pltpu.roll(taps, 0, 1, stride=1, stride_axis=0), 0.0
-                ).astype(BF16)
-        return 0
-
-    lax.fori_loop(0, peers, operators, 0, unroll=4)
+        at = height + o * rows_each
+        rows_ref[at : at + rows_each, :] = arrived_ref[o, :rows_each, :].astype(F32)
+    if not last:
+        extra = arrived_ref.shape[1] - rows_each
+        for o in range(peers):
+            bank_ref[o * extra : (o + 1) * extra, :] = arrived_ref[o, rows_each:, :].astype(F32)
+        gap = lane % height - place
+        near = (gap <= HALF) & (gap >= -HALF) & (lane < TAPS * height)
+
+        def operators(o, _):
+            for n in range(batches_each):
+                for m, ref in enumerate((blur_ref, back_ref)):
+                    taps = jnp.broadcast_to(bank_ref[pl.ds(o * extra + 2 * n + m, 1), :], (height, LANES))
+                    ref[o * batches_each + n] = jnp.where(
+                        near, pltpu.roll(taps, 0, 1, stride=1, stride_axis=0), 0.0
+                    ).astype(BF16)
+            return 0
+
+        lax.fori_loop(0, peers, operators, 0, unroll=4)
 
     def shifted(x):
         parts = []
@@ -335,47 +332,40 @@
         parts.append(jnp.zeros((LANES - TAPS * height, LANES), BF16))
         return jnp.concatenate(parts, axis=0)
 
-    def correlate(s):
-        for q in range(abreast):
-            e = s * abreast + q
-            result = jnp.dot(
-                back_ref[high(table_ref[e])],
-                shifted(held_ref[e * height : (e + 1) * height, :]),
-                preferred_element_type=F32,
-            )
-            words = [table_ref[k * exposures + e] for k in range(pieces)]
-            for k, word in enumerate(words):
-                mask = place >= high(word) if k else None
-                if k + 1 < pieces:
-                    before = place < high(words[k + 1])
-                    mask = before if mask is None else mask & before
-                pltpu.store(packed_ref.at[pl.ds(low(word), height), :], result, mask=mask)
-
-    def blur(s):
-        for q in range(abreast):
-            e = s * abreast + q
-            stamp = rows_ref[pl.ds(low(table_ref[e]), height), :]
-            for k in range(1, pieces):
-                word = table_ref[k * exposures + e]
-                stamp = jnp.where(place >= high(word), rows_ref[pl.ds(low(word), height), :], stamp)
-            predicted = jnp.dot(
-                blur_ref[high(table_ref[e])], shifted(stamp.astype(BF16)), preferred_element_type=F32
-            )
-            residual = weight_ref[e] * (predicted - seen_ref[e].astype(F32))
-            if last:
-                residual_ref[e] = residual
-            held_ref[pl.ds(e * height, height), :] = residual.astype(BF16)
-
-    steps = exposures // abreast
-
-    for s in range(steps + 1):
-        if s > 0:
-            correlate(s - 1)
-        if s < steps:
-            blur(s)
+    def blur(e):
+        stamp = rows_ref[pl.ds(low(table_ref[e]), height), :]
+        for k in range(1, pieces):
+            word = table_ref[k * exposures + e]
+            stamp = jnp.where(place >= high(word), rows_ref[pl.ds(low(word), height), :], stamp)
+        predicted = jnp.dot(
+            blur_ref[high(table_ref[e])], shifted(stamp.astype(BF16)), preferred_element_type=F32
+        )
+        residual = weight_ref[e] * (predicted - seen_ref[e].astype(F32))
+        if last:
+            residual_ref[e] = residual
+        held_ref[e * height : (e + 1) * height, :] = residual.astype(BF16)
+
+    def correlate(e):
+        result = jnp.dot(
+            back_ref[high(table_ref[e])],
+            shifted(held_ref[e * height : (e + 1) * height, :]),
+            preferred_element_type=F32,
+        )
+        words = [table_ref[k * exposures + e] for k in range(pieces)]
+        for k, word in enumerate(words):
+            mask = place >= high(word) if k else None
+            if k + 1 < pieces:
+                before = place < high(words[k + 1])
+                mask = before if mask is None else mask & before
+            pltpu.store(packed_ref.at[pl.ds(low(word), height), :], result, mask=mask)
+
+    for e in range(exposures):
+        blur(e)
     if last:
+        send = pltpu.make_async_copy(residual_ref, residual_out_ref, sent)
         send.start()
-
+    for e in range(exposures):
+        correlate(e)
     for o in range(peers):
         at = height + o * rows_each
         out_ref[o, :, :] = packed_ref[at : at + rows_each, :].astype(BF16)
@@ -428,7 +418,7 @@
             pltpu.VMEM((peers * rows_each + height, columns), F32),
             pltpu.VMEM((extra, columns), F32),
             pltpu.VMEM((peers, block, columns), BF16),
-            pltpu.SemaphoreType.DMA((9,)),
+            pltpu.SemaphoreType.DMA((12,)),
         ],
         compiler_params=params(2.5),
         name="first_send",
@@ -466,28 +456,32 @@
         foot_lo,
         foot_hi,
     )
-    with_bank = arrived
+    operators = []
     for sweep in range(ITERS):
         last = sweep == ITERS - 1
         rows_shape = jax.ShapeDtypeStruct((peers, rows_each, columns), BF16)
-        outs = pl.pallas_call(
+        scratch = [
+            pltpu.VMEM((peers * rows_each + 2 * height, columns), F32),
+            pltpu.VMEM((peers * rows_each + 2 * height, columns), F32),
+            pltpu.VMEM((count * height, columns), BF16),
+        ]
+        if last:
+            scratch += [pltpu.VMEM(exposures.shape, F32), pltpu.SemaphoreType.DMA]
+            out_shape, out_specs = (rows_shape, jax.ShapeDtypeStruct(exposures.shape, F32)), (vmem(), hbm())
+        else:
+            scratch.append(pltpu.VMEM((peers * extra, columns), F32))
+            operator_shape = jax.ShapeDtypeStruct((peers * batches_each, height, columns), BF16)
+            out_shape, out_specs = (rows_shape, operator_shape, operator_shape), (vmem(),) * 3
+        outgoing, *others = pl.pallas_call(
             functools.partial(blur_kernel, height, pieces, batches_each, last),
-            out_shape=(rows_shape, jax.ShapeDtypeStruct(exposures.shape, F32)) if last else rows_shape,
-            in_specs=[smem()] * 2 + [vmem()] * 3,
-            out_specs=(vmem(), hbm()) if last else vmem(),
-            scratch_shapes=[
-                pltpu.VMEM((peers * rows_each + 2 * height, columns), F32),
-                pltpu.VMEM((peers * extra, columns), F32),
-                pltpu.VMEM((peers * rows_each + 2 * height, columns), F32),
-                pltpu.VMEM((count * height, columns), BF16),
-                pltpu.VMEM((peers * batches_each, height, LANES), BF16),
-                pltpu.VMEM((peers * batches_each, height, LANES), BF16),
-            ]
-            + [pltpu.VMEM(exposures.shape, F32), pltpu.SemaphoreType.DMA] * last,
+            out_shape=out_shape,
+            in_specs=[smem()] * 2 + [vmem()] * (4 if last else 2),
+            out_specs=out_specs,
+            scratch_shapes=scratch,
             compiler_params=params(),
             name="blur",
-        )(blur_table, inv_var, arrived, with_bank, exposures)
-        outgoing = outs[0] if last else outs
+        )(blur_table, inv_var, arrived, exposures, *operators)
+        operators = [] if last else others
         returned = swap(outgoing)
         new_shape = jax.ShapeDtypeStruct((total, columns), F32)
         padded = (total + height, columns)
@@ -513,7 +507,7 @@
         else:
             x, outbound = res
             arrived = swap(outbound)
-    return (x.reshape(model.shape), outs[1])
+    return (x.reshape(model.shape), others[0])
 
 
 def solution(mesh):

time: 95.4 us -> 95.1 us (level)
  no operation moved by 1% of the time
where the time goes in v11:
time: 95.1 us; the launch traced here: 94.8 us
  blocking collectives  55.4 us (58%)
  Pallas kernels  21.2 us (22%)
  waiting for transfers between devices  9.76 us (10%)
  starting transfers between devices  7.5 us (8%)
    all_to_all x3, blocking collectives, swap(): return lax.all_to_all(a, 'sky', split_axis=0, concat_axis=0, tiled=True)  55.4 us
    all_to_all x1, waiting for transfers between devices, swap(): return lax.all_to_all(a, 'sky', split_axis=0, concat_axis=0, tiled=True)  9.76 us
    all_to_all x1, starting transfers between devices, swap(): return lax.all_to_all(a, 'sky', split_axis=0, concat_axis=0, tiled=True)  7.5 us
    pallas_call x2, Pallas kernels, body(): pl.pallas_call(functools.partial(blur_kernel, height, pieces, batches_eac...  7 us
    pallas_call x1, Pallas kernels, body(): pl.pallas_call(functools.partial(tables_kernel, tile_rows, bands, height,...  5.68 us
    pallas_call x2, Pallas kernels, body(): pl.pallas_call(functools.partial(update_kernel, bands, tile_rows, height,...  5.39 us
    pallas_call x1, Pallas kernels, body(): pl.pallas_call(functools.partial(first_send_kernel, tile_rows, height, ro...  3.08 us
  transfers between devices with their start and end apart: 1, of which 1 were waited for; matrix products, arithmetic and copies ran while one was open for 0% of the time, Pallas kernels for 6%

profile of v11, /device:TPU:0, one launch (start us, length us, event | category | flops | bytes accessed | tf_op | source)
XLA Modules:
  0.0 94.8 jit_solution(1069563462561588060)
XLA Ops:
  0.6 0.0 copy-start.2
  0.6 0.0 copy-start.3
  0.7 0.0 copy-start.4
  0.7 0.0 copy-start.6
  0.7 0.0 copy-start.7
  0.7 0.0 copy-start.8
  0.7 0.0 copy-start.9
  0.7 0.0 copy-start.10
  0.7 0.0 copy-start.11
  0.7 0.0 copy-start.12
  0.7 0.0 copy-start.1
  0.7 0.0 copy-start.5
  0.8 3.1 %first_send.1 = bf16[16,144,128]{2,1,0:T(8,128)(2,1)} custom-call(s32[16,16]{1,0:T(8,128)} %plane_in_ref.1, s32[16,16]{1,0:T(8,128)} %row_in_ref.1, s32[16,16]{1,0:T(8,128)} %cover_in_ref.1, f32[2,56]{1,0:T(2,128)} %taps_in_ref.1, f32[3072,128]{1,0:T(8,128)} %bitcast.5), custom_call_target="tpu_custom_call" | custom-call | tf_op jit(solution)/shard_map/first_send/pallas_call | solution.py:407
  3.8 0.0 copy-start
  3.9 7.5 %all-to-all-start = ((bf16[16,144,128]{2,1,0:T(8,128)(2,1)}), bf16[16,144,128]{2,1,0:T(8,128)(2,1)S(1)}, u32[]{:S(2)}, u32[]{:S(2)}) async-start(bf16[16,144,128]{2,1,0:T(8,128)(2,1)} %first_send.1), calls=%async_computation | async-start | bytes 1179648 | tf_op jit(solution)/shard_map/all_to_all | solution.py:405
  11.4 0.0 copy-done.2
  11.4 0.0 copy-done.3
  11.4 0.0 copy-done.4
  11.4 0.0 copy-done.6
  11.4 0.0 copy-done.7
  11.4 0.0 copy-done.8
  11.4 0.0 copy-done.9
  11.4 0.0 copy-done.10
  11.4 0.0 copy-done.11
  11.5 0.0 copy-done.12
  11.5 5.7 %tables.1 = (s32[256]{0:T(256)S(1)}, s32[260]{0:T(512)S(1)}, f32[256]{0:T(256)S(1)}) custom-call(s32[2,128]{1,0:T(2,128)S(1)} %bitcast.7, s32[2,128]{1,0:T(2,128)S(1)} %bitcast.8, s32[2,128]{1,0:T(2,128)S(1)} %bitcast.9, s32[128]{0:T(128)S(1)} %copy-done.9, s32[16,16]{1,0:T(8,128)S(1)} %copy-done.2, s32[16,16]{1,0:T(8,128)S(1)} %copy-done.3, ...), custom_call_target="tpu_custom_call" | custom-call | flops 4000000 | bytes 8000000 | tf_op jit(solution)/shard_map/tables/pallas_call | solution.py:430
  17.2 9.8 %all-to-all-done.arrived_ref = bf16[16,144,128]{2,1,0:T(8,128)(2,1)S(1)} async-done(((bf16[16,144,128]{2,1,0:T(8,128)(2,1)}), bf16[16,144,128]{2,1,0:T(8,128)(2,1)S(1)}, u32[]{:S(2)}, u32[]{:S(2)}) %all-to-all-start) | async-done | bytes 589856 | tf_op jit(solution)/shard_map/all_to_all | solution.py:405
  26.9 0.0 copy-done.1
  26.9 0.0 copy-done.5
  26.9 3.2 %blur.2 = (bf16[16,128,128]{2,1,0:T(8,128)(2,1)S(1)}, bf16[32,16,128]{2,1,0:T(8,128)(2,1)S(1)}, bf16[32,16,128]{2,1,0:T(8,128)(2,1)S(1)}) custom-call(s32[256]{0:T(256)S(1)} %get-tuple-element.14.table_ref, f32[128]{0:T(128)S(1)} %copy-done.5, bf16[16,144,128]{2,1,0:T(8,128)(2,1)S(1)} %all-to-all-done.arrived_ref, bf16[128,16,128]{2,1,0:T(8,128)(2,1)S(1)} %copy-done.1), custom_call_target="tpu_custom_call" | custom-call | tf_op jit(solution)/shard_map/blur/pallas_call | solution.py:475
  30.2 18.7 %all_to_all.20.returned_ref = bf16[16,128,128]{2,1,0:T(8,128)(2,1)S(1)} all-to-all(bf16[16,128,128]{2,1,0:T(8,128)(2,1)S(1)} %get-tuple-element.15), channel_id=1, replica_groups=mesh['groups'=2,'sky'=16] {'sky'}, dimensions={0} | all-to-all | bytes 1048576 | tf_op jit(solution)/shard_map/all_to_all | solution.py:405
  48.9 0.0 copy-done
  48.9 2.6 %update.2 = (f32[3088,128]{1,0:T(8,128)S(1)}, bf16[16,128,128]{2,1,0:T(8,128)(2,1)S(1)}) custom-call(s32[260]{0:T(512)S(1)} %get-tuple-element.12.table_ref, f32[256]{0:T(256)S(1)} %get-tuple-element.13.factor_ref, bf16[16,128,128]{2,1,0:T(8,128)(2,1)S(1)} %all_to_all.20.returned_ref, f32[3072,128]{1,0:T(8,128)S(1)} %bitcast.6), custom_call_target="tpu_custom_call" | custom-call | tf_op jit(solution)/shard_map/update/pallas_call | solution.py:494
  51.4 18.4 %all_to_all.21.arrived_ref = bf16[16,128,128]{2,1,0:T(8,128)(2,1)S(1)} all-to-all(bf16[16,128,128]{2,1,0:T(8,128)(2,1)S(1)} %get-tuple-element.16), channel_id=1, replica_groups=mesh['groups'=2,'sky'=16] {'sky'}, dimensions={0} | all-to-all | bytes 1048576 | tf_op jit(solution)/shard_map/all_to_all | solution.py:405
  69.8 3.8 %blur.3 = (bf16[16,128,128]{2,1,0:T(8,128)(2,1)S(1)}, f32[128,16,128]{2,1,0:T(8,128)}) custom-call(s32[256]{0:T(256)S(1)} %get-tuple-element.14.table_ref, f32[128]{0:T(128)S(1)} %copy-done.5, bf16[16,128,128]{2,1,0:T(8,128)(2,1)S(1)} %all_to_all.21.arrived_ref, bf16[128,16,128]{2,1,0:T(8,128)(2,1)S(1)} %copy-done.1, ...), custom_call_target="tpu_custom_call" | custom-call | tf_op jit(solution)/shard_map/blur/pallas_call | solution.py:475
  73.6 18.4 %all_to_all.22.returned_ref = bf16[16,128,128]{2,1,0:T(8,128)(2,1)S(1)} all-to-all(bf16[16,128,128]{2,1,0:T(8,128)(2,1)S(1)} %get-tuple-element.19), channel_id=1, replica_groups=mesh['groups'=2,'sky'=16] {'sky'}, dimensions={0} | all-to-all | bytes 1048576 | tf_op jit(solution)/shard_map/all_to_all | solution.py:405
  91.9 2.8 %update.3 = f32[3072,128]{1,0:T(8,128)} custom-call(s32[260]{0:T(512)S(1)} %get-tuple-element.12.table_ref, f32[256]{0:T(256)S(1)} %get-tuple-element.13.factor_ref, bf16[16,128,128]{2,1,0:T(8,128)(2,1)S(1)} %all_to_all.22.returned_ref, f32[3088,128]{1,0:T(8,128)S(1)} %get-tuple-element.20.model_ref), custom_call_target="tpu_custom_call" | custom-call | tf_op jit(solution)/shard_map/update/pallas_call | solution.py:494
Async XLA Ops:
  0.6 10.7 %copy-start.2 = (s32[16,16]{1,0:T(8,128)S(1)}, s32[16,16]{1,0:T(8,128)}, u32[]{:S(2)}) copy-start(s32[16,16]{1,0:T(8,128)} %plane_in_ref.1) | copy-start | bytes 3076
  0.6 10.7 %copy-start.3 = (s32[16,16]{1,0:T(8,128)S(1)}, s32[16,16]{1,0:T(8,128)}, u32[]{:S(2)}) copy-start(s32[16,16]{1,0:T(8,128)} %row_in_ref.1) | copy-start | bytes 3076
  0.7 10.7 %copy-start.4 = (s32[16,16]{1,0:T(8,128)S(1)}, s32[16,16]{1,0:T(8,128)}, u32[]{:S(2)}) copy-start(s32[16,16]{1,0:T(8,128)} %cover_in_ref.1) | copy-start | bytes 3076
  0.7 10.7 %copy-start.6 = (s32[128,2]{0,1:T(2,128)S(1)}, s32[128,2]{0,1:T(2,128)}, u32[]{:S(2)}) copy-start(s32[128,2]{0,1:T(2,128)} %param.23) | copy-start | bytes 3076
  0.7 10.7 %copy-start.7 = (s32[128,2]{0,1:T(2,128)S(1)}, s32[128,2]{0,1:T(2,128)}, u32[]{:S(2)}) copy-start(s32[128,2]{0,1:T(2,128)} %param.24) | copy-start | bytes 3076
  0.7 10.7 %copy-start.8 = (s32[128,2]{0,1:T(2,128)S(1)}, s32[128,2]{0,1:T(2,128)}, u32[]{:S(2)}) copy-start(s32[128,2]{0,1:T(2,128)} %param.25) | copy-start | bytes 3076
  0.7 10.7 %copy-start.9 = (s32[128]{0:T(128)S(1)}, s32[128]{0:T(128)}, u32[]{:S(2)}) copy-start(s32[128]{0:T(128)} %batch_ref.1) | copy-start | bytes 1540
  0.7 10.7 %copy-start.10 = (f32[6]{0:T(128)S(1)}, f32[6]{0:T(128)}, u32[]{:S(2)}) copy-start(f32[6]{0:T(128)} %step_ref.1) | copy-start | bytes 76
  0.7 10.7 %copy-start.11 = (s32[2]{0:T(128)S(1)}, s32[2]{0:T(128)}, u32[]{:S(2)}) copy-start(s32[2]{0:T(128)} %lo_ref.1) | copy-start | bytes 28
  0.7 10.7 %copy-start.12 = (s32[2]{0:T(128)S(1)}, s32[2]{0:T(128)}, u32[]{:S(2)}) copy-start(s32[2]{0:T(128)} %hi_ref.1) | copy-start | bytes 28
  0.7 26.2 %copy-start.1 = (bf16[128,16,128]{2,1,0:T(8,128)(2,1)S(1)}, bf16[128,16,128]{2,1,0:T(8,128)(2,1)}, u32[]{:S(2)}) copy-start(bf16[128,16,128]{2,1,0:T(8,128)(2,1)} %seen_ref.3) | copy-start | bytes 1572868
  0.7 26.2 %copy-start.5 = (f32[128]{0:T(128)S(1)}, f32[128]{0:T(128)}, u32[]{:S(2)}) copy-start(f32[128]{0:T(128)} %weight_ref.3) | copy-start | bytes 1540
  3.8 45.0 %copy-start = (f32[2,6,256,128]{3,2,1,0:T(8,128)S(1)}, f32[2,6,256,128]{3,2,1,0:T(8,128)}, u32[]{:S(2)}) copy-start(f32[2,6,256,128]{3,2,1,0:T(8,128)} %param.14) | copy-start | bytes 4718596
  3.9 23.1 %all-to-all-start = ((bf16[16,144,128]{2,1,0:T(8,128)(2,1)}), bf16[16,144,128]{2,1,0:T(8,128)(2,1)S(1)}, u32[]{:S(2)}, u32[]{:S(2)}) async-start(bf16[16,144,128]{2,1,0:T(8,128)(2,1)} %first_send.1), calls=%async_computation | async-start | bytes 1179648 | tf_op jit(solution)/shard_map/all_to_all | solution.py:405

commit v12 on v11

--- a/solution.py
+++ b/solution.py
@@ -150,25 +150,35 @@
         send.wait()
 
 
-def update_kernel(bands, tile_rows, height, last, table_ref, factor_ref, returned_ref, model_ref, *rest):
+def update_kernel(bands, tile_rows, height, last, table_ref, factor_ref, returned_ref, *rest):
     if last:
-        new_ref, back_ref, x_ref, saved, *more_refs = rest
+        *model_refs, new_ref, back_ref, x_ref, more_ref, saved = rest
     else:
-        x_ref, out_ref, back_ref, packed_ref, *more_refs = rest
+        *model_refs, x_ref, more_ref, out_ref, back_ref, packed_ref = rest
     peers, rows_each, _ = returned_ref.shape
     capacity = 2 * rows_each // height
     slots = peers * capacity
     total = x_ref.shape[0] - height
     planes = total // tile_rows
     tiles = planes // bands
-    x_ref[:total, :] = model_ref[:total, :]
-    for ref in more_refs:
-        ref[...] = jnp.zeros(ref.shape, F32)
+
+    def clamped(value, pos, tile):
+        inside = (pos >= table_ref[2 * slots + tile]) & (pos < table_ref[2 * slots + tiles + tile])
+        return jnp.where(inside, jnp.maximum(value, 0.0), 0.0)
+
+    pos = lax.broadcasted_iota(I32, (tile_rows, LANES), 0)
+    for p in range(planes):
+        here = slice(p * tile_rows, (p + 1) * tile_rows)
+        if last:
+            x_ref[here, :] = clamped(model_refs[0][here, :] + model_refs[1][here, :], pos, p // bands)
+        else:
+            x_ref[here, :] = model_refs[0][here, :]
+    more_ref[...] = jnp.zeros(more_ref.shape, F32)
     for d in range(peers):
         back_ref[d * rows_each : (d + 1) * rows_each, :] = returned_ref[d].astype(F32)
     place = lax.broadcasted_iota(I32, (height, LANES), 0)
 
-    sums = [x_ref, *more_refs]
+    sums = [x_ref, more_ref] if peers % 2 == 0 else [x_ref]
 
     def some_peers(step, _):
         for c in range(capacity):
@@ -184,29 +194,30 @@
 
     lax.fori_loop(0, peers // len(sums), some_peers, 0)
 
-    pos = lax.broadcasted_iota(I32, (tile_rows, LANES), 0)
-    saves = []
-    for p in range(planes):
-        inside = (pos >= table_ref[slots + p // bands]) & (pos < table_ref[slots + tiles + p // bands])
-        here = slice(p * tile_rows, (p + 1) * tile_rows)
-        new = sum((ref[here, :] for ref in more_refs), x_ref[here, :])
-        x_ref[here, :] = jnp.where(inside, jnp.maximum(new, 0.0), 0.0)
-        if last:
+    if last:
+        saves = []
+        for p in range(planes):
+            here = slice(p * tile_rows, (p + 1) * tile_rows)
+            x_ref[here, :] = clamped(x_ref[here, :] + more_ref[here, :], pos, p // bands)
             rows = pl.ds(p * tile_rows, tile_rows)
             saves.append(pltpu.make_async_copy(x_ref.at[rows, :], new_ref.at[rows, :], saved.at[p]))
             saves[-1].start()
-    if not last:
-
-        def pack(slot, _):
-            first, sent = first_and_sent(table_ref[slot])
-            packed_ref[pl.ds(sent, height), :] = x_ref[pl.ds(first, height), :]
-            return 0
-
-        lax.fori_loop(0, slots, pack, 0, unroll=16)
-        for d in range(peers):
-            out_ref[d, :, :] = packed_ref[d * rows_each : (d + 1) * rows_each, :].astype(BF16)
-    for save in saves:
-        save.wait()
+        for save in saves:
+            save.wait()
+        return
+
+    def pack(slot, _):
+        first, sent = first_and_sent(table_ref[slot])
+        here = pl.ds(first, height)
+        bounds = table_ref[slots + slot]
+        inside = (place >= low(bounds)) & (place < high(bounds))
+        piece = jnp.where(inside, jnp.maximum(x_ref[here, :] + more_ref[here, :], 0.0), 0.0)
+        packed_ref[pl.ds(sent, height), :] = piece
+        return 0
+
+    lax.fori_loop(0, slots, pack, 0, unroll=16)
+    for d in range(peers):
+        out_ref[d] = packed_ref[d * rows_each : (d + 1) * rows_each, :].astype(BF16)
 
 
 def tables_kernel(
@@ -230,6 +241,7 @@
     length_ref,
     begin_ref,
     scale_ref,
+    foot_ref,
 ):
     pieces, exposures = slot_ref.shape
     peers, capacity = plane_ref.shape
@@ -240,12 +252,15 @@
         return 0
 
     lax.fori_loop(0, slots, clear, 0, unroll=16)
-    for p in range(scale_ref.shape[0]):
+    planes = scale_ref.shape[0]
+    for p in range(planes):
         scale_ref[p] = step_ref[p % bands]
+        foot_ref[p] = lo_ref[p // bands]
+        foot_ref[planes + p] = hi_ref[p // bands]
     tiles = lo_ref.shape[0]
     for t in range(tiles):
-        update_ref[slots + t] = lo_ref[t]
-        update_ref[slots + tiles + t] = hi_ref[t]
+        update_ref[2 * slots + t] = lo_ref[t]
+        update_ref[2 * slots + tiles + t] = hi_ref[t]
 
     def measure(e, _):
         for k in range(pieces):
@@ -264,7 +279,11 @@
             at = at + length_ref[s]
             p = jnp.maximum(plane_ref[o, c], 0)
             cover = cover_ref[o, c]
-            update_ref[s] = (p * tile_rows + row_ref[o, c]) | (sent << PLACE) | (cover << 2 * PLACE)
+            row = row_ref[o, c]
+            update_ref[s] = (p * tile_rows + row) | (sent << PLACE) | (cover << 2 * PLACE)
+            lo = jnp.clip(foot_ref[p] - row, 0, height)
+            hi = jnp.clip(foot_ref[planes + p] - row, 0, height)
+            update_ref[slots + s] = lo | (hi << SHIFT)
             factor_ref[s] = scale_ref[p]
             sent = sent + cover
         return 0
@@ -296,7 +315,7 @@
     *rest,
 ):
     if last:
-        blur_ref, back_ref, out_ref, residual_out_ref, rows_ref, packed_ref, held_ref, residual_ref, sent = rest
+        blur_ref, back_ref, out_ref, residual_ref, rows_ref, packed_ref, held_ref = rest
     else:
         out_ref, blur_ref, back_ref, rows_ref, packed_ref, held_ref, bank_ref = rest
     peers, rows_each, _ = out_ref.shape
@@ -361,16 +380,23 @@
 
     for e in range(exposures):
         blur(e)
-    if last:
-        send = pltpu.make_async_copy(residual_ref, residual_out_ref, sent)
-        send.start()
     for e in range(exposures):
         correlate(e)
     for o in range(peers):
         at = height + o * rows_each
         out_ref[o, :, :] = packed_ref[at : at + rows_each, :].astype(BF16)
-    if last:
-        send.wait()
+
+
+def save_kernel(from_ref, to_ref, sems):
+    parts = sems.shape[0]
+    some = from_ref.shape[0] // parts
+    copies = []
+    for n in range(parts):
+        here = pl.ds(n * some, some)
+        copies.append(pltpu.make_async_copy(from_ref.at[here], to_ref.at[here], sems.at[n]))
+        copies[-1].start()
+    for copy in copies:
+        copy.wait()
 
 
 def body(
@@ -431,7 +457,7 @@
         functools.partial(tables_kernel, tile_rows, bands, height, rows_each),
         out_shape=(
             jax.ShapeDtypeStruct((pieces * count,), I32),
-            jax.ShapeDtypeStruct((slots + 2 * tile_count,), I32),
+            jax.ShapeDtypeStruct((2 * slots + 2 * tile_count,), I32),
             jax.ShapeDtypeStruct((slots,), F32),
         ),
         in_specs=[smem()] * 10,
@@ -440,6 +466,7 @@
             pltpu.SMEM((slots + 1,), I32),
             pltpu.SMEM((slots,), I32),
             pltpu.SMEM((tile_count * bands,), F32),
+            pltpu.SMEM((2 * tile_count * bands,), I32),
         ],
         compiler_params=params(),
         cost_estimate=pl.CostEstimate(flops=4_000_000, bytes_accessed=8_000_000, transcendentals=0),
@@ -457,6 +484,7 @@
         foot_hi,
     )
     operators = []
+    x = [x]
     for sweep in range(ITERS):
         last = sweep == ITERS - 1
         rows_shape = jax.ShapeDtypeStruct((peers, rows_each, columns), BF16)
@@ -466,8 +494,7 @@
             pltpu.VMEM((count * height, columns), BF16),
         ]
         if last:
-            scratch += [pltpu.VMEM(exposures.shape, F32), pltpu.SemaphoreType.DMA]
-            out_shape, out_specs = (rows_shape, jax.ShapeDtypeStruct(exposures.shape, F32)), (vmem(), hbm())
+            out_shape, out_specs = (rows_shape, jax.ShapeDtypeStruct(exposures.shape, F32)), (vmem(), vmem())
         else:
             scratch.append(pltpu.VMEM((peers * extra, columns), F32))
             operator_shape = jax.ShapeDtypeStruct((peers * batches_each, height, columns), BF16)
@@ -485,29 +512,37 @@
         returned = swap(outgoing)
         new_shape = jax.ShapeDtypeStruct((total, columns), F32)
         padded = (total + height, columns)
-        scratch = [pltpu.VMEM((peers * rows_each + height, columns), F32)]
+        back = pltpu.VMEM((peers * rows_each + height, columns), F32)
         if last:
-            scratch += [pltpu.VMEM(padded, F32), pltpu.SemaphoreType.DMA((tile_count * bands,))]
+            out_shape, out_specs = jax.ShapeDtypeStruct((total, columns), F32), hbm()
+            scratch = [back, pltpu.VMEM(padded, F32), pltpu.VMEM(padded, F32)]
+            scratch.append(pltpu.SemaphoreType.DMA((tile_count * bands,)))
         else:
-            scratch.append(pltpu.VMEM((peers * rows_each + height, columns), F32))
-        sums = max(n for n in (1, 2) if peers % n == 0)
+            out_shape = (jax.ShapeDtypeStruct(padded, F32), jax.ShapeDtypeStruct(padded, F32), rows_shape)
+            out_specs, scratch = (vmem(),) * 3, [back, back]
         res = pl.pallas_call(
             functools.partial(update_kernel, bands, tile_rows, height, last),
-            out_shape=jax.ShapeDtypeStruct((total, columns), F32)
-            if last
-            else (jax.ShapeDtypeStruct(padded, F32), rows_shape),
-            in_specs=[smem()] * 2 + [vmem(), vmem()],
-            out_specs=hbm() if last else (vmem(), vmem()),
-            scratch_shapes=scratch + [pltpu.VMEM(padded, F32)] * (sums - 1),
+            out_shape=out_shape,
+            in_specs=[smem()] * 2 + [vmem()] * (1 + len(x)),
+            out_specs=out_specs,
+            scratch_shapes=scratch,
             compiler_params=params(),
             name="update",
-        )(update_table, factors, returned, x)
-        if last:
-            x = res
-        else:
-            x, outbound = res
+        )(update_table, factors, returned, *x)
+        if not last:
+            *x, outbound = res
             arrived = swap(outbound)
-    return (x.reshape(model.shape), others[0])
+    residual = pl.pallas_call(
+        save_kernel,
+        out_shape=jax.ShapeDtypeStruct(exposures.shape, F32),
+        in_specs=[vmem()],
+        out_specs=hbm(),
+        scratch_shapes=[pltpu.SemaphoreType.DMA((max(n for n in (1, 2, 4) if count % n == 0),))],
+        compiler_params=params(),
+        cost_estimate=pl.CostEstimate(flops=4_000_000, bytes_accessed=8_000_000, transcendentals=0),
+        name="save",
+    )(others[0])
+    return (res.reshape(model.shape), residual)
 
 
 def solution(mesh):

time: 95.1 us -> 101 us (1.062)
  blocking collectives: 55.4 us -> 37 us
  waiting for transfers between devices: 9.76 us -> 20.9 us
  local copies, waits for them, and re-layouts: 0.06 us -> 5.99 us
  starting transfers between devices: 7.5 us -> 11.7 us
  Pallas kernels: 21.2 us -> 23.5 us
    all_to_all x3 -> x2, blocking collectives: 55.4 us -> 37 us  [swap(): return lax.all_to_all(a, 'sky', split_axis=0, concat_axis=0, tiled=True)]
    all_to_all x1 -> x2, waiting for transfers between devices: 9.76 us -> 20.9 us  [swap(): return lax.all_to_all(a, 'sky', split_axis=0, concat_axis=0, tiled=True)]
    unnamed x26 -> x38, local copies, waits for them, and re-layouts: 0.06 us -> 5.99 us
    all_to_all x1 -> x2, starting transfers between devices: 7.5 us -> 11.7 us  [swap(): return lax.all_to_all(a, 'sky', split_axis=0, concat_axis=0, tiled=True)]
    pallas_call x1, Pallas kernels: 5.68 us -> 6.79 us  [body(): pl.pallas_call(functools.partial(tables_kernel, tile_rows, bands, height,...]
  transfers between devices with their start and end apart: 1 -> 2, of which waited for: 1 -> 2; matrix products, arithmetic and copies ran while one was open for 0% -> 0% of each run, Pallas kernels for 6% -> 8%
where the time goes in v12:
time: 101 us; the launch traced here: 100 us
  blocking collectives  37 us (37%)
  Pallas kernels  23.5 us (23%)
  waiting for transfers between devices  20.9 us (21%)
  starting transfers between devices  11.7 us (12%)
  local copies, waits for them, and re-layouts  5.99 us (6%)
    all_to_all x2, blocking collectives, swap(): return lax.all_to_all(a, 'sky', split_axis=0, concat_axis=0, tiled=True)  37 us
    all_to_all x2, waiting for transfers between devices, swap(): return lax.all_to_all(a, 'sky', split_axis=0, concat_axis=0, tiled=True)  20.9 us
    all_to_all x2, starting transfers between devices, swap(): return lax.all_to_all(a, 'sky', split_axis=0, concat_axis=0, tiled=True)  11.7 us
    pallas_call x2, Pallas kernels, body(): pl.pallas_call(functools.partial(blur_kernel, height, pieces, batches_eac...  6.95 us
    pallas_call x1, Pallas kernels, body(): pl.pallas_call(functools.partial(tables_kernel, tile_rows, bands, height,...  6.79 us
    unnamed x38, local copies, waits for them, and re-layouts  5.99 us
    pallas_call x2, Pallas kernels, body(): pl.pallas_call(functools.partial(update_kernel, bands, tile_rows, height,...  5.73 us
    pallas_call x1, Pallas kernels, body(): pl.pallas_call(functools.partial(first_send_kernel, tile_rows, height, ro...  3.08 us
  transfers between devices with their start and end apart: 2, of which 2 were waited for; matrix products, arithmetic and copies ran while one was open for 0% of the time, Pallas kernels for 8%

profile of v12, /device:TPU:0, one launch (start us, length us, event | category | flops | bytes accessed | tf_op | source)
XLA Modules:
  0.0 100.1 jit_solution(3872195492015486254)
XLA Ops:
  0.6 0.0 copy-start.8
  0.6 0.0 copy-start.9
  0.7 0.0 copy-start.10
  0.7 0.0 copy-start.12
  0.7 0.0 copy-start.13
  0.7 0.0 copy-start.14
  0.7 0.0 copy-start.15
  0.7 0.0 copy-start.16
  0.7 0.0 copy-start.17
  0.7 0.0 copy-start.18
  0.7 0.0 copy-start.1
  0.7 0.0 copy-start.11
  0.8 3.1 %first_send.1 = bf16[16,144,128]{2,1,0:T(8,128)(2,1)} custom-call(s32[16,16]{1,0:T(8,128)} %plane_in_ref.1, s32[16,16]{1,0:T(8,128)} %row_in_ref.1, s32[16,16]{1,0:T(8,128)} %cover_in_ref.1, f32[2,56]{1,0:T(2,128)} %taps_in_ref.1, f32[3072,128]{1,0:T(8,128)} %bitcast.5), custom_call_target="tpu_custom_call" | custom-call | tf_op jit(solution)/shard_map/first_send/pallas_call | solution.py:433
  3.8 0.0 copy-start
  3.9 7.5 %all-to-all-start = ((bf16[16,144,128]{2,1,0:T(8,128)(2,1)}), bf16[16,144,128]{2,1,0:T(8,128)(2,1)S(1)}, u32[]{:S(2)}, u32[]{:S(2)}) async-start(bf16[16,144,128]{2,1,0:T(8,128)(2,1)} %first_send.1), calls=%async_computation | async-start | bytes 1179648 | tf_op jit(solution)/shard_map/all_to_all | solution.py:431
  11.4 0.0 copy-done.8
  11.4 0.0 copy-done.9
  11.4 0.0 copy-done.10
  11.4 0.0 copy-done.12
  11.4 0.0 copy-done.13
  11.4 0.0 copy-done.14
  11.4 0.0 copy-done.15
  11.4 0.0 copy-done.16
  11.4 0.0 copy-done.17
  11.5 0.0 copy-done.18
  11.5 6.8 %tables.1 = (s32[256]{0:T(256)S(1)}, s32[516]{0:T(1024)S(1)}, f32[256]{0:T(256)S(1)}) custom-call(s32[2,128]{1,0:T(2,128)S(1)} %bitcast.7, s32[2,128]{1,0:T(2,128)S(1)} %bitcast.8, s32[2,128]{1,0:T(2,128)S(1)} %bitcast.9, s32[128]{0:T(128)S(1)} %copy-done.15, s32[16,16]{1,0:T(8,128)S(1)} %copy-done.8, s32[16,16]{1,0:T(8,128)S(1)} %copy-done.9, ...), custom_call_target="tpu_custom_call" | custom-call | flops 4000000 | bytes 8000000 | tf_op jit(solution)/shard_map/tables/pallas_call | solution.py:456
  18.3 8.7 %all-to-all-done.arrived_ref = bf16[16,144,128]{2,1,0:T(8,128)(2,1)S(1)} async-done(((bf16[16,144,128]{2,1,0:T(8,128)(2,1)}), bf16[16,144,128]{2,1,0:T(8,128)(2,1)S(1)}, u32[]{:S(2)}, u32[]{:S(2)}) %all-to-all-start) | async-done | bytes 589856 | tf_op jit(solution)/shard_map/all_to_all | solution.py:431
  26.9 0.0 copy-done.1
  26.9 0.0 copy-done.11
  26.9 3.3 %blur.2 = (bf16[16,128,128]{2,1,0:T(8,128)(2,1)S(1)}, bf16[32,16,128]{2,1,0:T(8,128)(2,1)S(1)}, bf16[32,16,128]{2,1,0:T(8,128)(2,1)S(1)}) custom-call(s32[256]{0:T(256)S(1)} %get-tuple-element.15.table_ref, f32[128]{0:T(128)S(1)} %copy-done.11, bf16[16,144,128]{2,1,0:T(8,128)(2,1)S(1)} %all-to-all-done.arrived_ref, bf16[128,16,128]{2,1,0:T(8,128)(2,1)S(1)} %copy-done.1), custom_call_target="tpu_custom_call" | custom-call | tf_op jit(solution)/shard_map/blur/pallas_call | solution.py:502
  30.2 18.7 %all_to_all.20.returned_ref = bf16[16,128,128]{2,1,0:T(8,128)(2,1)S(1)} all-to-all(bf16[16,128,128]{2,1,0:T(8,128)(2,1)S(1)} %get-tuple-element.16), channel_id=1, replica_groups=mesh['groups'=2,'sky'=16] {'sky'}, dimensions={0} | all-to-all | bytes 1048576 | tf_op jit(solution)/shard_map/all_to_all | solution.py:431
  48.9 0.0 copy-done
  48.9 2.6 %update.2 = (f32[3088,128]{1,0:T(8,128)S(1)}, f32[3088,128]{1,0:T(8,128)S(1)}, bf16[16,128,128]{2,1,0:T(8,128)(2,1)S(1)}) custom-call(s32[516]{0:T(1024)S(1)} %get-tuple-element.13.table_ref, f32[256]{0:T(256)S(1)} %get-tuple-element.14.factor_ref, bf16[16,128,128]{2,1,0:T(8,128)(2,1)S(1)} %all_to_all.20.returned_ref, f32[3072,128]{1,0:T(8,128)S(1)} %bitcast.6), custom_call_target="tpu_custom_call" | custom-call | tf_op jit(solution)/shard_map/update/pallas_call | solution.py:523
  51.4 0.0 copy-start.2
  51.4 1.2 %copy-done.2 = f32[3088,128]{1,0:T(8,128)} copy-done((f32[3088,128]{1,0:T(8,128)}, f32[3088,128]{1,0:T(8,128)S(1)}, u32[]{:S(2)}) %copy-start.2) | copy-done | bytes 1581080
  52.6 0.0 copy-start.4
  52.6 1.1 %copy-done.4 = f32[3088,128]{1,0:T(8,128)} copy-done((f32[3088,128]{1,0:T(8,128)}, f32[3088,128]{1,0:T(8,128)S(1)}, u32[]{:S(2)}) %copy-start.4) | copy-done | bytes 1581080
  53.8 18.4 %all_to_all.21.arrived_ref = bf16[16,128,128]{2,1,0:T(8,128)(2,1)S(1)} all-to-all(bf16[16,128,128]{2,1,0:T(8,128)(2,1)S(1)} %get-tuple-element.17), channel_id=1, replica_groups=mesh['groups'=2,'sky'=16] {'sky'}, dimensions={0} | all-to-all | bytes 1048576 | tf_op jit(solution)/shard_map/all_to_all | solution.py:431
  72.1 3.7 %blur.3 = (bf16[16,128,128]{2,1,0:T(8,128)(2,1)}, f32[128,16,128]{2,1,0:T(8,128)S(1)}) custom-call(s32[256]{0:T(256)S(1)} %get-tuple-element.15.table_ref, f32[128]{0:T(128)S(1)} %copy-done.11, bf16[16,128,128]{2,1,0:T(8,128)(2,1)S(1)} %all_to_all.21.arrived_ref, bf16[128,16,128]{2,1,0:T(8,128)(2,1)S(1)} %copy-done.1, ...), custom_call_target="tpu_custom_call" | custom-call | tf_op jit(solution)/shard_map/blur/pallas_call | solution.py:502
  75.8 0.0 copy-start.6
  75.8 1.0 copy-done.6
  76.8 0.0 copy-start.3
  76.8 4.2 %all-to-all-start.3 = ((bf16[16,128,128]{2,1,0:T(8,128)(2,1)}), bf16[16,128,128]{2,1,0:T(8,128)(2,1)S(1)}, u32[]{:S(2)}, u32[]{:S(2)}) async-start(bf16[16,128,128]{2,1,0:T(8,128)(2,1)} %get-tuple-element.20), calls=%async_computation.3 | async-start | bytes 1048576 | tf_op jit(solution)/shard_map/all_to_all | solution.py:431
  81.0 0.0 copy-start.7
  81.0 1.2 %copy-done.7 = f32[128,16,128]{2,1,0:T(8,128)S(1)} copy-done((f32[128,16,128]{2,1,0:T(8,128)S(1)}, f32[128,16,128]{2,1,0:T(8,128)}, u32[]{:S(2)}) %copy-start.7) | copy-done | bytes 1048600
  82.3 1.0 save.1
  83.3 12.2 %all-to-all-done.3.returned_ref = bf16[16,128,128]{2,1,0:T(8,128)(2,1)S(1)} async-done(((bf16[16,128,128]{2,1,0:T(8,128)(2,1)}), bf16[16,128,128]{2,1,0:T(8,128)(2,1)S(1)}, u32[]{:S(2)}, u32[]{:S(2)}) %all-to-all-start.3) | async-done | bytes 524320 | tf_op jit(solution)/shard_map/all_to_all | solution.py:431
  95.5 0.0 copy-done.3
  95.5 0.0 copy-start.5
  95.5 1.4 %copy-done.5 = f32[3088,128]{1,0:T(8,128)S(1)} copy-done((f32[3088,128]{1,0:T(8,128)S(1)}, f32[3088,128]{1,0:T(8,128)}, u32[]{:S(2)}) %copy-start.5) | copy-done | bytes 1581080
  96.9 3.2 %update.3 = f32[3072,128]{1,0:T(8,128)} custom-call(s32[516]{0:T(1024)S(1)} %get-tuple-element.13.table_ref, f32[256]{0:T(256)S(1)} %get-tuple-element.14.factor_ref, bf16[16,128,128]{2,1,0:T(8,128)(2,1)S(1)} %all-to-all-done.3.returned_ref, f32[3088,128]{1,0:T(8,128)S(1)} %copy-done.3, f32[3088,128]{1,0:T(8,128)S(1)} %copy-done.5), custom_call_target="tpu_custom_call" | custom-call | tf_op jit(solution)/shard_map/update/pallas_call | solution.py:523
Async XLA Ops:
  0.6 10.7 %copy-start.8 = (s32[16,16]{1,0:T(8,128)S(1)}, s32[16,16]{1,0:T(8,128)}, u32[]{:S(2)}) copy-start(s32[16,16]{1,0:T(8,128)} %plane_in_ref.1) | copy-start | bytes 3076
  0.6 10.7 %copy-start.9 = (s32[16,16]{1,0:T(8,128)S(1)}, s32[16,16]{1,0:T(8,128)}, u32[]{:S(2)}) copy-start(s32[16,16]{1,0:T(8,128)} %row_in_ref.1) | copy-start | bytes 3076
  0.7 10.7 %copy-start.10 = (s32[16,16]{1,0:T(8,128)S(1)}, s32[16,16]{1,0:T(8,128)}, u32[]{:S(2)}) copy-start(s32[16,16]{1,0:T(8,128)} %cover_in_ref.1) | copy-start | bytes 3076
  0.7 10.7 %copy-start.12 = (s32[128,2]{0,1:T(2,128)S(1)}, s32[128,2]{0,1:T(2,128)}, u32[]{:S(2)}) copy-start(s32[128,2]{0,1:T(2,128)} %param.23) | copy-start | bytes 3076
  0.7 10.7 %copy-start.13 = (s32[128,2]{0,1:T(2,128)S(1)}, s32[128,2]{0,1:T(2,128)}, u32[]{:S(2)}) copy-start(s32[128,2]{0,1:T(2,128)} %param.24) | copy-start | bytes 3076
  0.7 10.7 %copy-start.14 = (s32[128,2]{0,1:T(2,128)S(1)}, s32[128,2]{0,1:T(2,128)}, u32[]{:S(2)}) copy-start(s32[128,2]{0,1:T(2,128)} %param.25) | copy-start | bytes 3076
  0.7 10.7 %copy-start.15 = (s32[128]{0:T(128)S(1)}, s32[128]{0:T(128)}, u32[]{:S(2)}) copy-start(s32[128]{0:T(128)} %batch_ref.1) | copy-start | bytes 1540
  0.7 10.7 %copy-start.16 = (f32[6]{0:T(128)S(1)}, f32[6]{0:T(128)}, u32[]{:S(2)}) copy-start(f32[6]{0:T(128)} %step_ref.1) | copy-start | bytes 76
  0.7 10.7 %copy-start.17 = (s32[2]{0:T(128)S(1)}, s32[2]{0:T(128)}, u32[]{:S(2)}) copy-start(s32[2]{0:T(128)} %lo_ref.1) | copy-start | bytes 28
  0.7 10.7 %copy-start.18 = (s32[2]{0:T(128)S(1)}, s32[2]{0:T(128)}, u32[]{:S(2)}) copy-start(s32[2]{0:T(128)} %hi_ref.1) | copy-start | bytes 28
  0.7 26.2 %copy-start.1 = (bf16[128,16,128]{2,1,0:T(8,128)(2,1)S(1)}, bf16[128,16,128]{2,1,0:T(8,128)(2,1)}, u32[]{:S(2)}) copy-start(bf16[128,16,128]{2,1,0:T(8,128)(2,1)} %seen_ref.3) | copy-start | bytes 1572868
  0.7 26.2 %copy-start.11 = (f32[128]{0:T(128)S(1)}, f32[128]{0:T(128)}, u32[]{:S(2)}) copy-start(f32[128]{0:T(128)} %weight_ref.3) | copy-start | bytes 1540
  3.8 45.0 %copy-start = (f32[2,6,256,128]{3,2,1,0:T(8,128)S(1)}, f32[2,6,256,128]{3,2,1,0:T(8,128)}, u32[]{:S(2)}) copy-start(f32[2,6,256,128]{3,2,1,0:T(8,128)} %param.14) | copy-start | bytes 4718596
  3.9 23.1 %all-to-all-start = ((bf16[16,144,128]{2,1,0:T(8,128)(2,1)}), bf16[16,144,128]{2,1,0:T(8,128)(2,1)S(1)}, u32[]{:S(2)}, u32[]{:S(2)}) async-start(bf16[16,144,128]{2,1,0:T(8,128)(2,1)} %first_send.1), calls=%async_computation | async-start | bytes 1179648 | tf_op jit(solution)/shard_map/all_to_all | solution.py:431
  51.4 1.2 %copy-start.2 = (f32[3088,128]{1,0:T(8,128)}, f32[3088,128]{1,0:T(8,128)S(1)}, u32[]{:S(2)}) copy-start(f32[3088,128]{1,0:T(8,128)S(1)} %get-tuple-element.21.rest_0_) | copy-start | bytes 4743172
  52.6 1.2 %copy-start.4 = (f32[3088,128]{1,0:T(8,128)}, f32[3088,128]{1,0:T(8,128)S(1)}, u32[]{:S(2)}) copy-start(f32[3088,128]{1,0:T(8,128)S(1)} %get-tuple-element.22.rest_1_) | copy-start | bytes 4743172
  75.8 1.0 copy-start.6
  76.8 18.7 %copy-start.3 = (f32[3088,128]{1,0:T(8,128)S(1)}, f32[3088,128]{1,0:T(8,128)}, u32[]{:S(2)}) copy-start(f32[3088,128]{1,0:T(8,128)} %copy-done.2) | copy-start | bytes 4743172
  76.8 18.7 %all-to-all-start.3 = ((bf16[16,128,128]{2,1,0:T(8,128)(2,1)}), bf16[16,128,128]{2,1,0:T(8,128)(2,1)S(1)}, u32[]{:S(2)}, u32[]{:S(2)}) async-start(bf16[16,128,128]{2,1,0:T(8,128)(2,1)} %get-tuple-element.20), calls=%async_computation.3 | async-start | bytes 1048576 | tf_op jit(solution)/shard_map/all_to_all | solution.py:431
  81.0 1.2 %copy-start.7 = (f32[128,16,128]{2,1,0:T(8,128)S(1)}, f32[128,16,128]{2,1,0:T(8,128)}, u32[]{:S(2)}) copy-start(f32[128,16,128]{2,1,0:T(8,128)} %copy-done.6) | copy-start | bytes 3145732
  95.5 1.4 %copy-start.5 = (f32[3088,128]{1,0:T(8,128)S(1)}, f32[3088,128]{1,0:T(8,128)}, u32[]{:S(2)}) copy-start(f32[3088,128]{1,0:T(8,128)} %copy-done.4) | copy-start | bytes 4743172

commit v13 on v11

--- a/solution.py
+++ b/solution.py
@@ -58,7 +58,7 @@
             at = at + cover_ref[d, c]
         return 0
 
-    lax.fori_loop(begin, begin + count, peer, 0, unroll=2)
+    lax.fori_loop(begin, begin + count, peer, 0, unroll=min(4, count))
 
 
 def bank_rows(taps, height):
@@ -80,17 +80,16 @@
         )
         return picked[:count] + picked[count : 2 * count] + picked[2 * count :]
 
-    k, l = grid(width)
-    unit = taps / select(taps, k // TAPS == l // TAPS)
     k, l = grid(2 * NPSF * LANES)
     mirror, j, l = l // (NPSF * LANES), l // LANES % NPSF, (l + HALF) % LANES
     i, t = l // height, l % height
     valid = (i < TAPS) & (t < TAPS)
     row_tap = j * TAPS + jnp.where(mirror == 1, t, TAPS - 1 - t)
     col_tap = (NPSF + j) * TAPS + jnp.where(mirror == 1, TAPS - 1 - i, i)
-    row_part = select(unit, valid & (k == row_tap))
-    col_part = select(unit, valid & (k == col_tap))
-    product = row_part * col_part * (1.0 / NPSF)
+    picked = select(taps, valid & (k == row_tap)) * select(taps, valid & (k == col_tap))
+    k, l = grid(NPSF * LANES)
+    whole = select(taps, k // TAPS == l // LANES) * select(taps, k // TAPS == NPSF + l // LANES)
+    product = picked / (jnp.concatenate([whole, whole], axis=1) * NPSF)
     return [
         sum(product[:, (m * NPSF + j) * LANES : (m * NPSF + j + 1) * LANES] for j in range(NPSF)) for m in range(2)
     ]
@@ -182,7 +181,7 @@
                 ref[here, :] = ref[here, :] - factor_ref[slot] * piece
         return 0
 
-    lax.fori_loop(0, peers // len(sums), some_peers, 0)
+    lax.fori_loop(0, peers // len(sums), some_peers, 0, unroll=2)
 
     pos = lax.broadcasted_iota(I32, (tile_rows, LANES), 0)
     saves = []
@@ -202,7 +201,7 @@
             packed_ref[pl.ds(sent, height), :] = x_ref[pl.ds(first, height), :]
             return 0
 
-        lax.fori_loop(0, slots, pack, 0, unroll=16)
+        lax.fori_loop(0, slots, pack, 0, unroll=64)
         for d in range(peers):
             out_ref[d, :, :] = packed_ref[d * rows_each : (d + 1) * rows_each, :].astype(BF16)
     for save in saves:
@@ -322,7 +321,7 @@
                     ).astype(BF16)
             return 0
 
-        lax.fori_loop(0, peers, operators, 0, unroll=4)
+        lax.fori_loop(0, peers, operators, 0, unroll=min(16, peers))
 
     def shifted(x):
         parts = []

time: 95.1 us -> 94.4 us (level)
  no operation moved by 1% of the time
where the time goes in v13:
time: 94.4 us; the launch traced here: 94.1 us
  blocking collectives  55.4 us (59%)
  Pallas kernels  20.4 us (22%)
  waiting for transfers between devices  9.76 us (10%)
  starting transfers between devices  7.5 us (8%)
    all_to_all x3, blocking collectives, swap(): return lax.all_to_all(a, 'sky', split_axis=0, concat_axis=0, tiled=True)  55.4 us
    all_to_all x1, waiting for transfers between devices, swap(): return lax.all_to_all(a, 'sky', split_axis=0, concat_axis=0, tiled=True)  9.76 us
    all_to_all x1, starting transfers between devices, swap(): return lax.all_to_all(a, 'sky', split_axis=0, concat_axis=0, tiled=True)  7.5 us
    pallas_call x2, Pallas kernels, body(): pl.pallas_call(functools.partial(blur_kernel, height, pieces, batches_eac...  6.63 us
    pallas_call x1, Pallas kernels, body(): pl.pallas_call(functools.partial(tables_kernel, tile_rows, bands, height,...  5.68 us
    pallas_call x2, Pallas kernels, body(): pl.pallas_call(functools.partial(update_kernel, bands, tile_rows, height,...  5.27 us
    pallas_call x1, Pallas kernels, body(): pl.pallas_call(functools.partial(first_send_kernel, tile_rows, height, ro...  2.86 us
  transfers between devices with their start and end apart: 1, of which 1 were waited for; matrix products, arithmetic and copies ran while one was open for 0% of the time, Pallas kernels for 6%

profile of v13, /device:TPU:0, one launch (start us, length us, event | category | flops | bytes accessed | tf_op | source)
XLA Modules:
  0.0 94.1 jit_solution(7009250341861105683)
XLA Ops:
  0.6 0.0 copy-start.2
  0.6 0.0 copy-start.3
  0.7 0.0 copy-start.4
  0.7 0.0 copy-start.6
  0.7 0.0 copy-start.7
  0.7 0.0 copy-start.8
  0.7 0.0 copy-start.9
  0.7 0.0 copy-start.10
  0.7 0.0 copy-start.11
  0.7 0.0 copy-start.12
  0.7 0.0 copy-start.1
  0.7 0.0 copy-start.5
  0.8 2.9 %first_send.1 = bf16[16,144,128]{2,1,0:T(8,128)(2,1)} custom-call(s32[16,16]{1,0:T(8,128)} %plane_in_ref.1, s32[16,16]{1,0:T(8,128)} %row_in_ref.1, s32[16,16]{1,0:T(8,128)} %cover_in_ref.1, f32[2,56]{1,0:T(2,128)} %taps_in_ref.1, f32[3072,128]{1,0:T(8,128)} %bitcast.5), custom_call_target="tpu_custom_call" | custom-call | tf_op jit(solution)/shard_map/first_send/pallas_call | solution.py:406
  3.6 0.0 copy-start
  3.6 7.5 %all-to-all-start = ((bf16[16,144,128]{2,1,0:T(8,128)(2,1)}), bf16[16,144,128]{2,1,0:T(8,128)(2,1)S(1)}, u32[]{:S(2)}, u32[]{:S(2)}) async-start(bf16[16,144,128]{2,1,0:T(8,128)(2,1)} %first_send.1), calls=%async_computation | async-start | bytes 1179648 | tf_op jit(solution)/shard_map/all_to_all | solution.py:404
  11.1 0.0 copy-done.2
  11.2 0.0 copy-done.3
  11.2 0.0 copy-done.4
  11.2 0.0 copy-done.6
  11.2 0.0 copy-done.7
  11.2 0.0 copy-done.8
  11.2 0.0 copy-done.9
  11.2 0.0 copy-done.10
  11.2 0.0 copy-done.11
  11.2 0.0 copy-done.12
  11.2 5.7 %tables.1 = (s32[256]{0:T(256)S(1)}, s32[260]{0:T(512)S(1)}, f32[256]{0:T(256)S(1)}) custom-call(s32[2,128]{1,0:T(2,128)S(1)} %bitcast.7, s32[2,128]{1,0:T(2,128)S(1)} %bitcast.8, s32[2,128]{1,0:T(2,128)S(1)} %bitcast.9, s32[128]{0:T(128)S(1)} %copy-done.9, s32[16,16]{1,0:T(8,128)S(1)} %copy-done.2, s32[16,16]{1,0:T(8,128)S(1)} %copy-done.3, ...), custom_call_target="tpu_custom_call" | custom-call | flops 4000000 | bytes 8000000 | tf_op jit(solution)/shard_map/tables/pallas_call | solution.py:429
  16.9 9.8 %all-to-all-done.arrived_ref = bf16[16,144,128]{2,1,0:T(8,128)(2,1)S(1)} async-done(((bf16[16,144,128]{2,1,0:T(8,128)(2,1)}), bf16[16,144,128]{2,1,0:T(8,128)(2,1)S(1)}, u32[]{:S(2)}, u32[]{:S(2)}) %all-to-all-start) | async-done | bytes 589856 | tf_op jit(solution)/shard_map/all_to_all | solution.py:404
  26.7 0.0 copy-done.1
  26.7 0.0 copy-done.5
  26.7 2.9 %blur.2 = (bf16[16,128,128]{2,1,0:T(8,128)(2,1)S(1)}, bf16[32,16,128]{2,1,0:T(8,128)(2,1)S(1)}, bf16[32,16,128]{2,1,0:T(8,128)(2,1)S(1)}) custom-call(s32[256]{0:T(256)S(1)} %get-tuple-element.14.table_ref, f32[128]{0:T(128)S(1)} %copy-done.5, bf16[16,144,128]{2,1,0:T(8,128)(2,1)S(1)} %all-to-all-done.arrived_ref, bf16[128,16,128]{2,1,0:T(8,128)(2,1)S(1)} %copy-done.1), custom_call_target="tpu_custom_call" | custom-call | tf_op jit(solution)/shard_map/blur/pallas_call | solution.py:474
  29.6 18.7 %all_to_all.20.returned_ref = bf16[16,128,128]{2,1,0:T(8,128)(2,1)S(1)} all-to-all(bf16[16,128,128]{2,1,0:T(8,128)(2,1)S(1)} %get-tuple-element.15), channel_id=1, replica_groups=mesh['groups'=2,'sky'=16] {'sky'}, dimensions={0} | all-to-all | bytes 1048576 | tf_op jit(solution)/shard_map/all_to_all | solution.py:404
  48.3 0.0 copy-done
  48.3 2.5 %update.2 = (f32[3088,128]{1,0:T(8,128)S(1)}, bf16[16,128,128]{2,1,0:T(8,128)(2,1)S(1)}) custom-call(s32[260]{0:T(512)S(1)} %get-tuple-element.12.table_ref, f32[256]{0:T(256)S(1)} %get-tuple-element.13.factor_ref, bf16[16,128,128]{2,1,0:T(8,128)(2,1)S(1)} %all_to_all.20.returned_ref, f32[3072,128]{1,0:T(8,128)S(1)} %bitcast.6), custom_call_target="tpu_custom_call" | custom-call | tf_op jit(solution)/shard_map/update/pallas_call | solution.py:493
  50.7 18.4 %all_to_all.21.arrived_ref = bf16[16,128,128]{2,1,0:T(8,128)(2,1)S(1)} all-to-all(bf16[16,128,128]{2,1,0:T(8,128)(2,1)S(1)} %get-tuple-element.16), channel_id=1, replica_groups=mesh['groups'=2,'sky'=16] {'sky'}, dimensions={0} | all-to-all | bytes 1048576 | tf_op jit(solution)/shard_map/all_to_all | solution.py:404
  69.1 3.8 %blur.3 = (bf16[16,128,128]{2,1,0:T(8,128)(2,1)S(1)}, f32[128,16,128]{2,1,0:T(8,128)}) custom-call(s32[256]{0:T(256)S(1)} %get-tuple-element.14.table_ref, f32[128]{0:T(128)S(1)} %copy-done.5, bf16[16,128,128]{2,1,0:T(8,128)(2,1)S(1)} %all_to_all.21.arrived_ref, bf16[128,16,128]{2,1,0:T(8,128)(2,1)S(1)} %copy-done.1, ...), custom_call_target="tpu_custom_call" | custom-call | tf_op jit(solution)/shard_map/blur/pallas_call | solution.py:474
  72.9 18.4 %all_to_all.22.returned_ref = bf16[16,128,128]{2,1,0:T(8,128)(2,1)S(1)} all-to-all(bf16[16,128,128]{2,1,0:T(8,128)(2,1)S(1)} %get-tuple-element.19), channel_id=1, replica_groups=mesh['groups'=2,'sky'=16] {'sky'}, dimensions={0} | all-to-all | bytes 1048576 | tf_op jit(solution)/shard_map/all_to_all | solution.py:404
  91.3 2.8 %update.3 = f32[3072,128]{1,0:T(8,128)} custom-call(s32[260]{0:T(512)S(1)} %get-tuple-element.12.table_ref, f32[256]{0:T(256)S(1)} %get-tuple-element.13.factor_ref, bf16[16,128,128]{2,1,0:T(8,128)(2,1)S(1)} %all_to_all.22.returned_ref, f32[3088,128]{1,0:T(8,128)S(1)} %get-tuple-element.20.model_ref), custom_call_target="tpu_custom_call" | custom-call | tf_op jit(solution)/shard_map/update/pallas_call | solution.py:493
Async XLA Ops:
  0.6 10.5 %copy-start.2 = (s32[16,16]{1,0:T(8,128)S(1)}, s32[16,16]{1,0:T(8,128)}, u32[]{:S(2)}) copy-start(s32[16,16]{1,0:T(8,128)} %plane_in_ref.1) | copy-start | bytes 3076
  0.6 10.5 %copy-start.3 = (s32[16,16]{1,0:T(8,128)S(1)}, s32[16,16]{1,0:T(8,128)}, u32[]{:S(2)}) copy-start(s32[16,16]{1,0:T(8,128)} %row_in_ref.1) | copy-start | bytes 3076
  0.7 10.5 %copy-start.4 = (s32[16,16]{1,0:T(8,128)S(1)}, s32[16,16]{1,0:T(8,128)}, u32[]{:S(2)}) copy-start(s32[16,16]{1,0:T(8,128)} %cover_in_ref.1) | copy-start | bytes 3076
  0.7 10.5 %copy-start.6 = (s32[128,2]{0,1:T(2,128)S(1)}, s32[128,2]{0,1:T(2,128)}, u32[]{:S(2)}) copy-start(s32[128,2]{0,1:T(2,128)} %param.23) | copy-start | bytes 3076
  0.7 10.5 %copy-start.7 = (s32[128,2]{0,1:T(2,128)S(1)}, s32[128,2]{0,1:T(2,128)}, u32[]{:S(2)}) copy-start(s32[128,2]{0,1:T(2,128)} %param.24) | copy-start | bytes 3076
  0.7 10.5 %copy-start.8 = (s32[128,2]{0,1:T(2,128)S(1)}, s32[128,2]{0,1:T(2,128)}, u32[]{:S(2)}) copy-start(s32[128,2]{0,1:T(2,128)} %param.25) | copy-start | bytes 3076
  0.7 10.5 %copy-start.9 = (s32[128]{0:T(128)S(1)}, s32[128]{0:T(128)}, u32[]{:S(2)}) copy-start(s32[128]{0:T(128)} %batch_ref.1) | copy-start | bytes 1540
  0.7 10.5 %copy-start.10 = (f32[6]{0:T(128)S(1)}, f32[6]{0:T(128)}, u32[]{:S(2)}) copy-start(f32[6]{0:T(128)} %step_ref.1) | copy-start | bytes 76
  0.7 10.5 %copy-start.11 = (s32[2]{0:T(128)S(1)}, s32[2]{0:T(128)}, u32[]{:S(2)}) copy-start(s32[2]{0:T(128)} %lo_ref.1) | copy-start | bytes 28
  0.7 10.5 %copy-start.12 = (s32[2]{0:T(128)S(1)}, s32[2]{0:T(128)}, u32[]{:S(2)}) copy-start(s32[2]{0:T(128)} %hi_ref.1) | copy-start | bytes 28
  0.7 26.0 %copy-start.1 = (bf16[128,16,128]{2,1,0:T(8,128)(2,1)S(1)}, bf16[128,16,128]{2,1,0:T(8,128)(2,1)}, u32[]{:S(2)}) copy-start(bf16[128,16,128]{2,1,0:T(8,128)(2,1)} %seen_ref.3) | copy-start | bytes 1572868
  0.7 25.9 %copy-start.5 = (f32[128]{0:T(128)S(1)}, f32[128]{0:T(128)}, u32[]{:S(2)}) copy-start(f32[128]{0:T(128)} %weight_ref.3) | copy-start | bytes 1540
  3.6 44.6 %copy-start = (f32[2,6,256,128]{3,2,1,0:T(8,128)S(1)}, f32[2,6,256,128]{3,2,1,0:T(8,128)}, u32[]{:S(2)}) copy-start(f32[2,6,256,128]{3,2,1,0:T(8,128)} %param.14) | copy-start | bytes 4718596
  3.6 23.1 %all-to-all-start = ((bf16[16,144,128]{2,1,0:T(8,128)(2,1)}), bf16[16,144,128]{2,1,0:T(8,128)(2,1)S(1)}, u32[]{:S(2)}, u32[]{:S(2)}) async-start(bf16[16,144,128]{2,1,0:T(8,128)(2,1)} %first_send.1), calls=%async_computation | async-start | bytes 1179648 | tf_op jit(solution)/shard_map/all_to_all | solution.py:404

commit v14 on v13

--- a/solution.py
+++ b/solution.py
@@ -360,15 +360,19 @@
 
     for e in range(exposures):
         blur(e)
-    if last:
-        send = pltpu.make_async_copy(residual_ref, residual_out_ref, sent)
-        send.start()
+    sends = []
     for e in range(exposures):
+        if last and e == exposures // 2:
+            parts = sent.shape[0]
+            for n in range(parts):
+                here = pl.ds(n * (exposures // parts), exposures // parts)
+                sends.append(pltpu.make_async_copy(residual_ref.at[here], residual_out_ref.at[here], sent.at[n]))
+                sends[-1].start()
         correlate(e)
     for o in range(peers):
         at = height + o * rows_each
         out_ref[o, :, :] = packed_ref[at : at + rows_each, :].astype(BF16)
-    if last:
+    for send in sends:
         send.wait()
 
 
@@ -465,7 +469,8 @@
             pltpu.VMEM((count * height, columns), BF16),
         ]
         if last:
-            scratch += [pltpu.VMEM(exposures.shape, F32), pltpu.SemaphoreType.DMA]
+            copies = max(n for n in (1, 2, 4) if count % n == 0)
+            scratch += [pltpu.VMEM(exposures.shape, F32), pltpu.SemaphoreType.DMA((copies,))]
             out_shape, out_specs = (rows_shape, jax.ShapeDtypeStruct(exposures.shape, F32)), (vmem(), hbm())
         else:
             scratch.append(pltpu.VMEM((peers * extra, columns), F32))

time: 94.4 us -> 94.4 us (level)
  no operation moved by 1% of the time
where the time goes in v14:
time: 94.4 us; the launch traced here: 94.1 us
  blocking collectives  55.4 us (59%)
  Pallas kernels  20.5 us (22%)
  waiting for transfers between devices  9.76 us (10%)
  starting transfers between devices  7.5 us (8%)
    all_to_all x3, blocking collectives, swap(): return lax.all_to_all(a, 'sky', split_axis=0, concat_axis=0, tiled=True)  55.4 us
    all_to_all x1, waiting for transfers between devices, swap(): return lax.all_to_all(a, 'sky', split_axis=0, concat_axis=0, tiled=True)  9.76 us
    all_to_all x1, starting transfers between devices, swap(): return lax.all_to_all(a, 'sky', split_axis=0, concat_axis=0, tiled=True)  7.5 us
    pallas_call x2, Pallas kernels, body(): pl.pallas_call(functools.partial(blur_kernel, height, pieces, batches_eac...  6.65 us
    pallas_call x1, Pallas kernels, body(): pl.pallas_call(functools.partial(tables_kernel, tile_rows, bands, height,...  5.68 us
    pallas_call x2, Pallas kernels, body(): pl.pallas_call(functools.partial(update_kernel, bands, tile_rows, height,...  5.27 us
    pallas_call x1, Pallas kernels, body(): pl.pallas_call(functools.partial(first_send_kernel, tile_rows, height, ro...  2.86 us
  transfers between devices with their start and end apart: 1, of which 1 were waited for; matrix products, arithmetic and copies ran while one was open for 0% of the time, Pallas kernels for 6%

profile of v14, /device:TPU:0, one launch (start us, length us, event | category | flops | bytes accessed | tf_op | source)
XLA Modules:
  0.0 94.1 jit_solution(3289765892594765626)
XLA Ops:
  0.6 0.0 copy-start.2
  0.6 0.0 copy-start.3
  0.7 0.0 copy-start.4
  0.7 0.0 copy-start.6
  0.7 0.0 copy-start.7
  0.7 0.0 copy-start.8
  0.7 0.0 copy-start.9
  0.7 0.0 copy-start.10
  0.7 0.0 copy-start.11
  0.7 0.0 copy-start.12
  0.7 0.0 copy-start.1
  0.7 0.0 copy-start.5
  0.8 2.9 %first_send.1 = bf16[16,144,128]{2,1,0:T(8,128)(2,1)} custom-call(s32[16,16]{1,0:T(8,128)} %plane_in_ref.1, s32[16,16]{1,0:T(8,128)} %row_in_ref.1, s32[16,16]{1,0:T(8,128)} %cover_in_ref.1, f32[2,56]{1,0:T(2,128)} %taps_in_ref.1, f32[3072,128]{1,0:T(8,128)} %bitcast.5), custom_call_target="tpu_custom_call" | custom-call | tf_op jit(solution)/shard_map/first_send/pallas_call | solution.py:410
  3.6 0.0 copy-start
  3.6 7.5 %all-to-all-start = ((bf16[16,144,128]{2,1,0:T(8,128)(2,1)}), bf16[16,144,128]{2,1,0:T(8,128)(2,1)S(1)}, u32[]{:S(2)}, u32[]{:S(2)}) async-start(bf16[16,144,128]{2,1,0:T(8,128)(2,1)} %first_send.1), calls=%async_computation | async-start | bytes 1179648 | tf_op jit(solution)/shard_map/all_to_all | solution.py:408
  11.1 0.0 copy-done.2
  11.2 0.0 copy-done.3
  11.2 0.0 copy-done.4
  11.2 0.0 copy-done.6
  11.2 0.0 copy-done.7
  11.2 0.0 copy-done.8
  11.2 0.0 copy-done.9
  11.2 0.0 copy-done.10
  11.2 0.0 copy-done.11
  11.2 0.0 copy-done.12
  11.2 5.7 %tables.1 = (s32[256]{0:T(256)S(1)}, s32[260]{0:T(512)S(1)}, f32[256]{0:T(256)S(1)}) custom-call(s32[2,128]{1,0:T(2,128)S(1)} %bitcast.7, s32[2,128]{1,0:T(2,128)S(1)} %bitcast.8, s32[2,128]{1,0:T(2,128)S(1)} %bitcast.9, s32[128]{0:T(128)S(1)} %copy-done.9, s32[16,16]{1,0:T(8,128)S(1)} %copy-done.2, s32[16,16]{1,0:T(8,128)S(1)} %copy-done.3, ...), custom_call_target="tpu_custom_call" | custom-call | flops 4000000 | bytes 8000000 | tf_op jit(solution)/shard_map/tables/pallas_call | solution.py:433
  16.9 9.8 %all-to-all-done.arrived_ref = bf16[16,144,128]{2,1,0:T(8,128)(2,1)S(1)} async-done(((bf16[16,144,128]{2,1,0:T(8,128)(2,1)}), bf16[16,144,128]{2,1,0:T(8,128)(2,1)S(1)}, u32[]{:S(2)}, u32[]{:S(2)}) %all-to-all-start) | async-done | bytes 589856 | tf_op jit(solution)/shard_map/all_to_all | solution.py:408
  26.7 0.0 copy-done.1
  26.7 0.0 copy-done.5
  26.7 2.9 %blur.2 = (bf16[16,128,128]{2,1,0:T(8,128)(2,1)S(1)}, bf16[32,16,128]{2,1,0:T(8,128)(2,1)S(1)}, bf16[32,16,128]{2,1,0:T(8,128)(2,1)S(1)}) custom-call(s32[256]{0:T(256)S(1)} %get-tuple-element.14.table_ref, f32[128]{0:T(128)S(1)} %copy-done.5, bf16[16,144,128]{2,1,0:T(8,128)(2,1)S(1)} %all-to-all-done.arrived_ref, bf16[128,16,128]{2,1,0:T(8,128)(2,1)S(1)} %copy-done.1), custom_call_target="tpu_custom_call" | custom-call | tf_op jit(solution)/shard_map/blur/pallas_call | solution.py:479
  29.6 18.7 %all_to_all.20.returned_ref = bf16[16,128,128]{2,1,0:T(8,128)(2,1)S(1)} all-to-all(bf16[16,128,128]{2,1,0:T(8,128)(2,1)S(1)} %get-tuple-element.15), channel_id=1, replica_groups=mesh['groups'=2,'sky'=16] {'sky'}, dimensions={0} | all-to-all | bytes 1048576 | tf_op jit(solution)/shard_map/all_to_all | solution.py:408
  48.3 0.0 copy-done
  48.3 2.5 %update.2 = (f32[3088,128]{1,0:T(8,128)S(1)}, bf16[16,128,128]{2,1,0:T(8,128)(2,1)S(1)}) custom-call(s32[260]{0:T(512)S(1)} %get-tuple-element.12.table_ref, f32[256]{0:T(256)S(1)} %get-tuple-element.13.factor_ref, bf16[16,128,128]{2,1,0:T(8,128)(2,1)S(1)} %all_to_all.20.returned_ref, f32[3072,128]{1,0:T(8,128)S(1)} %bitcast.6), custom_call_target="tpu_custom_call" | custom-call | tf_op jit(solution)/shard_map/update/pallas_call | solution.py:498
  50.7 18.4 %all_to_all.21.arrived_ref = bf16[16,128,128]{2,1,0:T(8,128)(2,1)S(1)} all-to-all(bf16[16,128,128]{2,1,0:T(8,128)(2,1)S(1)} %get-tuple-element.16), channel_id=1, replica_groups=mesh['groups'=2,'sky'=16] {'sky'}, dimensions={0} | all-to-all | bytes 1048576 | tf_op jit(solution)/shard_map/all_to_all | solution.py:408
  69.1 3.8 %blur.3 = (bf16[16,128,128]{2,1,0:T(8,128)(2,1)S(1)}, f32[128,16,128]{2,1,0:T(8,128)}) custom-call(s32[256]{0:T(256)S(1)} %get-tuple-element.14.table_ref, f32[128]{0:T(128)S(1)} %copy-done.5, bf16[16,128,128]{2,1,0:T(8,128)(2,1)S(1)} %all_to_all.21.arrived_ref, bf16[128,16,128]{2,1,0:T(8,128)(2,1)S(1)} %copy-done.1, ...), custom_call_target="tpu_custom_call" | custom-call | tf_op jit(solution)/shard_map/blur/pallas_call | solution.py:479
  72.9 18.4 %all_to_all.22.returned_ref = bf16[16,128,128]{2,1,0:T(8,128)(2,1)S(1)} all-to-all(bf16[16,128,128]{2,1,0:T(8,128)(2,1)S(1)} %get-tuple-element.19), channel_id=1, replica_groups=mesh['groups'=2,'sky'=16] {'sky'}, dimensions={0} | all-to-all | bytes 1048576 | tf_op jit(solution)/shard_map/all_to_all | solution.py:408
  91.3 2.8 %update.3 = f32[3072,128]{1,0:T(8,128)} custom-call(s32[260]{0:T(512)S(1)} %get-tuple-element.12.table_ref, f32[256]{0:T(256)S(1)} %get-tuple-element.13.factor_ref, bf16[16,128,128]{2,1,0:T(8,128)(2,1)S(1)} %all_to_all.22.returned_ref, f32[3088,128]{1,0:T(8,128)S(1)} %get-tuple-element.20.model_ref), custom_call_target="tpu_custom_call" | custom-call | tf_op jit(solution)/shard_map/update/pallas_call | solution.py:498
Async XLA Ops:
  0.6 10.5 %copy-start.2 = (s32[16,16]{1,0:T(8,128)S(1)}, s32[16,16]{1,0:T(8,128)}, u32[]{:S(2)}) copy-start(s32[16,16]{1,0:T(8,128)} %plane_in_ref.1) | copy-start | bytes 3076
  0.6 10.5 %copy-start.3 = (s32[16,16]{1,0:T(8,128)S(1)}, s32[16,16]{1,0:T(8,128)}, u32[]{:S(2)}) copy-start(s32[16,16]{1,0:T(8,128)} %row_in_ref.1) | copy-start | bytes 3076
  0.7 10.5 %copy-start.4 = (s32[16,16]{1,0:T(8,128)S(1)}, s32[16,16]{1,0:T(8,128)}, u32[]{:S(2)}) copy-start(s32[16,16]{1,0:T(8,128)} %cover_in_ref.1) | copy-start | bytes 3076
  0.7 10.5 %copy-start.6 = (s32[128,2]{0,1:T(2,128)S(1)}, s32[128,2]{0,1:T(2,128)}, u32[]{:S(2)}) copy-start(s32[128,2]{0,1:T(2,128)} %param.23) | copy-start | bytes 3076
  0.7 10.5 %copy-start.7 = (s32[128,2]{0,1:T(2,128)S(1)}, s32[128,2]{0,1:T(2,128)}, u32[]{:S(2)}) copy-start(s32[128,2]{0,1:T(2,128)} %param.24) | copy-start | bytes 3076
  0.7 10.5 %copy-start.8 = (s32[128,2]{0,1:T(2,128)S(1)}, s32[128,2]{0,1:T(2,128)}, u32[]{:S(2)}) copy-start(s32[128,2]{0,1:T(2,128)} %param.25) | copy-start | bytes 3076
  0.7 10.5 %copy-start.9 = (s32[128]{0:T(128)S(1)}, s32[128]{0:T(128)}, u32[]{:S(2)}) copy-start(s32[128]{0:T(128)} %batch_ref.1) | copy-start | bytes 1540
  0.7 10.5 %copy-start.10 = (f32[6]{0:T(128)S(1)}, f32[6]{0:T(128)}, u32[]{:S(2)}) copy-start(f32[6]{0:T(128)} %step_ref.1) | copy-start | bytes 76
  0.7 10.5 %copy-start.11 = (s32[2]{0:T(128)S(1)}, s32[2]{0:T(128)}, u32[]{:S(2)}) copy-start(s32[2]{0:T(128)} %lo_ref.1) | copy-start | bytes 28
  0.7 10.5 %copy-start.12 = (s32[2]{0:T(128)S(1)}, s32[2]{0:T(128)}, u32[]{:S(2)}) copy-start(s32[2]{0:T(128)} %hi_ref.1) | copy-start | bytes 28
  0.7 26.0 %copy-start.1 = (bf16[128,16,128]{2,1,0:T(8,128)(2,1)S(1)}, bf16[128,16,128]{2,1,0:T(8,128)(2,1)}, u32[]{:S(2)}) copy-start(bf16[128,16,128]{2,1,0:T(8,128)(2,1)} %seen_ref.3) | copy-start | bytes 1572868
  0.7 25.9 %copy-start.5 = (f32[128]{0:T(128)S(1)}, f32[128]{0:T(128)}, u32[]{:S(2)}) copy-start(f32[128]{0:T(128)} %weight_ref.3) | copy-start | bytes 1540
  3.6 44.6 %copy-start = (f32[2,6,256,128]{3,2,1,0:T(8,128)S(1)}, f32[2,6,256,128]{3,2,1,0:T(8,128)}, u32[]{:S(2)}) copy-start(f32[2,6,256,128]{3,2,1,0:T(8,128)} %param.14) | copy-start | bytes 4718596
  3.6 23.1 %all-to-all-start = ((bf16[16,144,128]{2,1,0:T(8,128)(2,1)}), bf16[16,144,128]{2,1,0:T(8,128)(2,1)S(1)}, u32[]{:S(2)}, u32[]{:S(2)}) async-start(bf16[16,144,128]{2,1,0:T(8,128)(2,1)} %first_send.1), calls=%async_computation | async-start | bytes 1179648 | tf_op jit(solution)/shard_map/all_to_all | solution.py:408

commit v15 on v13

--- a/solution.py
+++ b/solution.py
@@ -145,8 +145,8 @@
             block_ref[d, rows_each:, :] = bank
         sends.append(pltpu.make_async_copy(block_ref.at[here], out_ref.at[here], sems.at[len(pairs) + part]))
         sends[-1].start()
-    for send in sends:
-        send.wait()
+    for copy in sends:
+        copy.wait()
 
 
 def update_kernel(bands, tile_rows, height, last, table_ref, factor_ref, returned_ref, model_ref, *rest):
@@ -358,18 +358,32 @@
                 mask = before if mask is None else mask & before
             pltpu.store(packed_ref.at[pl.ds(low(word), height), :], result, mask=mask)
 
-    for e in range(exposures):
+    quarter = exposures // 4
+    sends = []
+
+    def send(n):
+        here = pl.ds(n * quarter, quarter)
+        sends.append(pltpu.make_async_copy(residual_ref.at[here], residual_out_ref.at[here], sent.at[n]))
+        sends[-1].start()
+
+    for e in range(3 * quarter):
         blur(e)
+    for e in range(quarter):
+        correlate(e)
     if last:
-        send = pltpu.make_async_copy(residual_ref, residual_out_ref, sent)
-        send.start()
-    for e in range(exposures):
+        for n in range(3):
+            send(n)
+    for e in range(3 * quarter, exposures):
+        blur(e)
+    for e in range(quarter, exposures):
         correlate(e)
+    if last:
+        send(3)
     for o in range(peers):
         at = height + o * rows_each
         out_ref[o, :, :] = packed_ref[at : at + rows_each, :].astype(BF16)
-    if last:
-        send.wait()
+    for copy in sends:
+        copy.wait()
 
 
 def body(
@@ -397,7 +411,7 @@
     batches_each = psf_taps.shape[0]
     extra = aligned(batches_each * 2)
     block = rows_each + extra
-    assert columns == LANES and rows_each % extra == 0 and TAPS * height <= LANES - HALF
+    assert columns == LANES and rows_each % extra == 0 and TAPS * height <= LANES - HALF and count % 4 == 0
     x = model.reshape(total, columns)
 
     def swap(a):
@@ -465,7 +479,7 @@
             pltpu.VMEM((count * height, columns), BF16),
         ]
         if last:
-            scratch += [pltpu.VMEM(exposures.shape, F32), pltpu.SemaphoreType.DMA]
+            scratch += [pltpu.VMEM(exposures.shape, F32), pltpu.SemaphoreType.DMA((4,))]
             out_shape, out_specs = (rows_shape, jax.ShapeDtypeStruct(exposures.shape, F32)), (vmem(), hbm())
         else:
             scratch.append(pltpu.VMEM((peers * extra, columns), F32))

time: 94.4 us -> 94.2 us (level)
  no operation moved by 1% of the time
where the time goes in v15:
time: 94.2 us; the launch traced here: 93.9 us
  blocking collectives  55.4 us (59%)
  Pallas kernels  20.3 us (22%)
  waiting for transfers between devices  9.76 us (10%)
  starting transfers between devices  7.5 us (8%)
    all_to_all x3, blocking collectives, swap(): return lax.all_to_all(a, 'sky', split_axis=0, concat_axis=0, tiled=True)  55.4 us
    all_to_all x1, waiting for transfers between devices, swap(): return lax.all_to_all(a, 'sky', split_axis=0, concat_axis=0, tiled=True)  9.76 us
    all_to_all x1, starting transfers between devices, swap(): return lax.all_to_all(a, 'sky', split_axis=0, concat_axis=0, tiled=True)  7.5 us
    pallas_call x2, Pallas kernels, body(): pl.pallas_call(functools.partial(blur_kernel, height, pieces, batches_eac...  6.44 us
    pallas_call x1, Pallas kernels, body(): pl.pallas_call(functools.partial(tables_kernel, tile_rows, bands, height,...  5.68 us
    pallas_call x2, Pallas kernels, body(): pl.pallas_call(functools.partial(update_kernel, bands, tile_rows, height,...  5.28 us
    pallas_call x1, Pallas kernels, body(): pl.pallas_call(functools.partial(first_send_kernel, tile_rows, height, ro...  2.86 us
  transfers between devices with their start and end apart: 1, of which 1 were waited for; matrix products, arithmetic and copies ran while one was open for 0% of the time, Pallas kernels for 6%

profile of v15, /device:TPU:0, one launch (start us, length us, event | category | flops | bytes accessed | tf_op | source)
XLA Modules:
  0.0 93.9 jit_solution(10426691102370805069)
XLA Ops:
  0.6 0.0 copy-start.2
  0.6 0.0 copy-start.3
  0.7 0.0 copy-start.4
  0.7 0.0 copy-start.6
  0.7 0.0 copy-start.7
  0.7 0.0 copy-start.8
  0.7 0.0 copy-start.9
  0.7 0.0 copy-start.10
  0.7 0.0 copy-start.11
  0.7 0.0 copy-start.12
  0.7 0.0 copy-start.1
  0.7 0.0 copy-start.5
  0.8 2.9 %first_send.1 = bf16[16,144,128]{2,1,0:T(8,128)(2,1)} custom-call(s32[16,16]{1,0:T(8,128)} %plane_in_ref.1, s32[16,16]{1,0:T(8,128)} %row_in_ref.1, s32[16,16]{1,0:T(8,128)} %cover_in_ref.1, f32[2,56]{1,0:T(2,128)} %taps_in_ref.1, f32[3072,128]{1,0:T(8,128)} %bitcast.5), custom_call_target="tpu_custom_call" | custom-call | tf_op jit(solution)/shard_map/first_send/pallas_call | solution.py:420
  3.6 0.0 copy-start
  3.6 7.5 %all-to-all-start = ((bf16[16,144,128]{2,1,0:T(8,128)(2,1)}), bf16[16,144,128]{2,1,0:T(8,128)(2,1)S(1)}, u32[]{:S(2)}, u32[]{:S(2)}) async-start(bf16[16,144,128]{2,1,0:T(8,128)(2,1)} %first_send.1), calls=%async_computation | async-start | bytes 1179648 | tf_op jit(solution)/shard_map/all_to_all | solution.py:418
  11.1 0.0 copy-done.2
  11.2 0.0 copy-done.3
  11.2 0.0 copy-done.4
  11.2 0.0 copy-done.6
  11.2 0.0 copy-done.7
  11.2 0.0 copy-done.8
  11.2 0.0 copy-done.9
  11.2 0.0 copy-done.10
  11.2 0.0 copy-done.11
  11.2 0.0 copy-done.12
  11.2 5.7 %tables.1 = (s32[256]{0:T(256)S(1)}, s32[260]{0:T(512)S(1)}, f32[256]{0:T(256)S(1)}) custom-call(s32[2,128]{1,0:T(2,128)S(1)} %bitcast.7, s32[2,128]{1,0:T(2,128)S(1)} %bitcast.8, s32[2,128]{1,0:T(2,128)S(1)} %bitcast.9, s32[128]{0:T(128)S(1)} %copy-done.9, s32[16,16]{1,0:T(8,128)S(1)} %copy-done.2, s32[16,16]{1,0:T(8,128)S(1)} %copy-done.3, ...), custom_call_target="tpu_custom_call" | custom-call | flops 4000000 | bytes 8000000 | tf_op jit(solution)/shard_map/tables/pallas_call | solution.py:443
  16.9 9.8 %all-to-all-done.arrived_ref = bf16[16,144,128]{2,1,0:T(8,128)(2,1)S(1)} async-done(((bf16[16,144,128]{2,1,0:T(8,128)(2,1)}), bf16[16,144,128]{2,1,0:T(8,128)(2,1)S(1)}, u32[]{:S(2)}, u32[]{:S(2)}) %all-to-all-start) | async-done | bytes 589856 | tf_op jit(solution)/shard_map/all_to_all | solution.py:418
  26.7 0.0 copy-done.1
  26.7 0.0 copy-done.5
  26.7 2.9 %blur.2 = (bf16[16,128,128]{2,1,0:T(8,128)(2,1)S(1)}, bf16[32,16,128]{2,1,0:T(8,128)(2,1)S(1)}, bf16[32,16,128]{2,1,0:T(8,128)(2,1)S(1)}) custom-call(s32[256]{0:T(256)S(1)} %get-tuple-element.14.table_ref, f32[128]{0:T(128)S(1)} %copy-done.5, bf16[16,144,128]{2,1,0:T(8,128)(2,1)S(1)} %all-to-all-done.arrived_ref, bf16[128,16,128]{2,1,0:T(8,128)(2,1)S(1)} %copy-done.1), custom_call_target="tpu_custom_call" | custom-call | tf_op jit(solution)/shard_map/blur/pallas_call | solution.py:488
  29.6 18.7 %all_to_all.20.returned_ref = bf16[16,128,128]{2,1,0:T(8,128)(2,1)S(1)} all-to-all(bf16[16,128,128]{2,1,0:T(8,128)(2,1)S(1)} %get-tuple-element.15), channel_id=1, replica_groups=mesh['groups'=2,'sky'=16] {'sky'}, dimensions={0} | all-to-all | bytes 1048576 | tf_op jit(solution)/shard_map/all_to_all | solution.py:418
  48.3 0.0 copy-done
  48.3 2.5 %update.2 = (f32[3088,128]{1,0:T(8,128)S(1)}, bf16[16,128,128]{2,1,0:T(8,128)(2,1)S(1)}) custom-call(s32[260]{0:T(512)S(1)} %get-tuple-element.12.table_ref, f32[256]{0:T(256)S(1)} %get-tuple-element.13.factor_ref, bf16[16,128,128]{2,1,0:T(8,128)(2,1)S(1)} %all_to_all.20.returned_ref, f32[3072,128]{1,0:T(8,128)S(1)} %bitcast.6), custom_call_target="tpu_custom_call" | custom-call | tf_op jit(solution)/shard_map/update/pallas_call | solution.py:507
  50.8 18.4 %all_to_all.21.arrived_ref = bf16[16,128,128]{2,1,0:T(8,128)(2,1)S(1)} all-to-all(bf16[16,128,128]{2,1,0:T(8,128)(2,1)S(1)} %get-tuple-element.16), channel_id=1, replica_groups=mesh['groups'=2,'sky'=16] {'sky'}, dimensions={0} | all-to-all | bytes 1048576 | tf_op jit(solution)/shard_map/all_to_all | solution.py:418
  69.2 3.5 %blur.3 = (bf16[16,128,128]{2,1,0:T(8,128)(2,1)S(1)}, f32[128,16,128]{2,1,0:T(8,128)}) custom-call(s32[256]{0:T(256)S(1)} %get-tuple-element.14.table_ref, f32[128]{0:T(128)S(1)} %copy-done.5, bf16[16,128,128]{2,1,0:T(8,128)(2,1)S(1)} %all_to_all.21.arrived_ref, bf16[128,16,128]{2,1,0:T(8,128)(2,1)S(1)} %copy-done.1, ...), custom_call_target="tpu_custom_call" | custom-call | tf_op jit(solution)/shard_map/blur/pallas_call | solution.py:488
  72.7 18.4 %all_to_all.22.returned_ref = bf16[16,128,128]{2,1,0:T(8,128)(2,1)S(1)} all-to-all(bf16[16,128,128]{2,1,0:T(8,128)(2,1)S(1)} %get-tuple-element.19), channel_id=1, replica_groups=mesh['groups'=2,'sky'=16] {'sky'}, dimensions={0} | all-to-all | bytes 1048576 | tf_op jit(solution)/shard_map/all_to_all | solution.py:418
  91.1 2.8 %update.3 = f32[3072,128]{1,0:T(8,128)} custom-call(s32[260]{0:T(512)S(1)} %get-tuple-element.12.table_ref, f32[256]{0:T(256)S(1)} %get-tuple-element.13.factor_ref, bf16[16,128,128]{2,1,0:T(8,128)(2,1)S(1)} %all_to_all.22.returned_ref, f32[3088,128]{1,0:T(8,128)S(1)} %get-tuple-element.20.model_ref), custom_call_target="tpu_custom_call" | custom-call | tf_op jit(solution)/shard_map/update/pallas_call | solution.py:507
Async XLA Ops:
  0.6 10.5 %copy-start.2 = (s32[16,16]{1,0:T(8,128)S(1)}, s32[16,16]{1,0:T(8,128)}, u32[]{:S(2)}) copy-start(s32[16,16]{1,0:T(8,128)} %plane_in_ref.1) | copy-start | bytes 3076
  0.6 10.5 %copy-start.3 = (s32[16,16]{1,0:T(8,128)S(1)}, s32[16,16]{1,0:T(8,128)}, u32[]{:S(2)}) copy-start(s32[16,16]{1,0:T(8,128)} %row_in_ref.1) | copy-start | bytes 3076
  0.7 10.5 %copy-start.4 = (s32[16,16]{1,0:T(8,128)S(1)}, s32[16,16]{1,0:T(8,128)}, u32[]{:S(2)}) copy-start(s32[16,16]{1,0:T(8,128)} %cover_in_ref.1) | copy-start | bytes 3076
  0.7 10.5 %copy-start.6 = (s32[128,2]{0,1:T(2,128)S(1)}, s32[128,2]{0,1:T(2,128)}, u32[]{:S(2)}) copy-start(s32[128,2]{0,1:T(2,128)} %param.23) | copy-start | bytes 3076
  0.7 10.5 %copy-start.7 = (s32[128,2]{0,1:T(2,128)S(1)}, s32[128,2]{0,1:T(2,128)}, u32[]{:S(2)}) copy-start(s32[128,2]{0,1:T(2,128)} %param.24) | copy-start | bytes 3076
  0.7 10.5 %copy-start.8 = (s32[128,2]{0,1:T(2,128)S(1)}, s32[128,2]{0,1:T(2,128)}, u32[]{:S(2)}) copy-start(s32[128,2]{0,1:T(2,128)} %param.25) | copy-start | bytes 3076
  0.7 10.5 %copy-start.9 = (s32[128]{0:T(128)S(1)}, s32[128]{0:T(128)}, u32[]{:S(2)}) copy-start(s32[128]{0:T(128)} %batch_ref.1) | copy-start | bytes 1540
  0.7 10.5 %copy-start.10 = (f32[6]{0:T(128)S(1)}, f32[6]{0:T(128)}, u32[]{:S(2)}) copy-start(f32[6]{0:T(128)} %step_ref.1) | copy-start | bytes 76
  0.7 10.5 %copy-start.11 = (s32[2]{0:T(128)S(1)}, s32[2]{0:T(128)}, u32[]{:S(2)}) copy-start(s32[2]{0:T(128)} %lo_ref.1) | copy-start | bytes 28
  0.7 10.5 %copy-start.12 = (s32[2]{0:T(128)S(1)}, s32[2]{0:T(128)}, u32[]{:S(2)}) copy-start(s32[2]{0:T(128)} %hi_ref.1) | copy-start | bytes 28
  0.7 26.0 %copy-start.1 = (bf16[128,16,128]{2,1,0:T(8,128)(2,1)S(1)}, bf16[128,16,128]{2,1,0:T(8,128)(2,1)}, u32[]{:S(2)}) copy-start(bf16[128,16,128]{2,1,0:T(8,128)(2,1)} %seen_ref.3) | copy-start | bytes 1572868
  0.7 25.9 %copy-start.5 = (f32[128]{0:T(128)S(1)}, f32[128]{0:T(128)}, u32[]{:S(2)}) copy-start(f32[128]{0:T(128)} %weight_ref.3) | copy-start | bytes 1540
  3.6 44.7 %copy-start = (f32[2,6,256,128]{3,2,1,0:T(8,128)S(1)}, f32[2,6,256,128]{3,2,1,0:T(8,128)}, u32[]{:S(2)}) copy-start(f32[2,6,256,128]{3,2,1,0:T(8,128)} %param.14) | copy-start | bytes 4718596
  3.6 23.1 %all-to-all-start = ((bf16[16,144,128]{2,1,0:T(8,128)(2,1)}), bf16[16,144,128]{2,1,0:T(8,128)(2,1)S(1)}, u32[]{:S(2)}, u32[]{:S(2)}) async-start(bf16[16,144,128]{2,1,0:T(8,128)(2,1)} %first_send.1), calls=%async_computation | async-start | bytes 1179648 | tf_op jit(solution)/shard_map/all_to_all | solution.py:418

commit v16 on v15

--- a/solution.py
+++ b/solution.py
@@ -366,19 +366,16 @@
         sends.append(pltpu.make_async_copy(residual_ref.at[here], residual_out_ref.at[here], sent.at[n]))
         sends[-1].start()
 
-    for e in range(3 * quarter):
-        blur(e)
-    for e in range(quarter):
+    for stage in range(2):
+        for e in range(2 * stage * quarter, 2 * (stage + 1) * quarter):
+            blur(e)
+        for e in range(stage * quarter, (2 * stage + 1) * quarter):
+            correlate(e)
+        if last:
+            send(2 * stage)
+            send(2 * stage + 1)
+    for e in range(3 * quarter, exposures):
         correlate(e)
-    if last:
-        for n in range(3):
-            send(n)
-    for e in range(3 * quarter, exposures):
-        blur(e)
-    for e in range(quarter, exposures):
-        correlate(e)
-    if last:
-        send(3)
     for o in range(peers):
         at = height + o * rows_each
         out_ref[o, :, :] = packed_ref[at : at + rows_each, :].astype(BF16)

time: 94.2 us -> 94.3 us (level)
  no operation moved by 1% of the time
where the time goes in v16:
time: 94.3 us; the launch traced here: 94 us
  blocking collectives  55.4 us (59%)
  Pallas kernels  20.4 us (22%)
  waiting for transfers between devices  9.76 us (10%)
  starting transfers between devices  7.5 us (8%)
    all_to_all x3, blocking collectives, swap(): return lax.all_to_all(a, 'sky', split_axis=0, concat_axis=0, tiled=True)  55.4 us
    all_to_all x1, waiting for transfers between devices, swap(): return lax.all_to_all(a, 'sky', split_axis=0, concat_axis=0, tiled=True)  9.76 us
    all_to_all x1, starting transfers between devices, swap(): return lax.all_to_all(a, 'sky', split_axis=0, concat_axis=0, tiled=True)  7.5 us
    pallas_call x2, Pallas kernels, body(): pl.pallas_call(functools.partial(blur_kernel, height, pieces, batches_eac...  6.54 us
    pallas_call x1, Pallas kernels, body(): pl.pallas_call(functools.partial(tables_kernel, tile_rows, bands, height,...  5.68 us
    pallas_call x2, Pallas kernels, body(): pl.pallas_call(functools.partial(update_kernel, bands, tile_rows, height,...  5.27 us
    pallas_call x1, Pallas kernels, body(): pl.pallas_call(functools.partial(first_send_kernel, tile_rows, height, ro...  2.86 us
  transfers between devices with their start and end apart: 1, of which 1 were waited for; matrix products, arithmetic and copies ran while one was open for 0% of the time, Pallas kernels for 6%

profile of v16, /device:TPU:0, one launch (start us, length us, event | category | flops | bytes accessed | tf_op | source)
XLA Modules:
  0.0 94.0 jit_solution(10380022243894820357)
XLA Ops:
  0.6 0.0 copy-start.2
  0.6 0.0 copy-start.3
  0.7 0.0 copy-start.4
  0.7 0.0 copy-start.6
  0.7 0.0 copy-start.7
  0.7 0.0 copy-start.8
  0.7 0.0 copy-start.9
  0.7 0.0 copy-start.10
  0.7 0.0 copy-start.11
  0.7 0.0 copy-start.12
  0.7 0.0 copy-start.1
  0.7 0.0 copy-start.5
  0.8 2.9 %first_send.1 = bf16[16,144,128]{2,1,0:T(8,128)(2,1)} custom-call(s32[16,16]{1,0:T(8,128)} %plane_in_ref.1, s32[16,16]{1,0:T(8,128)} %row_in_ref.1, s32[16,16]{1,0:T(8,128)} %cover_in_ref.1, f32[2,56]{1,0:T(2,128)} %taps_in_ref.1, f32[3072,128]{1,0:T(8,128)} %bitcast.5), custom_call_target="tpu_custom_call" | custom-call | tf_op jit(solution)/shard_map/first_send/pallas_call | solution.py:417
  3.6 0.0 copy-start
  3.6 7.5 %all-to-all-start = ((bf16[16,144,128]{2,1,0:T(8,128)(2,1)}), bf16[16,144,128]{2,1,0:T(8,128)(2,1)S(1)}, u32[]{:S(2)}, u32[]{:S(2)}) async-start(bf16[16,144,128]{2,1,0:T(8,128)(2,1)} %first_send.1), calls=%async_computation | async-start | bytes 1179648 | tf_op jit(solution)/shard_map/all_to_all | solution.py:415
  11.1 0.0 copy-done.2
  11.2 0.0 copy-done.3
  11.2 0.0 copy-done.4
  11.2 0.0 copy-done.6
  11.2 0.0 copy-done.7
  11.2 0.0 copy-done.8
  11.2 0.0 copy-done.9
  11.2 0.0 copy-done.10
  11.2 0.0 copy-done.11
  11.2 0.0 copy-done.12
  11.2 5.7 %tables.1 = (s32[256]{0:T(256)S(1)}, s32[260]{0:T(512)S(1)}, f32[256]{0:T(256)S(1)}) custom-call(s32[2,128]{1,0:T(2,128)S(1)} %bitcast.7, s32[2,128]{1,0:T(2,128)S(1)} %bitcast.8, s32[2,128]{1,0:T(2,128)S(1)} %bitcast.9, s32[128]{0:T(128)S(1)} %copy-done.9, s32[16,16]{1,0:T(8,128)S(1)} %copy-done.2, s32[16,16]{1,0:T(8,128)S(1)} %copy-done.3, ...), custom_call_target="tpu_custom_call" | custom-call | flops 4000000 | bytes 8000000 | tf_op jit(solution)/shard_map/tables/pallas_call | solution.py:440
  16.9 9.8 %all-to-all-done.arrived_ref = bf16[16,144,128]{2,1,0:T(8,128)(2,1)S(1)} async-done(((bf16[16,144,128]{2,1,0:T(8,128)(2,1)}), bf16[16,144,128]{2,1,0:T(8,128)(2,1)S(1)}, u32[]{:S(2)}, u32[]{:S(2)}) %all-to-all-start) | async-done | bytes 589856 | tf_op jit(solution)/shard_map/all_to_all | solution.py:415
  26.7 0.0 copy-done.1
  26.7 0.0 copy-done.5
  26.7 2.9 %blur.2 = (bf16[16,128,128]{2,1,0:T(8,128)(2,1)S(1)}, bf16[32,16,128]{2,1,0:T(8,128)(2,1)S(1)}, bf16[32,16,128]{2,1,0:T(8,128)(2,1)S(1)}) custom-call(s32[256]{0:T(256)S(1)} %get-tuple-element.14.table_ref, f32[128]{0:T(128)S(1)} %copy-done.5, bf16[16,144,128]{2,1,0:T(8,128)(2,1)S(1)} %all-to-all-done.arrived_ref, bf16[128,16,128]{2,1,0:T(8,128)(2,1)S(1)} %copy-done.1), custom_call_target="tpu_custom_call" | custom-call | tf_op jit(solution)/shard_map/blur/pallas_call | solution.py:485
  29.6 18.7 %all_to_all.20.returned_ref = bf16[16,128,128]{2,1,0:T(8,128)(2,1)S(1)} all-to-all(bf16[16,128,128]{2,1,0:T(8,128)(2,1)S(1)} %get-tuple-element.15), channel_id=1, replica_groups=mesh['groups'=2,'sky'=16] {'sky'}, dimensions={0} | all-to-all | bytes 1048576 | tf_op jit(solution)/shard_map/all_to_all | solution.py:415
  48.3 0.0 copy-done
  48.3 2.5 %update.2 = (f32[3088,128]{1,0:T(8,128)S(1)}, bf16[16,128,128]{2,1,0:T(8,128)(2,1)S(1)}) custom-call(s32[260]{0:T(512)S(1)} %get-tuple-element.12.table_ref, f32[256]{0:T(256)S(1)} %get-tuple-element.13.factor_ref, bf16[16,128,128]{2,1,0:T(8,128)(2,1)S(1)} %all_to_all.20.returned_ref, f32[3072,128]{1,0:T(8,128)S(1)} %bitcast.6), custom_call_target="tpu_custom_call" | custom-call | tf_op jit(solution)/shard_map/update/pallas_call | solution.py:504
  50.8 18.4 %all_to_all.21.arrived_ref = bf16[16,128,128]{2,1,0:T(8,128)(2,1)S(1)} all-to-all(bf16[16,128,128]{2,1,0:T(8,128)(2,1)S(1)} %get-tuple-element.16), channel_id=1, replica_groups=mesh['groups'=2,'sky'=16] {'sky'}, dimensions={0} | all-to-all | bytes 1048576 | tf_op jit(solution)/shard_map/all_to_all | solution.py:415
  69.2 3.6 %blur.3 = (bf16[16,128,128]{2,1,0:T(8,128)(2,1)S(1)}, f32[128,16,128]{2,1,0:T(8,128)}) custom-call(s32[256]{0:T(256)S(1)} %get-tuple-element.14.table_ref, f32[128]{0:T(128)S(1)} %copy-done.5, bf16[16,128,128]{2,1,0:T(8,128)(2,1)S(1)} %all_to_all.21.arrived_ref, bf16[128,16,128]{2,1,0:T(8,128)(2,1)S(1)} %copy-done.1, ...), custom_call_target="tpu_custom_call" | custom-call | tf_op jit(solution)/shard_map/blur/pallas_call | solution.py:485
  72.8 18.4 %all_to_all.22.returned_ref = bf16[16,128,128]{2,1,0:T(8,128)(2,1)S(1)} all-to-all(bf16[16,128,128]{2,1,0:T(8,128)(2,1)S(1)} %get-tuple-element.19), channel_id=1, replica_groups=mesh['groups'=2,'sky'=16] {'sky'}, dimensions={0} | all-to-all | bytes 1048576 | tf_op jit(solution)/shard_map/all_to_all | solution.py:415
  91.2 2.8 %update.3 = f32[3072,128]{1,0:T(8,128)} custom-call(s32[260]{0:T(512)S(1)} %get-tuple-element.12.table_ref, f32[256]{0:T(256)S(1)} %get-tuple-element.13.factor_ref, bf16[16,128,128]{2,1,0:T(8,128)(2,1)S(1)} %all_to_all.22.returned_ref, f32[3088,128]{1,0:T(8,128)S(1)} %get-tuple-element.20.model_ref), custom_call_target="tpu_custom_call" | custom-call | tf_op jit(solution)/shard_map/update/pallas_call | solution.py:504
Async XLA Ops:
  0.6 10.5 %copy-start.2 = (s32[16,16]{1,0:T(8,128)S(1)}, s32[16,16]{1,0:T(8,128)}, u32[]{:S(2)}) copy-start(s32[16,16]{1,0:T(8,128)} %plane_in_ref.1) | copy-start | bytes 3076
  0.6 10.5 %copy-start.3 = (s32[16,16]{1,0:T(8,128)S(1)}, s32[16,16]{1,0:T(8,128)}, u32[]{:S(2)}) copy-start(s32[16,16]{1,0:T(8,128)} %row_in_ref.1) | copy-start | bytes 3076
  0.7 10.5 %copy-start.4 = (s32[16,16]{1,0:T(8,128)S(1)}, s32[16,16]{1,0:T(8,128)}, u32[]{:S(2)}) copy-start(s32[16,16]{1,0:T(8,128)} %cover_in_ref.1) | copy-start | bytes 3076
  0.7 10.5 %copy-start.6 = (s32[128,2]{0,1:T(2,128)S(1)}, s32[128,2]{0,1:T(2,128)}, u32[]{:S(2)}) copy-start(s32[128,2]{0,1:T(2,128)} %param.23) | copy-start | bytes 3076
  0.7 10.5 %copy-start.7 = (s32[128,2]{0,1:T(2,128)S(1)}, s32[128,2]{0,1:T(2,128)}, u32[]{:S(2)}) copy-start(s32[128,2]{0,1:T(2,128)} %param.24) | copy-start | bytes 3076
  0.7 10.5 %copy-start.8 = (s32[128,2]{0,1:T(2,128)S(1)}, s32[128,2]{0,1:T(2,128)}, u32[]{:S(2)}) copy-start(s32[128,2]{0,1:T(2,128)} %param.25) | copy-start | bytes 3076
  0.7 10.5 %copy-start.9 = (s32[128]{0:T(128)S(1)}, s32[128]{0:T(128)}, u32[]{:S(2)}) copy-start(s32[128]{0:T(128)} %batch_ref.1) | copy-start | bytes 1540
  0.7 10.5 %copy-start.10 = (f32[6]{0:T(128)S(1)}, f32[6]{0:T(128)}, u32[]{:S(2)}) copy-start(f32[6]{0:T(128)} %step_ref.1) | copy-start | bytes 76
  0.7 10.5 %copy-start.11 = (s32[2]{0:T(128)S(1)}, s32[2]{0:T(128)}, u32[]{:S(2)}) copy-start(s32[2]{0:T(128)} %lo_ref.1) | copy-start | bytes 28
  0.7 10.5 %copy-start.12 = (s32[2]{0:T(128)S(1)}, s32[2]{0:T(128)}, u32[]{:S(2)}) copy-start(s32[2]{0:T(128)} %hi_ref.1) | copy-start | bytes 28
  0.7 26.0 %copy-start.1 = (bf16[128,16,128]{2,1,0:T(8,128)(2,1)S(1)}, bf16[128,16,128]{2,1,0:T(8,128)(2,1)}, u32[]{:S(2)}) copy-start(bf16[128,16,128]{2,1,0:T(8,128)(2,1)} %seen_ref.3) | copy-start | bytes 1572868
  0.7 25.9 %copy-start.5 = (f32[128]{0:T(128)S(1)}, f32[128]{0:T(128)}, u32[]{:S(2)}) copy-start(f32[128]{0:T(128)} %weight_ref.3) | copy-start | bytes 1540
  3.6 44.7 %copy-start = (f32[2,6,256,128]{3,2,1,0:T(8,128)S(1)}, f32[2,6,256,128]{3,2,1,0:T(8,128)}, u32[]{:S(2)}) copy-start(f32[2,6,256,128]{3,2,1,0:T(8,128)} %param.14) | copy-start | bytes 4718596
  3.6 23.1 %all-to-all-start = ((bf16[16,144,128]{2,1,0:T(8,128)(2,1)}), bf16[16,144,128]{2,1,0:T(8,128)(2,1)S(1)}, u32[]{:S(2)}, u32[]{:S(2)}) async-start(bf16[16,144,128]{2,1,0:T(8,128)(2,1)} %first_send.1), calls=%async_computation | async-start | bytes 1179648 | tf_op jit(solution)/shard_map/all_to_all | solution.py:415
